TPU v7x, 512 devices: a whole 4x4x16 slice. The times are simulated.
512 devices in a mesh: node: 16 (over z_hi, y, core), local: 8 (over z_lo), rep: 4 (over x).
Axes of the slice: x: 4, y: 4, z: 16 (z_hi: 2, z_lo: 8; z = z_hi * 8 + z_lo), core: 2. Of those that a mesh axis runs over, the one named last changes fastest.
Arguments:
- tokens: bfloat16 [8192, 2048], P(('node', 'local', 'rep')), may hold values from -6 to 6
- out_grad: bfloat16 [8192, 2048], P(('node', 'local', 'rep')), may hold values from -6 to 6
- expert_ids: int32 [8192, 8], P(('node', 'local', 'rep')), may hold values from 0 to 127, all different within a row; in each aligned block of 16 rows (0 to 15, 16 to 31, ...) at most 2 rows name the same one
- keep_flags: int32 [8192, 8], P(('node', 'local', 'rep')), may hold values 0 or 1
- route_weights: bfloat16 [8192, 8], P(('node', 'local', 'rep')), may hold values from 0.049804688 to 0.59765625
- gate_w: bfloat16 [128, 768, 2048], P(('node', 'local'), 'rep'), may hold values from -0.125 to 0.125
- up_w: bfloat16 [128, 768, 2048], P(('node', 'local'), 'rep'), may hold values from -0.125 to 0.125
- down_w: bfloat16 [128, 768, 2048], P(('node', 'local'), 'rep'), may hold values from -0.21875 to 0.21875
Outputs:
- input_grad: bfloat16 [8192, 2048], P(('node', 'local', 'rep'))
- route_grad: bfloat16 [8192, 8], P(('node', 'local', 'rep'))
- gate_grad: bfloat16 [128, 768, 2048], P(('node', 'local'), 'rep')
- up_grad: bfloat16 [128, 768, 2048], P(('node', 'local'), 'rep')
- down_grad: bfloat16 [128, 768, 2048], P(('node', 'local'), 'rep')
Inputs may be any that keep to these rules, and one draw needn't show every extreme that they name: `expert_ids`: among the tokens of one device (each aligned block of 16 tokens) no expert is named more than 2 times, a bound that some block reaches. A token names 8 different experts.
All inputs are finite; a program needn't handle non-finite values. No bound on the sum of `keep_flags` on one device may be relied on, other than what follows from the above.
Results may differ from a plain program's by a relative error of at most 0.019.
Values may be sent and summed in bfloat16 or wider, within the bound.
No kernel may reach another device: no remote copies, remote signals or barrier semaphores. Data moves between devices by JAX's collectives and lax.ppermute only.
A program may use at most 64 MiB of HBM per device.

v0:
```python
import jax
import jax.numpy as jnp
from jax import lax
from jax.sharding import PartitionSpec as P


def slot_tables(chosen, kept, groups, capacity, experts):
    width = chosen.shape[0] * chosen.shape[1] // groups
    chosen_g = chosen.reshape(groups, width)
    kept_g = kept.reshape(groups, width)
    order = lax.broadcasted_iota(jnp.int32, (width, width), 1)
    later = lax.broadcasted_iota(jnp.int32, (width, width), 0)
    before = order < later
    matches = (
        (chosen_g[:, :, None] == chosen_g[:, None, :]) & before[None] & (kept_g[:, None, :] > 0)
    )
    position = jnp.sum(matches.astype(jnp.int32), axis=2)
    group_ids = lax.broadcasted_iota(jnp.int32, chosen_g.shape, 0)
    target = chosen_g * (groups * capacity) + group_ids * capacity + position
    target = jnp.where(kept_g > 0, target, -1).reshape(groups * width)
    places = experts * groups * capacity
    hits = (lax.broadcasted_iota(jnp.int32, (places, groups * width), 0) == target[None, :]).astype(
        jnp.bfloat16
    )
    return (hits, target)


def token_matrix(hits, top_count):
    places, slots = hits.shape
    summed = jnp.sum(
        hits.reshape(places, slots // top_count, top_count).astype(jnp.float32), axis=2
    )
    return summed.astype(jnp.bfloat16)


def local(tokens, out_grad, expert_ids, keep_flags, route_weights, gate_w, up_w, down_w):
    node_count = lax.axis_size("node")
    local_count = lax.axis_size("local")
    experts = node_count * local_count
    replicas = lax.axis_size("rep")
    tok_rows, top_count = expert_ids.shape
    features = tokens.shape[1]
    capacity = max(2, min(tok_rows, 2 * tok_rows * top_count // experts))
    slot_width = replicas * capacity
    peer_ids, peer_kept = (
        lax.all_gather(expert_ids, "rep", axis=0, tiled=True),
        lax.all_gather(keep_flags, "rep", axis=0, tiled=True),
    )
    group_hits, group_target = slot_tables(peer_ids, peer_kept, replicas, capacity, experts)
    group_matrix = token_matrix(group_hits, top_count)
    all_tokens, all_grads, all_weights = (
        lax.all_gather(tokens, "rep", axis=0, tiled=True),
        lax.all_gather(out_grad, "rep", axis=0, tiled=True),
        lax.all_gather(route_weights, "rep", axis=0, tiled=True),
    )
    stacked = jnp.concatenate([all_tokens, all_grads], axis=1)
    packed = jnp.dot(group_matrix, stacked, preferred_element_type=jnp.float32).astype(jnp.bfloat16)
    packed = packed.reshape(experts, slot_width, 2 * features)
    coef_rows = jnp.dot(group_hits, all_weights.reshape(-1), preferred_element_type=jnp.float32)
    coef_rows = coef_rows.astype(jnp.bfloat16).reshape(experts, slot_width)
    rows_in, coef_in = (
        lax.all_to_all(packed, ("node", "local"), split_axis=0, concat_axis=0, tiled=True),
        lax.all_to_all(coef_rows, ("node", "local"), split_axis=0, concat_axis=0, tiled=True),
    )
    total_rows = experts * slot_width
    flat = rows_in.reshape(total_rows, 2 * features)
    inputs = flat[:, :features]
    grads_in = flat[:, features:]
    coef_col = coef_in.reshape(total_rows, 1).astype(jnp.float32)
    gate_part = gate_w[0]
    up_part = up_w[0]
    down_part = down_w[0]
    hidden_dev = gate_part.shape[0]
    joined_w = jnp.concatenate([gate_part, up_part], axis=0)
    pre = lax.dot_general(
        inputs, joined_w, (((1,), (1,)), ((), ())), preferred_element_type=jnp.float32
    )
    gate_pre = pre[:, :hidden_dev]
    up_pre = pre[:, hidden_dev:]
    sigma = jax.nn.sigmoid(gate_pre)
    active = gate_pre * sigma
    hidden = (active * up_pre).astype(jnp.bfloat16)
    scaled_grad = (coef_col * grads_in).astype(jnp.bfloat16)
    back_hidden = lax.dot_general(
        grads_in, down_part, (((1,), (1,)), ((), ())), preferred_element_type=jnp.float32
    )
    scores = jnp.sum(hidden.astype(jnp.float32) * back_hidden, axis=1).astype(jnp.bfloat16)
    d_hidden = coef_col * back_hidden
    d_gate = d_hidden * up_pre * sigma * (1.0 + gate_pre * (1.0 - sigma))
    d_up = d_hidden * active
    d_joined = jnp.concatenate([d_gate, d_up], axis=1).astype(jnp.bfloat16)
    grad_down = lax.dot_general(
        hidden, scaled_grad, (((0,), (0,)), ((), ())), preferred_element_type=jnp.float32
    )
    grad_joined = lax.dot_general(
        d_joined, inputs, (((0,), (0,)), ((), ())), preferred_element_type=jnp.float32
    )
    partial_value = jnp.dot(d_joined, joined_w, preferred_element_type=jnp.float32)
    back_rows = partial_value.astype(jnp.bfloat16).reshape(experts, slot_width, features)
    back_scores = scores.reshape(experts, slot_width)
    places = experts * slot_width
    rows_out, scores_out = (
        lax.all_to_all(back_rows, ("node", "local"), split_axis=0, concat_axis=0, tiled=True),
        lax.all_to_all(back_scores, ("node", "local"), split_axis=0, concat_axis=0, tiled=True),
    )
    token_grads = lax.dot_general(
        group_matrix,
        rows_out.reshape(places, features),
        (((0,), (0,)), ((), ())),
        preferred_element_type=jnp.float32,
    )
    flat_scores = scores_out.reshape(places).astype(jnp.float32)
    picked = jnp.take(flat_scores, jnp.maximum(group_target, 0))
    slot_scores = jnp.where(group_target >= 0, picked, 0.0).reshape(replicas * tok_rows, top_count)
    own_grads, own_scores = (
        lax.psum_scatter(
            token_grads.astype(jnp.bfloat16), "rep", scatter_dimension=0, tiled=True
        ).astype(jnp.float32),
        lax.psum_scatter(
            slot_scores.astype(jnp.bfloat16), "rep", scatter_dimension=0, tiled=True
        ).astype(jnp.float32),
    )
    grad_gate = grad_joined[:hidden_dev].astype(jnp.bfloat16)
    grad_up = grad_joined[hidden_dev:].astype(jnp.bfloat16)
    return (
        own_grads.astype(jnp.bfloat16),
        own_scores.astype(jnp.bfloat16),
        grad_gate[None],
        grad_up[None],
        grad_down.astype(jnp.bfloat16)[None],
    )


def solution(mesh):
    placed = (
        P(("node", "local", "rep"), None),
        P(("node", "local", "rep"), None),
        P(("node", "local", "rep"), None),
        P(("node", "local", "rep"), None),
        P(("node", "local", "rep"), None),
        P(("node", "local"), "rep", None),
        P(("node", "local"), "rep", None),
        P(("node", "local"), "rep", None),
    )
    return jax.shard_map(
        local,
        mesh=mesh,
        in_specs=placed,
        out_specs=(
            P(("node", "local", "rep"), None),
            P(("node", "local", "rep"), None),
            P(("node", "local"), "rep", None),
            P(("node", "local"), "rep", None),
            P(("node", "local"), "rep", None),
        ),
        check_vma=False,
    )
```

profile of v0, /device:TPU:6, one launch (start us, length us, event | category | flops | bytes accessed | tf_op | source)
XLA Modules:
  0.0 741.7 jit_solution(4185083102904277462)
XLA Ops:
  7.2 14.9 %all-gather.1 = s32[4,16,8]{1,2,0:T(8,128)S(1)} all-gather(s32[1,16,8]{1,2,0:T(8,128)} %bitcast.50), channel_id=1, replica_groups=mesh['node'=16,'local'=8,'rep'=4] {'rep'}, dimensions={0}, use_global_device_ids=true | all-gather | bytes 2560 | tf_op jit(solution)/shard_map/all_gather | solution.py:46
  22.2 12.1 %all-gather = s32[4,16,8]{1,2,0:T(8,128)S(1)} all-gather(s32[1,16,8]{1,2,0:T(8,128)} %bitcast.51), channel_id=1, replica_groups=mesh['node'=16,'local'=8,'rep'=4] {'rep'}, dimensions={0}, use_global_device_ids=true | all-gather | bytes 2560 | tf_op jit(solution)/shard_map/all_gather | solution.py:47
  34.5 10.3 %all-gather.2 = bf16[4,16,8]{1,2,0:T(8,128)(2,1)S(1)} all-gather(bf16[1,16,8]{1,2,0:T(8,128)(2,1)} %bitcast.53), channel_id=1, replica_groups=mesh['node'=16,'local'=8,'rep'=4] {'rep'}, dimensions={0}, use_global_device_ids=true | all-gather | bytes 1280 | tf_op jit(solution)/shard_map/all_gather | solution.py:54
  46.0 0.8 all_to_all.21
  46.8 17.2 %all-to-all-start = ((bf16[128,1,8]{2,1,0:T(2,128)(2,1)}), bf16[128,1,8]{2,1,0:T(2,128)(2,1)S(1)}, u32[]{:S(2)}, u32[]{:S(2)}) async-start(bf16[128,1,8]{2,1,0:T(2,128)(2,1)} %all_to_all.21), calls=%async_computation | async-start | bytes 131072 | tf_op jit(solution)/shard_map/all_to_all | solution.py:63
  65.4 12.6 %all_gather.18 = bf16[64,2048]{1,0:T(8,128)(2,1)S(1)} all-gather(bf16[16,2048]{1,0:T(8,128)(2,1)} %param.8), channel_id=1, replica_groups=mesh['node'=16,'local'=8,'rep'=4] {'rep'}, dimensions={0}, use_global_device_ids=true | all-gather | bytes 327680 | tf_op jit(solution)/shard_map/all_gather | solution.py:52
  78.0 12.5 %all_gather.19 = bf16[64,2048]{1,0:T(8,128)(2,1)S(1)} all-gather(bf16[16,2048]{1,0:T(8,128)(2,1)} %param.9), channel_id=1, replica_groups=mesh['node'=16,'local'=8,'rep'=4] {'rep'}, dimensions={0}, use_global_device_ids=true | all-gather | bytes 327680 | tf_op jit(solution)/shard_map/all_gather | solution.py:53
  90.4 5.6 convert_bitcast_fusion
  96.0 17.0 %all-to-all-start.1 = ((bf16[128,8,4096]{2,1,0:T(8,128)(2,1)}), bf16[128,8,4096]{2,1,0:T(8,128)(2,1)}, u32[]{:S(2)}, u32[]{:S(2)}) async-start(bf16[128,8,4096]{2,1,0:T(8,128)(2,1)} %convert_bitcast_fusion), calls=%async_computation.1 | async-start | bytes 16777216 | tf_op jit(solution)/shard_map/all_to_all | solution.py:62
  113.3 363.5 %all-to-all-done.1 = bf16[128,8,4096]{2,1,0:T(8,128)(2,1)} async-done(((bf16[128,8,4096]{2,1,0:T(8,128)(2,1)}), bf16[128,8,4096]{2,1,0:T(8,128)(2,1)}, u32[]{:S(2)}, u32[]{:S(2)}) %all-to-all-start.1) | async-done | bytes 8388640 | tf_op jit(solution)/shard_map/all_to_all | solution.py:62
  476.8 4.0 fusion.6
  480.9 4.8 multiply_reduce_fusion
  486.4 13.3 %all-to-all-start.3 = ((bf16[128,1,8]{2,1,0:T(2,128)(2,1)}), bf16[128,1,8]{2,1,0:T(2,128)(2,1)S(1)}, u32[]{:S(2)}, u32[]{:S(2)}) async-start(bf16[128,1,8]{2,1,0:T(2,128)(2,1)} %convert_element_type.97), calls=%async_computation.4 | async-start | bytes 131072 | tf_op jit(solution)/shard_map/all_to_all | solution.py:104
  499.7 4.3 convert_bitcast_fusion.1
  504.0 11.0 %all-to-all-done.3 = bf16[128,1,8]{2,1,0:T(2,128)(2,1)S(1)} async-done(((bf16[128,1,8]{2,1,0:T(2,128)(2,1)}), bf16[128,1,8]{2,1,0:T(2,128)(2,1)S(1)}, u32[]{:S(2)}, u32[]{:S(2)}) %all-to-all-start.3) | async-done | bytes 2080 | tf_op jit(solution)/shard_map/all_to_all | solution.py:104
  515.0 7.5 %all-to-all-start.2 = ((bf16[128,8,2048]{2,1,0:T(8,128)(2,1)}), bf16[128,8,2048]{2,1,0:T(8,128)(2,1)}, u32[]{:S(2)}, u32[]{:S(2)}) async-start(bf16[128,8,2048]{2,1,0:T(8,128)(2,1)} %convert_bitcast_fusion.1), calls=%async_computation.2 | async-start | bytes 8388608 | tf_op jit(solution)/shard_map/all_to_all | solution.py:103
  522.9 4.0 fusion.11
  527.2 3.5 gather_fusion
  531.7 177.0 %all-to-all-done.2 = bf16[128,8,2048]{2,1,0:T(8,128)(2,1)} async-done(((bf16[128,8,2048]{2,1,0:T(8,128)(2,1)}), bf16[128,8,2048]{2,1,0:T(8,128)(2,1)}, u32[]{:S(2)}, u32[]{:S(2)}) %all-to-all-start.2) | async-done | bytes 4194336 | tf_op jit(solution)/shard_map/all_to_all | solution.py:103
  708.7 3.7 fusion.16
  712.5 4.2 fusion.15
  716.7 1.2 slice_bitcast_fusion
  717.9 1.3 copy.55
  719.2 15.7 %reduce-scatter.5.cloned.1.call-done = bf16[16,2048]{1,0:T(8,128)(2,1)} async-done(((bf16[64,2048]{1,0:T(8,128)(2,1)}), bf16[16,2048]{1,0:T(8,128)(2,1)}) %reduce-scatter.5.cloned.1.call-update) | async-done | bytes 65552 | tf_op jit(solution)/shard_map/reduce_scatter | solution.py:116
  (60 shorter events, 5.5 us)
Async XLA Ops:
  7.2 473.7 %copy-start = (bf16[1,192,2048]{2,1,0:T(8,128)(2,1)S(1)}, bf16[1,192,2048]{2,1,0:T(8,128)(2,1)}, u32[]{:S(2)}) copy-start(bf16[1,192,2048]{2,1,0:T(8,128)(2,1)} %param.15) | copy-start | bytes 2359300
  46.8 49.2 %all-to-all-start = ((bf16[128,1,8]{2,1,0:T(2,128)(2,1)}), bf16[128,1,8]{2,1,0:T(2,128)(2,1)S(1)}, u32[]{:S(2)}, u32[]{:S(2)}) async-start(bf16[128,1,8]{2,1,0:T(2,128)(2,1)} %all_to_all.21), calls=%async_computation | async-start | bytes 131072 | tf_op jit(solution)/shard_map/all_to_all | solution.py:63
  96.0 380.8 %copy-start.1 = (bf16[1,192,2048]{2,1,0:T(8,128)(2,1)S(1)}, bf16[1,192,2048]{2,1,0:T(8,128)(2,1)}, u32[]{:S(2)}) copy-start(bf16[1,192,2048]{2,1,0:T(8,128)(2,1)} %param.14) | copy-start | bytes 2359300
  96.0 380.8 %copy-start.2 = (bf16[1,192,2048]{2,1,0:T(8,128)(2,1)S(1)}, bf16[1,192,2048]{2,1,0:T(8,128)(2,1)}, u32[]{:S(2)}) copy-start(bf16[1,192,2048]{2,1,0:T(8,128)(2,1)} %param.13) | copy-start | bytes 2359300
  96.0 380.8 %all-to-all-start.1 = ((bf16[128,8,4096]{2,1,0:T(8,128)(2,1)}), bf16[128,8,4096]{2,1,0:T(8,128)(2,1)}, u32[]{:S(2)}, u32[]{:S(2)}) async-start(bf16[128,8,4096]{2,1,0:T(8,128)(2,1)} %convert_bitcast_fusion), calls=%async_computation.1 | async-start | bytes 16777216 | tf_op jit(solution)/shard_map/all_to_all | solution.py:62
  485.6 18.4 %copy-start.3 = (bf16[1024,192]{0,1:T(8,128)(2,1)}, bf16[1024,192]{0,1:T(8,128)(2,1)S(1)}, u32[]{:S(2)}) copy-start(bf16[1024,192]{0,1:T(8,128)(2,1)S(1)} %get-tuple-element.9) | copy-start | bytes 1179652
  486.4 28.6 %all-to-all-start.3 = ((bf16[128,1,8]{2,1,0:T(2,128)(2,1)}), bf16[128,1,8]{2,1,0:T(2,128)(2,1)S(1)}, u32[]{:S(2)}, u32[]{:S(2)}) async-start(bf16[128,1,8]{2,1,0:T(2,128)(2,1)} %convert_element_type.97), calls=%async_computation.4 | async-start | bytes 131072 | tf_op jit(solution)/shard_map/all_to_all | solution.py:104
  515.0 7.9 %copy-start.4 = (bf16[1024,192]{0,1:T(8,128)(2,1)S(1)}, bf16[1024,192]{0,1:T(8,128)(2,1)}, u32[]{:S(2)}) copy-start(bf16[1024,192]{0,1:T(8,128)(2,1)} %copy-done.3) | copy-start | bytes 1179652
  515.0 193.7 %all-to-all-start.2 = ((bf16[128,8,2048]{2,1,0:T(8,128)(2,1)}), bf16[128,8,2048]{2,1,0:T(8,128)(2,1)}, u32[]{:S(2)}, u32[]{:S(2)}) async-start(bf16[128,8,2048]{2,1,0:T(8,128)(2,1)} %convert_bitcast_fusion.1), calls=%async_computation.2 | async-start | bytes 8388608 | tf_op jit(solution)/shard_map/all_to_all | solution.py:103
  522.6 195.3 %reduce-scatter.7.cloned.1.call-start = ((), (), s32[]{:S(2)}) async-start(), calls=%async_computation.7 | async-start | bytes 20480
  526.9 185.6 %copy-start.5 = (bf16[1024,192]{0,1:T(8,128)(2,1)S(1)}, bf16[1024,192]{0,1:T(8,128)(2,1)}, u32[]{:S(2)}) copy-start(bf16[1024,192]{0,1:T(8,128)(2,1)} %get-tuple-element.6) | copy-start | bytes 1179652
  531.6 203.3 %reduce-scatter.5.cloned.1.call-start = ((), (), s32[]{:S(2)}) async-start(), calls=%async_computation.6 | async-start | bytes 327680 | tf_op jit(solution)/shard_map/reduce_scatter | solution.py:116
Sparse Core Ops, SparseCore 0:
  531.8 27.1 reduce-scatter.6
  712.6 22.2 reduce-scatter.4
where the time goes:
time: 744 us; the launch traced here: 742 us
  waiting for transfers between devices  567 us (76%)
  blocking collectives  62.3 us (8%)
  starting transfers between devices  55.1 us (7%)
  matrix products  31.1 us (4%)
  between operations  14.2 us (2%)
  local copies, waits for them, and re-layouts  10.3 us (1%)
    all_to_all x1, waiting for transfers between devices, local(): lax.all_to_all(packed, ('node', 'local'), split_axis=0, concat_axis=0, ti...  364 us
    all_to_all x1, waiting for transfers between devices, local(): lax.all_to_all(back_rows, ('node', 'local'), split_axis=0, concat_axis=0,...  177 us
    all_to_all x1, starting transfers between devices, local(): lax.all_to_all(coef_rows, ('node', 'local'), split_axis=0, concat_axis=0,...  17.2 us
    all_to_all x1, starting transfers between devices, local(): lax.all_to_all(packed, ('node', 'local'), split_axis=0, concat_axis=0, ti...  17 us
    reduce_scatter x1, waiting for transfers between devices, local(): lax.psum_scatter(token_grads.astype(jnp.bfloat16), 'rep', scatter_dimensi...  15.7 us
    all_gather x1, blocking collectives, local(): lax.all_gather(expert_ids, 'rep', axis=0, tiled=True)  14.9 us
  transfers between devices with their start and end apart: 6, of which 4 were waited for; matrix products, arithmetic and copies ran while one was open for 4% of the time, Pallas kernels for 0%

commit v1 on v0

v1 whole, which is shorter than its diff:
```python
import jax
import jax.numpy as jnp
from jax import lax
from jax.sharding import PartitionSpec as P

BF = jnp.bfloat16
F32 = jnp.float32


def dot(a, b, da, db):
    return lax.dot_general(a, b, (((da,), (db,)), ((), ())), preferred_element_type=F32)


def slots_of(ids, keep, capacity):
    width = ids.shape[0] * ids.shape[1]
    chosen = ids.reshape(width)
    kept = keep.reshape(width) > 0
    other = lax.broadcasted_iota(jnp.int32, (width, width), 1)
    own = lax.broadcasted_iota(jnp.int32, (width, width), 0)
    earlier = (other < own) & (chosen[:, None] == chosen[None, :]) & kept[None, :]
    position = jnp.sum(earlier.astype(jnp.int32), axis=1)
    return jnp.where(kept, chosen * capacity + position, -1)


def ring(step, n):
    return [(i, (i + step) % n) for i in range(n)]


def spread(block, axis, n):
    half = block.shape[0] // 2
    left = lax.ppermute(block, axis, ring(1, n))
    right = lax.ppermute(block, axis, ring(-1, n))
    far_a = lax.ppermute(right[:half], axis, ring(-1, n))
    far_b = lax.ppermute(left[half:], axis, ring(1, n))
    return block, left, right, jnp.concatenate([far_a, far_b], axis=0)


def collect(own, to_left, to_right, to_far, axis, n):
    half = own.shape[0] // 2
    far_a = lax.ppermute(to_far[:half], axis, ring(1, n))
    far_b = lax.ppermute(to_far[half:], axis, ring(-1, n))
    to_right = jnp.concatenate(
        [(to_right[:half].astype(F32) + far_a.astype(F32)).astype(BF), to_right[half:]], axis=0
    )
    to_left = jnp.concatenate(
        [to_left[:half], (to_left[half:].astype(F32) + far_b.astype(F32)).astype(BF)], axis=0
    )
    from_left = lax.ppermute(to_right, axis, ring(1, n))
    from_right = lax.ppermute(to_left, axis, ring(-1, n))
    return (own + from_left.astype(F32) + from_right.astype(F32)).astype(BF)


def local(tokens, out_grad, expert_ids, keep_flags, route_weights, gate_w, up_w, down_w):
    experts = lax.axis_size("node") * lax.axis_size("local")
    n = lax.axis_size("rep")
    tok_rows, top = expert_ids.shape
    features = tokens.shape[1]
    capacity = 2
    places = experts * capacity
    hidden_dev = gate_w.shape[1]
    slots = tok_rows * top

    target = slots_of(expert_ids, keep_flags, capacity)
    hits = lax.broadcasted_iota(jnp.int32, (places, slots), 0) == target[None, :]
    by_slot = hits.astype(BF)
    by_token = jnp.sum(hits.reshape(places, tok_rows, top).astype(F32), axis=2).astype(BF)

    rows = dot(by_token, jnp.concatenate([tokens, out_grad], axis=1), 1, 0).astype(BF)
    coef = jnp.sum(
        jnp.where(hits, route_weights.reshape(1, slots).astype(F32), 0.0), axis=1, keepdims=True
    ).astype(BF)
    packed = jnp.concatenate([rows, jnp.broadcast_to(coef, (places, 128))], axis=1)
    sent = lax.all_to_all(
        packed.reshape(experts, capacity, 2 * features + 128),
        ("node", "local"),
        split_axis=0,
        concat_axis=0,
        tiled=True,
    )

    gu_own = jnp.concatenate([gate_w[0], up_w[0]], axis=0)
    gu = jnp.concatenate(spread(gu_own, "rep", n), axis=0)
    dn = jnp.concatenate(spread(down_w[0], "rep", n), axis=0)

    flat = sent.reshape(places, 2 * features + 128)
    inputs = flat[:, :features]
    grads_in = flat[:, features : 2 * features]
    coef_col = flat[:, 2 * features : 2 * features + 1].astype(F32)
    scaled = (coef_col * grads_in.astype(F32)).astype(BF)

    pre = dot(inputs, gu, 1, 1).reshape(places, n, 2, hidden_dev)
    back = dot(grads_in, dn, 1, 1).reshape(places, n, hidden_dev)
    gate_pre, up_pre = pre[:, :, 0], pre[:, :, 1]
    sigma = jax.nn.sigmoid(gate_pre)
    active = gate_pre * sigma
    hidden = (active * up_pre).astype(BF)
    score = jnp.sum(hidden.astype(F32) * back, axis=(1, 2)).astype(BF)
    d_hidden = coef_col[:, :, None] * back
    d_gate = (d_hidden * up_pre * sigma * (1.0 + gate_pre * (1.0 - sigma))).astype(BF)
    d_up = (d_hidden * active).astype(BF)
    d_gu = jnp.stack([d_gate, d_up], axis=2)

    def gu_grad(i):
        return dot(d_gu[:, i].reshape(places, 2 * hidden_dev), inputs, 0, 0)

    def down_grad(i):
        return dot(hidden[:, i], scaled, 0, 0)

    part = [gu_grad(i) for i in range(n)]
    part_d = [down_grad(i) for i in range(n)]
    grad_gu = collect(part[0], *[p.astype(BF) for p in part[1:]], "rep", n)
    grad_dn = collect(part_d[0], *[p.astype(BF) for p in part_d[1:]], "rep", n)

    back_rows = dot(d_gu.reshape(places, n * 2 * hidden_dev), gu, 1, 0).astype(BF)
    back_pack = jnp.concatenate(
        [back_rows, jnp.broadcast_to(score[:, None], (places, 128))], axis=1
    )
    home = lax.all_to_all(
        back_pack.reshape(experts, capacity, features + 128),
        ("node", "local"),
        split_axis=0,
        concat_axis=0,
        tiled=True,
    ).reshape(places, features + 128)
    token_grad = dot(by_token, home[:, :features], 0, 0).astype(BF)
    slot_score = dot(by_slot, home[:, features:], 0, 0)[:, 0].reshape(tok_rows, top).astype(BF)
    return (
        token_grad,
        slot_score,
        grad_gu[:hidden_dev][None],
        grad_gu[hidden_dev:][None],
        grad_dn[None],
    )


def solution(mesh):
    by_row = P(("node", "local", "rep"), None)
    by_expert = P(("node", "local"), "rep", None)
    return jax.shard_map(
        local,
        mesh=mesh,
        in_specs=(by_row,) * 5 + (by_expert,) * 3,
        out_specs=(by_row,) * 2 + (by_expert,) * 3,
        check_vma=False,
    )
```

time: 744 us -> 275 us (0.37)
  waiting for transfers between devices: 567 us -> 134 us
  blocking collectives: 62.3 us -> 0 us
  starting transfers between devices: 55.1 us -> 77.7 us
  local copies, waits for them, and re-layouts: 10.3 us -> 26.8 us
  between operations: 14.2 us -> 1.38 us
  matrix products: 31.1 us -> 23.1 us
    all_to_all x4 -> x2, waiting for transfers between devices: 552 us -> 11.6 us  [the longest x1 11.6 us: local(): lax.all_to_all(packed.reshape(experts, capacity, 2 * features + 128), ('n...]
    ppermute x0 -> x16, waiting for transfers between devices: none -> 123 us  [the longest x2 44.2 us: spread(): right = lax.ppermute(block, axis, ring(-1, n))]
    all_gather x5 -> x0, blocking collectives: 62.3 us -> none  [the longest x1 14.9 us: local(): lax.all_gather(expert_ids, 'rep', axis=0, tiled=True)]
    ppermute x0 -> x16, starting transfers between devices: none -> 49.6 us  [the longest x2 8.19 us: collect(): from_left = lax.ppermute(to_right, axis, ring(1, n))]
    all_to_all x4 -> x2, starting transfers between devices: 55 us -> 28.1 us  [the longest x1 20.6 us: local(): lax.all_to_all(packed.reshape(experts, capacity, 2 * features + 128), ('n...]
    reduce_scatter x1 -> x0, waiting for transfers between devices: 15.7 us -> none  [local(): lax.psum_scatter(token_grads.astype(jnp.bfloat16), 'rep', scatter_dimensi...]
    dot_general x8 -> x14, matrix products: 31.1 us -> 23.1 us  [dot(): lax.dot_general(a, b, (((da,), (db,)), ((), ())), preferred_element_type=...]
    unnamed x14 -> x40, local copies, waits for them, and re-layouts: 2.06 us -> 9.96 us
  transfers between devices with their start and end apart: 6 -> 18, of which waited for: 4 -> 9; matrix products, arithmetic and copies ran while one was open for 4% -> 6% of each run, Pallas kernels for 0% -> 0%
where the time goes in v1:
time: 275 us; the launch traced here: 271 us
  waiting for transfers between devices  134 us (49%)
  starting transfers between devices  77.7 us (28%)
  local copies, waits for them, and re-layouts  26.8 us (10%)
  matrix products  23.1 us (8%)
  other arithmetic  7.03 us (3%)
    ppermute x2, waiting for transfers between devices, spread(): right = lax.ppermute(block, axis, ring(-1, n))  44.2 us
    ppermute x2, waiting for transfers between devices, collect(): from_left = lax.ppermute(to_right, axis, ring(1, n))  39 us
    dot_general x14, matrix products, dot(): lax.dot_general(a, b, (((da,), (db,)), ((), ())), preferred_element_type=...  23.1 us
    all_to_all x1, starting transfers between devices, local(): lax.all_to_all(packed.reshape(experts, capacity, 2 * features + 128), ('n...  20.6 us
    ppermute x2, waiting for transfers between devices, collect(): far_b = lax.ppermute(to_far[half:], axis, ring(-1, n))  15.3 us
    ppermute x2, waiting for transfers between devices, spread(): far_a = lax.ppermute(right[:half], axis, ring(-1, n))  15.1 us
    all_to_all x1, waiting for transfers between devices, local(): lax.all_to_all(packed.reshape(experts, capacity, 2 * features + 128), ('n...  11.6 us
    unnamed x40, local copies, waits for them, and re-layouts  9.96 us
  transfers between devices with their start and end apart: 18, of which 9 were waited for; matrix products, arithmetic and copies ran while one was open for 6% of the time, Pallas kernels for 0%

profile of v1, /device:TPU:6, one launch (start us, length us, event | category | flops | bytes accessed | tf_op | source)
XLA Modules:
  0.0 270.5 jit_solution(15718525599385208088)
XLA Ops:
  7.9 20.6 %all-to-all-start = ((bf16[128,2,4224]{2,1,0:T(2,128)(2,1)}), bf16[128,2,4224]{2,1,0:T(2,128)(2,1)}, u32[]{:S(2)}, u32[]{:S(2)}) async-start(bf16[128,2,4224]{2,1,0:T(2,128)(2,1)} %reshape.94), calls=%async_computation | async-start | bytes 4325376 | tf_op jit(solution)/shard_map/all_to_all | solution.py:73
  28.6 2.5 collective-permute-start.4
  31.1 3.5 %collective-permute-start.5 = (bf16[384,2048]{1,0:T(8,128)(2,1)S(1)}, bf16[384,2048]{1,0:T(8,128)(2,1)S(1)}, u32[]{:S(2)}, u32[]{:S(2)}) collective-permute-start(bf16[384,2048]{1,0:T(8,128)(2,1)S(1)} %pad_maximum_fusion.1), channel_id=1, source_target_pairs={{0,3},{1,0},{2,1},{3,2},{4,7},{5,4},{6,5},{7,6},{8,11},{9,8},{10,9... | collective-permute-start | bytes 4718600 | tf_op jit(solution)/shard_map/ppermute | solution.py:32
  34.6 3.6 %collective-permute-start = (bf16[192,2048]{1,0:T(8,128)(2,1)S(1)}, bf16[192,2048]{1,0:T(8,128)(2,1)S(1)}, u32[]{:S(2)}, u32[]{:S(2)}) collective-permute-start(bf16[192,2048]{1,0:T(8,128)(2,1)S(1)} %bitcast.104), channel_id=1, source_target_pairs={{0,1},{1,2},{2,3},{3,0},{4,5},{5,6},{6,7},{7,4},{8,9},{9,10},{10,1... | collective-permute-start | bytes 2359304 | tf_op jit(solution)/shard_map/ppermute | solution.py:31
  42.5 44.2 %collective-permute-done.1 = bf16[192,2048]{1,0:T(8,128)(2,1)S(1)} collective-permute-done((bf16[192,2048]{1,0:T(8,128)(2,1)S(1)}, bf16[192,2048]{1,0:T(8,128)(2,1)S(1)}, u32[]{:S(2)}, u32[]{:S(2)}) %collective-permute-start.1) | collective-permute-done | bytes 786464 | tf_op jit(solution)/shard_map/ppermute | solution.py:32
  89.0 4.8 %collective-permute-start.3 = (bf16[96,2048]{1,0:T(8,128)(2,1)S(1)}, bf16[96,2048]{1,0:T(8,128)(2,1)S(1)}, u32[]{:S(2)}, u32[]{:S(2)}) collective-permute-start(bf16[96,2048]{1,0:T(8,128)(2,1)S(1)} %slice.140), channel_id=1, source_target_pairs={{0,1},{1,2},{2,3},{3,0},{4,5},{5,6},{6,7},{7,4},{8,9},{9,10},{10,1... | collective-permute-start | bytes 1179656 | tf_op jit(solution)/shard_map/ppermute | solution.py:34
  95.9 5.0 %collective-permute-done.2 = bf16[96,2048]{1,0:T(8,128)(2,1)S(1)} collective-permute-done((bf16[96,2048]{1,0:T(8,128)(2,1)S(1)}, bf16[96,2048]{1,0:T(8,128)(2,1)S(1)}, u32[]{:S(2)}, u32[]{:S(2)}) %collective-permute-start.2) | collective-permute-done | bytes 393248 | tf_op jit(solution)/shard_map/ppermute | solution.py:33
  105.9 10.2 %collective-permute-done.6 = bf16[192,2048]{1,0:T(8,128)(2,1)S(1)} collective-permute-done((bf16[192,2048]{1,0:T(8,128)(2,1)S(1)}, bf16[192,2048]{1,0:T(8,128)(2,1)S(1)}, u32[]{:S(2)}, u32[]{:S(2)}) %collective-permute-start.6) | collective-permute-done | bytes 786464 | tf_op jit(solution)/shard_map/ppermute | solution.py:33
  119.3 11.6 %all-to-all-done = bf16[128,2,4224]{2,1,0:T(2,128)(2,1)} async-done(((bf16[128,2,4224]{2,1,0:T(2,128)(2,1)}), bf16[128,2,4224]{2,1,0:T(2,128)(2,1)}, u32[]{:S(2)}, u32[]{:S(2)}) %all-to-all-start) | async-done | bytes 2162720 | tf_op jit(solution)/shard_map/all_to_all | solution.py:73
  130.9 2.8 %reshape.95 = bf16[256,4224]{1,0:T(8,128)(2,1)S(1)} reshape(bf16[128,2,4224]{2,1,0:T(2,128)(2,1)} %all-to-all-done) | data formatting | bytes 4325376 | tf_op jit(solution)/shard_map/reshape | solution.py:85
  133.8 4.7 %fusion.22 = f32[256,1536]{0,1:T(8,128)S(1)} fusion(bf16[1536,2048]{1,0:T(8,128)(2,1)} %constant_dynamic-update-slice_fusion.5, bf16[256,4224]{1,0:T(8,128)(2,1)S(1)} %reshape.95), kind=kOutput, calls=%fused_computation.65 | convolution fusion | flops 1610612736 | bytes 8912896 | tf_op jit(solution)/shard_map/dot_general | solution.py:11
  144.0 4.2 %multiply_reduce_fusion = (bf16[256]{0:T(256)(128)(2,1)S(1)}, f32[256,768]{1,0:T(8,128)}) fusion(f32[256,768]{1,0:T(8,128)} %copy.58, f32[256,768]{1,0:T(8,128)} %copy.57, bf16[768,2048]{1,0:T(8,128)(2,1)} %copy-done.13, bf16[256,4224]{1,0:T(8,128)(2,1)S(1)} %reshape.95), kind=kOutput, calls=%fused_computation.58 | convolution fusion | flops 807075584 | bytes 6554112 | tf_op jit(solution)/shard_map/dot_general | solution.py:11
  156.0 4.6 %convolution_convert_fusion.4 = bf16[256,2048]{1,0:T(8,128)(2,1)S(1)} fusion(bf16[256,1536]{0,1:T(8,128)(2,1)S(1)} %bitcast.97, bf16[1536,2048]{1,0:T(8,128)(2,1)} %constant_dynamic-update-slice_fusion.5), kind=kOutput, calls=%fused_computation.5 | convolution fusion | flops 1611137024 | bytes 8126464 | tf_op jit(solution)/shard_map/dot_general | solution.py:11
  162.1 7.5 %all-to-all-start.1 = ((bf16[128,2,2176]{2,1,0:T(2,128)(2,1)}), bf16[128,2,2176]{2,1,0:T(2,128)(2,1)S(1)}, u32[]{:S(2)}, u32[]{:S(2)}) async-start(bf16[128,2,2176]{2,1,0:T(2,128)(2,1)} %reshape.99), calls=%async_computation.1 | async-start | bytes 2228224 | tf_op jit(solution)/shard_map/all_to_all | solution.py:118
  171.4 2.9 %collective-permute-start.10 = (bf16[192,2048]{1,0:T(8,128)(2,1)S(1)}, bf16[192,2048]{1,0:T(8,128)(2,1)S(1)}, u32[]{:S(2)}, u32[]{:S(2)}) collective-permute-start(bf16[192,2048]{1,0:T(8,128)(2,1)S(1)} %get-tuple-element.30), channel_id=1, source_target_pairs={{0,3},{1,0},{2,1},{3,2},{4,7},{5,4},{6,5},{7,6},{8,11},{9,8},{10,9... | collective-permute-start | bytes 2359304 | tf_op jit(solution)/shard_map/ppermute | solution.py:41
  178.2 4.7 %collective-permute-start.8 = (bf16[192,2048]{1,0:T(8,128)(2,1)S(1)}, bf16[192,2048]{1,0:T(8,128)(2,1)S(1)}, u32[]{:S(2)}, u32[]{:S(2)}) collective-permute-start(bf16[192,2048]{1,0:T(8,128)(2,1)S(1)} %get-tuple-element.29), channel_id=1, source_target_pairs={{0,1},{1,2},{2,3},{3,0},{4,5},{5,6},{6,7},{7,4},{8,9},{9,10},{10,1... | collective-permute-start | bytes 2359304 | tf_op jit(solution)/shard_map/ppermute | solution.py:40
  183.4 3.3 %collective-permute-start.12 = (bf16[96,2048]{1,0:T(8,128)(2,1)S(1)}, bf16[96,2048]{1,0:T(8,128)(2,1)S(1)}, u32[]{:S(2)}, u32[]{:S(2)}) collective-permute-start(bf16[96,2048]{1,0:T(8,128)(2,1)S(1)} %get-tuple-element.33), channel_id=1, source_target_pairs={{0,1},{1,2},{2,3},{3,0},{4,5},{5,6},{6,7},{7,4},{8,9},{9,10},{10,1... | collective-permute-start | bytes 1179656 | tf_op jit(solution)/shard_map/ppermute | solution.py:40
  186.8 15.3 %collective-permute-done.14 = bf16[96,2048]{1,0:T(8,128)(2,1)S(1)} collective-permute-done((bf16[96,2048]{1,0:T(8,128)(2,1)S(1)}, bf16[96,2048]{1,0:T(8,128)(2,1)S(1)}, u32[]{:S(2)}, u32[]{:S(2)}) %collective-permute-start.14) | collective-permute-done | bytes 393248 | tf_op jit(solution)/shard_map/ppermute | solution.py:41
  204.2 3.1 %collective-permute-done.12 = bf16[96,2048]{1,0:T(8,128)(2,1)S(1)} collective-permute-done((bf16[96,2048]{1,0:T(8,128)(2,1)S(1)}, bf16[96,2048]{1,0:T(8,128)(2,1)S(1)}, u32[]{:S(2)}, u32[]{:S(2)}) %collective-permute-start.12) | collective-permute-done | bytes 393248 | tf_op jit(solution)/shard_map/ppermute | solution.py:40
  207.9 3.3 %collective-permute-start.11 = (bf16[384,2048]{1,0:T(8,128)(2,1)S(1)}, bf16[384,2048]{1,0:T(8,128)(2,1)S(1)}, u32[]{:S(2)}, u32[]{:S(2)}) collective-permute-start(bf16[384,2048]{1,0:T(8,128)(2,1)S(1)} %pad_maximum_fusion.3), channel_id=1, source_target_pairs={{0,3},{1,0},{2,1},{3,2},{4,7},{5,4},{6,5},{7,6},{8,11},{9,8},{10,9... | collective-permute-start | bytes 4718600 | tf_op jit(solution)/shard_map/ppermute | solution.py:49
  211.7 4.3 %collective-permute-start.9 = (bf16[384,2048]{1,0:T(8,128)(2,1)S(1)}, bf16[384,2048]{1,0:T(8,128)(2,1)S(1)}, u32[]{:S(2)}, u32[]{:S(2)}) collective-permute-start(bf16[384,2048]{1,0:T(8,128)(2,1)S(1)} %pad_maximum_fusion.2), channel_id=1, source_target_pairs={{0,1},{1,2},{2,3},{3,0},{4,5},{5,6},{6,7},{7,4},{8,9},{9,10},{10,1... | collective-permute-start | bytes 4718600 | tf_op jit(solution)/shard_map/ppermute | solution.py:48
  216.0 3.9 %collective-permute-start.13 = (bf16[192,2048]{1,0:T(8,128)(2,1)S(1)}, bf16[192,2048]{1,0:T(8,128)(2,1)S(1)}, u32[]{:S(2)}, u32[]{:S(2)}) collective-permute-start(bf16[192,2048]{1,0:T(8,128)(2,1)S(1)} %pad_maximum_fusion.6), channel_id=1, source_target_pairs={{0,1},{1,2},{2,3},{3,0},{4,5},{5,6},{6,7},{7,4},{8,9},{9,10},{10,1... | collective-permute-start | bytes 2359304 | tf_op jit(solution)/shard_map/ppermute | solution.py:48
  221.0 4.9 %collective-permute-done.15 = bf16[192,2048]{1,0:T(8,128)(2,1)S(1)} collective-permute-done((bf16[192,2048]{1,0:T(8,128)(2,1)S(1)}, bf16[192,2048]{1,0:T(8,128)(2,1)S(1)}, u32[]{:S(2)}, u32[]{:S(2)}) %collective-permute-start.15) | collective-permute-done | bytes 786464 | tf_op jit(solution)/shard_map/ppermute | solution.py:49
  225.9 39.0 %collective-permute-done.13 = bf16[192,2048]{1,0:T(8,128)(2,1)S(1)} collective-permute-done((bf16[192,2048]{1,0:T(8,128)(2,1)S(1)}, bf16[192,2048]{1,0:T(8,128)(2,1)S(1)}, u32[]{:S(2)}, u32[]{:S(2)}) %collective-permute-start.13) | collective-permute-done | bytes 786464 | tf_op jit(solution)/shard_map/ppermute | solution.py:48
  (123 shorter events, 54.8 us)
Async XLA Ops:
  7.9 20.6 %copy-start.2 = (bf16[1,192,2048]{2,1,0:T(8,128)(2,1)S(1)}, bf16[1,192,2048]{2,1,0:T(8,128)(2,1)}, u32[]{:S(2)}) copy-start(bf16[1,192,2048]{2,1,0:T(8,128)(2,1)} %param.13) | copy-start | bytes 2359300
  7.9 20.6 %copy-start.3 = (bf16[1,192,2048]{2,1,0:T(8,128)(2,1)S(1)}, bf16[1,192,2048]{2,1,0:T(8,128)(2,1)}, u32[]{:S(2)}) copy-start(bf16[1,192,2048]{2,1,0:T(8,128)(2,1)} %param.14) | copy-start | bytes 2359300
  7.9 123.0 %all-to-all-start = ((bf16[128,2,4224]{2,1,0:T(2,128)(2,1)}), bf16[128,2,4224]{2,1,0:T(2,128)(2,1)}, u32[]{:S(2)}, u32[]{:S(2)}) async-start(bf16[128,2,4224]{2,1,0:T(2,128)(2,1)} %reshape.94), calls=%async_computation | async-start | bytes 4325376 | tf_op jit(solution)/shard_map/all_to_all | solution.py:73
  28.6 12.9 %copy-start.4 = (bf16[1,192,2048]{2,1,0:T(8,128)(2,1)S(1)}, bf16[1,192,2048]{2,1,0:T(8,128)(2,1)}, u32[]{:S(2)}) copy-start(bf16[1,192,2048]{2,1,0:T(8,128)(2,1)} %param.14) | copy-start | bytes 2359300
  28.6 72.3 %collective-permute-start.4 = (bf16[384,2048]{1,0:T(8,128)(2,1)S(1)}, bf16[384,2048]{1,0:T(8,128)(2,1)S(1)}, u32[]{:S(2)}, u32[]{:S(2)}) collective-permute-start(bf16[384,2048]{1,0:T(8,128)(2,1)S(1)} %pad_maximum_fusion.1), channel_id=1, source_target_pairs={{0,1},{1,2},{2,3},{3,0},{4,5},{5,6},{6,7},{7,4},{8,9},{9,10},{10,1... | collective-permute-start | bytes 4718600 | tf_op jit(solution)/shard_map/ppermute | solution.py:31
  31.1 62.8 %collective-permute-start.5 = (bf16[384,2048]{1,0:T(8,128)(2,1)S(1)}, bf16[384,2048]{1,0:T(8,128)(2,1)S(1)}, u32[]{:S(2)}, u32[]{:S(2)}) collective-permute-start(bf16[384,2048]{1,0:T(8,128)(2,1)S(1)} %pad_maximum_fusion.1), channel_id=1, source_target_pairs={{0,3},{1,0},{2,1},{3,2},{4,7},{5,4},{6,5},{7,6},{8,11},{9,8},{10,9... | collective-permute-start | bytes 4718600 | tf_op jit(solution)/shard_map/ppermute | solution.py:32
  34.6 54.3 %collective-permute-start = (bf16[192,2048]{1,0:T(8,128)(2,1)S(1)}, bf16[192,2048]{1,0:T(8,128)(2,1)S(1)}, u32[]{:S(2)}, u32[]{:S(2)}) collective-permute-start(bf16[192,2048]{1,0:T(8,128)(2,1)S(1)} %bitcast.104), channel_id=1, source_target_pairs={{0,1},{1,2},{2,3},{3,0},{4,5},{5,6},{6,7},{7,4},{8,9},{9,10},{10,1... | collective-permute-start | bytes 2359304 | tf_op jit(solution)/shard_map/ppermute | solution.py:31
  38.2 48.5 %collective-permute-start.1 = (bf16[192,2048]{1,0:T(8,128)(2,1)S(1)}, bf16[192,2048]{1,0:T(8,128)(2,1)S(1)}, u32[]{:S(2)}, u32[]{:S(2)}) collective-permute-start(bf16[192,2048]{1,0:T(8,128)(2,1)S(1)} %bitcast.105), channel_id=1, source_target_pairs={{0,3},{1,0},{2,1},{3,2},{4,7},{5,4},{6,5},{7,6},{8,11},{9,8},{10,9... | collective-permute-start | bytes 2359304 | tf_op jit(solution)/shard_map/ppermute | solution.py:32
  86.7 14.2 %collective-permute-start.2 = (bf16[96,2048]{1,0:T(8,128)(2,1)S(1)}, bf16[96,2048]{1,0:T(8,128)(2,1)S(1)}, u32[]{:S(2)}, u32[]{:S(2)}) collective-permute-start(bf16[96,2048]{1,0:T(8,128)(2,1)S(1)} %slice.139), channel_id=1, source_target_pairs={{0,3},{1,0},{2,1},{3,2},{4,7},{5,4},{6,5},{7,6},{8,11},{9,8},{10,9... | collective-permute-start | bytes 1179656 | tf_op jit(solution)/shard_map/ppermute | solution.py:33
  89.0 14.1 %collective-permute-start.3 = (bf16[96,2048]{1,0:T(8,128)(2,1)S(1)}, bf16[96,2048]{1,0:T(8,128)(2,1)S(1)}, u32[]{:S(2)}, u32[]{:S(2)}) collective-permute-start(bf16[96,2048]{1,0:T(8,128)(2,1)S(1)} %slice.140), channel_id=1, source_target_pairs={{0,1},{1,2},{2,3},{3,0},{4,5},{5,6},{6,7},{7,4},{8,9},{9,10},{10,1... | collective-permute-start | bytes 1179656 | tf_op jit(solution)/shard_map/ppermute | solution.py:34
  94.0 22.1 %collective-permute-start.6 = (bf16[192,2048]{1,0:T(8,128)(2,1)S(1)}, bf16[192,2048]{1,0:T(8,128)(2,1)S(1)}, u32[]{:S(2)}, u32[]{:S(2)}) collective-permute-start(bf16[192,2048]{1,0:T(8,128)(2,1)S(1)} %slice.142), channel_id=1, source_target_pairs={{0,3},{1,0},{2,1},{3,2},{4,7},{5,4},{6,5},{7,6},{8,11},{9,8},{10,9... | collective-permute-start | bytes 2359304 | tf_op jit(solution)/shard_map/ppermute | solution.py:33
  101.0 17.4 %collective-permute-start.7 = (bf16[192,2048]{1,0:T(8,128)(2,1)S(1)}, bf16[192,2048]{1,0:T(8,128)(2,1)S(1)}, u32[]{:S(2)}, u32[]{:S(2)}) collective-permute-start(bf16[192,2048]{1,0:T(8,128)(2,1)S(1)} %slice.143), channel_id=1, source_target_pairs={{0,1},{1,2},{2,3},{3,0},{4,5},{5,6},{6,7},{7,4},{8,9},{9,10},{10,1... | collective-permute-start | bytes 2359304 | tf_op jit(solution)/shard_map/ppermute | solution.py:34
  162.1 106.1 %all-to-all-start.1 = ((bf16[128,2,2176]{2,1,0:T(2,128)(2,1)}), bf16[128,2,2176]{2,1,0:T(2,128)(2,1)S(1)}, u32[]{:S(2)}, u32[]{:S(2)}) async-start(bf16[128,2,2176]{2,1,0:T(2,128)(2,1)} %reshape.99), calls=%async_computation.1 | async-start | bytes 2228224 | tf_op jit(solution)/shard_map/all_to_all | solution.py:118
  171.4 36.1 %collective-permute-start.10 = (bf16[192,2048]{1,0:T(8,128)(2,1)S(1)}, bf16[192,2048]{1,0:T(8,128)(2,1)S(1)}, u32[]{:S(2)}, u32[]{:S(2)}) collective-permute-start(bf16[192,2048]{1,0:T(8,128)(2,1)S(1)} %get-tuple-element.30), channel_id=1, source_target_pairs={{0,3},{1,0},{2,1},{3,2},{4,7},{5,4},{6,5},{7,6},{8,11},{9,8},{10,9... | collective-permute-start | bytes 2359304 | tf_op jit(solution)/shard_map/ppermute | solution.py:41
  174.9 27.2 %collective-permute-start.14 = (bf16[96,2048]{1,0:T(8,128)(2,1)S(1)}, bf16[96,2048]{1,0:T(8,128)(2,1)S(1)}, u32[]{:S(2)}, u32[]{:S(2)}) collective-permute-start(bf16[96,2048]{1,0:T(8,128)(2,1)S(1)} %get-tuple-element.34), channel_id=1, source_target_pairs={{0,3},{1,0},{2,1},{3,2},{4,7},{5,4},{6,5},{7,6},{8,11},{9,8},{10,9... | collective-permute-start | bytes 1179656 | tf_op jit(solution)/shard_map/ppermute | solution.py:41
  178.1 24.0 %copy-start.6 = (bf16[192,2048]{1,0:T(8,128)(2,1)S(1)}, bf16[192,2048]{1,0:T(8,128)(2,1)}, u32[]{:S(2)}) copy-start(bf16[192,2048]{1,0:T(8,128)(2,1)} %convolution_convert_fusion.5) | copy-start | bytes 2359300
  178.2 33.0 %collective-permute-start.8 = (bf16[192,2048]{1,0:T(8,128)(2,1)S(1)}, bf16[192,2048]{1,0:T(8,128)(2,1)S(1)}, u32[]{:S(2)}, u32[]{:S(2)}) collective-permute-start(bf16[192,2048]{1,0:T(8,128)(2,1)S(1)} %get-tuple-element.29), channel_id=1, source_target_pairs={{0,1},{1,2},{2,3},{3,0},{4,5},{5,6},{6,7},{7,4},{8,9},{9,10},{10,1... | collective-permute-start | bytes 2359304 | tf_op jit(solution)/shard_map/ppermute | solution.py:40
  182.9 19.3 %slice-start.1 = ((bf16[192,2048]{1,0:T(8,128)(2,1)}), bf16[96,2048]{1,0:T(8,128)(2,1)S(1)}, s32[]{:S(2)}) async-start(bf16[192,2048]{1,0:T(8,128)(2,1)} %convolution_convert_fusion.5), calls=%async_computation.3 | async-start | bytes 786432 | tf_op jit(solution)/shard_map/slice | solution.py:46
  183.4 24.0 %copy-start.5 = (bf16[192,2048]{1,0:T(8,128)(2,1)}, bf16[192,2048]{1,0:T(8,128)(2,1)S(1)}, u32[]{:S(2)}) copy-start(bf16[192,2048]{1,0:T(8,128)(2,1)S(1)} %convolution_convert_fusion.7) | copy-start | bytes 2359300
  183.4 23.9 %collective-permute-start.12 = (bf16[96,2048]{1,0:T(8,128)(2,1)S(1)}, bf16[96,2048]{1,0:T(8,128)(2,1)S(1)}, u32[]{:S(2)}, u32[]{:S(2)}) collective-permute-start(bf16[96,2048]{1,0:T(8,128)(2,1)S(1)} %get-tuple-element.33), channel_id=1, source_target_pairs={{0,1},{1,2},{2,3},{3,0},{4,5},{5,6},{6,7},{7,4},{8,9},{9,10},{10,1... | collective-permute-start | bytes 1179656 | tf_op jit(solution)/shard_map/ppermute | solution.py:40
  202.3 23.6 %collective-permute-start.15 = (bf16[192,2048]{1,0:T(8,128)(2,1)S(1)}, bf16[192,2048]{1,0:T(8,128)(2,1)S(1)}, u32[]{:S(2)}, u32[]{:S(2)}) collective-permute-start(bf16[192,2048]{1,0:T(8,128)(2,1)S(1)} %pad_maximum_fusion.7), channel_id=1, source_target_pairs={{0,3},{1,0},{2,1},{3,2},{4,7},{5,4},{6,5},{7,6},{8,11},{9,8},{10,9... | collective-permute-start | bytes 2359304 | tf_op jit(solution)/shard_map/ppermute | solution.py:49
  207.9 58.2 %collective-permute-start.11 = (bf16[384,2048]{1,0:T(8,128)(2,1)S(1)}, bf16[384,2048]{1,0:T(8,128)(2,1)S(1)}, u32[]{:S(2)}, u32[]{:S(2)}) collective-permute-start(bf16[384,2048]{1,0:T(8,128)(2,1)S(1)} %pad_maximum_fusion.3), channel_id=1, source_target_pairs={{0,3},{1,0},{2,1},{3,2},{4,7},{5,4},{6,5},{7,6},{8,11},{9,8},{10,9... | collective-permute-start | bytes 4718600 | tf_op jit(solution)/shard_map/ppermute | solution.py:49
  211.7 54.4 %collective-permute-start.9 = (bf16[384,2048]{1,0:T(8,128)(2,1)S(1)}, bf16[384,2048]{1,0:T(8,128)(2,1)S(1)}, u32[]{:S(2)}, u32[]{:S(2)}) collective-permute-start(bf16[384,2048]{1,0:T(8,128)(2,1)S(1)} %pad_maximum_fusion.2), channel_id=1, source_target_pairs={{0,1},{1,2},{2,3},{3,0},{4,5},{5,6},{6,7},{7,4},{8,9},{9,10},{10,1... | collective-permute-start | bytes 4718600 | tf_op jit(solution)/shard_map/ppermute | solution.py:48
  216.0 48.8 %collective-permute-start.13 = (bf16[192,2048]{1,0:T(8,128)(2,1)S(1)}, bf16[192,2048]{1,0:T(8,128)(2,1)S(1)}, u32[]{:S(2)}, u32[]{:S(2)}) collective-permute-start(bf16[192,2048]{1,0:T(8,128)(2,1)S(1)} %pad_maximum_fusion.6), channel_id=1, source_target_pairs={{0,1},{1,2},{2,3},{3,0},{4,5},{5,6},{6,7},{7,4},{8,9},{9,10},{10,1... | collective-permute-start | bytes 2359304 | tf_op jit(solution)/shard_map/ppermute | solution.py:48
  (10 other events, 33.5 us)

commit v2 on v1

v2 whole, which is shorter than its diff:
```python
import jax
import jax.numpy as jnp
from jax import lax
from jax.experimental import pallas as pl
from jax.experimental.pallas import tpu as pltpu
from jax.sharding import PartitionSpec as P

BF = jnp.bfloat16
F32 = jnp.float32
LANES = 128


def dot(a, b, da, db):
    return lax.dot_general(a, b, (((da,), (db,)), ((), ())), preferred_element_type=F32)


def slots_of(ids, keep, capacity):
    width = ids.shape[0] * ids.shape[1]
    chosen = ids.reshape(width)
    kept = keep.reshape(width) > 0
    other = lax.broadcasted_iota(jnp.int32, (width, width), 1)
    own = lax.broadcasted_iota(jnp.int32, (width, width), 0)
    earlier = (other < own) & (chosen[:, None] == chosen[None, :]) & kept[None, :]
    position = jnp.sum(earlier.astype(jnp.int32), axis=1)
    return jnp.where(kept, chosen * capacity + position, -1)


def shift(block, step, n):
    return lax.ppermute(block, "rep", [(i, (i + step) % n) for i in range(n)])


def spread(block, n):
    half = block.shape[0] // 2
    left = shift(block, 1, n)
    right = shift(block, -1, n)
    return left, right, shift(right[:half], -1, n), shift(left[half:], 1, n)


def rows_kernel(*refs):
    srcs, (p_ref, *d_refs), (gu, dn, x, g, sems) = refs[:13], refs[13:18], refs[18:]
    hid = dn.shape[1]
    half = hid // 2
    features = x.shape[1]
    targets = [
        x,
        g,
        gu.at[0, pl.ds(0, hid)],
        gu.at[0, pl.ds(hid, hid)],
        dn.at[0],
        gu.at[1],
        dn.at[1],
        gu.at[2],
        dn.at[2],
        gu.at[3, pl.ds(0, hid)],
        gu.at[3, pl.ds(hid, hid)],
        dn.at[3, pl.ds(0, half)],
        dn.at[3, pl.ds(half, half)],
    ]
    order = [(0, 1, 2, 3, 4), (5, 6), (7, 8), (9, 10, 11, 12)]
    copies = [pltpu.make_async_copy(s, t, sems.at[i]) for i, (s, t) in enumerate(zip(srcs, targets))]
    for copy in copies:
        copy.start()
    score = None
    for q, needed in enumerate(order):
        for i in needed:
            copies[i].wait()
        if q == 0:
            coef = g[:, features:].astype(F32).T[0:1, :]
        pre = dot(gu[q], x[...], 1, 1)
        back = dot(dn[q], g[:, :features], 1, 1)
        gate_pre, up_pre = pre[:hid], pre[hid:]
        sigma = jax.nn.sigmoid(gate_pre)
        active = gate_pre * sigma
        hidden = active * up_pre
        part = jnp.sum(hidden.astype(BF).astype(F32) * back, axis=0, keepdims=True)
        score = part if score is None else score + part
        d_hidden = coef * back
        d_refs[q][0:hid, :] = (
            d_hidden * up_pre * sigma * (1.0 + gate_pre * (1.0 - sigma))
        ).astype(BF)
        d_refs[q][hid : 2 * hid, :] = (d_hidden * active).astype(BF)
        d_refs[q][2 * hid :, :] = (coef * hidden).astype(BF)
    tile = 512
    for j in range(0, features, tile):
        total = None
        for q in range(4):
            part = dot(d_refs[q][: 2 * hid, :], gu[q, :, j : j + tile], 0, 0)
            total = part if total is None else total + part
        p_ref[:, j : j + tile] = total.astype(BF)
    p_ref[:, features:] = jnp.broadcast_to(score, (LANES, score.shape[1])).T.astype(BF)


def rows_call(x, g, gate, up, down, gu_far, dn_far):
    rows, features = x.shape
    hid = gate.shape[0]
    gu_left, gu_right, gu_a, gu_b = gu_far
    dn_left, dn_right, dn_a, dn_b = dn_far
    srcs = [x, g, gate, up, down, gu_left, dn_left, gu_right, dn_right, gu_a, gu_b, dn_a, dn_b]
    return pl.pallas_call(
        rows_kernel,
        out_shape=[jax.ShapeDtypeStruct((rows, features + LANES), BF)]
        + [jax.ShapeDtypeStruct((3 * hid, rows), BF)] * 4,
        in_specs=[pl.BlockSpec(memory_space=pl.ANY)] * len(srcs),
        out_specs=[pl.BlockSpec(memory_space=pltpu.VMEM)] * 5,
        scratch_shapes=[
            pltpu.VMEM((4, 2 * hid, features), BF),
            pltpu.VMEM((4, hid, features), BF),
            pltpu.VMEM((rows, features), BF),
            pltpu.VMEM((rows, features + LANES), BF),
            pltpu.SemaphoreType.DMA((len(srcs),)),
        ],
        compiler_params=pltpu.CompilerParams(vmem_limit_bytes=36 * 1024 * 1024),
        cost_estimate=pl.CostEstimate(
            flops=2 * rows * features * hid * 4 * 5,
            bytes_accessed=2 * features * hid * 12 + 6 * rows * features,
            transcendentals=rows * hid * 4,
        ),
        name="rows",
    )(*srcs)


def weights_kernel(*refs):
    d_refs, x_refs, g_refs, outs = refs[:4], refs[4:9], refs[9:14], refs[14:]
    hid = outs[0].shape[0]
    half = d_refs[3].shape[1] // 2

    def total(first, last, row_refs):
        parts = [dot(d[first:last, :], r[...], 1, 0) for d, r in zip(d_refs[:3], row_refs[:3])]
        parts.append(dot(d_refs[3][first:last, :half], row_refs[3][...], 1, 0))
        parts.append(dot(d_refs[3][first:last, half:], row_refs[4][...], 1, 0))
        return sum(parts[1:], parts[0]).astype(BF)

    gu = total(0, 2 * hid, x_refs)
    outs[0][...] = gu[:hid]
    outs[1][...] = gu[hid:]
    outs[2][...] = total(2 * hid, 3 * hid, g_refs)


def weights_call(ds, xs, gs, features):
    tile = 512
    hid = ds[0].shape[0] // 3
    whole = [pl.BlockSpec(d.shape, lambda j: (0, 0)) for d in ds]
    tiled = [pl.BlockSpec((a.shape[0], tile), lambda j: (0, j)) for a in [*xs, *gs]]
    rows = sum(d.shape[1] for d in ds)
    return pl.pallas_call(
        weights_kernel,
        grid=(features // tile,),
        out_shape=[jax.ShapeDtypeStruct((hid, features), BF)] * 3,
        in_specs=whole + tiled,
        out_specs=[pl.BlockSpec((hid, tile), lambda j: (0, j))] * 3,
        compiler_params=pltpu.CompilerParams(vmem_limit_bytes=24 * 1024 * 1024),
        cost_estimate=pl.CostEstimate(
            flops=2 * rows * features * hid * 3,
            bytes_accessed=2 * features * (2 * rows + 3 * hid),
            transcendentals=0,
        ),
        name="weight_grads",
    )(*ds, *xs, *gs)


def local(tokens, out_grad, expert_ids, keep_flags, route_weights, gate_w, up_w, down_w):
    experts = lax.axis_size("node") * lax.axis_size("local")
    n = lax.axis_size("rep")
    tok_rows, top = expert_ids.shape
    features = tokens.shape[1]
    capacity = 2
    places = experts * capacity
    slots = tok_rows * top

    target = slots_of(expert_ids, keep_flags, capacity)
    hits = lax.broadcasted_iota(jnp.int32, (places, slots), 0) == target[None, :]
    by_slot = hits.astype(BF)
    by_token = jnp.sum(hits.reshape(places, tok_rows, top).astype(F32), axis=2).astype(BF)

    def exchange(block):
        width = block.shape[1]
        return lax.all_to_all(
            block.reshape(experts, capacity, width),
            ("node", "local"),
            split_axis=0,
            concat_axis=0,
            tiled=True,
        ).reshape(places, width)

    x = exchange(dot(by_token, tokens, 1, 0).astype(BF))
    coef = jnp.sum(
        jnp.where(hits, route_weights.reshape(1, slots).astype(F32), 0.0), axis=1, keepdims=True
    ).astype(BF)
    g = exchange(
        jnp.concatenate(
            [dot(by_token, out_grad, 1, 0).astype(BF), jnp.broadcast_to(coef, (places, LANES))],
            axis=1,
        )
    )

    gate, up, down = gate_w[0], up_w[0], down_w[0]
    gu_far = spread(jnp.concatenate([gate, up], axis=0), n)
    dn_far = spread(down, n)
    x_far = spread(x, n)
    g_far = spread(g, n)

    rows, d_own, d_left, d_right, d_two = rows_call(x, g, gate, up, down, gu_far, dn_far)
    home = exchange(rows)
    ds = [d_own, shift(d_right, 1, n), shift(d_left, -1, n), shift(d_two, 2, n)]
    grad_gate, grad_up, grad_down = weights_call(ds, [x, *x_far], [g, *g_far], features)

    token_grad = dot(by_token, home[:, :features], 0, 0).astype(BF)
    slot_score = dot(by_slot, home[:, features:], 0, 0)[:, 0].reshape(tok_rows, top).astype(BF)
    return (token_grad, slot_score, grad_gate[None], grad_up[None], grad_down[None])


def solution(mesh):
    by_row = P(("node", "local", "rep"), None)
    by_expert = P(("node", "local"), "rep", None)
    return jax.shard_map(
        local,
        mesh=mesh,
        in_specs=(by_row,) * 5 + (by_expert,) * 3,
        out_specs=(by_row,) * 2 + (by_expert,) * 3,
        check_vma=False,
    )
```

time: 275 us -> 315 us (1.15)
  starting transfers between devices: 77.7 us -> 110 us
  matrix products: 23.1 us -> 2 us
  waiting for transfers between devices: 134 us -> 154 us
  Pallas kernels: 0 us -> 13.2 us
  other arithmetic: 7.03 us -> 0.65 us
    all_to_all x2 -> x3, waiting for transfers between devices: 11.6 us -> 54.3 us  [exchange(): lax.all_to_all(block.reshape(experts, capacity, width), ('node', 'local')...]
    ppermute x16 -> x19, waiting for transfers between devices: 123 us -> 100 us  [shift(): return lax.ppermute(block, 'rep', [(i, (i + step) % n) for i in range(n)])]
    dot_general x14 -> x4, matrix products: 23.1 us -> 2 us  [dot(): lax.dot_general(a, b, (((da,), (db,)), ((), ())), preferred_element_type=...]
    all_to_all x2 -> x3, starting transfers between devices: 28.1 us -> 44.9 us  [exchange(): lax.all_to_all(block.reshape(experts, capacity, width), ('node', 'local')...]
    ppermute x16 -> x19, starting transfers between devices: 49.6 us -> 64.7 us  [shift(): return lax.ppermute(block, 'rep', [(i, (i + step) % n) for i in range(n)])]
    pallas_call x0 -> x2, Pallas kernels: none -> 13.2 us  [the longest x1 7.53 us: rows_call(): pl.pallas_call(rows_kernel, out_shape=[jax.ShapeDtypeStruct((rows, featur...]
    unnamed x40 -> x65, local copies, waits for them, and re-layouts: 9.96 us -> 17.5 us
    convert_element_type x7 -> x0, other arithmetic: 3.48 us -> none  [the longest x1 1.76 us: local(): (d_hidden * up_pre * sigma * (1.0 + gate_pre * (1.0 - sigma))).astype(BF)]
  transfers between devices with their start and end apart: 18 -> 22, of which waited for: 9 -> 9; matrix products, arithmetic and copies ran while one was open for 6% -> 3% of each run, Pallas kernels for 0% -> 2%
where the time goes in v2:
time: 315 us; the launch traced here: 310 us
  waiting for transfers between devices  154 us (49%)
  starting transfers between devices  110 us (35%)
  local copies, waits for them, and re-layouts  29.6 us (9%)
  Pallas kernels  13.2 us (4%)
    ppermute x19, waiting for transfers between devices, shift(): return lax.ppermute(block, 'rep', [(i, (i + step) % n) for i in range(n)])  100 us
    ppermute x19, starting transfers between devices, shift(): return lax.ppermute(block, 'rep', [(i, (i + step) % n) for i in range(n)])  64.7 us
    all_to_all x3, waiting for transfers between devices, exchange(): lax.all_to_all(block.reshape(experts, capacity, width), ('node', 'local')...  54.3 us
    all_to_all x3, starting transfers between devices, exchange(): lax.all_to_all(block.reshape(experts, capacity, width), ('node', 'local')...  44.9 us
    unnamed x65, local copies, waits for them, and re-layouts  17.5 us
    pallas_call x1, Pallas kernels, rows_call(): pl.pallas_call(rows_kernel, out_shape=[jax.ShapeDtypeStruct((rows, featur...  7.53 us
  transfers between devices with their start and end apart: 22, of which 9 were waited for; matrix products, arithmetic and copies ran while one was open for 3% of the time, Pallas kernels for 2%

profile of v2, /device:TPU:6, one launch (start us, length us, event | category | flops | bytes accessed | tf_op | source)
XLA Modules:
  0.0 310.5 jit_solution(4089343879972367727)
XLA Ops:
  4.8 20.1 %all-to-all-start = ((bf16[128,2,2048]{2,1,0:T(2,128)(2,1)}), bf16[128,2,2048]{2,1,0:T(2,128)(2,1)S(1)}, u32[]{:S(2)}, u32[]{:S(2)}) async-start(bf16[128,2,2048]{2,1,0:T(2,128)(2,1)} %reshape.74), calls=%async_computation | async-start | bytes 2097152 | tf_op jit(solution)/shard_map/all_to_all | solution.py:177
  27.2 54.3 %all-to-all-done = bf16[128,2,2048]{2,1,0:T(2,128)(2,1)S(1)} async-done(((bf16[128,2,2048]{2,1,0:T(2,128)(2,1)}), bf16[128,2,2048]{2,1,0:T(2,128)(2,1)S(1)}, u32[]{:S(2)}, u32[]{:S(2)}) %all-to-all-start) | async-done | bytes 1048608 | tf_op jit(solution)/shard_map/all_to_all | solution.py:177
  81.5 7.3 %all-to-all-start.1 = ((bf16[128,2,2176]{2,1,0:T(2,128)(2,1)}), bf16[128,2,2176]{2,1,0:T(2,128)(2,1)}, u32[]{:S(2)}, u32[]{:S(2)}) async-start(bf16[128,2,2176]{2,1,0:T(2,128)(2,1)} %reshape.76), calls=%async_computation.1 | async-start | bytes 2228224 | tf_op jit(solution)/shard_map/all_to_all | solution.py:177
  88.9 2.9 collective-permute-start.2
  91.8 4.3 %collective-permute-start = (bf16[384,2048]{1,0:T(8,128)(2,1)S(1)}, bf16[384,2048]{1,0:T(8,128)(2,1)S(1)}, u32[]{:S(2)}, u32[]{:S(2)}) collective-permute-start(bf16[384,2048]{1,0:T(8,128)(2,1)S(1)} %pad_maximum_fusion), channel_id=1, source_target_pairs={{0,1},{1,2},{2,3},{3,0},{4,5},{5,6},{6,7},{7,4},{8,9},{9,10},{10,1... | collective-permute-start | bytes 4718600 | tf_op jit(solution)/shard_map/ppermute | solution.py:29
  98.0 5.1 %collective-permute-start.1 = (bf16[192,2048]{1,0:T(8,128)(2,1)S(1)}, bf16[192,2048]{1,0:T(8,128)(2,1)S(1)}, u32[]{:S(2)}, u32[]{:S(2)}) collective-permute-start(bf16[192,2048]{1,0:T(8,128)(2,1)S(1)} %bitcast.16), channel_id=1, source_target_pairs={{0,1},{1,2},{2,3},{3,0},{4,5},{5,6},{6,7},{7,4},{8,9},{9,10},{10,1... | collective-permute-start | bytes 2359304 | tf_op jit(solution)/shard_map/ppermute | solution.py:29
  103.2 26.3 %collective-permute-done.2.refs_7_ = bf16[384,2048]{1,0:T(8,128)(2,1)S(1)} collective-permute-done((bf16[384,2048]{1,0:T(8,128)(2,1)S(1)}, bf16[384,2048]{1,0:T(8,128)(2,1)S(1)}, u32[]{:S(2)}, u32[]{:S(2)}) %collective-permute-start.2) | collective-permute-done | bytes 1572896 | tf_op jit(solution)/shard_map/ppermute | solution.py:29
  133.6 5.3 %collective-permute-start.5 = (bf16[192,2048]{1,0:T(8,128)(2,1)}, bf16[192,2048]{1,0:T(8,128)(2,1)}, u32[]{:S(2)}, u32[]{:S(2)}) collective-permute-start(bf16[192,2048]{1,0:T(8,128)(2,1)} %slice.46), channel_id=1, source_target_pairs={{0,1},{1,2},{2,3},{3,0},{4,5},{5,6},{6,7},{7,4},{8,9},{9,10},{10,1... | collective-permute-start | bytes 2359304 | tf_op jit(solution)/shard_map/ppermute | solution.py:29
  138.8 7.5 %collective-permute-done.3.refs_8_ = bf16[192,2048]{1,0:T(8,128)(2,1)S(1)} collective-permute-done((bf16[192,2048]{1,0:T(8,128)(2,1)S(1)}, bf16[192,2048]{1,0:T(8,128)(2,1)S(1)}, u32[]{:S(2)}, u32[]{:S(2)}) %collective-permute-start.3) | collective-permute-done | bytes 786464 | tf_op jit(solution)/shard_map/ppermute | solution.py:29
  150.1 5.3 %collective-permute-start.7 = (bf16[96,2048]{1,0:T(8,128)(2,1)}, bf16[96,2048]{1,0:T(8,128)(2,1)}, u32[]{:S(2)}, u32[]{:S(2)}) collective-permute-start(bf16[96,2048]{1,0:T(8,128)(2,1)} %slice.48), channel_id=1, source_target_pairs={{0,1},{1,2},{2,3},{3,0},{4,5},{5,6},{6,7},{7,4},{8,9},{9,10},{10,1... | collective-permute-start | bytes 1179656 | tf_op jit(solution)/shard_map/ppermute | solution.py:29
  157.4 12.7 %collective-permute-done.6.refs_11_ = bf16[96,2048]{1,0:T(8,128)(2,1)S(1)} collective-permute-done((bf16[96,2048]{1,0:T(8,128)(2,1)}, bf16[96,2048]{1,0:T(8,128)(2,1)S(1)}, u32[]{:S(2)}, u32[]{:S(2)}) %collective-permute-start.6) | collective-permute-done | bytes 393248 | tf_op jit(solution)/shard_map/ppermute | solution.py:29
  182.9 7.5 %rows.1 = (bf16[256,2176]{1,0:T(8,128)(2,1)S(1)}, bf16[576,256]{1,0:T(8,128)(2,1)S(1)}, bf16[576,256]{1,0:T(8,128)(2,1)S(1)}, bf16[576,256]{1,0:T(8,128)(2,1)S(1)}, bf16[576,256]{1,0:T(8,128)(2,1)S(1)}) custom-call(bf16[256,2048]{1,0:T(8,128)(2,1)S(1)} %reshape.75.refs_0_.refs_4_, bf16[256,2176]{1,0:T(8,128)(2,1)S(1)} %reshape.77.refs_1_.refs_9_, ...), custom_call_target="tpu_custom_call" | custom-call | flops 4026531840 | bytes 12582912 | tf_op jit(solution)/shard_map/rows/pallas_call | solution.py:99
  194.5 17.5 %all-to-all-start.2 = ((bf16[128,2,2176]{2,1,0:T(2,128)(2,1)}), bf16[128,2,2176]{2,1,0:T(2,128)(2,1)}, u32[]{:S(2)}, u32[]{:S(2)}) async-start(bf16[128,2,2176]{2,1,0:T(2,128)(2,1)} %reshape.78), calls=%async_computation.2 | async-start | bytes 2228224 | tf_op jit(solution)/shard_map/all_to_all | solution.py:177
  212.1 2.4 collective-permute-start.16
  214.5 5.0 %collective-permute-start.15 = (bf16[256,2176]{1,0:T(8,128)(2,1)S(1)}, bf16[256,2176]{1,0:T(8,128)(2,1)S(1)}, u32[]{:S(2)}, u32[]{:S(2)}) collective-permute-start(bf16[256,2176]{1,0:T(8,128)(2,1)S(1)} %reshape.77.refs_1_.refs_9_), channel_id=1, source_target_pairs={{0,1},{1,2},{2,3},{3,0},{4,5},{5,6},{6,7},{7,4},{8,9},{9,10},{10,1... | collective-permute-start | bytes 3342344 | tf_op jit(solution)/shard_map/ppermute | solution.py:29
  221.5 5.1 %collective-permute-start.11 = (bf16[256,2048]{1,0:T(8,128)(2,1)S(1)}, bf16[256,2048]{1,0:T(8,128)(2,1)S(1)}, u32[]{:S(2)}, u32[]{:S(2)}) collective-permute-start(bf16[256,2048]{1,0:T(8,128)(2,1)S(1)} %reshape.75.refs_0_.refs_4_), channel_id=1, source_target_pairs={{0,1},{1,2},{2,3},{3,0},{4,5},{5,6},{6,7},{7,4},{8,9},{9,10},{10,1... | collective-permute-start | bytes 3145736 | tf_op jit(solution)/shard_map/ppermute | solution.py:29
  226.6 2.7 collective-permute-start.8
  229.3 13.7 %collective-permute-done.16.refs_11_ = bf16[256,2176]{1,0:T(8,128)(2,1)S(1)} collective-permute-done((bf16[256,2176]{1,0:T(8,128)(2,1)S(1)}, bf16[256,2176]{1,0:T(8,128)(2,1)S(1)}, u32[]{:S(2)}, u32[]{:S(2)}) %collective-permute-start.16) | collective-permute-done | bytes 1114144 | tf_op jit(solution)/shard_map/ppermute | solution.py:29
  245.0 3.3 %collective-permute-start.17 = (bf16[128,2176]{1,0:T(8,128)(2,1)S(1)}, bf16[128,2176]{1,0:T(8,128)(2,1)S(1)}, u32[]{:S(2)}, u32[]{:S(2)}) collective-permute-start(bf16[128,2176]{1,0:T(8,128)(2,1)S(1)} %slice.54), channel_id=1, source_target_pairs={{0,3},{1,0},{2,1},{3,2},{4,7},{5,4},{6,5},{7,6},{8,11},{9,8},{10,9... | collective-permute-start | bytes 1671176 | tf_op jit(solution)/shard_map/ppermute | solution.py:29
  248.4 17.1 %collective-permute-done.12.refs_6_ = bf16[256,2048]{1,0:T(8,128)(2,1)S(1)} collective-permute-done((bf16[256,2048]{1,0:T(8,128)(2,1)S(1)}, bf16[256,2048]{1,0:T(8,128)(2,1)S(1)}, u32[]{:S(2)}, u32[]{:S(2)}) %collective-permute-start.12) | collective-permute-done | bytes 1048608 | tf_op jit(solution)/shard_map/ppermute | solution.py:29
  265.5 3.9 %collective-permute-start.18 = (bf16[128,2176]{1,0:T(8,128)(2,1)S(1)}, bf16[128,2176]{1,0:T(8,128)(2,1)S(1)}, u32[]{:S(2)}, u32[]{:S(2)}) collective-permute-start(bf16[128,2176]{1,0:T(8,128)(2,1)S(1)} %slice.55), channel_id=1, source_target_pairs={{0,1},{1,2},{2,3},{3,0},{4,5},{5,6},{6,7},{7,4},{8,9},{9,10},{10,1... | collective-permute-start | bytes 1671176 | tf_op jit(solution)/shard_map/ppermute | solution.py:29
  273.3 5.6 %collective-permute-start.14 = (bf16[128,2048]{1,0:T(8,128)(2,1)S(1)}, bf16[128,2048]{1,0:T(8,128)(2,1)S(1)}, u32[]{:S(2)}, u32[]{:S(2)}) collective-permute-start(bf16[128,2048]{1,0:T(8,128)(2,1)S(1)} %slice.53), channel_id=1, source_target_pairs={{0,1},{1,2},{2,3},{3,0},{4,5},{5,6},{6,7},{7,4},{8,9},{9,10},{10,1... | collective-permute-start | bytes 1572872 | tf_op jit(solution)/shard_map/ppermute | solution.py:29
  281.1 20.2 %collective-permute-done.10.refs_3_ = bf16[576,256]{1,0:T(8,128)(2,1)S(1)} collective-permute-done((bf16[576,256]{1,0:T(8,128)(2,1)S(1)}, bf16[576,256]{1,0:T(8,128)(2,1)S(1)}, u32[]{:S(2)}, u32[]{:S(2)}) %collective-permute-start.10) | collective-permute-done | bytes 294944 | tf_op jit(solution)/shard_map/ppermute | solution.py:29
  301.4 5.7 %weight_grads.1 = (bf16[192,2048]{1,0:T(8,128)(2,1)}, bf16[192,2048]{1,0:T(8,128)(2,1)}, bf16[192,2048]{1,0:T(8,128)(2,1)}) custom-call(bf16[576,256]{1,0:T(8,128)(2,1)S(1)} %copy-done.10, bf16[576,256]{1,0:T(8,128)(2,1)S(1)} %collective-permute-done.8.refs_1_, bf16[576,256]{1,0:T(8,128)(2,1)S(1)} %collective-permute-done.9.refs_2_, ...), custom_call_target="tpu_custom_call" | custom-call | flops 2415919104 | bytes 10747904 | tf_op jit(solution)/shard_map/weight_grads/pallas_call | solution.py:145
  (121 shorter events, 48.4 us)
Async XLA Ops:
  4.8 76.7 %all-to-all-start = ((bf16[128,2,2048]{2,1,0:T(2,128)(2,1)}), bf16[128,2,2048]{2,1,0:T(2,128)(2,1)S(1)}, u32[]{:S(2)}, u32[]{:S(2)}) async-start(bf16[128,2,2048]{2,1,0:T(2,128)(2,1)} %reshape.74), calls=%async_computation | async-start | bytes 2097152 | tf_op jit(solution)/shard_map/all_to_all | solution.py:177
  27.2 61.6 %copy-start.1 = (bf16[1,192,2048]{2,1,0:T(8,128)(2,1)S(1)}, bf16[1,192,2048]{2,1,0:T(8,128)(2,1)}, u32[]{:S(2)}) copy-start(bf16[1,192,2048]{2,1,0:T(8,128)(2,1)} %param.13) | copy-start | bytes 2359300
  27.2 61.6 %copy-start.3 = (bf16[1,192,2048]{2,1,0:T(8,128)(2,1)S(1)}, bf16[1,192,2048]{2,1,0:T(8,128)(2,1)}, u32[]{:S(2)}) copy-start(bf16[1,192,2048]{2,1,0:T(8,128)(2,1)} %param.14) | copy-start | bytes 2359300
  81.5 74.4 %all-to-all-start.1 = ((bf16[128,2,2176]{2,1,0:T(2,128)(2,1)}), bf16[128,2,2176]{2,1,0:T(2,128)(2,1)}, u32[]{:S(2)}, u32[]{:S(2)}) async-start(bf16[128,2,2176]{2,1,0:T(2,128)(2,1)} %reshape.76), calls=%async_computation.1 | async-start | bytes 2228224 | tf_op jit(solution)/shard_map/all_to_all | solution.py:177
  88.9 40.6 %collective-permute-start.2 = (bf16[384,2048]{1,0:T(8,128)(2,1)S(1)}, bf16[384,2048]{1,0:T(8,128)(2,1)S(1)}, u32[]{:S(2)}, u32[]{:S(2)}) collective-permute-start(bf16[384,2048]{1,0:T(8,128)(2,1)S(1)} %pad_maximum_fusion), channel_id=1, source_target_pairs={{0,3},{1,0},{2,1},{3,2},{4,7},{5,4},{6,5},{7,6},{8,11},{9,8},{10,9... | collective-permute-start | bytes 4718600 | tf_op jit(solution)/shard_map/ppermute | solution.py:29
  91.8 40.6 %collective-permute-start = (bf16[384,2048]{1,0:T(8,128)(2,1)S(1)}, bf16[384,2048]{1,0:T(8,128)(2,1)S(1)}, u32[]{:S(2)}, u32[]{:S(2)}) collective-permute-start(bf16[384,2048]{1,0:T(8,128)(2,1)S(1)} %pad_maximum_fusion), channel_id=1, source_target_pairs={{0,1},{1,2},{2,3},{3,0},{4,5},{5,6},{6,7},{7,4},{8,9},{9,10},{10,1... | collective-permute-start | bytes 4718600 | tf_op jit(solution)/shard_map/ppermute | solution.py:29
  96.1 50.2 %collective-permute-start.3 = (bf16[192,2048]{1,0:T(8,128)(2,1)S(1)}, bf16[192,2048]{1,0:T(8,128)(2,1)S(1)}, u32[]{:S(2)}, u32[]{:S(2)}) collective-permute-start(bf16[192,2048]{1,0:T(8,128)(2,1)S(1)} %bitcast.15), channel_id=1, source_target_pairs={{0,3},{1,0},{2,1},{3,2},{4,7},{5,4},{6,5},{7,6},{8,11},{9,8},{10,9... | collective-permute-start | bytes 2359304 | tf_op jit(solution)/shard_map/ppermute | solution.py:29
  98.0 51.0 %collective-permute-start.1 = (bf16[192,2048]{1,0:T(8,128)(2,1)S(1)}, bf16[192,2048]{1,0:T(8,128)(2,1)S(1)}, u32[]{:S(2)}, u32[]{:S(2)}) collective-permute-start(bf16[192,2048]{1,0:T(8,128)(2,1)S(1)} %bitcast.16), channel_id=1, source_target_pairs={{0,1},{1,2},{2,3},{3,0},{4,5},{5,6},{6,7},{7,4},{8,9},{9,10},{10,1... | collective-permute-start | bytes 2359304 | tf_op jit(solution)/shard_map/ppermute | solution.py:29
  130.5 40.9 %collective-permute-start.4 = (bf16[192,2048]{1,0:T(8,128)(2,1)}, bf16[192,2048]{1,0:T(8,128)(2,1)S(1)}, u32[]{:S(2)}, u32[]{:S(2)}) collective-permute-start(bf16[192,2048]{1,0:T(8,128)(2,1)} %slice.45), channel_id=1, source_target_pairs={{0,3},{1,0},{2,1},{3,2},{4,7},{5,4},{6,5},{7,6},{8,11},{9,8},{10,9... | collective-permute-start | bytes 2359304 | tf_op jit(solution)/shard_map/ppermute | solution.py:29
  133.6 38.7 %collective-permute-start.5 = (bf16[192,2048]{1,0:T(8,128)(2,1)}, bf16[192,2048]{1,0:T(8,128)(2,1)}, u32[]{:S(2)}, u32[]{:S(2)}) collective-permute-start(bf16[192,2048]{1,0:T(8,128)(2,1)} %slice.46), channel_id=1, source_target_pairs={{0,1},{1,2},{2,3},{3,0},{4,5},{5,6},{6,7},{7,4},{8,9},{9,10},{10,1... | collective-permute-start | bytes 2359304 | tf_op jit(solution)/shard_map/ppermute | solution.py:29
  147.1 22.9 %collective-permute-start.6 = (bf16[96,2048]{1,0:T(8,128)(2,1)}, bf16[96,2048]{1,0:T(8,128)(2,1)S(1)}, u32[]{:S(2)}, u32[]{:S(2)}) collective-permute-start(bf16[96,2048]{1,0:T(8,128)(2,1)} %slice.47), channel_id=1, source_target_pairs={{0,3},{1,0},{2,1},{3,2},{4,7},{5,4},{6,5},{7,6},{8,11},{9,8},{10,9... | collective-permute-start | bytes 1179656 | tf_op jit(solution)/shard_map/ppermute | solution.py:29
  150.1 21.3 %collective-permute-start.7 = (bf16[96,2048]{1,0:T(8,128)(2,1)}, bf16[96,2048]{1,0:T(8,128)(2,1)}, u32[]{:S(2)}, u32[]{:S(2)}) collective-permute-start(bf16[96,2048]{1,0:T(8,128)(2,1)} %slice.48), channel_id=1, source_target_pairs={{0,1},{1,2},{2,3},{3,0},{4,5},{5,6},{6,7},{7,4},{8,9},{9,10},{10,1... | collective-permute-start | bytes 1179656 | tf_op jit(solution)/shard_map/ppermute | solution.py:29
  194.5 112.5 %all-to-all-start.2 = ((bf16[128,2,2176]{2,1,0:T(2,128)(2,1)}), bf16[128,2,2176]{2,1,0:T(2,128)(2,1)}, u32[]{:S(2)}, u32[]{:S(2)}) async-start(bf16[128,2,2176]{2,1,0:T(2,128)(2,1)} %reshape.78), calls=%async_computation.2 | async-start | bytes 2228224 | tf_op jit(solution)/shard_map/all_to_all | solution.py:177
  212.1 31.0 %collective-permute-start.16 = (bf16[256,2176]{1,0:T(8,128)(2,1)S(1)}, bf16[256,2176]{1,0:T(8,128)(2,1)S(1)}, u32[]{:S(2)}, u32[]{:S(2)}) collective-permute-start(bf16[256,2176]{1,0:T(8,128)(2,1)S(1)} %reshape.77.refs_1_.refs_9_), channel_id=1, source_target_pairs={{0,3},{1,0},{2,1},{3,2},{4,7},{5,4},{6,5},{7,6},{8,11},{9,8},{10,9... | collective-permute-start | bytes 3342344 | tf_op jit(solution)/shard_map/ppermute | solution.py:29
  214.5 30.5 %collective-permute-start.15 = (bf16[256,2176]{1,0:T(8,128)(2,1)S(1)}, bf16[256,2176]{1,0:T(8,128)(2,1)S(1)}, u32[]{:S(2)}, u32[]{:S(2)}) collective-permute-start(bf16[256,2176]{1,0:T(8,128)(2,1)S(1)} %reshape.77.refs_1_.refs_9_), channel_id=1, source_target_pairs={{0,1},{1,2},{2,3},{3,0},{4,5},{5,6},{6,7},{7,4},{8,9},{9,10},{10,1... | collective-permute-start | bytes 3342344 | tf_op jit(solution)/shard_map/ppermute | solution.py:29
  219.5 46.0 %collective-permute-start.12 = (bf16[256,2048]{1,0:T(8,128)(2,1)S(1)}, bf16[256,2048]{1,0:T(8,128)(2,1)S(1)}, u32[]{:S(2)}, u32[]{:S(2)}) collective-permute-start(bf16[256,2048]{1,0:T(8,128)(2,1)S(1)} %reshape.75.refs_0_.refs_4_), channel_id=1, source_target_pairs={{0,3},{1,0},{2,1},{3,2},{4,7},{5,4},{6,5},{7,6},{8,11},{9,8},{10,9... | collective-permute-start | bytes 3145736 | tf_op jit(solution)/shard_map/ppermute | solution.py:29
  221.5 48.0 %collective-permute-start.11 = (bf16[256,2048]{1,0:T(8,128)(2,1)S(1)}, bf16[256,2048]{1,0:T(8,128)(2,1)S(1)}, u32[]{:S(2)}, u32[]{:S(2)}) collective-permute-start(bf16[256,2048]{1,0:T(8,128)(2,1)S(1)} %reshape.75.refs_0_.refs_4_), channel_id=1, source_target_pairs={{0,1},{1,2},{2,3},{3,0},{4,5},{5,6},{6,7},{7,4},{8,9},{9,10},{10,1... | collective-permute-start | bytes 3145736 | tf_op jit(solution)/shard_map/ppermute | solution.py:29
  226.6 46.7 %collective-permute-start.8 = (bf16[576,256]{1,0:T(8,128)(2,1)S(1)}, bf16[576,256]{1,0:T(8,128)(2,1)S(1)}, u32[]{:S(2)}, u32[]{:S(2)}) collective-permute-start(bf16[576,256]{1,0:T(8,128)(2,1)S(1)} %copy-done.26), channel_id=1, source_target_pairs={{0,1},{1,2},{2,3},{3,0},{4,5},{5,6},{6,7},{7,4},{8,9},{9,10},{10,1... | collective-permute-start | bytes 884744 | tf_op jit(solution)/shard_map/ppermute | solution.py:29
  243.0 35.9 %collective-permute-start.9 = (bf16[576,256]{1,0:T(8,128)(2,1)S(1)}, bf16[576,256]{1,0:T(8,128)(2,1)S(1)}, u32[]{:S(2)}, u32[]{:S(2)}) collective-permute-start(bf16[576,256]{1,0:T(8,128)(2,1)S(1)} %copy-done.24), channel_id=1, source_target_pairs={{0,3},{1,0},{2,1},{3,2},{4,7},{5,4},{6,5},{7,6},{8,11},{9,8},{10,9... | collective-permute-start | bytes 884744 | tf_op jit(solution)/shard_map/ppermute | solution.py:29
  245.0 56.3 %collective-permute-start.17 = (bf16[128,2176]{1,0:T(8,128)(2,1)S(1)}, bf16[128,2176]{1,0:T(8,128)(2,1)S(1)}, u32[]{:S(2)}, u32[]{:S(2)}) collective-permute-start(bf16[128,2176]{1,0:T(8,128)(2,1)S(1)} %slice.54), channel_id=1, source_target_pairs={{0,3},{1,0},{2,1},{3,2},{4,7},{5,4},{6,5},{7,6},{8,11},{9,8},{10,9... | collective-permute-start | bytes 1671176 | tf_op jit(solution)/shard_map/ppermute | solution.py:29
  265.5 35.9 %collective-permute-start.18 = (bf16[128,2176]{1,0:T(8,128)(2,1)S(1)}, bf16[128,2176]{1,0:T(8,128)(2,1)S(1)}, u32[]{:S(2)}, u32[]{:S(2)}) collective-permute-start(bf16[128,2176]{1,0:T(8,128)(2,1)S(1)} %slice.55), channel_id=1, source_target_pairs={{0,1},{1,2},{2,3},{3,0},{4,5},{5,6},{6,7},{7,4},{8,9},{9,10},{10,1... | collective-permute-start | bytes 1671176 | tf_op jit(solution)/shard_map/ppermute | solution.py:29
  269.5 31.8 %collective-permute-start.13 = (bf16[128,2048]{1,0:T(8,128)(2,1)S(1)}, bf16[128,2048]{1,0:T(8,128)(2,1)S(1)}, u32[]{:S(2)}, u32[]{:S(2)}) collective-permute-start(bf16[128,2048]{1,0:T(8,128)(2,1)S(1)} %slice.52), channel_id=1, source_target_pairs={{0,3},{1,0},{2,1},{3,2},{4,7},{5,4},{6,5},{7,6},{8,11},{9,8},{10,9... | collective-permute-start | bytes 1572872 | tf_op jit(solution)/shard_map/ppermute | solution.py:29
  273.3 28.0 %collective-permute-start.14 = (bf16[128,2048]{1,0:T(8,128)(2,1)S(1)}, bf16[128,2048]{1,0:T(8,128)(2,1)S(1)}, u32[]{:S(2)}, u32[]{:S(2)}) collective-permute-start(bf16[128,2048]{1,0:T(8,128)(2,1)S(1)} %slice.53), channel_id=1, source_target_pairs={{0,1},{1,2},{2,3},{3,0},{4,5},{5,6},{6,7},{7,4},{8,9},{9,10},{10,1... | collective-permute-start | bytes 1572872 | tf_op jit(solution)/shard_map/ppermute | solution.py:29
  278.9 22.4 %collective-permute-start.10 = (bf16[576,256]{1,0:T(8,128)(2,1)S(1)}, bf16[576,256]{1,0:T(8,128)(2,1)S(1)}, u32[]{:S(2)}, u32[]{:S(2)}) collective-permute-start(bf16[576,256]{1,0:T(8,128)(2,1)S(1)} %copy-done.22), channel_id=1, source_target_pairs={{0,2},{1,3},{2,0},{3,1},{4,6},{5,7},{6,4},{7,5},{8,10},{9,11},{10,... | collective-permute-start | bytes 884744 | tf_op jit(solution)/shard_map/ppermute | solution.py:29
  (29 other events, 281.8 us)

commit v3 on v2

v3 whole, which is shorter than its diff:
```python
import jax
import jax.numpy as jnp
from jax import lax
from jax.experimental import pallas as pl
from jax.experimental.pallas import tpu as pltpu
from jax.sharding import Mesh, PartitionSpec as P

BF = jnp.bfloat16
F32 = jnp.float32
LANES = 128
CAPACITY = 2
MIB = 1024 * 1024
Z = ("zh", "zl")
YC = ("y", "c")
PLACE = ("zh", "y", "c", "zl")


def dot(a, b, da, db):
    return lax.dot_general(a, b, (((da,), (db,)), ((), ())), preferred_element_type=F32)


def iota(shape, axis):
    return lax.broadcasted_iota(jnp.int32, shape, axis)


def shift(block, step, axes, n):
    return lax.ppermute(block, axes, [(i, (i + step) % n) for i in range(n)])


def tied(*values):
    return lax.optimization_barrier(values)


def vmem():
    return pl.BlockSpec(memory_space=pltpu.VMEM)


def payload_kernel(tok_ref, grad_ref, ids_ref, keep_ref, weight_ref, out_ref, code_ref):
    features = tok_ref.shape[1]
    top, rows = ids_ref.shape
    experts = LANES
    ids, kept = ids_ref[...], keep_ref[...] > 0
    names = iota((experts, rows), 0)
    named = [names == ids[k : k + 1, :] for k in range(top)]
    tally = sum(jnp.where(named[k] & kept[k : k + 1, :], 1.0, 0.0) for k in range(top))
    before = (iota((rows, rows), 0) < iota((rows, rows), 1)).astype(BF)
    earlier = dot(tally.astype(BF), before, 1, 0)
    position = jnp.concatenate(
        [jnp.sum(jnp.where(named[k], earlier, 0.0), axis=0, keepdims=True) for k in range(top)],
        axis=0,
    )
    code = jnp.where(kept, ids.astype(F32) * CAPACITY + position + 1.0, 0.0)
    code_ref[...] = code
    spread = (iota((rows, LANES), 0) == iota((rows, LANES), 1)).astype(BF)
    both = jnp.concatenate([code.astype(BF), weight_ref[...]], axis=0)
    out_ref[:, :features] = tok_ref[...]
    out_ref[:, features : 2 * features] = grad_ref[...]
    out_ref[:, 2 * features :] = dot(both, spread, 1, 0).astype(BF)


def payload_call(tokens, out_grad, ids, keep, weights):
    rows, features = tokens.shape
    return pl.pallas_call(
        payload_kernel,
        out_shape=[
            jax.ShapeDtypeStruct((rows, 2 * features + LANES), BF),
            jax.ShapeDtypeStruct(ids.shape, F32),
        ],
        in_specs=[vmem()] * 5,
        out_specs=[vmem()] * 2,
        name="payload",
    )(tokens, out_grad, ids, keep, weights)


def pack_kernel(step, zs_ref, *refs):
    blocks, out_ref = refs[:-1], refs[-1]
    count = sum(b.shape[0] for b in blocks)
    zn = count // step
    rows, width = out_ref.shape
    features = (width - LANES) // 2
    half = step // 2
    codes = jnp.zeros((half, count), F32)
    weights = jnp.zeros((half, count), F32)
    at = 0
    for block in blocks:
        for first in range(0, block.shape[0], step):
            place = (iota((LANES, count), 0) + at == iota((LANES, count), 1)) & (
                iota((LANES, count), 0) < step
            )
            both = dot(
                block[first : first + step, 2 * features :], place.astype(BF), 1, 0
            )
            codes = codes + both[:half]
            weights = weights + both[half:]
            at += step
    zh, zl = zs_ref[0], zs_ref[1]
    row, col = iota((rows, count), 0), iota((rows, count), 1)
    dest = row // (zn * CAPACITY)
    wanted = ((zh * 64 + dest * 8 + zl) * CAPACITY + row % CAPACITY + 1).astype(F32)
    wanted = jnp.where((row // CAPACITY) % zn == col // step, wanted, -1.0)
    pick = jnp.zeros((rows, count), F32)
    coef = jnp.zeros((rows, count), F32)
    for k in range(half):
        hit = wanted == codes[k : k + 1, :]
        pick = pick + jnp.where(hit, 1.0, 0.0)
        coef = coef + jnp.where(hit, weights[k : k + 1, :], 0.0)
    pick = pick.astype(BF)
    tile = 1024
    for j in range(0, 2 * features, tile):
        total, at = None, 0
        for block in blocks:
            size = block.shape[0]
            part = dot(pick[:, at : at + size], block[:, j : j + tile], 1, 0)
            total = part if total is None else total + part
            at += size
        out_ref[:, j : j + tile] = total.astype(BF)
    out_ref[:, 2 * features :] = jnp.broadcast_to(
        jnp.sum(coef, axis=1, keepdims=True), (rows, LANES)
    ).astype(BF)


def pack_call(zs, blocks, step):
    count, width = sum(b.shape[0] for b in blocks), blocks[0].shape[1]
    rows = 8 * (count // step) * CAPACITY

    def body(*refs):
        pack_kernel(step, *refs)

    return pl.pallas_call(
        body,
        out_shape=jax.ShapeDtypeStruct((rows, width), BF),
        in_specs=[pl.BlockSpec(memory_space=pltpu.SMEM)] + [vmem()] * len(blocks),
        out_specs=vmem(),
        name="pack",
    )(zs, *blocks)


def homes(z, rows):
    row, place = iota((rows, rows), 0), iota((rows, rows), 1)
    quarter = rows // 4
    first, last = row < quarter, row >= 3 * quarter
    inside = jnp.where(first, row, jnp.where(last, row - 3 * quarter, row - quarter))
    zn = jnp.where(first | last, 4, 8)
    source = inside // (zn * CAPACITY)
    zi = (inside // CAPACITY) % zn
    near = jnp.where(zi < 4, -1 - 4 * zi, 17 - 4 * zi)
    offset = jnp.where(first, -4 * zi, jnp.where(last, 2 - 4 * zi, near))
    zed = (z + offset + 32) % 16
    home = ((zed // 8) * 64 + source * 8 + zed % 8) * CAPACITY + inside % CAPACITY
    return (home == place).astype(BF)


def rows_kernel(zs_ref, *refs):
    srcs, p_ref, dgu_refs, pd_refs = refs[:14], refs[14], refs[15:19], refs[19:23]
    gu, dn, rows, sems = refs[23:]
    hid = dn.shape[1]
    half = hid // 2
    count, width = rows.shape
    features = (width - LANES) // 2
    quarter = count // 4
    targets = [
        rows.at[pl.ds(0, quarter)],
        rows.at[pl.ds(quarter, 2 * quarter)],
        rows.at[pl.ds(3 * quarter, quarter)],
        gu.at[0, pl.ds(0, hid)],
        gu.at[0, pl.ds(hid, hid)],
        dn.at[0],
        gu.at[1],
        dn.at[1],
        gu.at[2],
        dn.at[2],
        gu.at[3, pl.ds(0, hid)],
        gu.at[3, pl.ds(hid, hid)],
        dn.at[3, pl.ds(0, half)],
        dn.at[3, pl.ds(half, half)],
    ]
    order = [(0, 1, 2, 3, 4, 5), (6, 7), (8, 9), (10, 11, 12, 13)]
    copies = [pltpu.make_async_copy(s, t, sems.at[i]) for i, (s, t) in enumerate(zip(srcs, targets))]
    for copy in copies:
        copy.start()
    home = homes(zs_ref[0] * 8 + zs_ref[1], count)
    score = None
    scaled = []
    for q, needed in enumerate(order):
        for i in needed:
            copies[i].wait()
        if q == 0:
            coef = rows[:, 2 * features :].astype(F32).T[0:1, :]
        pre = dot(gu[q], rows[:, :features], 1, 1)
        back = dot(dn[q], rows[:, features : 2 * features], 1, 1)
        gate_pre, up_pre = pre[:hid], pre[hid:]
        sigma = jax.nn.sigmoid(gate_pre)
        active = gate_pre * sigma
        hidden = active * up_pre
        part = jnp.sum(hidden.astype(BF).astype(F32) * back, axis=0, keepdims=True)
        score = part if score is None else score + part
        d_hidden = coef * back
        dgu_refs[q][0:hid, :] = (
            d_hidden * up_pre * sigma * (1.0 + gate_pre * (1.0 - sigma))
        ).astype(BF)
        dgu_refs[q][hid:, :] = (d_hidden * active).astype(BF)
        scaled.append((coef * hidden).astype(BF))
    moved = [dot(d[...], home, 1, 0).astype(BF) for d in dgu_refs]
    tile = 512
    for j in range(0, features, tile):
        total = None
        for q in range(4):
            part = dot(moved[q], gu[q, :, j : j + tile], 0, 0)
            total = part if total is None else total + part
        p_ref[:, j : j + tile] = total.astype(BF)
    score = dot(jnp.broadcast_to(score, (LANES, count)).astype(BF), home, 1, 0)
    p_ref[:, features:] = score.T.astype(BF)
    for j in range(0, features, tile):
        grads = rows[:, features + j : features + j + tile]
        for q in range(4):
            pd_refs[q][:, j : j + tile] = dot(scaled[q], grads, 1, 0).astype(pd_refs[q].dtype)


def rows_call(zs, chunks, gate, up, down, gu_far, dn_far):
    count = sum(c.shape[0] for c in chunks)
    width = chunks[0].shape[1]
    hid, features = gate.shape
    gu_left, gu_right, gu_a, gu_b = gu_far
    dn_left, dn_right, dn_a, dn_b = dn_far
    srcs = [*chunks, gate, up, down, gu_left, dn_left, gu_right, dn_right, gu_a, gu_b, dn_a, dn_b]
    return pl.pallas_call(
        rows_kernel,
        out_shape=[jax.ShapeDtypeStruct((count, features + LANES), BF)]
        + [jax.ShapeDtypeStruct((2 * hid, count), BF)] * 4
        + [jax.ShapeDtypeStruct((hid, features), F32)]
        + [jax.ShapeDtypeStruct((hid, features), BF)] * 3,
        in_specs=[pl.BlockSpec(memory_space=pltpu.SMEM)]
        + [pl.BlockSpec(memory_space=pl.ANY)] * len(srcs),
        out_specs=[vmem()] * 9,
        scratch_shapes=[
            pltpu.VMEM((4, 2 * hid, features), BF),
            pltpu.VMEM((4, hid, features), BF),
            pltpu.VMEM((count, width), BF),
            pltpu.SemaphoreType.DMA((len(srcs),)),
        ],
        compiler_params=pltpu.CompilerParams(vmem_limit_bytes=58 * MIB),
        cost_estimate=pl.CostEstimate(
            flops=2 * count * features * hid * 4 * 6,
            bytes_accessed=2 * features * hid * 18 + 6 * count * features,
            transcendentals=count * hid * 4,
        ),
        name="rows",
    )(zs, *srcs)


def weights_kernel(*refs):
    d_refs, x_refs, (gate_ref, up_ref) = refs[:4], refs[4:9], refs[9:]
    hid = gate_ref.shape[0]
    half = d_refs[3].shape[1] // 2
    parts = [dot(d[...], x[...], 1, 0) for d, x in zip(d_refs[:3], x_refs[:3])]
    parts.append(dot(d_refs[3][:, :half], x_refs[3][...], 1, 0))
    parts.append(dot(d_refs[3][:, half:], x_refs[4][...], 1, 0))
    total = sum(parts[1:], parts[0]).astype(BF)
    gate_ref[...] = total[:hid]
    up_ref[...] = total[hid:]


def weights_call(ds, xs):
    tile = 512
    hid, features = ds[0].shape[0] // 2, xs[0].shape[1]
    whole = [pl.BlockSpec(d.shape, lambda j: (0, 0)) for d in ds]
    tiled = [pl.BlockSpec((x.shape[0], tile), lambda j: (0, j)) for x in xs]
    rows = sum(d.shape[1] for d in ds)
    return pl.pallas_call(
        weights_kernel,
        grid=(features // tile,),
        out_shape=[jax.ShapeDtypeStruct((hid, features), BF)] * 2,
        in_specs=whole + tiled,
        out_specs=[pl.BlockSpec((hid, tile), lambda j: (0, j))] * 2,
        compiler_params=pltpu.CompilerParams(vmem_limit_bytes=24 * MIB),
        cost_estimate=pl.CostEstimate(
            flops=4 * rows * features * hid,
            bytes_accessed=2 * features * (rows + 2 * hid),
            transcendentals=0,
        ),
        name="weight_grads",
    )(*ds, *xs)


def home_kernel(code_ref, home_ref, grad_ref, score_ref):
    top, rows = code_ref.shape
    places = home_ref.shape[0]
    features = grad_ref.shape[1]
    wanted = (iota((places, rows), 0) + 1).astype(F32)
    hits = [jnp.where(wanted == code_ref[k : k + 1, :], 1.0, 0.0) for k in range(top)]
    score = home_ref[:, features : features + 1].astype(F32)
    score_ref[...] = jnp.concatenate(
        [jnp.sum(hit * score, axis=0, keepdims=True) for hit in hits], axis=0
    ).astype(BF)
    pick = sum(hits).astype(BF)
    grad_ref[...] = dot(pick, home_ref[:, :features], 0, 0).astype(BF)


def home_call(code, home, features):
    return pl.pallas_call(
        home_kernel,
        out_shape=[
            jax.ShapeDtypeStruct((code.shape[1], features), BF),
            jax.ShapeDtypeStruct(code.shape, BF),
        ],
        in_specs=[vmem()] * 2,
        out_specs=[vmem()] * 2,
        name="home",
    )(code, home)


def local(tokens, out_grad, expert_ids, keep_flags, route_weights, gate_w, up_w, down_w):
    nz, n = lax.axis_size(Z), lax.axis_size("x")
    step, features = tokens.shape
    zs = jnp.stack([lax.axis_index("zh"), lax.axis_index("zl")]).astype(jnp.int32)
    gate, up, down = gate_w[0], up_w[0], down_w[0]
    half = gate.shape[0] // 2

    own, code = payload_call(tokens, out_grad, expert_ids.T, keep_flags.T, route_weights.T)

    gu = jnp.concatenate([gate, up], axis=0)
    gu_left, gu_right = shift(gu, 1, "x", n), shift(gu, -1, "x", n)
    dn_left, dn_right = shift(down, 1, "x", n), shift(down, -1, "x", n)

    far = [shift(own, s, Z, nz) for s in (4, 8, 12)]
    chunk = jnp.concatenate([own, *far], axis=0)
    left, right = shift(chunk, 1, Z, nz), shift(chunk, -1, Z, nz)

    def exchange(packed):
        rows, width = packed.shape
        return lax.all_to_all(
            packed.reshape(8, rows // 8, width), YC, split_axis=0, concat_axis=0, tiled=True
        ).reshape(rows, width)

    rows_a = exchange(pack_call(zs, [chunk], step))
    rest_a = shift(right[: 2 * step], -1, Z, nz)
    rest_b = shift(left[step : 3 * step], 1, Z, nz)
    left, right, rows_a = tied(left, right, rows_a)
    packed = pack_call(zs, [left, right], step)

    hid = gate.shape[0]
    gu_a, gu_b = shift(gu_right[:hid], -1, "x", n), shift(gu_left[hid:], 1, "x", n)
    rows_b = exchange(packed)
    rest_a, rest_b, rows_b, dn_left, dn_right = tied(rest_a, rest_b, rows_b, dn_left, dn_right)
    dn_a, dn_b = shift(dn_right[:half], -1, "x", n), shift(dn_left[half:], 1, "x", n)
    rows_c = exchange(pack_call(zs, [rest_a, rest_b], step))

    chunks = [rows_a, rows_b, rows_c]
    x = jnp.concatenate([c[:, :features] for c in chunks], axis=0)
    mid = x.shape[0] // 2
    x_left, x_right = shift(x, 1, "x", n), shift(x, -1, "x", n)
    x_a, x_b = shift(x_right[:mid], -1, "x", n), shift(x_left[mid:], 1, "x", n)

    result = rows_call(
        zs,
        chunks,
        gate,
        up,
        down,
        (gu_left, gu_right, gu_a, gu_b),
        (dn_left, dn_right, dn_a, dn_b),
    )
    back, (d_own, d_left, d_right, d_two) = result[0], result[1:5]
    p_own, p_left, p_right, p_two = result[5:]
    home = lax.all_to_all(
        back.reshape(-1, CAPACITY, back.shape[1]), PLACE, split_axis=0, concat_axis=0, tiled=True
    ).reshape(back.shape)

    ds = [d_own, shift(d_right, 1, "x", n), shift(d_left, -1, "x", n), shift(d_two, 2, "x", n)]
    grad_gate, grad_up = weights_call(ds, [x, x_left, x_right, x_a, x_b])

    via_a = shift(p_two[:half], 1, "x", n)
    via_b = shift(p_two[half:], -1, "x", n)
    left_low = shift(p_right[half:], 1, "x", n)
    right_top = shift(p_left[:half], -1, "x", n)
    left_top = shift((p_right[:half].astype(F32) + via_a.astype(F32)).astype(BF), 1, "x", n)
    right_low = shift((p_left[half:].astype(F32) + via_b.astype(F32)).astype(BF), -1, "x", n)
    grad_down = jnp.concatenate(
        [
            (p_own[:half] + left_top.astype(F32) + right_top.astype(F32)).astype(BF),
            (p_own[half:] + left_low.astype(F32) + right_low.astype(F32)).astype(BF),
        ],
        axis=0,
    )

    token_grad, slot_score = home_call(code, home, features)
    return (token_grad, slot_score.T, grad_gate[None], grad_up[None], grad_down[None])


def solution(mesh):
    fine = Mesh(mesh.devices.reshape(2, 4, 2, 8, 4), ("zh", "y", "c", "zl", "x"))
    by_row = P(("zh", "y", "c", "zl", "x"), None)
    by_expert = P(PLACE, "x", None)
    return jax.shard_map(
        local,
        mesh=fine,
        in_specs=(by_row,) * 5 + (by_expert,) * 3,
        out_specs=(by_row,) * 2 + (by_expert,) * 3,
        check_vma=False,
    )
```

time: 315 us -> 259 us (0.82)
  waiting for transfers between devices: 154 us -> 70.3 us
  starting transfers between devices: 110 us -> 134 us
  Pallas kernels: 13.2 us -> 29.4 us
  local copies, waits for them, and re-layouts: 29.6 us -> 18.2 us
    all_to_all x3 -> x4, waiting for transfers between devices: 54.3 us -> 8.15 us  [the longest x3 8.15 us: exchange(): lax.all_to_all(packed.reshape(8, rows // 8, width), YC, split_axis=0, con...]
    ppermute x19 -> x28, starting transfers between devices: 64.7 us -> 107 us  [shift(): return lax.ppermute(block, axes, [(i, (i + step) % n) for i in range(n)])]
    ppermute x19 -> x28, waiting for transfers between devices: 100 us -> 62.2 us  [shift(): return lax.ppermute(block, axes, [(i, (i + step) % n) for i in range(n)])]
    pallas_call x1 -> x6, Pallas kernels: 7.53 us -> 25.6 us  [the longest x1 13.1 us: rows_call(): pl.pallas_call(rows_kernel, out_shape=[jax.ShapeDtypeStruct((count, featu...]
    all_to_all x3 -> x4, starting transfers between devices: 44.9 us -> 27.2 us  [the longest x1 14.5 us: local(): lax.all_to_all(back.reshape(-1, CAPACITY, back.shape[1]), PLACE, split_ax...]
    unnamed x65 -> x41, local copies, waits for them, and re-layouts: 17.5 us -> 6.17 us
    reshape x6 -> x2, local copies, waits for them, and re-layouts: 7.47 us -> 3.58 us  [the longest x1 2.32 us: local(): back.reshape(-1, CAPACITY, back.shape[1])]
    slice x8 -> x14, local copies, waits for them, and re-layouts: 4.02 us -> 7.74 us  [the longest x3 3.09 us: local(): x = jnp.concatenate([c[:, :features] for c in chunks], axis=0)]
  transfers between devices with their start and end apart: 22 -> 32, of which waited for: 9 -> 10; matrix products, arithmetic and copies ran while one was open for 3% -> 5% of each run, Pallas kernels for 2% -> 5%
where the time goes in v3:
time: 259 us; the launch traced here: 257 us
  starting transfers between devices  134 us (52%)
  waiting for transfers between devices  70.3 us (27%)
  Pallas kernels  29.4 us (11%)
  local copies, waits for them, and re-layouts  18.2 us (7%)
  other arithmetic  3.71 us (1%)
    ppermute x28, starting transfers between devices, shift(): return lax.ppermute(block, axes, [(i, (i + step) % n) for i in range(n)])  107 us
    ppermute x28, waiting for transfers between devices, shift(): return lax.ppermute(block, axes, [(i, (i + step) % n) for i in range(n)])  62.2 us
    all_to_all x1, starting transfers between devices, local(): lax.all_to_all(back.reshape(-1, CAPACITY, back.shape[1]), PLACE, split_ax...  14.5 us
    pallas_call x1, Pallas kernels, rows_call(): pl.pallas_call(rows_kernel, out_shape=[jax.ShapeDtypeStruct((count, featu...  13.1 us
    all_to_all x3, starting transfers between devices, exchange(): lax.all_to_all(packed.reshape(8, rows // 8, width), YC, split_axis=0, con...  12.7 us
    pallas_call x3, Pallas kernels, pack_call(): pl.pallas_call(body, out_shape=jax.ShapeDtypeStruct((rows, width), BF), i...  8.3 us
    all_to_all x3, waiting for transfers between devices, exchange(): lax.all_to_all(packed.reshape(8, rows // 8, width), YC, split_axis=0, con...  8.15 us
    unnamed x41, local copies, waits for them, and re-layouts  6.17 us
  transfers between devices with their start and end apart: 32, of which 10 were waited for; matrix products, arithmetic and copies ran while one was open for 5% of the time, Pallas kernels for 5%

profile of v3, /device:TPU:6, one launch (start us, length us, event | category | flops | bytes accessed | tf_op | source)
XLA Modules:
  0.0 257.1 jit_solution(14193486582147370494)
XLA Ops:
  2.5 9.1 %collective-permute-start = (bf16[16,4224]{1,0:T(8,128)(2,1)}, bf16[16,4224]{1,0:T(8,128)(2,1)S(1)}, u32[]{:S(2)}, u32[]{:S(2)}) collective-permute-start(bf16[16,4224]{1,0:T(8,128)(2,1)} %get-tuple-element.29), channel_id=1, source_target_pairs={{0,16},{4,20},{8,24},{12,28},{16,256},{20,260},{24,264},{28,268},{... | collective-permute-start | bytes 405512 | tf_op jit(solution)/shard_map/ppermute | solution.py:27
  11.6 10.9 %collective-permute-start.1 = (bf16[16,4224]{1,0:T(8,128)(2,1)}, bf16[16,4224]{1,0:T(8,128)(2,1)S(1)}, u32[]{:S(2)}, u32[]{:S(2)}) collective-permute-start(bf16[16,4224]{1,0:T(8,128)(2,1)} %get-tuple-element.29), channel_id=1, source_target_pairs={{0,256},{4,260},{8,264},{12,268},{16,272},{20,276},{24,280},{28,28... | collective-permute-start | bytes 405512 | tf_op jit(solution)/shard_map/ppermute | solution.py:27
  22.6 5.5 %collective-permute-start.2 = (bf16[16,4224]{1,0:T(8,128)(2,1)}, bf16[16,4224]{1,0:T(8,128)(2,1)S(1)}, u32[]{:S(2)}, u32[]{:S(2)}) collective-permute-start(bf16[16,4224]{1,0:T(8,128)(2,1)} %get-tuple-element.29), channel_id=1, source_target_pairs={{0,272},{4,276},{8,280},{12,284},{16,0},{20,4},{24,8},{28,12},{256... | collective-permute-start | bytes 405512 | tf_op jit(solution)/shard_map/ppermute | solution.py:27
  36.8 4.7 %collective-permute-done.1 = bf16[16,4224]{1,0:T(8,128)(2,1)S(1)} collective-permute-done((bf16[16,4224]{1,0:T(8,128)(2,1)}, bf16[16,4224]{1,0:T(8,128)(2,1)S(1)}, u32[]{:S(2)}, u32[]{:S(2)}) %collective-permute-start.1) | collective-permute-done | bytes 135200 | tf_op jit(solution)/shard_map/ppermute | solution.py:27
  42.1 4.9 %collective-permute-done.2 = bf16[16,4224]{1,0:T(8,128)(2,1)S(1)} collective-permute-done((bf16[16,4224]{1,0:T(8,128)(2,1)}, bf16[16,4224]{1,0:T(8,128)(2,1)S(1)}, u32[]{:S(2)}, u32[]{:S(2)}) %collective-permute-start.2) | collective-permute-done | bytes 135200 | tf_op jit(solution)/shard_map/ppermute | solution.py:27
  49.5 5.1 %collective-permute-start.4 = (bf16[64,4224]{1,0:T(8,128)(2,1)}, bf16[64,4224]{1,0:T(8,128)(2,1)S(1)}, u32[]{:S(2)}, u32[]{:S(2)}) collective-permute-start(bf16[64,4224]{1,0:T(8,128)(2,1)} %constant_dynamic-update-slice_fusion.refs_1_), channel_id=1, source_target_pairs={{0,284},{4,0},{8,4},{12,8},{16,12},{20,16},{24,20},{28,24},{256,28... | collective-permute-start | bytes 1622024 | tf_op jit(solution)/shard_map/ppermute | solution.py:27
  57.6 4.5 %all-to-all-start = ((bf16[8,8,4224]{2,1,0:T(8,128)(2,1)}), bf16[8,8,4224]{2,1,0:T(8,128)(2,1)S(1)}, u32[]{:S(2)}, u32[]{:S(2)}) async-start(bf16[8,8,4224]{2,1,0:T(8,128)(2,1)} %bitcast.23), calls=%async_computation | async-start | bytes 1081344 | tf_op jit(solution)/shard_map/all_to_all | solution.py:331
  64.5 8.1 %all-to-all-done = bf16[8,8,4224]{2,1,0:T(8,128)(2,1)S(1)} async-done(((bf16[8,8,4224]{2,1,0:T(8,128)(2,1)}), bf16[8,8,4224]{2,1,0:T(8,128)(2,1)S(1)}, u32[]{:S(2)}, u32[]{:S(2)}) %all-to-all-start) | async-done | bytes 540704 | tf_op jit(solution)/shard_map/all_to_all | solution.py:331
  88.2 4.6 %collective-permute-start.12 = (bf16[192,2048]{1,0:T(8,128)(2,1)S(1)}, bf16[192,2048]{1,0:T(8,128)(2,1)}, u32[]{:S(2)}, u32[]{:S(2)}) collective-permute-start(bf16[192,2048]{1,0:T(8,128)(2,1)S(1)} %slice.79), channel_id=1, source_target_pairs={{0,1},{1,2},{2,3},{3,0},{4,5},{5,6},{6,7},{7,4},{8,9},{9,10},{10,1... | collective-permute-start | bytes 2359304 | tf_op jit(solution)/shard_map/ppermute | solution.py:27
  94.9 3.8 %collective-permute-start.6 = (bf16[32,4224]{1,0:T(8,128)(2,1)S(1)}, bf16[32,4224]{1,0:T(8,128)(2,1)}, u32[]{:S(2)}, u32[]{:S(2)}) collective-permute-start(bf16[32,4224]{1,0:T(8,128)(2,1)S(1)} %slice.77), channel_id=1, source_target_pairs={{0,4},{4,8},{8,12},{12,16},{16,20},{20,24},{24,28},{28,256},{256,2... | collective-permute-start | bytes 811016 | tf_op jit(solution)/shard_map/ppermute | solution.py:27
  98.7 5.5 %collective-permute-done.8.refs_9_ = bf16[192,2048]{1,0:T(8,128)(2,1)S(1)} collective-permute-done((bf16[192,2048]{1,0:T(8,128)(2,1)}, bf16[192,2048]{1,0:T(8,128)(2,1)S(1)}, u32[]{:S(2)}, u32[]{:S(2)}) %collective-permute-start.8) | collective-permute-done | bytes 786464 | tf_op jit(solution)/shard_map/ppermute | solution.py:27
  108.8 4.6 %all-to-all-start.2 = ((bf16[8,8,4224]{2,1,0:T(8,128)(2,1)}), bf16[8,8,4224]{2,1,0:T(8,128)(2,1)S(1)}, u32[]{:S(2)}, u32[]{:S(2)}) async-start(bf16[8,8,4224]{2,1,0:T(8,128)(2,1)} %bitcast.22), calls=%async_computation.2 | async-start | bytes 1081344 | tf_op jit(solution)/shard_map/all_to_all | solution.py:331
  117.4 5.3 %collective-permute-start.14 = (bf16[96,2048]{1,0:T(8,128)(2,1)S(1)}, bf16[96,2048]{1,0:T(8,128)(2,1)}, u32[]{:S(2)}, u32[]{:S(2)}) collective-permute-start(bf16[96,2048]{1,0:T(8,128)(2,1)S(1)} %slice.62), channel_id=1, source_target_pairs={{0,1},{1,2},{2,3},{3,0},{4,5},{5,6},{6,7},{7,4},{8,9},{9,10},{10,1... | collective-permute-start | bytes 1179656 | tf_op jit(solution)/shard_map/ppermute | solution.py:27
  122.7 6.3 %collective-permute-done.13.refs_12_ = bf16[96,2048]{1,0:T(8,128)(2,1)S(1)} collective-permute-done((bf16[96,2048]{1,0:T(8,128)(2,1)S(1)}, bf16[96,2048]{1,0:T(8,128)(2,1)S(1)}, u32[]{:S(2)}, u32[]{:S(2)}) %collective-permute-start.13) | collective-permute-done | bytes 393248 | tf_op jit(solution)/shard_map/ppermute | solution.py:27
  132.1 13.1 %rows.1 = (bf16[256,2176]{1,0:T(8,128)(2,1)}, bf16[384,256]{1,0:T(8,128)(2,1)}, bf16[384,256]{1,0:T(8,128)(2,1)}, bf16[384,256]{1,0:T(8,128)(2,1)}, bf16[384,256...) custom-call(s32[2]{0:T(128)} %pad_add_fusion.refs_0_.zs_ref, ...), custom_call_target="tpu_custom_call" | custom-call | flops 4831838208 | bytes 17301504 | tf_op jit(solution)/shard_map/rows/pallas_call | solution.py:226
  147.5 14.5 %all-to-all-start.3 = ((bf16[128,2,2176]{2,1,0:T(2,128)(2,1)}), bf16[128,2,2176]{2,1,0:T(2,128)(2,1)S(1)}, u32[]{:S(2)}, u32[]{:S(2)}) async-start(bf16[128,2,2176]{2,1,0:T(2,128)(2,1)} %reshape.40), calls=%async_computation.3 | async-start | bytes 2228224 | tf_op jit(solution)/shard_map/all_to_all | solution.py:365
  162.1 5.7 %collective-permute-start.22 = (bf16[96,2048]{1,0:T(8,128)(2,1)S(1)}, bf16[96,2048]{1,0:T(8,128)(2,1)S(1)}, u32[]{:S(2)}, u32[]{:S(2)}) collective-permute-start(bf16[96,2048]{1,0:T(8,128)(2,1)S(1)} %get-tuple-element.53), channel_id=1, source_target_pairs={{0,1},{1,2},{2,3},{3,0},{4,5},{5,6},{6,7},{7,4},{8,9},{9,10},{10,1... | collective-permute-start | bytes 1179656 | tf_op jit(solution)/shard_map/ppermute | solution.py:27
  173.1 5.1 %collective-permute-start.18 = (bf16[256,2048]{1,0:T(8,128)(2,1)S(1)}, bf16[256,2048]{1,0:T(8,128)(2,1)S(1)}, u32[]{:S(2)}, u32[]{:S(2)}) collective-permute-start(bf16[256,2048]{1,0:T(8,128)(2,1)S(1)} %pad_maximum_fusion.1.refs_4_), channel_id=1, source_target_pairs={{0,1},{1,2},{2,3},{3,0},{4,5},{5,6},{6,7},{7,4},{8,9},{9,10},{10,1... | collective-permute-start | bytes 3145736 | tf_op jit(solution)/shard_map/ppermute | solution.py:27
  182.2 5.3 %collective-permute-start.25 = (bf16[96,2048]{1,0:T(8,128)(2,1)S(1)}, bf16[96,2048]{1,0:T(8,128)(2,1)S(1)}, u32[]{:S(2)}, u32[]{:S(2)}) collective-permute-start(bf16[96,2048]{1,0:T(8,128)(2,1)S(1)} %slice.73), channel_id=1, source_target_pairs={{0,1},{1,2},{2,3},{3,0},{4,5},{5,6},{6,7},{7,4},{8,9},{9,10},{10,1... | collective-permute-start | bytes 1179656 | tf_op jit(solution)/shard_map/ppermute | solution.py:27
  187.6 27.9 %collective-permute-done.26 = bf16[96,2048]{1,0:T(8,128)(2,1)S(1)} collective-permute-done((bf16[96,2048]{1,0:T(8,128)(2,1)S(1)}, bf16[96,2048]{1,0:T(8,128)(2,1)S(1)}, u32[]{:S(2)}, u32[]{:S(2)}) %collective-permute-start.26) | collective-permute-done | bytes 393248 | tf_op jit(solution)/shard_map/ppermute | solution.py:27
  217.6 3.9 %collective-permute-start.27 = (bf16[96,2048]{1,0:T(8,128)(2,1)S(1)}, bf16[96,2048]{1,0:T(8,128)(2,1)S(1)}, u32[]{:S(2)}, u32[]{:S(2)}) collective-permute-start(bf16[96,2048]{1,0:T(8,128)(2,1)S(1)} %add_convert_fusion.1), channel_id=1, source_target_pairs={{0,3},{1,0},{2,1},{3,2},{4,7},{5,4},{6,5},{7,6},{8,11},{9,8},{10,9... | collective-permute-start | bytes 1179656 | tf_op jit(solution)/shard_map/ppermute | solution.py:27
  230.1 4.5 %collective-permute-start.20 = (bf16[128,2048]{1,0:T(8,128)(2,1)S(1)}, bf16[128,2048]{1,0:T(8,128)(2,1)S(1)}, u32[]{:S(2)}, u32[]{:S(2)}) collective-permute-start(bf16[128,2048]{1,0:T(8,128)(2,1)S(1)} %slice.81), channel_id=1, source_target_pairs={{0,3},{1,0},{2,1},{3,2},{4,7},{5,4},{6,5},{7,6},{8,11},{9,8},{10,9... | collective-permute-start | bytes 1572872 | tf_op jit(solution)/shard_map/ppermute | solution.py:27
  240.3 9.5 %collective-permute-done.20.refs_7_ = bf16[128,2048]{1,0:T(8,128)(2,1)S(1)} collective-permute-done((bf16[128,2048]{1,0:T(8,128)(2,1)S(1)}, bf16[128,2048]{1,0:T(8,128)(2,1)S(1)}, u32[]{:S(2)}, u32[]{:S(2)}) %collective-permute-start.20) | collective-permute-done | bytes 524320 | tf_op jit(solution)/shard_map/ppermute | solution.py:27
  249.8 3.8 %weight_grads.1 = (bf16[192,2048]{1,0:T(8,128)(2,1)}, bf16[192,2048]{1,0:T(8,128)(2,1)}) custom-call(bf16[384,256]{1,0:T(8,128)(2,1)S(1)} %copy-done, bf16[384,256]{1,0:T(8,128)(2,1)S(1)} %collective-permute-done.15.refs_1_, bf16[384,256]{1,0:T(8,128)(2,1)S(1)} %collective-permute-done.16.refs_2_, bf16[384,256]{1,0:T(8,128)(2,1)S(1)} %collective-permute-done.17.refs_3_, ...), custom_call_target="tpu_custom_call" | custom-call | flops 1610612736 | bytes 5767168 | tf_op jit(solution)/shard_map/weight_grads/pallas_call | solution.py:269
  (112 shorter events, 79.4 us)
Async XLA Ops:
  2.5 33.5 %collective-permute-start = (bf16[16,4224]{1,0:T(8,128)(2,1)}, bf16[16,4224]{1,0:T(8,128)(2,1)S(1)}, u32[]{:S(2)}, u32[]{:S(2)}) collective-permute-start(bf16[16,4224]{1,0:T(8,128)(2,1)} %get-tuple-element.29), channel_id=1, source_target_pairs={{0,16},{4,20},{8,24},{12,28},{16,256},{20,260},{24,264},{28,268},{... | collective-permute-start | bytes 405512 | tf_op jit(solution)/shard_map/ppermute | solution.py:27
  11.6 29.8 %collective-permute-start.1 = (bf16[16,4224]{1,0:T(8,128)(2,1)}, bf16[16,4224]{1,0:T(8,128)(2,1)S(1)}, u32[]{:S(2)}, u32[]{:S(2)}) collective-permute-start(bf16[16,4224]{1,0:T(8,128)(2,1)} %get-tuple-element.29), channel_id=1, source_target_pairs={{0,256},{4,260},{8,264},{12,268},{16,272},{20,276},{24,280},{28,28... | collective-permute-start | bytes 405512 | tf_op jit(solution)/shard_map/ppermute | solution.py:27
  22.6 24.4 %collective-permute-start.2 = (bf16[16,4224]{1,0:T(8,128)(2,1)}, bf16[16,4224]{1,0:T(8,128)(2,1)S(1)}, u32[]{:S(2)}, u32[]{:S(2)}) collective-permute-start(bf16[16,4224]{1,0:T(8,128)(2,1)} %get-tuple-element.29), channel_id=1, source_target_pairs={{0,272},{4,276},{8,280},{12,284},{16,0},{20,4},{24,8},{28,12},{256... | collective-permute-start | bytes 405512 | tf_op jit(solution)/shard_map/ppermute | solution.py:27
  29.6 57.4 %collective-permute-start.9 = (bf16[384,2048]{1,0:T(8,128)(2,1)S(1)}, bf16[384,2048]{1,0:T(8,128)(2,1)}, u32[]{:S(2)}, u32[]{:S(2)}) collective-permute-start(bf16[384,2048]{1,0:T(8,128)(2,1)S(1)} %pad_maximum_fusion), channel_id=1, source_target_pairs={{0,1},{1,2},{2,3},{3,0},{4,5},{5,6},{6,7},{7,4},{8,9},{9,10},{10,1... | collective-permute-start | bytes 4718600 | tf_op jit(solution)/shard_map/ppermute | solution.py:27
  31.9 51.4 %collective-permute-start.10 = (bf16[384,2048]{1,0:T(8,128)(2,1)S(1)}, bf16[384,2048]{1,0:T(8,128)(2,1)}, u32[]{:S(2)}, u32[]{:S(2)}) collective-permute-start(bf16[384,2048]{1,0:T(8,128)(2,1)S(1)} %pad_maximum_fusion), channel_id=1, source_target_pairs={{0,3},{1,0},{2,1},{3,2},{4,7},{5,4},{6,5},{7,6},{8,11},{9,8},{10,9... | collective-permute-start | bytes 4718600 | tf_op jit(solution)/shard_map/ppermute | solution.py:27
  47.6 25.0 %collective-permute-start.3 = (bf16[64,4224]{1,0:T(8,128)(2,1)}, bf16[64,4224]{1,0:T(8,128)(2,1)S(1)}, u32[]{:S(2)}, u32[]{:S(2)}) collective-permute-start(bf16[64,4224]{1,0:T(8,128)(2,1)} %constant_dynamic-update-slice_fusion.refs_1_), channel_id=1, source_target_pairs={{0,4},{4,8},{8,12},{12,16},{16,20},{20,24},{24,28},{28,256},{256,2... | collective-permute-start | bytes 1622024 | tf_op jit(solution)/shard_map/ppermute | solution.py:27
  49.5 23.1 %collective-permute-start.4 = (bf16[64,4224]{1,0:T(8,128)(2,1)}, bf16[64,4224]{1,0:T(8,128)(2,1)S(1)}, u32[]{:S(2)}, u32[]{:S(2)}) collective-permute-start(bf16[64,4224]{1,0:T(8,128)(2,1)} %constant_dynamic-update-slice_fusion.refs_1_), channel_id=1, source_target_pairs={{0,284},{4,0},{8,4},{12,8},{16,12},{20,16},{24,20},{28,24},{256,28... | collective-permute-start | bytes 1622024 | tf_op jit(solution)/shard_map/ppermute | solution.py:27
  62.1 32.8 %collective-permute-start.7 = (bf16[192,2048]{1,0:T(8,128)(2,1)}, bf16[192,2048]{1,0:T(8,128)(2,1)}, u32[]{:S(2)}, u32[]{:S(2)}) collective-permute-start(bf16[192,2048]{1,0:T(8,128)(2,1)} %bitcast.9.refs_5_), channel_id=1, source_target_pairs={{0,1},{1,2},{2,3},{3,0},{4,5},{5,6},{6,7},{7,4},{8,9},{9,10},{10,1... | collective-permute-start | bytes 2359304 | tf_op jit(solution)/shard_map/ppermute | solution.py:27
  76.8 29.1 %all-to-all-start.1 = ((bf16[8,16,4224]{2,1,0:T(8,128)(2,1)}), bf16[8,16,4224]{2,1,0:T(8,128)(2,1)S(1)}, u32[]{:S(2)}, u32[]{:S(2)}) async-start(bf16[8,16,4224]{2,1,0:T(8,128)(2,1)} %bitcast.19), calls=%async_computation.1 | async-start | bytes 2162688 | tf_op jit(solution)/shard_map/all_to_all | solution.py:331
  80.4 23.8 %collective-permute-start.8 = (bf16[192,2048]{1,0:T(8,128)(2,1)}, bf16[192,2048]{1,0:T(8,128)(2,1)S(1)}, u32[]{:S(2)}, u32[]{:S(2)}) collective-permute-start(bf16[192,2048]{1,0:T(8,128)(2,1)} %bitcast.9.refs_5_), channel_id=1, source_target_pairs={{0,3},{1,0},{2,1},{3,2},{4,7},{5,4},{6,5},{7,6},{8,11},{9,8},{10,9... | collective-permute-start | bytes 2359304 | tf_op jit(solution)/shard_map/ppermute | solution.py:27
  84.5 46.8 %collective-permute-start.11 = (bf16[192,2048]{1,0:T(8,128)(2,1)S(1)}, bf16[192,2048]{1,0:T(8,128)(2,1)}, u32[]{:S(2)}, u32[]{:S(2)}) collective-permute-start(bf16[192,2048]{1,0:T(8,128)(2,1)S(1)} %slice.78), channel_id=1, source_target_pairs={{0,3},{1,0},{2,1},{3,2},{4,7},{5,4},{6,5},{7,6},{8,11},{9,8},{10,9... | collective-permute-start | bytes 2359304 | tf_op jit(solution)/shard_map/ppermute | solution.py:27
  88.2 43.1 %collective-permute-start.12 = (bf16[192,2048]{1,0:T(8,128)(2,1)S(1)}, bf16[192,2048]{1,0:T(8,128)(2,1)}, u32[]{:S(2)}, u32[]{:S(2)}) collective-permute-start(bf16[192,2048]{1,0:T(8,128)(2,1)S(1)} %slice.79), channel_id=1, source_target_pairs={{0,1},{1,2},{2,3},{3,0},{4,5},{5,6},{6,7},{7,4},{8,9},{9,10},{10,1... | collective-permute-start | bytes 2359304 | tf_op jit(solution)/shard_map/ppermute | solution.py:27
  108.8 22.5 %all-to-all-start.2 = ((bf16[8,8,4224]{2,1,0:T(8,128)(2,1)}), bf16[8,8,4224]{2,1,0:T(8,128)(2,1)S(1)}, u32[]{:S(2)}, u32[]{:S(2)}) async-start(bf16[8,8,4224]{2,1,0:T(8,128)(2,1)} %bitcast.22), calls=%async_computation.2 | async-start | bytes 1081344 | tf_op jit(solution)/shard_map/all_to_all | solution.py:331
  147.5 106.0 %all-to-all-start.3 = ((bf16[128,2,2176]{2,1,0:T(2,128)(2,1)}), bf16[128,2,2176]{2,1,0:T(2,128)(2,1)S(1)}, u32[]{:S(2)}, u32[]{:S(2)}) async-start(bf16[128,2,2176]{2,1,0:T(2,128)(2,1)} %reshape.40), calls=%async_computation.3 | async-start | bytes 2228224 | tf_op jit(solution)/shard_map/all_to_all | solution.py:365
  162.1 20.1 %collective-permute-start.22 = (bf16[96,2048]{1,0:T(8,128)(2,1)S(1)}, bf16[96,2048]{1,0:T(8,128)(2,1)S(1)}, u32[]{:S(2)}, u32[]{:S(2)}) collective-permute-start(bf16[96,2048]{1,0:T(8,128)(2,1)S(1)} %get-tuple-element.53), channel_id=1, source_target_pairs={{0,1},{1,2},{2,3},{3,0},{4,5},{5,6},{6,7},{7,4},{8,9},{9,10},{10,1... | collective-permute-start | bytes 1179656 | tf_op jit(solution)/shard_map/ppermute | solution.py:27
  171.0 46.5 %collective-permute-start.19 = (bf16[256,2048]{1,0:T(8,128)(2,1)S(1)}, bf16[256,2048]{1,0:T(8,128)(2,1)S(1)}, u32[]{:S(2)}, u32[]{:S(2)}) collective-permute-start(bf16[256,2048]{1,0:T(8,128)(2,1)S(1)} %pad_maximum_fusion.1.refs_4_), channel_id=1, source_target_pairs={{0,3},{1,0},{2,1},{3,2},{4,7},{5,4},{6,5},{7,6},{8,11},{9,8},{10,9... | collective-permute-start | bytes 3145736 | tf_op jit(solution)/shard_map/ppermute | solution.py:27
  173.1 48.4 %collective-permute-start.18 = (bf16[256,2048]{1,0:T(8,128)(2,1)S(1)}, bf16[256,2048]{1,0:T(8,128)(2,1)S(1)}, u32[]{:S(2)}, u32[]{:S(2)}) collective-permute-start(bf16[256,2048]{1,0:T(8,128)(2,1)S(1)} %pad_maximum_fusion.1.refs_4_), channel_id=1, source_target_pairs={{0,1},{1,2},{2,3},{3,0},{4,5},{5,6},{6,7},{7,4},{8,9},{9,10},{10,1... | collective-permute-start | bytes 3145736 | tf_op jit(solution)/shard_map/ppermute | solution.py:27
  178.3 46.5 %collective-permute-start.24 = (bf16[96,2048]{1,0:T(8,128)(2,1)S(1)}, bf16[96,2048]{1,0:T(8,128)(2,1)S(1)}, u32[]{:S(2)}, u32[]{:S(2)}) collective-permute-start(bf16[96,2048]{1,0:T(8,128)(2,1)S(1)} %slice.71), channel_id=1, source_target_pairs={{0,3},{1,0},{2,1},{3,2},{4,7},{5,4},{6,5},{7,6},{8,11},{9,8},{10,9... | collective-permute-start | bytes 1179656 | tf_op jit(solution)/shard_map/ppermute | solution.py:27
  180.2 35.3 %collective-permute-start.26 = (bf16[96,2048]{1,0:T(8,128)(2,1)S(1)}, bf16[96,2048]{1,0:T(8,128)(2,1)S(1)}, u32[]{:S(2)}, u32[]{:S(2)}) collective-permute-start(bf16[96,2048]{1,0:T(8,128)(2,1)S(1)} %get-tuple-element.54), channel_id=1, source_target_pairs={{0,3},{1,0},{2,1},{3,2},{4,7},{5,4},{6,5},{7,6},{8,11},{9,8},{10,9... | collective-permute-start | bytes 1179656 | tf_op jit(solution)/shard_map/ppermute | solution.py:27
  182.2 45.3 %collective-permute-start.25 = (bf16[96,2048]{1,0:T(8,128)(2,1)S(1)}, bf16[96,2048]{1,0:T(8,128)(2,1)S(1)}, u32[]{:S(2)}, u32[]{:S(2)}) collective-permute-start(bf16[96,2048]{1,0:T(8,128)(2,1)S(1)} %slice.73), channel_id=1, source_target_pairs={{0,1},{1,2},{2,3},{3,0},{4,5},{5,6},{6,7},{7,4},{8,9},{9,10},{10,1... | collective-permute-start | bytes 1179656 | tf_op jit(solution)/shard_map/ppermute | solution.py:27
  217.6 17.1 %collective-permute-start.27 = (bf16[96,2048]{1,0:T(8,128)(2,1)S(1)}, bf16[96,2048]{1,0:T(8,128)(2,1)S(1)}, u32[]{:S(2)}, u32[]{:S(2)}) collective-permute-start(bf16[96,2048]{1,0:T(8,128)(2,1)S(1)} %add_convert_fusion.1), channel_id=1, source_target_pairs={{0,3},{1,0},{2,1},{3,2},{4,7},{5,4},{6,5},{7,6},{8,11},{9,8},{10,9... | collective-permute-start | bytes 1179656 | tf_op jit(solution)/shard_map/ppermute | solution.py:27
  221.6 16.9 %collective-permute-start.15 = (bf16[384,256]{1,0:T(8,128)(2,1)S(1)}, bf16[384,256]{1,0:T(8,128)(2,1)S(1)}, u32[]{:S(2)}, u32[]{:S(2)}) collective-permute-start(bf16[384,256]{1,0:T(8,128)(2,1)S(1)} %copy-done.18), channel_id=1, source_target_pairs={{0,1},{1,2},{2,3},{3,0},{4,5},{5,6},{6,7},{7,4},{8,9},{9,10},{10,1... | collective-permute-start | bytes 589832 | tf_op jit(solution)/shard_map/ppermute | solution.py:27
  224.8 15.5 %collective-permute-start.16 = (bf16[384,256]{1,0:T(8,128)(2,1)S(1)}, bf16[384,256]{1,0:T(8,128)(2,1)S(1)}, u32[]{:S(2)}, u32[]{:S(2)}) collective-permute-start(bf16[384,256]{1,0:T(8,128)(2,1)S(1)} %copy-done.17), channel_id=1, source_target_pairs={{0,3},{1,0},{2,1},{3,2},{4,7},{5,4},{6,5},{7,6},{8,11},{9,8},{10,9... | collective-permute-start | bytes 589832 | tf_op jit(solution)/shard_map/ppermute | solution.py:27
  230.1 19.7 %collective-permute-start.20 = (bf16[128,2048]{1,0:T(8,128)(2,1)S(1)}, bf16[128,2048]{1,0:T(8,128)(2,1)S(1)}, u32[]{:S(2)}, u32[]{:S(2)}) collective-permute-start(bf16[128,2048]{1,0:T(8,128)(2,1)S(1)} %slice.81), channel_id=1, source_target_pairs={{0,3},{1,0},{2,1},{3,2},{4,7},{5,4},{6,5},{7,6},{8,11},{9,8},{10,9... | collective-permute-start | bytes 1572872 | tf_op jit(solution)/shard_map/ppermute | solution.py:27
  (27 other events, 375.5 us)

commit v4 on v3

--- a/solution.py
+++ b/solution.py
@@ -25,10 +25,6 @@
 
 def shift(block, step, axes, n):
     return lax.ppermute(block, axes, [(i, (i + step) % n) for i in range(n)])
-
-
-def tied(*values):
-    return lax.optimization_barrier(values)
 
 
 def vmem():
@@ -150,42 +146,33 @@
     return (home == place).astype(BF)
 
 
-def rows_kernel(zs_ref, *refs):
-    srcs, p_ref, dgu_refs, pd_refs = refs[:14], refs[14], refs[15:19], refs[19:23]
-    gu, dn, rows, sems = refs[23:]
+def rows_kernel(zs_ref, a_ref, b_ref, c_ref, w_ref, p_ref, *refs):
+    d_refs, s_ref, (gu, dn, rows, sems) = refs[:4], refs[4], refs[5:]
     hid = dn.shape[1]
-    half = hid // 2
     count, width = rows.shape
     features = (width - LANES) // 2
     quarter = count // 4
-    targets = [
-        rows.at[pl.ds(0, quarter)],
-        rows.at[pl.ds(quarter, 2 * quarter)],
-        rows.at[pl.ds(3 * quarter, quarter)],
-        gu.at[0, pl.ds(0, hid)],
-        gu.at[0, pl.ds(hid, hid)],
-        dn.at[0],
-        gu.at[1],
-        dn.at[1],
-        gu.at[2],
-        dn.at[2],
-        gu.at[3, pl.ds(0, hid)],
-        gu.at[3, pl.ds(hid, hid)],
-        dn.at[3, pl.ds(0, half)],
-        dn.at[3, pl.ds(half, half)],
+    me = zs_ref[2]
+    places = [(me + offset) % 4 for offset in (0, 3, 1, 2)]
+    pairs = [
+        (a_ref, rows.at[pl.ds(0, quarter)]),
+        (b_ref, rows.at[pl.ds(quarter, 2 * quarter)]),
+        (c_ref, rows.at[pl.ds(3 * quarter, quarter)]),
     ]
-    order = [(0, 1, 2, 3, 4, 5), (6, 7), (8, 9), (10, 11, 12, 13)]
-    copies = [pltpu.make_async_copy(s, t, sems.at[i]) for i, (s, t) in enumerate(zip(srcs, targets))]
+    for q, place in enumerate(places):
+        pairs.append((w_ref.at[place, pl.ds(0, 2 * hid)], gu.at[q]))
+        pairs.append((w_ref.at[place, pl.ds(2 * hid, hid)], dn.at[q]))
+    copies = [pltpu.make_async_copy(s, t, sems.at[i]) for i, (s, t) in enumerate(pairs)]
     for copy in copies:
         copy.start()
+    for copy in copies[:3]:
+        copy.wait()
     home = homes(zs_ref[0] * 8 + zs_ref[1], count)
+    coef = rows[:, 2 * features :].astype(F32).T[0:1, :]
     score = None
-    scaled = []
-    for q, needed in enumerate(order):
-        for i in needed:
-            copies[i].wait()
-        if q == 0:
-            coef = rows[:, 2 * features :].astype(F32).T[0:1, :]
+    for q in range(4):
+        copies[3 + 2 * q].wait()
+        copies[4 + 2 * q].wait()
         pre = dot(gu[q], rows[:, :features], 1, 1)
         back = dot(dn[q], rows[:, features : 2 * features], 1, 1)
         gate_pre, up_pre = pre[:hid], pre[hid:]
@@ -195,12 +182,11 @@
         part = jnp.sum(hidden.astype(BF).astype(F32) * back, axis=0, keepdims=True)
         score = part if score is None else score + part
         d_hidden = coef * back
-        dgu_refs[q][0:hid, :] = (
-            d_hidden * up_pre * sigma * (1.0 + gate_pre * (1.0 - sigma))
-        ).astype(BF)
-        dgu_refs[q][hid:, :] = (d_hidden * active).astype(BF)
-        scaled.append((coef * hidden).astype(BF))
-    moved = [dot(d[...], home, 1, 0).astype(BF) for d in dgu_refs]
+        d_gate = d_hidden * up_pre * sigma * (1.0 + gate_pre * (1.0 - sigma))
+        d_refs[q][0:hid, :] = d_gate.astype(BF)
+        d_refs[q][hid:, :] = (d_hidden * active).astype(BF)
+        s_ref[q] = (coef * hidden).astype(BF)
+    moved = [dot(d[...], home, 1, 0).astype(BF) for d in d_refs]
     tile = 512
     for j in range(0, features, tile):
         total = None
@@ -210,76 +196,104 @@
         p_ref[:, j : j + tile] = total.astype(BF)
     score = dot(jnp.broadcast_to(score, (LANES, count)).astype(BF), home, 1, 0)
     p_ref[:, features:] = score.T.astype(BF)
-    for j in range(0, features, tile):
-        grads = rows[:, features + j : features + j + tile]
-        for q in range(4):
-            pd_refs[q][:, j : j + tile] = dot(scaled[q], grads, 1, 0).astype(pd_refs[q].dtype)
-
-
-def rows_call(zs, chunks, gate, up, down, gu_far, dn_far):
+
+
+def rows_call(zs, chunks, weights):
     count = sum(c.shape[0] for c in chunks)
     width = chunks[0].shape[1]
-    hid, features = gate.shape
-    gu_left, gu_right, gu_a, gu_b = gu_far
-    dn_left, dn_right, dn_a, dn_b = dn_far
-    srcs = [*chunks, gate, up, down, gu_left, dn_left, gu_right, dn_right, gu_a, gu_b, dn_a, dn_b]
+    n, hid, features = weights.shape[0], weights.shape[1] // 3, weights.shape[2]
     return pl.pallas_call(
         rows_kernel,
-        out_shape=[jax.ShapeDtypeStruct((count, features + LANES), BF)]
-        + [jax.ShapeDtypeStruct((2 * hid, count), BF)] * 4
-        + [jax.ShapeDtypeStruct((hid, features), F32)]
-        + [jax.ShapeDtypeStruct((hid, features), BF)] * 3,
-        in_specs=[pl.BlockSpec(memory_space=pltpu.SMEM)]
-        + [pl.BlockSpec(memory_space=pl.ANY)] * len(srcs),
-        out_specs=[vmem()] * 9,
+        out_shape=[
+            jax.ShapeDtypeStruct((count, features + LANES), BF),
+            *[jax.ShapeDtypeStruct((2 * hid, count), BF)] * n,
+            jax.ShapeDtypeStruct((n, hid, count), BF),
+        ],
+        in_specs=[pl.BlockSpec(memory_space=pltpu.SMEM)] + [pl.BlockSpec(memory_space=pl.ANY)] * 4,
+        out_specs=[vmem()] * (n + 2),
         scratch_shapes=[
-            pltpu.VMEM((4, 2 * hid, features), BF),
-            pltpu.VMEM((4, hid, features), BF),
+            pltpu.VMEM((n, 2 * hid, features), BF),
+            pltpu.VMEM((n, hid, features), BF),
             pltpu.VMEM((count, width), BF),
-            pltpu.SemaphoreType.DMA((len(srcs),)),
-        ],
-        compiler_params=pltpu.CompilerParams(vmem_limit_bytes=58 * MIB),
+            pltpu.SemaphoreType.DMA((3 + 2 * n,)),
+        ],
+        compiler_params=pltpu.CompilerParams(vmem_limit_bytes=56 * MIB),
         cost_estimate=pl.CostEstimate(
-            flops=2 * count * features * hid * 4 * 6,
-            bytes_accessed=2 * features * hid * 18 + 6 * count * features,
-            transcendentals=count * hid * 4,
+            flops=2 * count * features * hid * n * 5,
+            bytes_accessed=2 * features * hid * 12 + 6 * count * features,
+            transcendentals=count * hid * n,
         ),
         name="rows",
-    )(zs, *srcs)
-
-
-def weights_kernel(*refs):
-    d_refs, x_refs, (gate_ref, up_ref) = refs[:4], refs[4:9], refs[9:]
+    )(zs, *chunks, weights)
+
+
+def down_kernel(s_ref, a_ref, b_ref, c_ref, own_ref, left_ref, right_ref, two_ref, rows):
+    quarter = a_ref.shape[0]
+    rows[0:quarter, :] = a_ref[...]
+    rows[quarter : 3 * quarter, :] = b_ref[...]
+    rows[3 * quarter :, :] = c_ref[...]
+    grads = rows[...]
+    for q, out in enumerate((own_ref, left_ref, right_ref, two_ref)):
+        out[...] = dot(s_ref[q], grads, 1, 0).astype(out.dtype)
+
+
+def down_call(scaled, chunks, features):
+    tile = 512
+    n, hid, count = scaled.shape
+    first = features // tile
+    tiled = [pl.BlockSpec((c.shape[0], tile), lambda j: (0, first + j)) for c in chunks]
+    return pl.pallas_call(
+        down_kernel,
+        grid=(features // tile,),
+        out_shape=[jax.ShapeDtypeStruct((hid, features), F32)]
+        + [jax.ShapeDtypeStruct((hid, features), BF)] * 3,
+        in_specs=[pl.BlockSpec(scaled.shape, lambda j: (0, 0, 0))] + tiled,
+        out_specs=[pl.BlockSpec((hid, tile), lambda j: (0, j))] * 4,
+        scratch_shapes=[pltpu.VMEM((count, tile), BF)],
+        compiler_params=pltpu.CompilerParams(vmem_limit_bytes=24 * MIB),
+        cost_estimate=pl.CostEstimate(
+            flops=2 * n * count * features * hid,
+            bytes_accessed=2 * features * (count + 5 * hid),
+            transcendentals=0,
+        ),
+        name="down_parts",
+    )(scaled, *chunks)
+
+
+def weights_kernel(zs_ref, *refs):
+    d_refs, x_refs, (gate_ref, up_ref) = refs[:4], refs[4:8], refs[8:]
     hid = gate_ref.shape[0]
-    half = d_refs[3].shape[1] // 2
-    parts = [dot(d[...], x[...], 1, 0) for d, x in zip(d_refs[:3], x_refs[:3])]
-    parts.append(dot(d_refs[3][:, :half], x_refs[3][...], 1, 0))
-    parts.append(dot(d_refs[3][:, half:], x_refs[4][...], 1, 0))
-    total = sum(parts[1:], parts[0]).astype(BF)
+    total = sum(dot(d[...], x[0], 1, 0) for d, x in zip(d_refs, x_refs)).astype(BF)
     gate_ref[...] = total[:hid]
     up_ref[...] = total[hid:]
 
 
-def weights_call(ds, xs):
+def weights_call(zs, ds, xs):
     tile = 512
-    hid, features = ds[0].shape[0] // 2, xs[0].shape[1]
-    whole = [pl.BlockSpec(d.shape, lambda j: (0, 0)) for d in ds]
-    tiled = [pl.BlockSpec((x.shape[0], tile), lambda j: (0, j)) for x in xs]
-    rows = sum(d.shape[1] for d in ds)
+    n, count, features = xs.shape
+    hid = ds[0].shape[0] // 2
+    whole = [pl.BlockSpec(d.shape, lambda j, zs: (0, 0)) for d in ds]
+    tiled = [
+        pl.BlockSpec((1, count, tile), lambda j, zs, at=at: ((zs[2] + at) % 4, 0, j))
+        for at in (0, 3, 1, 2)
+    ]
     return pl.pallas_call(
         weights_kernel,
-        grid=(features // tile,),
+        grid_spec=pltpu.PrefetchScalarGridSpec(
+            num_scalar_prefetch=1,
+            grid=(features // tile,),
+            in_specs=whole + tiled,
+            out_specs=[pl.BlockSpec((hid, tile), lambda j, zs: (0, j))] * 2,
+        ),
         out_shape=[jax.ShapeDtypeStruct((hid, features), BF)] * 2,
-        in_specs=whole + tiled,
-        out_specs=[pl.BlockSpec((hid, tile), lambda j: (0, j))] * 2,
         compiler_params=pltpu.CompilerParams(vmem_limit_bytes=24 * MIB),
         cost_estimate=pl.CostEstimate(
-            flops=4 * rows * features * hid,
-            bytes_accessed=2 * features * (rows + 2 * hid),
+            flops=4 * n * count * features * hid,
+            bytes_accessed=2 * features * (n * count + 2 * hid),
             transcendentals=0,
         ),
         name="weight_grads",
-    )(*ds, *xs)
+    )(zs, *ds, *[xs] * n)
 
 
 def home_kernel(code_ref, home_ref, grad_ref, score_ref):
@@ -312,15 +326,12 @@
 def local(tokens, out_grad, expert_ids, keep_flags, route_weights, gate_w, up_w, down_w):
     nz, n = lax.axis_size(Z), lax.axis_size("x")
     step, features = tokens.shape
-    zs = jnp.stack([lax.axis_index("zh"), lax.axis_index("zl")]).astype(jnp.int32)
-    gate, up, down = gate_w[0], up_w[0], down_w[0]
-    half = gate.shape[0] // 2
-
+    zs = jnp.stack([lax.axis_index(a) for a in ("zh", "zl", "x")]).astype(jnp.int32)
+    half = gate_w.shape[1] // 2
+
+    joined = jnp.concatenate([gate_w[0], up_w[0], down_w[0]], axis=0)
+    weights = lax.all_gather(joined, "x", axis=0)
     own, code = payload_call(tokens, out_grad, expert_ids.T, keep_flags.T, route_weights.T)
-
-    gu = jnp.concatenate([gate, up], axis=0)
-    gu_left, gu_right = shift(gu, 1, "x", n), shift(gu, -1, "x", n)
-    dn_left, dn_right = shift(down, 1, "x", n), shift(down, -1, "x", n)
 
     far = [shift(own, s, Z, nz) for s in (4, 8, 12)]
     chunk = jnp.concatenate([own, *far], axis=0)
@@ -335,40 +346,22 @@
     rows_a = exchange(pack_call(zs, [chunk], step))
     rest_a = shift(right[: 2 * step], -1, Z, nz)
     rest_b = shift(left[step : 3 * step], 1, Z, nz)
-    left, right, rows_a = tied(left, right, rows_a)
-    packed = pack_call(zs, [left, right], step)
-
-    hid = gate.shape[0]
-    gu_a, gu_b = shift(gu_right[:hid], -1, "x", n), shift(gu_left[hid:], 1, "x", n)
-    rows_b = exchange(packed)
-    rest_a, rest_b, rows_b, dn_left, dn_right = tied(rest_a, rest_b, rows_b, dn_left, dn_right)
-    dn_a, dn_b = shift(dn_right[:half], -1, "x", n), shift(dn_left[half:], 1, "x", n)
+    packed_b = pack_call(zs, [left, right], step)
+    rest_a, rest_b, _ = lax.optimization_barrier((rest_a, rest_b, packed_b))
+    rows_b = exchange(packed_b)
     rows_c = exchange(pack_call(zs, [rest_a, rest_b], step))
 
     chunks = [rows_a, rows_b, rows_c]
-    x = jnp.concatenate([c[:, :features] for c in chunks], axis=0)
-    mid = x.shape[0] // 2
-    x_left, x_right = shift(x, 1, "x", n), shift(x, -1, "x", n)
-    x_a, x_b = shift(x_right[:mid], -1, "x", n), shift(x_left[mid:], 1, "x", n)
-
-    result = rows_call(
-        zs,
-        chunks,
-        gate,
-        up,
-        down,
-        (gu_left, gu_right, gu_a, gu_b),
-        (dn_left, dn_right, dn_a, dn_b),
-    )
-    back, (d_own, d_left, d_right, d_two) = result[0], result[1:5]
-    p_own, p_left, p_right, p_two = result[5:]
+    x = lax.all_gather(jnp.concatenate([c[:, :features] for c in chunks], axis=0), "x", axis=0)
+
+    back, d_own, d_left, d_right, d_two, scaled = rows_call(zs, chunks, weights)
     home = lax.all_to_all(
         back.reshape(-1, CAPACITY, back.shape[1]), PLACE, split_axis=0, concat_axis=0, tiled=True
     ).reshape(back.shape)
-
     ds = [d_own, shift(d_right, 1, "x", n), shift(d_left, -1, "x", n), shift(d_two, 2, "x", n)]
-    grad_gate, grad_up = weights_call(ds, [x, x_left, x_right, x_a, x_b])
-
+    grad_gate, grad_up = weights_call(zs, ds, x)
+
+    p_own, p_left, p_right, p_two = down_call(scaled, chunks, features)
     via_a = shift(p_two[:half], 1, "x", n)
     via_b = shift(p_two[half:], -1, "x", n)
     left_low = shift(p_right[half:], 1, "x", n)

time: 259 us -> 242 us (0.934)
  starting transfers between devices: 134 us -> 86.8 us
  blocking collectives: 0 us -> 15 us
  between operations: 1.28 us -> 14.5 us
  local copies, waits for them, and re-layouts: 18.2 us -> 11 us
  other arithmetic: 3.71 us -> 8.6 us
  waiting for transfers between devices: 70.3 us -> 73.7 us
    ppermute x28 -> x16, starting transfers between devices: 107 us -> 65.5 us  [shift(): return lax.ppermute(block, axes, [(i, (i + step) % n) for i in range(n)])]
    all_to_all x0 -> x1, blocking collectives: none -> 15 us  [exchange(): lax.all_to_all(packed.reshape(8, rows // 8, width), YC, split_axis=0, con...]
    all_to_all x3 -> x2, waiting for transfers between devices: 8.15 us -> 16.1 us  [exchange(): lax.all_to_all(packed.reshape(8, rows // 8, width), YC, split_axis=0, con...]
    slice x9 -> x3, local copies, waits for them, and re-layouts: 7.57 us -> 0.08 us  [local(): c[:, :features]]
    ppermute x28 -> x16, waiting for transfers between devices: 62.2 us -> 57.5 us  [shift(): return lax.ppermute(block, axes, [(i, (i + step) % n) for i in range(n)])]
    all_to_all x3 -> x2, starting transfers between devices: 12.7 us -> 8.04 us  [exchange(): lax.all_to_all(packed.reshape(8, rows // 8, width), YC, split_axis=0, con...]
    concatenate x2, other arithmetic: 1.58 us -> 4.48 us  [the longest x1 3.29 us: local(): joined = jnp.concatenate([gate_w[0], up_w[0], down_w[0]], axis=0)]
    pallas_call x1 -> x2, Pallas kernels: 3.77 us -> 6.34 us  [the longest x1 4.08 us: weights_call(): pl.pallas_call(weights_kernel, grid_spec=pltpu.PrefetchScalarGridSpec(num...]
  transfers between devices with their start and end apart: 32 -> 21, of which waited for: 10 -> 9; matrix products, arithmetic and copies ran while one was open for 5% -> 4% of each run, Pallas kernels for 5% -> 12%
where the time goes in v4:
time: 242 us; the launch traced here: 241 us
  starting transfers between devices  86.8 us (36%)
  waiting for transfers between devices  73.7 us (30%)
  Pallas kernels  31.1 us (13%)
  blocking collectives  15 us (6%)
  between operations  14.5 us (6%)
  local copies, waits for them, and re-layouts  11 us (5%)
  other arithmetic  8.6 us (4%)
    ppermute x16, starting transfers between devices, shift(): return lax.ppermute(block, axes, [(i, (i + step) % n) for i in range(n)])  65.5 us
    ppermute x16, waiting for transfers between devices, shift(): return lax.ppermute(block, axes, [(i, (i + step) % n) for i in range(n)])  57.5 us
    all_to_all x2, waiting for transfers between devices, exchange(): lax.all_to_all(packed.reshape(8, rows // 8, width), YC, split_axis=0, con...  16.1 us
    all_to_all x1, blocking collectives, exchange(): lax.all_to_all(packed.reshape(8, rows // 8, width), YC, split_axis=0, con...  15 us
    all_to_all x1, starting transfers between devices, local(): lax.all_to_all(back.reshape(-1, CAPACITY, back.shape[1]), PLACE, split_ax...  13.1 us
    pallas_call x1, Pallas kernels, rows_call(): pl.pallas_call(rows_kernel, out_shape=[jax.ShapeDtypeStruct((count, featu...  12.6 us
    all_to_all x2, starting transfers between devices, exchange(): lax.all_to_all(packed.reshape(8, rows // 8, width), YC, split_axis=0, con...  8.04 us
    pallas_call x3, Pallas kernels, pack_call(): pl.pallas_call(body, out_shape=jax.ShapeDtypeStruct((rows, width), BF), i...  7.93 us
  transfers between devices with their start and end apart: 21, of which 9 were waited for; matrix products, arithmetic and copies ran while one was open for 4% of the time, Pallas kernels for 12%

profile of v4, /device:TPU:6, one launch (start us, length us, event | category | flops | bytes accessed | tf_op | source)
XLA Modules:
  0.0 240.7 jit_solution(11583650546217343913)
XLA Ops:
  7.2 3.3 %pad_maximum_fusion = bf16[576,2048]{1,0:T(8,128)(2,1)} fusion(bf16[192,2048]{1,0:T(8,128)(2,1)} %bitcast.37, bf16[192,2048]{1,0:T(8,128)(2,1)} %bitcast.38, bf16[192,2048]{1,0:T(8,128)(2,1)} %bitcast.39), kind=kLoop, calls=%fused_computation | loop fusion | flops 7077888 | bytes 4718592 | tf_op jit(solution)/shard_map/concatenate | solution.py:332
  12.4 9.1 %collective-permute-start = (bf16[16,4224]{1,0:T(8,128)(2,1)}, bf16[16,4224]{1,0:T(8,128)(2,1)S(1)}, u32[]{:S(2)}, u32[]{:S(2)}) collective-permute-start(bf16[16,4224]{1,0:T(8,128)(2,1)} %get-tuple-element.24), channel_id=1, source_target_pairs={{0,16},{4,20},{8,24},{12,28},{16,256},{20,260},{24,264},{28,268},{... | collective-permute-start | bytes 405512 | tf_op jit(solution)/shard_map/ppermute | solution.py:27
  21.5 10.9 %collective-permute-start.1 = (bf16[16,4224]{1,0:T(8,128)(2,1)}, bf16[16,4224]{1,0:T(8,128)(2,1)S(1)}, u32[]{:S(2)}, u32[]{:S(2)}) collective-permute-start(bf16[16,4224]{1,0:T(8,128)(2,1)} %get-tuple-element.24), channel_id=1, source_target_pairs={{0,256},{4,260},{8,264},{12,268},{16,272},{20,276},{24,280},{28,28... | collective-permute-start | bytes 405512 | tf_op jit(solution)/shard_map/ppermute | solution.py:27
  32.5 5.5 %collective-permute-start.2 = (bf16[16,4224]{1,0:T(8,128)(2,1)}, bf16[16,4224]{1,0:T(8,128)(2,1)S(1)}, u32[]{:S(2)}, u32[]{:S(2)}) collective-permute-start(bf16[16,4224]{1,0:T(8,128)(2,1)} %get-tuple-element.24), channel_id=1, source_target_pairs={{0,272},{4,276},{8,280},{12,284},{16,0},{20,4},{24,8},{28,12},{256... | collective-permute-start | bytes 405512 | tf_op jit(solution)/shard_map/ppermute | solution.py:27
  38.9 12.4 %collective-permute-done.1 = bf16[16,4224]{1,0:T(8,128)(2,1)S(1)} collective-permute-done((bf16[16,4224]{1,0:T(8,128)(2,1)}, bf16[16,4224]{1,0:T(8,128)(2,1)S(1)}, u32[]{:S(2)}, u32[]{:S(2)}) %collective-permute-start.1) | collective-permute-done | bytes 135200 | tf_op jit(solution)/shard_map/ppermute | solution.py:27
  51.3 5.5 %collective-permute-done.2 = bf16[16,4224]{1,0:T(8,128)(2,1)S(1)} collective-permute-done((bf16[16,4224]{1,0:T(8,128)(2,1)}, bf16[16,4224]{1,0:T(8,128)(2,1)S(1)}, u32[]{:S(2)}, u32[]{:S(2)}) %collective-permute-start.2) | collective-permute-done | bytes 135200 | tf_op jit(solution)/shard_map/ppermute | solution.py:27
  58.8 3.9 %collective-permute-start.3 = (bf16[64,4224]{1,0:T(8,128)(2,1)S(1)}, bf16[64,4224]{1,0:T(8,128)(2,1)S(1)}, u32[]{:S(2)}, u32[]{:S(2)}) collective-permute-start(bf16[64,4224]{1,0:T(8,128)(2,1)S(1)} %constant_dynamic-update-slice_fusion.refs_1_), channel_id=1, source_target_pairs={{0,4},{4,8},{8,12},{12,16},{16,20},{20,24},{24,28},{28,256},{256,2... | collective-permute-start | bytes 1622024 | tf_op jit(solution)/shard_map/ppermute | solution.py:27
  65.6 4.5 %all-to-all-start = ((bf16[8,8,4224]{2,1,0:T(8,128)(2,1)}), bf16[8,8,4224]{2,1,0:T(8,128)(2,1)S(1)}, u32[]{:S(2)}, u32[]{:S(2)}) async-start(bf16[8,8,4224]{2,1,0:T(8,128)(2,1)} %bitcast.35), calls=%async_computation | async-start | bytes 1081344 | tf_op jit(solution)/shard_map/all_to_all | solution.py:342
  72.9 3.4 %collective-permute-start.5 = (bf16[32,4224]{1,0:T(8,128)(2,1)S(1)}, bf16[32,4224]{1,0:T(8,128)(2,1)S(1)}, u32[]{:S(2)}, u32[]{:S(2)}) collective-permute-start(bf16[32,4224]{1,0:T(8,128)(2,1)S(1)} %slice.52), channel_id=1, source_target_pairs={{0,284},{4,0},{8,4},{12,8},{16,12},{20,16},{24,20},{28,24},{256,28... | collective-permute-start | bytes 811016 | tf_op jit(solution)/shard_map/ppermute | solution.py:27
  82.4 4.7 %collective-permute-done.6.refs_2_ = bf16[32,4224]{1,0:T(8,128)(2,1)S(1)} collective-permute-done((bf16[32,4224]{1,0:T(8,128)(2,1)S(1)}, bf16[32,4224]{1,0:T(8,128)(2,1)S(1)}, u32[]{:S(2)}, u32[]{:S(2)}) %collective-permute-start.6) | collective-permute-done | bytes 270368 | tf_op jit(solution)/shard_map/ppermute | solution.py:27
  90.3 15.0 %all_to_all.20 = bf16[8,8,4224]{2,1,0:T(8,128)(2,1)S(1)} all-to-all(bf16[8,8,4224]{2,1,0:T(8,128)(2,1)} %bitcast.36), channel_id=1, replica_groups=mesh['zh'=2,'y'=4,'c'=2,'zl'=8,'x'=4] {'y','c'}, dimensions={0} | all-to-all | bytes 1081344 | tf_op jit(solution)/shard_map/all_to_all | solution.py:342
  105.4 3.6 %all-to-all-start.1 = ((bf16[8,16,4224]{2,1,0:T(8,128)(2,1)}), bf16[8,16,4224]{2,1,0:T(8,128)(2,1)S(1)}, u32[]{:S(2)}, u32[]{:S(2)}) async-start(bf16[8,16,4224]{2,1,0:T(8,128)(2,1)} %bitcast.8), calls=%async_computation.1 | async-start | bytes 2162688 | tf_op jit(solution)/shard_map/all_to_all | solution.py:342
  109.1 16.1 %all-to-all-done.1 = bf16[8,16,4224]{2,1,0:T(8,128)(2,1)S(1)} async-done(((bf16[8,16,4224]{2,1,0:T(8,128)(2,1)}), bf16[8,16,4224]{2,1,0:T(8,128)(2,1)S(1)}, u32[]{:S(2)}, u32[]{:S(2)}) %all-to-all-start.1) | async-done | bytes 1081376 | tf_op jit(solution)/shard_map/all_to_all | solution.py:342
  126.5 12.6 %rows.1 = (bf16[256,2176]{1,0:T(8,128)(2,1)}, bf16[384,256]{1,0:T(8,128)(2,1)}, bf16[384,256]{1,0:T(8,128)(2,1)}, bf16[384,256]{1,0:T(8,128)(2,1)}, bf16[384,256...) custom-call(s32[3]{0:T(128)} %pad_add_fusion.refs_0_.zs_ref, bf16[64,4224]{1,0:T(8,128)(2,1)} %bitcast.30, ...), custom_call_target="tpu_custom_call" | custom-call | flops 4026531840 | bytes 12582912 | tf_op jit(solution)/shard_map/rows/pallas_call | solution.py:205
  141.7 13.1 %all-to-all-start.3 = ((bf16[128,2,2176]{2,1,0:T(2,128)(2,1)}), bf16[128,2,2176]{2,1,0:T(2,128)(2,1)}, u32[]{:S(2)}, u32[]{:S(2)}) async-start(bf16[128,2,2176]{2,1,0:T(2,128)(2,1)} %reshape.40), calls=%async_computation.3 | async-start | bytes 2228224 | tf_op jit(solution)/shard_map/all_to_all | solution.py:358
  161.8 3.3 %collective-permute-start.7 = (bf16[384,256]{1,0:T(8,128)(2,1)S(1)}, bf16[384,256]{1,0:T(8,128)(2,1)S(1)}, u32[]{:S(2)}, u32[]{:S(2)}) collective-permute-start(bf16[384,256]{1,0:T(8,128)(2,1)S(1)} %copy-done.16), channel_id=1, source_target_pairs={{0,1},{1,2},{2,3},{3,0},{4,5},{5,6},{6,7},{7,4},{8,9},{9,10},{10,1... | collective-permute-start | bytes 589832 | tf_op jit(solution)/shard_map/ppermute | solution.py:27
  167.7 3.4 %collective-permute-start.12 = (bf16[96,2048]{1,0:T(8,128)(2,1)S(1)}, bf16[96,2048]{1,0:T(8,128)(2,1)}, u32[]{:S(2)}, u32[]{:S(2)}) collective-permute-start(bf16[96,2048]{1,0:T(8,128)(2,1)S(1)} %slice.47), channel_id=1, source_target_pairs={{0,3},{1,0},{2,1},{3,2},{4,7},{5,4},{6,5},{7,6},{8,11},{9,8},{10,9... | collective-permute-start | bytes 1179656 | tf_op jit(solution)/shard_map/ppermute | solution.py:27
  173.8 7.8 %collective-permute-done.10 = bf16[96,2048]{1,0:T(8,128)(2,1)S(1)} collective-permute-done((bf16[96,2048]{1,0:T(8,128)(2,1)S(1)}, bf16[96,2048]{1,0:T(8,128)(2,1)S(1)}, u32[]{:S(2)}, u32[]{:S(2)}) %collective-permute-start.10) | collective-permute-done | bytes 393248 | tf_op jit(solution)/shard_map/ppermute | solution.py:27
  181.6 3.6 %collective-permute-start.13 = (bf16[96,2048]{1,0:T(8,128)(2,1)S(1)}, bf16[96,2048]{1,0:T(8,128)(2,1)}, u32[]{:S(2)}, u32[]{:S(2)}) collective-permute-start(bf16[96,2048]{1,0:T(8,128)(2,1)S(1)} %slice.49), channel_id=1, source_target_pairs={{0,1},{1,2},{2,3},{3,0},{4,5},{5,6},{6,7},{7,4},{8,9},{9,10},{10,1... | collective-permute-start | bytes 1179656 | tf_op jit(solution)/shard_map/ppermute | solution.py:27
  185.3 13.0 %collective-permute-done.14 = bf16[96,2048]{1,0:T(8,128)(2,1)S(1)} collective-permute-done((bf16[96,2048]{1,0:T(8,128)(2,1)S(1)}, bf16[96,2048]{1,0:T(8,128)(2,1)S(1)}, u32[]{:S(2)}, u32[]{:S(2)}) %collective-permute-start.14) | collective-permute-done | bytes 393248 | tf_op jit(solution)/shard_map/ppermute | solution.py:27
  198.3 3.6 %collective-permute-start.11 = (bf16[96,2048]{1,0:T(8,128)(2,1)S(1)}, bf16[96,2048]{1,0:T(8,128)(2,1)}, u32[]{:S(2)}, u32[]{:S(2)}) collective-permute-start(bf16[96,2048]{1,0:T(8,128)(2,1)S(1)} %add_convert_fusion.3), channel_id=1, source_target_pairs={{0,1},{1,2},{2,3},{3,0},{4,5},{5,6},{6,7},{7,4},{8,9},{9,10},{10,1... | collective-permute-start | bytes 1179656 | tf_op jit(solution)/shard_map/ppermute | solution.py:27
  205.0 4.5 %collective-permute-start.9 = (bf16[384,256]{1,0:T(8,128)(2,1)}, bf16[384,256]{1,0:T(8,128)(2,1)S(1)}, u32[]{:S(2)}, u32[]{:S(2)}) collective-permute-start(bf16[384,256]{1,0:T(8,128)(2,1)} %get-tuple-element.33), channel_id=1, source_target_pairs={{0,2},{1,3},{2,0},{3,1},{4,6},{5,7},{6,4},{7,5},{8,10},{9,11},{10,... | collective-permute-start | bytes 589832 | tf_op jit(solution)/shard_map/ppermute | solution.py:27
  209.5 10.8 %collective-permute-done.9.refs_3_ = bf16[384,256]{1,0:T(8,128)(2,1)S(1)} collective-permute-done((bf16[384,256]{1,0:T(8,128)(2,1)}, bf16[384,256]{1,0:T(8,128)(2,1)S(1)}, u32[]{:S(2)}, u32[]{:S(2)}) %collective-permute-start.9) | collective-permute-done | bytes 196640 | tf_op jit(solution)/shard_map/ppermute | solution.py:27
  222.6 4.1 %weight_grads.1 = (bf16[192,2048]{1,0:T(8,128)(2,1)}, bf16[192,2048]{1,0:T(8,128)(2,1)}) custom-call(s32[3]{0:T(128)S(1)} %copy-done.8, bf16[384,256]{1,0:T(8,128)(2,1)S(1)} %copy-done.7, bf16[384,256]{1,0:T(8,128)(2,1)S(1)} %collective-permute-done.7.refs_1_, bf16[384,256]{1,0:T(8,128)(2,1)S(1)} %collective-permute-done.8.refs_2_, ...), custom_call_target="tpu_custom_call" | custom-call | flops 1610612736 | bytes 5767168 | tf_op jit(solution)/shard_map/weight_grads/pallas_call | solution.py:280
  (84 shorter events, 48.4 us)
Async XLA Ops:
  7.2 119.3 %all-gather.5.cloned.1.call-start = ((), (), s32[]{:S(2)}) async-start(), calls=%async_computation.4 | async-start | bytes 11796480 | tf_op jit(solution)/shard_map/all_gather | solution.py:333
  12.4 26.4 %collective-permute-start = (bf16[16,4224]{1,0:T(8,128)(2,1)}, bf16[16,4224]{1,0:T(8,128)(2,1)S(1)}, u32[]{:S(2)}, u32[]{:S(2)}) collective-permute-start(bf16[16,4224]{1,0:T(8,128)(2,1)} %get-tuple-element.24), channel_id=1, source_target_pairs={{0,16},{4,20},{8,24},{12,28},{16,256},{20,260},{24,264},{28,268},{... | collective-permute-start | bytes 405512 | tf_op jit(solution)/shard_map/ppermute | solution.py:27
  21.5 29.8 %collective-permute-start.1 = (bf16[16,4224]{1,0:T(8,128)(2,1)}, bf16[16,4224]{1,0:T(8,128)(2,1)S(1)}, u32[]{:S(2)}, u32[]{:S(2)}) collective-permute-start(bf16[16,4224]{1,0:T(8,128)(2,1)} %get-tuple-element.24), channel_id=1, source_target_pairs={{0,256},{4,260},{8,264},{12,268},{16,272},{20,276},{24,280},{28,28... | collective-permute-start | bytes 405512 | tf_op jit(solution)/shard_map/ppermute | solution.py:27
  32.5 24.4 %collective-permute-start.2 = (bf16[16,4224]{1,0:T(8,128)(2,1)}, bf16[16,4224]{1,0:T(8,128)(2,1)S(1)}, u32[]{:S(2)}, u32[]{:S(2)}) collective-permute-start(bf16[16,4224]{1,0:T(8,128)(2,1)} %get-tuple-element.24), channel_id=1, source_target_pairs={{0,272},{4,276},{8,280},{12,284},{16,0},{20,4},{24,8},{28,12},{256... | collective-permute-start | bytes 405512 | tf_op jit(solution)/shard_map/ppermute | solution.py:27
  56.9 16.0 %collective-permute-start.4 = (bf16[64,4224]{1,0:T(8,128)(2,1)S(1)}, bf16[64,4224]{1,0:T(8,128)(2,1)S(1)}, u32[]{:S(2)}, u32[]{:S(2)}) collective-permute-start(bf16[64,4224]{1,0:T(8,128)(2,1)S(1)} %constant_dynamic-update-slice_fusion.refs_1_), channel_id=1, source_target_pairs={{0,284},{4,0},{8,4},{12,8},{16,12},{20,16},{24,20},{28,24},{256,28... | collective-permute-start | bytes 1622024 | tf_op jit(solution)/shard_map/ppermute | solution.py:27
  58.8 17.6 %collective-permute-start.3 = (bf16[64,4224]{1,0:T(8,128)(2,1)S(1)}, bf16[64,4224]{1,0:T(8,128)(2,1)S(1)}, u32[]{:S(2)}, u32[]{:S(2)}) collective-permute-start(bf16[64,4224]{1,0:T(8,128)(2,1)S(1)} %constant_dynamic-update-slice_fusion.refs_1_), channel_id=1, source_target_pairs={{0,4},{4,8},{8,12},{12,16},{16,20},{20,24},{24,28},{28,256},{256,2... | collective-permute-start | bytes 1622024 | tf_op jit(solution)/shard_map/ppermute | solution.py:27
  65.6 24.7 %all-to-all-start = ((bf16[8,8,4224]{2,1,0:T(8,128)(2,1)}), bf16[8,8,4224]{2,1,0:T(8,128)(2,1)S(1)}, u32[]{:S(2)}, u32[]{:S(2)}) async-start(bf16[8,8,4224]{2,1,0:T(8,128)(2,1)} %bitcast.35), calls=%async_computation | async-start | bytes 1081344 | tf_op jit(solution)/shard_map/all_to_all | solution.py:342
  72.9 9.5 %collective-permute-start.5 = (bf16[32,4224]{1,0:T(8,128)(2,1)S(1)}, bf16[32,4224]{1,0:T(8,128)(2,1)S(1)}, u32[]{:S(2)}, u32[]{:S(2)}) collective-permute-start(bf16[32,4224]{1,0:T(8,128)(2,1)S(1)} %slice.52), channel_id=1, source_target_pairs={{0,284},{4,0},{8,4},{12,8},{16,12},{20,16},{24,20},{28,24},{256,28... | collective-permute-start | bytes 811016 | tf_op jit(solution)/shard_map/ppermute | solution.py:27
  76.4 10.7 %collective-permute-start.6 = (bf16[32,4224]{1,0:T(8,128)(2,1)S(1)}, bf16[32,4224]{1,0:T(8,128)(2,1)S(1)}, u32[]{:S(2)}, u32[]{:S(2)}) collective-permute-start(bf16[32,4224]{1,0:T(8,128)(2,1)S(1)} %slice.53), channel_id=1, source_target_pairs={{0,4},{4,8},{8,12},{12,16},{16,20},{20,24},{24,28},{28,256},{256,2... | collective-permute-start | bytes 811016 | tf_op jit(solution)/shard_map/ppermute | solution.py:27
  105.4 19.9 %copy-start.5 = (bf16[8,8,4224]{2,1,0:T(8,128)(2,1)}, bf16[8,8,4224]{2,1,0:T(8,128)(2,1)S(1)}, u32[]{:S(2)}) copy-start(bf16[8,8,4224]{2,1,0:T(8,128)(2,1)S(1)} %all_to_all.20) | copy-start | bytes 1622020
  105.4 19.8 %all-to-all-start.1 = ((bf16[8,16,4224]{2,1,0:T(8,128)(2,1)}), bf16[8,16,4224]{2,1,0:T(8,128)(2,1)S(1)}, u32[]{:S(2)}, u32[]{:S(2)}) async-start(bf16[8,16,4224]{2,1,0:T(8,128)(2,1)} %bitcast.8), calls=%async_computation.1 | async-start | bytes 2162688 | tf_op jit(solution)/shard_map/all_to_all | solution.py:342
  108.9 100.6 %all-gather.7.cloned.1.call-start = ((), (), s32[]{:S(2)}) async-start(), calls=%async_computation.5 | async-start | bytes 5242880 | tf_op jit(solution)/shard_map/all_gather | solution.py:355
  141.7 87.7 %all-to-all-start.3 = ((bf16[128,2,2176]{2,1,0:T(2,128)(2,1)}), bf16[128,2,2176]{2,1,0:T(2,128)(2,1)}, u32[]{:S(2)}, u32[]{:S(2)}) async-start(bf16[128,2,2176]{2,1,0:T(2,128)(2,1)} %reshape.40), calls=%async_computation.3 | async-start | bytes 2228224 | tf_op jit(solution)/shard_map/all_to_all | solution.py:358
  159.2 61.2 %copy-start.7 = (bf16[384,256]{1,0:T(8,128)(2,1)S(1)}, bf16[384,256]{1,0:T(8,128)(2,1)}, u32[]{:S(2)}) copy-start(bf16[384,256]{1,0:T(8,128)(2,1)} %get-tuple-element.30.refs_0_) | copy-start | bytes 589828
  159.2 61.2 %copy-start.8 = (s32[3]{0:T(128)S(1)}, s32[3]{0:T(128)}, u32[]{:S(2)}) copy-start(s32[3]{0:T(128)} %pad_add_fusion.refs_0_.zs_ref) | copy-start | bytes 40
  159.2 22.4 %collective-permute-start.10 = (bf16[96,2048]{1,0:T(8,128)(2,1)S(1)}, bf16[96,2048]{1,0:T(8,128)(2,1)S(1)}, u32[]{:S(2)}, u32[]{:S(2)}) collective-permute-start(bf16[96,2048]{1,0:T(8,128)(2,1)S(1)} %get-tuple-element.43), channel_id=1, source_target_pairs={{0,1},{1,2},{2,3},{3,0},{4,5},{5,6},{6,7},{7,4},{8,9},{9,10},{10,1... | collective-permute-start | bytes 1179656 | tf_op jit(solution)/shard_map/ppermute | solution.py:27
  161.8 41.0 %collective-permute-start.7 = (bf16[384,256]{1,0:T(8,128)(2,1)S(1)}, bf16[384,256]{1,0:T(8,128)(2,1)S(1)}, u32[]{:S(2)}, u32[]{:S(2)}) collective-permute-start(bf16[384,256]{1,0:T(8,128)(2,1)S(1)} %copy-done.16), channel_id=1, source_target_pairs={{0,1},{1,2},{2,3},{3,0},{4,5},{5,6},{6,7},{7,4},{8,9},{9,10},{10,1... | collective-permute-start | bytes 589832 | tf_op jit(solution)/shard_map/ppermute | solution.py:27
  165.1 39.9 %collective-permute-start.8 = (bf16[384,256]{1,0:T(8,128)(2,1)S(1)}, bf16[384,256]{1,0:T(8,128)(2,1)S(1)}, u32[]{:S(2)}, u32[]{:S(2)}) collective-permute-start(bf16[384,256]{1,0:T(8,128)(2,1)S(1)} %copy-done.15), channel_id=1, source_target_pairs={{0,3},{1,0},{2,1},{3,2},{4,7},{5,4},{6,5},{7,6},{8,11},{9,8},{10,9... | collective-permute-start | bytes 589832 | tf_op jit(solution)/shard_map/ppermute | solution.py:27
  167.7 59.0 %collective-permute-start.12 = (bf16[96,2048]{1,0:T(8,128)(2,1)S(1)}, bf16[96,2048]{1,0:T(8,128)(2,1)}, u32[]{:S(2)}, u32[]{:S(2)}) collective-permute-start(bf16[96,2048]{1,0:T(8,128)(2,1)S(1)} %slice.47), channel_id=1, source_target_pairs={{0,3},{1,0},{2,1},{3,2},{4,7},{5,4},{6,5},{7,6},{8,11},{9,8},{10,9... | collective-permute-start | bytes 1179656 | tf_op jit(solution)/shard_map/ppermute | solution.py:27
  171.1 27.2 %collective-permute-start.14 = (bf16[96,2048]{1,0:T(8,128)(2,1)S(1)}, bf16[96,2048]{1,0:T(8,128)(2,1)S(1)}, u32[]{:S(2)}, u32[]{:S(2)}) collective-permute-start(bf16[96,2048]{1,0:T(8,128)(2,1)S(1)} %get-tuple-element.44), channel_id=1, source_target_pairs={{0,3},{1,0},{2,1},{3,2},{4,7},{5,4},{6,5},{7,6},{8,11},{9,8},{10,9... | collective-permute-start | bytes 1179656 | tf_op jit(solution)/shard_map/ppermute | solution.py:27
  181.6 45.1 %collective-permute-start.13 = (bf16[96,2048]{1,0:T(8,128)(2,1)S(1)}, bf16[96,2048]{1,0:T(8,128)(2,1)}, u32[]{:S(2)}, u32[]{:S(2)}) collective-permute-start(bf16[96,2048]{1,0:T(8,128)(2,1)S(1)} %slice.49), channel_id=1, source_target_pairs={{0,1},{1,2},{2,3},{3,0},{4,5},{5,6},{6,7},{7,4},{8,9},{9,10},{10,1... | collective-permute-start | bytes 1179656 | tf_op jit(solution)/shard_map/ppermute | solution.py:27
  198.3 28.4 %collective-permute-start.11 = (bf16[96,2048]{1,0:T(8,128)(2,1)S(1)}, bf16[96,2048]{1,0:T(8,128)(2,1)}, u32[]{:S(2)}, u32[]{:S(2)}) collective-permute-start(bf16[96,2048]{1,0:T(8,128)(2,1)S(1)} %add_convert_fusion.3), channel_id=1, source_target_pairs={{0,1},{1,2},{2,3},{3,0},{4,5},{5,6},{6,7},{7,4},{8,9},{9,10},{10,1... | collective-permute-start | bytes 1179656 | tf_op jit(solution)/shard_map/ppermute | solution.py:27
  202.8 23.9 %collective-permute-start.15 = (bf16[96,2048]{1,0:T(8,128)(2,1)}, bf16[96,2048]{1,0:T(8,128)(2,1)}, u32[]{:S(2)}, u32[]{:S(2)}) collective-permute-start(bf16[96,2048]{1,0:T(8,128)(2,1)} %add_convert_fusion.1), channel_id=1, source_target_pairs={{0,3},{1,0},{2,1},{3,2},{4,7},{5,4},{6,5},{7,6},{8,11},{9,8},{10,9... | collective-permute-start | bytes 1179656 | tf_op jit(solution)/shard_map/ppermute | solution.py:27
  205.0 15.4 %collective-permute-start.9 = (bf16[384,256]{1,0:T(8,128)(2,1)}, bf16[384,256]{1,0:T(8,128)(2,1)S(1)}, u32[]{:S(2)}, u32[]{:S(2)}) collective-permute-start(bf16[384,256]{1,0:T(8,128)(2,1)} %get-tuple-element.33), channel_id=1, source_target_pairs={{0,2},{1,3},{2,0},{3,1},{4,6},{5,7},{6,4},{7,5},{8,10},{9,11},{10,... | collective-permute-start | bytes 589832 | tf_op jit(solution)/shard_map/ppermute | solution.py:27
  (14 other events, 88.9 us)
Sparse Core Ops, SparseCore 0:
  10.6 102.8 all-gather.4
  126.6 64.4 all-gather.6

commit v5 on v4

--- a/solution.py
+++ b/solution.py
@@ -10,9 +10,10 @@
 LANES = 128
 CAPACITY = 2
 MIB = 1024 * 1024
-Z = ("zh", "zl")
+FAR = ("zh", "zq")
+Z = ("zh", "zq", "zr")
 YC = ("y", "c")
-PLACE = ("zh", "y", "c", "zl")
+PLACE = ("zh", "y", "c", "zq", "zr")
 
 
 def dot(a, b, da, db):
@@ -139,15 +140,14 @@
     zn = jnp.where(first | last, 4, 8)
     source = inside // (zn * CAPACITY)
     zi = (inside // CAPACITY) % zn
-    near = jnp.where(zi < 4, -1 - 4 * zi, 17 - 4 * zi)
-    offset = jnp.where(first, -4 * zi, jnp.where(last, 2 - 4 * zi, near))
-    zed = (z + offset + 32) % 16
+    turn = jnp.where(first, 0, jnp.where(last, 2, jnp.where(zi < 4, 3, 1)))
+    zed = 4 * (zi % 4) + (z + turn) % 4
     home = ((zed // 8) * 64 + source * 8 + zed % 8) * CAPACITY + inside % CAPACITY
     return (home == place).astype(BF)
 
 
 def rows_kernel(zs_ref, a_ref, b_ref, c_ref, w_ref, p_ref, *refs):
-    d_refs, s_ref, (gu, dn, rows, sems) = refs[:4], refs[4], refs[5:]
+    d_refs, s_ref, (gu, dn, rows, d_all, sems) = refs[:4], refs[4], refs[5:]
     hid = dn.shape[1]
     count, width = rows.shape
     features = (width - LANES) // 2
@@ -160,7 +160,7 @@
         (c_ref, rows.at[pl.ds(3 * quarter, quarter)]),
     ]
     for q, place in enumerate(places):
-        pairs.append((w_ref.at[place, pl.ds(0, 2 * hid)], gu.at[q]))
+        pairs.append((w_ref.at[place, pl.ds(0, 2 * hid)], gu.at[pl.ds(q * 2 * hid, 2 * hid)]))
         pairs.append((w_ref.at[place, pl.ds(2 * hid, hid)], dn.at[q]))
     copies = [pltpu.make_async_copy(s, t, sems.at[i]) for i, (s, t) in enumerate(pairs)]
     for copy in copies:
@@ -173,7 +173,8 @@
     for q in range(4):
         copies[3 + 2 * q].wait()
         copies[4 + 2 * q].wait()
-        pre = dot(gu[q], rows[:, :features], 1, 1)
+        first = q * 2 * hid
+        pre = dot(gu[first : first + 2 * hid, :], rows[:, :features], 1, 1)
         back = dot(dn[q], rows[:, features : 2 * features], 1, 1)
         gate_pre, up_pre = pre[:hid], pre[hid:]
         sigma = jax.nn.sigmoid(gate_pre)
@@ -183,17 +184,14 @@
         score = part if score is None else score + part
         d_hidden = coef * back
         d_gate = d_hidden * up_pre * sigma * (1.0 + gate_pre * (1.0 - sigma))
-        d_refs[q][0:hid, :] = d_gate.astype(BF)
-        d_refs[q][hid:, :] = (d_hidden * active).astype(BF)
+        d_all[first : first + hid, :] = d_gate.astype(BF)
+        d_all[first + hid : first + 2 * hid, :] = (d_hidden * active).astype(BF)
+        d_refs[q][...] = d_all[first : first + 2 * hid, :]
         s_ref[q] = (coef * hidden).astype(BF)
-    moved = [dot(d[...], home, 1, 0).astype(BF) for d in d_refs]
+    moved = dot(d_all[...], home, 1, 0).astype(BF)
     tile = 512
     for j in range(0, features, tile):
-        total = None
-        for q in range(4):
-            part = dot(moved[q], gu[q, :, j : j + tile], 0, 0)
-            total = part if total is None else total + part
-        p_ref[:, j : j + tile] = total.astype(BF)
+        p_ref[:, j : j + tile] = dot(moved, gu[:, j : j + tile], 0, 0).astype(BF)
     score = dot(jnp.broadcast_to(score, (LANES, count)).astype(BF), home, 1, 0)
     p_ref[:, features:] = score.T.astype(BF)
 
@@ -212,9 +210,10 @@
         in_specs=[pl.BlockSpec(memory_space=pltpu.SMEM)] + [pl.BlockSpec(memory_space=pl.ANY)] * 4,
         out_specs=[vmem()] * (n + 2),
         scratch_shapes=[
-            pltpu.VMEM((n, 2 * hid, features), BF),
+            pltpu.VMEM((n * 2 * hid, features), BF),
             pltpu.VMEM((n, hid, features), BF),
             pltpu.VMEM((count, width), BF),
+            pltpu.VMEM((n * 2 * hid, count), BF),
             pltpu.SemaphoreType.DMA((3 + 2 * n,)),
         ],
         compiler_params=pltpu.CompilerParams(vmem_limit_bytes=56 * MIB),
@@ -227,14 +226,23 @@
     )(zs, *chunks, weights)
 
 
-def down_kernel(s_ref, a_ref, b_ref, c_ref, own_ref, left_ref, right_ref, two_ref, rows):
+def down_kernel(s_ref, a_ref, b_ref, c_ref, own_ref, go_ref, come_ref, right_ref, left_ref, rows):
     quarter = a_ref.shape[0]
     rows[0:quarter, :] = a_ref[...]
     rows[quarter : 3 * quarter, :] = b_ref[...]
     rows[3 * quarter :, :] = c_ref[...]
     grads = rows[...]
-    for q, out in enumerate((own_ref, left_ref, right_ref, two_ref)):
-        out[...] = dot(s_ref[q], grads, 1, 0).astype(out.dtype)
+    half = right_ref.shape[0]
+    own_ref[...] = dot(s_ref[0], grads, 1, 0)
+    left = dot(s_ref[1], grads, 1, 0).astype(BF)
+    right = dot(s_ref[2], grads, 1, 0).astype(BF)
+    two = dot(s_ref[3], grads, 1, 0).astype(BF)
+    go_ref[:half, :] = two[:half]
+    go_ref[half:, :] = right[half:]
+    come_ref[:half, :] = left[:half]
+    come_ref[half:, :] = two[half:]
+    right_ref[...] = right[:half]
+    left_ref[...] = left[half:]
 
 
 def down_call(scaled, chunks, features):
@@ -246,9 +254,11 @@
         down_kernel,
         grid=(features // tile,),
         out_shape=[jax.ShapeDtypeStruct((hid, features), F32)]
-        + [jax.ShapeDtypeStruct((hid, features), BF)] * 3,
+        + [jax.ShapeDtypeStruct((hid, features), BF)] * 2
+        + [jax.ShapeDtypeStruct((hid // 2, features), BF)] * 2,
         in_specs=[pl.BlockSpec(scaled.shape, lambda j: (0, 0, 0))] + tiled,
-        out_specs=[pl.BlockSpec((hid, tile), lambda j: (0, j))] * 4,
+        out_specs=[pl.BlockSpec((hid, tile), lambda j: (0, j))] * 3
+        + [pl.BlockSpec((hid // 2, tile), lambda j: (0, j))] * 2,
         scratch_shapes=[pltpu.VMEM((count, tile), BF)],
         compiler_params=pltpu.CompilerParams(vmem_limit_bytes=24 * MIB),
         cost_estimate=pl.CostEstimate(
@@ -326,15 +336,14 @@
 def local(tokens, out_grad, expert_ids, keep_flags, route_weights, gate_w, up_w, down_w):
     nz, n = lax.axis_size(Z), lax.axis_size("x")
     step, features = tokens.shape
-    zs = jnp.stack([lax.axis_index(a) for a in ("zh", "zl", "x")]).astype(jnp.int32)
+    zs = jnp.stack([lax.axis_index(a) for a in ("zh", ("zq", "zr"), "x")]).astype(jnp.int32)
     half = gate_w.shape[1] // 2
 
     joined = jnp.concatenate([gate_w[0], up_w[0], down_w[0]], axis=0)
     weights = lax.all_gather(joined, "x", axis=0)
     own, code = payload_call(tokens, out_grad, expert_ids.T, keep_flags.T, route_weights.T)
 
-    far = [shift(own, s, Z, nz) for s in (4, 8, 12)]
-    chunk = jnp.concatenate([own, *far], axis=0)
+    chunk = lax.all_gather(own, FAR, axis=0, tiled=True)
     left, right = shift(chunk, 1, Z, nz), shift(chunk, -1, Z, nz)
 
     def exchange(packed):
@@ -345,11 +354,14 @@
 
     rows_a = exchange(pack_call(zs, [chunk], step))
     rest_a = shift(right[: 2 * step], -1, Z, nz)
-    rest_b = shift(left[step : 3 * step], 1, Z, nz)
+    rest_b = shift(left[2 * step :], 1, Z, nz)
     packed_b = pack_call(zs, [left, right], step)
     rest_a, rest_b, _ = lax.optimization_barrier((rest_a, rest_b, packed_b))
+    packed_b, rows_a = lax.optimization_barrier((packed_b, rows_a))
     rows_b = exchange(packed_b)
-    rows_c = exchange(pack_call(zs, [rest_a, rest_b], step))
+    packed_c = pack_call(zs, [rest_a, rest_b], step)
+    packed_c, rows_b = lax.optimization_barrier((packed_c, rows_b))
+    rows_c = exchange(packed_c)
 
     chunks = [rows_a, rows_b, rows_c]
     x = lax.all_gather(jnp.concatenate([c[:, :features] for c in chunks], axis=0), "x", axis=0)
@@ -361,28 +373,26 @@
     ds = [d_own, shift(d_right, 1, "x", n), shift(d_left, -1, "x", n), shift(d_two, 2, "x", n)]
     grad_gate, grad_up = weights_call(zs, ds, x)
 
-    p_own, p_left, p_right, p_two = down_call(scaled, chunks, features)
-    via_a = shift(p_two[:half], 1, "x", n)
-    via_b = shift(p_two[half:], -1, "x", n)
-    left_low = shift(p_right[half:], 1, "x", n)
-    right_top = shift(p_left[:half], -1, "x", n)
-    left_top = shift((p_right[:half].astype(F32) + via_a.astype(F32)).astype(BF), 1, "x", n)
-    right_low = shift((p_left[half:].astype(F32) + via_b.astype(F32)).astype(BF), -1, "x", n)
+    p_own, p_go, p_come, p_right, p_left = down_call(scaled, chunks, features)
+    from_left, from_right = shift(p_go, 1, "x", n), shift(p_come, -1, "x", n)
+    p_right = (p_right.astype(F32) + from_left[:half].astype(F32)).astype(BF)
+    p_left = (p_left.astype(F32) + from_right[half:].astype(F32)).astype(BF)
+    left_top, right_low = shift(p_right, 1, "x", n), shift(p_left, -1, "x", n)
     grad_down = jnp.concatenate(
         [
-            (p_own[:half] + left_top.astype(F32) + right_top.astype(F32)).astype(BF),
-            (p_own[half:] + left_low.astype(F32) + right_low.astype(F32)).astype(BF),
+            p_own[:half] + left_top.astype(F32) + from_right[:half].astype(F32),
+            p_own[half:] + from_left[half:].astype(F32) + right_low.astype(F32),
         ],
         axis=0,
-    )
+    ).astype(BF)
 
     token_grad, slot_score = home_call(code, home, features)
     return (token_grad, slot_score.T, grad_gate[None], grad_up[None], grad_down[None])
 
 
 def solution(mesh):
-    fine = Mesh(mesh.devices.reshape(2, 4, 2, 8, 4), ("zh", "y", "c", "zl", "x"))
-    by_row = P(("zh", "y", "c", "zl", "x"), None)
+    fine = Mesh(mesh.devices.reshape(2, 4, 2, 2, 4, 4), (*PLACE, "x"))
+    by_row = P((*PLACE, "x"), None)
     by_expert = P(PLACE, "x", None)
     return jax.shard_map(
         local,

time: 242 us -> 237 us (0.979)
  starting transfers between devices: 86.8 us -> 65.5 us
  blocking collectives: 15 us -> 35.2 us
  waiting for transfers between devices: 73.7 us -> 70.2 us
    all_gather x0 -> x1, blocking collectives: none -> 35.2 us  [local(): chunk = lax.all_gather(own, FAR, axis=0, tiled=True)]
    ppermute x16 -> x11, starting transfers between devices: 65.5 us -> 35.4 us  [shift(): return lax.ppermute(block, axes, [(i, (i + step) % n) for i in range(n)])]
    all_to_all x1 -> x0, blocking collectives: 15 us -> none  [exchange(): lax.all_to_all(packed.reshape(8, rows // 8, width), YC, split_axis=0, con...]
    ppermute x16 -> x11, waiting for transfers between devices: 57.5 us -> 49.9 us  [shift(): return lax.ppermute(block, axes, [(i, (i + step) % n) for i in range(n)])]
    all_to_all x1, starting transfers between devices: 13.1 us -> 17.6 us  [local(): lax.all_to_all(back.reshape(-1, CAPACITY, back.shape[1]), PLACE, split_ax...]
    all_to_all x2 -> x3, starting transfers between devices: 8.04 us -> 12.5 us  [exchange(): lax.all_to_all(packed.reshape(8, rows // 8, width), YC, split_axis=0, con...]
    all_gather x1, waiting for transfers between devices: 0.01 us -> 4.1 us  [local(): weights = lax.all_gather(joined, 'x', axis=0)]
    unnamed x37 -> x38, local copies, waits for them, and re-layouts: 6.01 us -> 6.57 us
  transfers between devices with their start and end apart: 21 -> 17, of which waited for: 9 -> 7; matrix products, arithmetic and copies ran while one was open for 4% -> 3% of each run, Pallas kernels for 12% -> 12%
where the time goes in v5:
time: 237 us; the launch traced here: 236 us
  waiting for transfers between devices  70.2 us (30%)
  starting transfers between devices  65.5 us (28%)
  blocking collectives  35.2 us (15%)
  Pallas kernels  30.6 us (13%)
  between operations  14.4 us (6%)
  local copies, waits for them, and re-layouts  11.4 us (5%)
  other arithmetic  8.53 us (4%)
    ppermute x11, waiting for transfers between devices, shift(): return lax.ppermute(block, axes, [(i, (i + step) % n) for i in range(n)])  49.9 us
    ppermute x11, starting transfers between devices, shift(): return lax.ppermute(block, axes, [(i, (i + step) % n) for i in range(n)])  35.4 us
    all_gather x1, blocking collectives, local(): chunk = lax.all_gather(own, FAR, axis=0, tiled=True)  35.2 us
    all_to_all x1, starting transfers between devices, local(): lax.all_to_all(back.reshape(-1, CAPACITY, back.shape[1]), PLACE, split_ax...  17.6 us
    all_to_all x3, waiting for transfers between devices, exchange(): lax.all_to_all(packed.reshape(8, rows // 8, width), YC, split_axis=0, con...  16.2 us
    all_to_all x3, starting transfers between devices, exchange(): lax.all_to_all(packed.reshape(8, rows // 8, width), YC, split_axis=0, con...  12.5 us
    pallas_call x1, Pallas kernels, rows_call(): pl.pallas_call(rows_kernel, out_shape=[jax.ShapeDtypeStruct((count, featu...  12.1 us
    pallas_call x3, Pallas kernels, pack_call(): pl.pallas_call(body, out_shape=jax.ShapeDtypeStruct((rows, width), BF), i...  7.92 us
  transfers between devices with their start and end apart: 17, of which 7 were waited for; matrix products, arithmetic and copies ran while one was open for 3% of the time, Pallas kernels for 12%

profile of v5, /device:TPU:6, one launch (start us, length us, event | category | flops | bytes accessed | tf_op | source)
XLA Modules:
  0.0 235.8 jit_solution(17753976094874498993)
XLA Ops:
  7.2 3.3 %pad_maximum_fusion = bf16[576,2048]{1,0:T(8,128)(2,1)} fusion(bf16[192,2048]{1,0:T(8,128)(2,1)} %bitcast.40, bf16[192,2048]{1,0:T(8,128)(2,1)} %bitcast.41, bf16[192,2048]{1,0:T(8,128)(2,1)} %bitcast.42), kind=kLoop, calls=%fused_computation | loop fusion | flops 7077888 | bytes 4718592 | tf_op jit(solution)/shard_map/concatenate | solution.py:342
  12.4 35.2 %all_gather.15.refs_1_ = bf16[64,4224]{1,0:T(8,128)(2,1)S(1)} all-gather(bf16[16,4224]{1,0:T(8,128)(2,1)} %get-tuple-element.29), channel_id=1, replica_groups=mesh['zh'=2,'y'=4,'c'=2,'zq'=2,'zr'=4,'x'=4] {'zh','zq'}, dimensions={0}, use_global_device_ids=true | all-gather | bytes 675840 | tf_op jit(solution)/shard_map/all_gather | solution.py:346
  49.6 5.1 %collective-permute-start.1 = (bf16[64,4224]{1,0:T(8,128)(2,1)S(1)}, bf16[64,4224]{1,0:T(8,128)(2,1)S(1)}, u32[]{:S(2)}, u32[]{:S(2)}) collective-permute-start(bf16[64,4224]{1,0:T(8,128)(2,1)S(1)} %all_gather.15.refs_1_), channel_id=1, source_target_pairs={{0,284},{4,0},{8,4},{12,8},{16,12},{20,16},{24,20},{28,24},{256,28... | collective-permute-start | bytes 1622024 | tf_op jit(solution)/shard_map/ppermute | solution.py:28
  57.6 4.5 %all-to-all-start = ((bf16[8,8,4224]{2,1,0:T(8,128)(2,1)}), bf16[8,8,4224]{2,1,0:T(8,128)(2,1)S(1)}, u32[]{:S(2)}, u32[]{:S(2)}) async-start(bf16[8,8,4224]{2,1,0:T(8,128)(2,1)} %bitcast.39), calls=%async_computation | async-start | bytes 1081344 | tf_op jit(solution)/shard_map/all_to_all | solution.py:351
  63.7 3.1 %pack.3 = bf16[128,4224]{1,0:T(8,128)(2,1)} custom-call(s32[3]{0:T(128)} %pad_add_fusion.refs_0_.zs_ref, bf16[64,4224]{1,0:T(8,128)(2,1)} %copy-done.11, bf16[64,4224]{1,0:T(8,128)(2,1)} %copy-done.13), custom_call_target="tpu_custom_call" | custom-call | tf_op jit(solution)/shard_map/pack/pallas_call | solution.py:126
  66.9 5.8 %all-to-all-done = bf16[8,8,4224]{2,1,0:T(8,128)(2,1)S(1)} async-done(((bf16[8,8,4224]{2,1,0:T(8,128)(2,1)}), bf16[8,8,4224]{2,1,0:T(8,128)(2,1)S(1)}, u32[]{:S(2)}, u32[]{:S(2)}) %all-to-all-start) | async-done | bytes 540704 | tf_op jit(solution)/shard_map/all_to_all | solution.py:351
  72.6 3.6 %all-to-all-start.1 = ((bf16[8,16,4224]{2,1,0:T(8,128)(2,1)}), bf16[8,16,4224]{2,1,0:T(8,128)(2,1)S(1)}, u32[]{:S(2)}, u32[]{:S(2)}) async-start(bf16[8,16,4224]{2,1,0:T(8,128)(2,1)} %bitcast.37), calls=%async_computation.1 | async-start | bytes 2162688 | tf_op jit(solution)/shard_map/all_to_all | solution.py:351
  78.3 3.9 %collective-permute-start.3 = (bf16[32,4224]{1,0:T(8,128)(2,1)S(1)}, bf16[32,4224]{1,0:T(8,128)(2,1)S(1)}, u32[]{:S(2)}, u32[]{:S(2)}) collective-permute-start(bf16[32,4224]{1,0:T(8,128)(2,1)S(1)} %slice.45), channel_id=1, source_target_pairs={{0,4},{4,8},{8,12},{12,16},{16,20},{20,24},{24,28},{28,256},{256,2... | collective-permute-start | bytes 811016 | tf_op jit(solution)/shard_map/ppermute | solution.py:28
  82.2 4.7 %collective-permute-done.2.refs_1_ = bf16[32,4224]{1,0:T(8,128)(2,1)S(1)} collective-permute-done((bf16[32,4224]{1,0:T(8,128)(2,1)S(1)}, bf16[32,4224]{1,0:T(8,128)(2,1)S(1)}, u32[]{:S(2)}, u32[]{:S(2)}) %collective-permute-start.2) | collective-permute-done | bytes 270368 | tf_op jit(solution)/shard_map/ppermute | solution.py:28
  86.9 3.2 %collective-permute-done.3.refs_2_ = bf16[32,4224]{1,0:T(8,128)(2,1)S(1)} collective-permute-done((bf16[32,4224]{1,0:T(8,128)(2,1)S(1)}, bf16[32,4224]{1,0:T(8,128)(2,1)S(1)}, u32[]{:S(2)}, u32[]{:S(2)}) %collective-permute-start.3) | collective-permute-done | bytes 270368 | tf_op jit(solution)/shard_map/ppermute | solution.py:28
  90.8 2.5 %pack.5 = bf16[64,4224]{1,0:T(8,128)(2,1)} custom-call(s32[3]{0:T(128)} %pad_add_fusion.refs_0_.zs_ref, bf16[32,4224]{1,0:T(8,128)(2,1)} %copy-done.17, bf16[32,4224]{1,0:T(8,128)(2,1)} %copy-done.18), custom_call_target="tpu_custom_call" | custom-call | tf_op jit(solution)/shard_map/pack/pallas_call | solution.py:126
  93.3 4.5 %all-to-all-start.2 = ((bf16[8,8,4224]{2,1,0:T(8,128)(2,1)}), bf16[8,8,4224]{2,1,0:T(8,128)(2,1)S(1)}, u32[]{:S(2)}, u32[]{:S(2)}) async-start(bf16[8,8,4224]{2,1,0:T(8,128)(2,1)} %bitcast.38), calls=%async_computation.2 | async-start | bytes 1081344 | tf_op jit(solution)/shard_map/all_to_all | solution.py:351
  97.9 10.4 %all-to-all-done.2 = bf16[8,8,4224]{2,1,0:T(8,128)(2,1)S(1)} async-done(((bf16[8,8,4224]{2,1,0:T(8,128)(2,1)}), bf16[8,8,4224]{2,1,0:T(8,128)(2,1)S(1)}, u32[]{:S(2)}, u32[]{:S(2)}) %all-to-all-start.2) | async-done | bytes 540704 | tf_op jit(solution)/shard_map/all_to_all | solution.py:351
  109.5 4.1 %all-gather.5.cloned.1.call-done = bf16[2304,2048]{1,0:T(8,128)(2,1)} async-done(((bf16[576,2048]{1,0:T(8,128)(2,1)}), bf16[2304,2048]{1,0:T(8,128)(2,1)}) %all-gather.5.cloned.1.call-update) | async-done | bytes 9437200 | tf_op jit(solution)/shard_map/all_gather | solution.py:343
  113.6 12.1 %rows.1 = (bf16[256,2176]{1,0:T(8,128)(2,1)}, bf16[384,256]{1,0:T(8,128)(2,1)}, bf16[384,256]{1,0:T(8,128)(2,1)}, bf16[384,256]{1,0:T(8,128)(2,1)}, bf16[384,256...) custom-call(s32[3]{0:T(128)} %pad_add_fusion.refs_0_.zs_ref, bf16[64,4224]{1,0:T(8,128)(2,1)} %bitcast.32, ...), custom_call_target="tpu_custom_call" | custom-call | flops 4026531840 | bytes 12582912 | tf_op jit(solution)/shard_map/rows/pallas_call | solution.py:203
  128.1 17.6 %all-to-all-start.3 = ((bf16[128,2,2176]{2,1,0:T(2,128)(2,1)}), bf16[128,2,2176]{2,1,0:T(2,128)(2,1)}, u32[]{:S(2)}, u32[]{:S(2)}) async-start(bf16[128,2,2176]{2,1,0:T(2,128)(2,1)} %reshape.71), calls=%async_computation.3 | async-start | bytes 2228224 | tf_op jit(solution)/shard_map/all_to_all | solution.py:370
  150.1 3.4 %collective-permute-start.7 = (bf16[192,2048]{1,0:T(8,128)(2,1)S(1)}, bf16[192,2048]{1,0:T(8,128)(2,1)S(1)}, u32[]{:S(2)}, u32[]{:S(2)}) collective-permute-start(bf16[192,2048]{1,0:T(8,128)(2,1)S(1)} %get-tuple-element.48), channel_id=1, source_target_pairs={{0,1},{1,2},{2,3},{3,0},{4,5},{5,6},{6,7},{7,4},{8,9},{9,10},{10,1... | collective-permute-start | bytes 2359304 | tf_op jit(solution)/shard_map/ppermute | solution.py:28
  153.5 2.5 %collective-permute-start.9 = (bf16[192,2048]{1,0:T(8,128)(2,1)S(1)}, bf16[192,2048]{1,0:T(8,128)(2,1)S(1)}, u32[]{:S(2)}, u32[]{:S(2)}) collective-permute-start(bf16[192,2048]{1,0:T(8,128)(2,1)S(1)} %get-tuple-element.49), channel_id=1, source_target_pairs={{0,3},{1,0},{2,1},{3,2},{4,7},{5,4},{6,5},{7,6},{8,11},{9,8},{10,9... | collective-permute-start | bytes 2359304 | tf_op jit(solution)/shard_map/ppermute | solution.py:28
  155.9 32.5 %collective-permute-done.7 = bf16[192,2048]{1,0:T(8,128)(2,1)S(1)} collective-permute-done((bf16[192,2048]{1,0:T(8,128)(2,1)S(1)}, bf16[192,2048]{1,0:T(8,128)(2,1)S(1)}, u32[]{:S(2)}, u32[]{:S(2)}) %collective-permute-start.7) | collective-permute-done | bytes 786464 | tf_op jit(solution)/shard_map/ppermute | solution.py:28
  188.6 4.3 %collective-permute-start.8 = (bf16[96,2048]{1,0:T(8,128)(2,1)S(1)}, bf16[96,2048]{1,0:T(8,128)(2,1)}, u32[]{:S(2)}, u32[]{:S(2)}) collective-permute-start(bf16[96,2048]{1,0:T(8,128)(2,1)S(1)} %add_convert_fusion.3), channel_id=1, source_target_pairs={{0,1},{1,2},{2,3},{3,0},{4,5},{5,6},{6,7},{7,4},{8,9},{9,10},{10,1... | collective-permute-start | bytes 1179656 | tf_op jit(solution)/shard_map/ppermute | solution.py:28
  195.8 5.1 %collective-permute-start.4 = (bf16[384,256]{1,0:T(8,128)(2,1)}, bf16[384,256]{1,0:T(8,128)(2,1)S(1)}, u32[]{:S(2)}, u32[]{:S(2)}) collective-permute-start(bf16[384,256]{1,0:T(8,128)(2,1)} %get-tuple-element.40), channel_id=1, source_target_pairs={{0,1},{1,2},{2,3},{3,0},{4,5},{5,6},{6,7},{7,4},{8,9},{9,10},{10,1... | collective-permute-start | bytes 589832 | tf_op jit(solution)/shard_map/ppermute | solution.py:28
  202.9 3.4 %collective-permute-start.6 = (bf16[384,256]{1,0:T(8,128)(2,1)}, bf16[384,256]{1,0:T(8,128)(2,1)S(1)}, u32[]{:S(2)}, u32[]{:S(2)}) collective-permute-start(bf16[384,256]{1,0:T(8,128)(2,1)} %get-tuple-element.42), channel_id=1, source_target_pairs={{0,2},{1,3},{2,0},{3,1},{4,6},{5,7},{6,4},{7,5},{8,10},{9,11},{10,... | collective-permute-start | bytes 589832 | tf_op jit(solution)/shard_map/ppermute | solution.py:28
  206.3 9.4 %collective-permute-done.5.refs_2_ = bf16[384,256]{1,0:T(8,128)(2,1)S(1)} collective-permute-done((bf16[384,256]{1,0:T(8,128)(2,1)}, bf16[384,256]{1,0:T(8,128)(2,1)S(1)}, u32[]{:S(2)}, u32[]{:S(2)}) %collective-permute-start.5) | collective-permute-done | bytes 196640 | tf_op jit(solution)/shard_map/ppermute | solution.py:28
  217.9 4.1 %weight_grads.1 = (bf16[192,2048]{1,0:T(8,128)(2,1)}, bf16[192,2048]{1,0:T(8,128)(2,1)}) custom-call(s32[3]{0:T(128)S(1)} %copy-done.8, bf16[384,256]{1,0:T(8,128)(2,1)S(1)} %copy-done.7, bf16[384,256]{1,0:T(8,128)(2,1)S(1)} %collective-permute-done.4.refs_1_, bf16[384,256]{1,0:T(8,128)(2,1)S(1)} %collective-permute-done.5.refs_2_, ...), custom_call_target="tpu_custom_call" | custom-call | flops 1610612736 | bytes 5767168 | tf_op jit(solution)/shard_map/weight_grads/pallas_call | solution.py:290
  (73 shorter events, 33.2 us)
Async XLA Ops:
  7.2 106.4 %all-gather.5.cloned.1.call-start = ((), (), s32[]{:S(2)}) async-start(), calls=%async_computation.4 | async-start | bytes 11796480 | tf_op jit(solution)/shard_map/all_gather | solution.py:343
  47.6 14.5 %collective-permute-start = (bf16[64,4224]{1,0:T(8,128)(2,1)S(1)}, bf16[64,4224]{1,0:T(8,128)(2,1)S(1)}, u32[]{:S(2)}, u32[]{:S(2)}) collective-permute-start(bf16[64,4224]{1,0:T(8,128)(2,1)S(1)} %all_gather.15.refs_1_), channel_id=1, source_target_pairs={{0,4},{4,8},{8,12},{12,16},{16,20},{20,24},{24,28},{28,256},{256,2... | collective-permute-start | bytes 1622024 | tf_op jit(solution)/shard_map/ppermute | solution.py:28
  49.6 12.6 %collective-permute-start.1 = (bf16[64,4224]{1,0:T(8,128)(2,1)S(1)}, bf16[64,4224]{1,0:T(8,128)(2,1)S(1)}, u32[]{:S(2)}, u32[]{:S(2)}) collective-permute-start(bf16[64,4224]{1,0:T(8,128)(2,1)S(1)} %all_gather.15.refs_1_), channel_id=1, source_target_pairs={{0,284},{4,0},{8,4},{12,8},{16,12},{20,16},{24,20},{28,24},{256,28... | collective-permute-start | bytes 1622024 | tf_op jit(solution)/shard_map/ppermute | solution.py:28
  57.6 15.0 %all-to-all-start = ((bf16[8,8,4224]{2,1,0:T(8,128)(2,1)}), bf16[8,8,4224]{2,1,0:T(8,128)(2,1)S(1)}, u32[]{:S(2)}, u32[]{:S(2)}) async-start(bf16[8,8,4224]{2,1,0:T(8,128)(2,1)} %bitcast.39), calls=%async_computation | async-start | bytes 1081344 | tf_op jit(solution)/shard_map/all_to_all | solution.py:351
  66.9 11.4 %copy-start.12 = (bf16[64,4224]{1,0:T(8,128)(2,1)S(1)}, bf16[64,4224]{1,0:T(8,128)(2,1)}, u32[]{:S(2)}) copy-start(bf16[64,4224]{1,0:T(8,128)(2,1)} %copy-done.11) | copy-start | bytes 1622020
  72.6 25.2 %copy-start.3 = (bf16[8,8,4224]{2,1,0:T(8,128)(2,1)}, bf16[8,8,4224]{2,1,0:T(8,128)(2,1)S(1)}, u32[]{:S(2)}) copy-start(bf16[8,8,4224]{2,1,0:T(8,128)(2,1)S(1)} %all-to-all-done) | copy-start | bytes 1622020
  72.6 20.6 %all-to-all-start.1 = ((bf16[8,16,4224]{2,1,0:T(8,128)(2,1)}), bf16[8,16,4224]{2,1,0:T(8,128)(2,1)S(1)}, u32[]{:S(2)}, u32[]{:S(2)}) async-start(bf16[8,16,4224]{2,1,0:T(8,128)(2,1)} %bitcast.37), calls=%async_computation.1 | async-start | bytes 2162688 | tf_op jit(solution)/shard_map/all_to_all | solution.py:351
  76.2 10.7 %collective-permute-start.2 = (bf16[32,4224]{1,0:T(8,128)(2,1)S(1)}, bf16[32,4224]{1,0:T(8,128)(2,1)S(1)}, u32[]{:S(2)}, u32[]{:S(2)}) collective-permute-start(bf16[32,4224]{1,0:T(8,128)(2,1)S(1)} %slice.44), channel_id=1, source_target_pairs={{0,284},{4,0},{8,4},{12,8},{16,12},{20,16},{24,20},{28,24},{256,28... | collective-permute-start | bytes 811016 | tf_op jit(solution)/shard_map/ppermute | solution.py:28
  78.3 11.8 %collective-permute-start.3 = (bf16[32,4224]{1,0:T(8,128)(2,1)S(1)}, bf16[32,4224]{1,0:T(8,128)(2,1)S(1)}, u32[]{:S(2)}, u32[]{:S(2)}) collective-permute-start(bf16[32,4224]{1,0:T(8,128)(2,1)S(1)} %slice.45), channel_id=1, source_target_pairs={{0,4},{4,8},{8,12},{12,16},{16,20},{20,24},{24,28},{28,256},{256,2... | collective-permute-start | bytes 811016 | tf_op jit(solution)/shard_map/ppermute | solution.py:28
  93.3 16.2 %copy-start.1 = (bf16[8,16,4224]{2,1,0:T(8,128)(2,1)}, bf16[8,16,4224]{2,1,0:T(8,128)(2,1)S(1)}, u32[]{:S(2)}) copy-start(bf16[8,16,4224]{2,1,0:T(8,128)(2,1)S(1)} %all-to-all-done.1) | copy-start | bytes 3244036
  93.3 15.0 %all-to-all-start.2 = ((bf16[8,8,4224]{2,1,0:T(8,128)(2,1)}), bf16[8,8,4224]{2,1,0:T(8,128)(2,1)S(1)}, u32[]{:S(2)}, u32[]{:S(2)}) async-start(bf16[8,8,4224]{2,1,0:T(8,128)(2,1)} %bitcast.38), calls=%async_computation.2 | async-start | bytes 1081344 | tf_op jit(solution)/shard_map/all_to_all | solution.py:351
  97.7 108.5 %all-gather.7.cloned.1.call-start = ((), (), s32[]{:S(2)}) async-start(), calls=%async_computation.5 | async-start | bytes 5242880 | tf_op jit(solution)/shard_map/all_gather | solution.py:367
  125.7 20.0 %copy-start.2 = (bf16[8,16,4224]{2,1,0:T(8,128)(2,1)S(1)}, bf16[8,16,4224]{2,1,0:T(8,128)(2,1)}, u32[]{:S(2)}) copy-start(bf16[8,16,4224]{2,1,0:T(8,128)(2,1)} %copy-done.1) | copy-start | bytes 3244036
  125.7 20.0 %copy-start.4 = (bf16[8,8,4224]{2,1,0:T(8,128)(2,1)S(1)}, bf16[8,8,4224]{2,1,0:T(8,128)(2,1)}, u32[]{:S(2)}) copy-start(bf16[8,8,4224]{2,1,0:T(8,128)(2,1)} %copy-done.3) | copy-start | bytes 1622020
  128.1 96.3 %all-to-all-start.3 = ((bf16[128,2,2176]{2,1,0:T(2,128)(2,1)}), bf16[128,2,2176]{2,1,0:T(2,128)(2,1)}, u32[]{:S(2)}, u32[]{:S(2)}) async-start(bf16[128,2,2176]{2,1,0:T(2,128)(2,1)} %reshape.71), calls=%async_computation.3 | async-start | bytes 2228224 | tf_op jit(solution)/shard_map/all_to_all | solution.py:370
  147.8 67.9 %copy-start.7 = (bf16[384,256]{1,0:T(8,128)(2,1)S(1)}, bf16[384,256]{1,0:T(8,128)(2,1)}, u32[]{:S(2)}) copy-start(bf16[384,256]{1,0:T(8,128)(2,1)} %get-tuple-element.39.refs_0_) | copy-start | bytes 589828
  147.8 67.9 %copy-start.8 = (s32[3]{0:T(128)S(1)}, s32[3]{0:T(128)}, u32[]{:S(2)}) copy-start(s32[3]{0:T(128)} %pad_add_fusion.refs_0_.zs_ref) | copy-start | bytes 40
  150.1 38.4 %collective-permute-start.7 = (bf16[192,2048]{1,0:T(8,128)(2,1)S(1)}, bf16[192,2048]{1,0:T(8,128)(2,1)S(1)}, u32[]{:S(2)}, u32[]{:S(2)}) collective-permute-start(bf16[192,2048]{1,0:T(8,128)(2,1)S(1)} %get-tuple-element.48), channel_id=1, source_target_pairs={{0,1},{1,2},{2,3},{3,0},{4,5},{5,6},{6,7},{7,4},{8,9},{9,10},{10,1... | collective-permute-start | bytes 2359304 | tf_op jit(solution)/shard_map/ppermute | solution.py:28
  153.5 39.4 %collective-permute-start.9 = (bf16[192,2048]{1,0:T(8,128)(2,1)S(1)}, bf16[192,2048]{1,0:T(8,128)(2,1)S(1)}, u32[]{:S(2)}, u32[]{:S(2)}) collective-permute-start(bf16[192,2048]{1,0:T(8,128)(2,1)S(1)} %get-tuple-element.49), channel_id=1, source_target_pairs={{0,3},{1,0},{2,1},{3,2},{4,7},{5,4},{6,5},{7,6},{8,11},{9,8},{10,9... | collective-permute-start | bytes 2359304 | tf_op jit(solution)/shard_map/ppermute | solution.py:28
  188.6 33.4 %collective-permute-start.8 = (bf16[96,2048]{1,0:T(8,128)(2,1)S(1)}, bf16[96,2048]{1,0:T(8,128)(2,1)}, u32[]{:S(2)}, u32[]{:S(2)}) collective-permute-start(bf16[96,2048]{1,0:T(8,128)(2,1)S(1)} %add_convert_fusion.3), channel_id=1, source_target_pairs={{0,1},{1,2},{2,3},{3,0},{4,5},{5,6},{6,7},{7,4},{8,9},{9,10},{10,1... | collective-permute-start | bytes 1179656 | tf_op jit(solution)/shard_map/ppermute | solution.py:28
  193.9 28.1 %collective-permute-start.10 = (bf16[96,2048]{1,0:T(8,128)(2,1)}, bf16[96,2048]{1,0:T(8,128)(2,1)}, u32[]{:S(2)}, u32[]{:S(2)}) collective-permute-start(bf16[96,2048]{1,0:T(8,128)(2,1)} %add_convert_fusion.1), channel_id=1, source_target_pairs={{0,3},{1,0},{2,1},{3,2},{4,7},{5,4},{6,5},{7,6},{8,11},{9,8},{10,9... | collective-permute-start | bytes 1179656 | tf_op jit(solution)/shard_map/ppermute | solution.py:28
  195.8 10.5 %collective-permute-start.4 = (bf16[384,256]{1,0:T(8,128)(2,1)}, bf16[384,256]{1,0:T(8,128)(2,1)S(1)}, u32[]{:S(2)}, u32[]{:S(2)}) collective-permute-start(bf16[384,256]{1,0:T(8,128)(2,1)} %get-tuple-element.40), channel_id=1, source_target_pairs={{0,1},{1,2},{2,3},{3,0},{4,5},{5,6},{6,7},{7,4},{8,9},{9,10},{10,1... | collective-permute-start | bytes 589832 | tf_op jit(solution)/shard_map/ppermute | solution.py:28
  200.9 14.8 %collective-permute-start.5 = (bf16[384,256]{1,0:T(8,128)(2,1)}, bf16[384,256]{1,0:T(8,128)(2,1)S(1)}, u32[]{:S(2)}, u32[]{:S(2)}) collective-permute-start(bf16[384,256]{1,0:T(8,128)(2,1)} %get-tuple-element.41), channel_id=1, source_target_pairs={{0,3},{1,0},{2,1},{3,2},{4,7},{5,4},{6,5},{7,6},{8,11},{9,8},{10,9... | collective-permute-start | bytes 589832 | tf_op jit(solution)/shard_map/ppermute | solution.py:28
  202.9 12.9 %collective-permute-start.6 = (bf16[384,256]{1,0:T(8,128)(2,1)}, bf16[384,256]{1,0:T(8,128)(2,1)S(1)}, u32[]{:S(2)}, u32[]{:S(2)}) collective-permute-start(bf16[384,256]{1,0:T(8,128)(2,1)} %get-tuple-element.42), channel_id=1, source_target_pairs={{0,2},{1,3},{2,0},{3,1},{4,6},{5,7},{6,4},{7,5},{8,10},{9,11},{10,... | collective-permute-start | bytes 589832 | tf_op jit(solution)/shard_map/ppermute | solution.py:28
  (12 other events, 46.2 us)
Sparse Core Ops, SparseCore 0:
  10.7 102.8 all-gather.4
  115.7 73.0 all-gather.6

commit v6 on v5

--- a/solution.py
+++ b/solution.py
@@ -135,18 +135,18 @@
 def homes(z, rows):
     row, place = iota((rows, rows), 0), iota((rows, rows), 1)
     quarter = rows // 4
-    first, last = row < quarter, row >= 3 * quarter
-    inside = jnp.where(first, row, jnp.where(last, row - 3 * quarter, row - quarter))
-    zn = jnp.where(first | last, 4, 8)
+    second, last = row >= 2 * quarter, row >= 3 * quarter
+    inside = jnp.where(last, row - 3 * quarter, jnp.where(second, row - 2 * quarter, row))
+    zn = jnp.where(second, 4, 8)
     source = inside // (zn * CAPACITY)
     zi = (inside // CAPACITY) % zn
-    turn = jnp.where(first, 0, jnp.where(last, 2, jnp.where(zi < 4, 3, 1)))
+    turn = jnp.where(last, 2, jnp.where(second, 0, jnp.where(zi < 4, 3, 1)))
     zed = 4 * (zi % 4) + (z + turn) % 4
     home = ((zed // 8) * 64 + source * 8 + zed % 8) * CAPACITY + inside % CAPACITY
     return (home == place).astype(BF)
 
 
-def rows_kernel(zs_ref, a_ref, b_ref, c_ref, w_ref, p_ref, *refs):
+def rows_kernel(zs_ref, b_ref, a_ref, c_ref, w_ref, p_ref, *refs):
     d_refs, s_ref, (gu, dn, rows, d_all, sems) = refs[:4], refs[4], refs[5:]
     hid = dn.shape[1]
     count, width = rows.shape
@@ -155,8 +155,8 @@
     me = zs_ref[2]
     places = [(me + offset) % 4 for offset in (0, 3, 1, 2)]
     pairs = [
-        (a_ref, rows.at[pl.ds(0, quarter)]),
-        (b_ref, rows.at[pl.ds(quarter, 2 * quarter)]),
+        (b_ref, rows.at[pl.ds(0, 2 * quarter)]),
+        (a_ref, rows.at[pl.ds(2 * quarter, quarter)]),
         (c_ref, rows.at[pl.ds(3 * quarter, quarter)]),
     ]
     for q, place in enumerate(places):
@@ -226,10 +226,10 @@
     )(zs, *chunks, weights)
 
 
-def down_kernel(s_ref, a_ref, b_ref, c_ref, own_ref, go_ref, come_ref, right_ref, left_ref, rows):
+def down_kernel(s_ref, b_ref, a_ref, c_ref, own_ref, go_ref, come_ref, right_ref, left_ref, rows):
     quarter = a_ref.shape[0]
-    rows[0:quarter, :] = a_ref[...]
-    rows[quarter : 3 * quarter, :] = b_ref[...]
+    rows[0 : 2 * quarter, :] = b_ref[...]
+    rows[2 * quarter : 3 * quarter, :] = a_ref[...]
     rows[3 * quarter :, :] = c_ref[...]
     grads = rows[...]
     half = right_ref.shape[0]
@@ -271,18 +271,27 @@
 
 
 def weights_kernel(zs_ref, *refs):
-    d_refs, x_refs, (gate_ref, up_ref) = refs[:4], refs[4:8], refs[8:]
+    d_refs, b_refs, ac_refs, (gate_ref, up_ref, two) = refs[:4], refs[4:9], refs[9:13], refs[13:]
     hid = gate_ref.shape[0]
-    total = sum(dot(d[...], x[0], 1, 0) for d, x in zip(d_refs, x_refs)).astype(BF)
+    half, quarter = two.shape[0], two.shape[0] // 2
+    two[:quarter, :] = b_refs[3][...]
+    two[quarter:, :] = b_refs[4][...]
+    total = dot(d_refs[3][:, :half], two[...], 1, 0)
+    for d, x in zip(d_refs[:3], b_refs[:3]):
+        total = total + dot(d[:, :half], x[...], 1, 0)
+    for d, x in zip(d_refs, ac_refs):
+        total = total + dot(d[:, half:], x[0], 1, 0)
+    total = total.astype(BF)
     gate_ref[...] = total[:hid]
     up_ref[...] = total[hid:]
 
 
-def weights_call(zs, ds, xs):
+def weights_call(zs, ds, x_b, x_ac):
     tile = 512
-    n, count, features = xs.shape
+    n, count, features = x_ac.shape
     hid = ds[0].shape[0] // 2
     whole = [pl.BlockSpec(d.shape, lambda j, zs: (0, 0)) for d in ds]
+    near = [pl.BlockSpec((x.shape[0], tile), lambda j, zs: (0, j)) for x in x_b]
     tiled = [
         pl.BlockSpec((1, count, tile), lambda j, zs, at=at: ((zs[2] + at) % 4, 0, j))
         for at in (0, 3, 1, 2)
@@ -292,18 +301,19 @@
         grid_spec=pltpu.PrefetchScalarGridSpec(
             num_scalar_prefetch=1,
             grid=(features // tile,),
-            in_specs=whole + tiled,
+            in_specs=whole + near + tiled,
             out_specs=[pl.BlockSpec((hid, tile), lambda j, zs: (0, j))] * 2,
+            scratch_shapes=[pltpu.VMEM((count, tile), BF)],
         ),
         out_shape=[jax.ShapeDtypeStruct((hid, features), BF)] * 2,
         compiler_params=pltpu.CompilerParams(vmem_limit_bytes=24 * MIB),
         cost_estimate=pl.CostEstimate(
-            flops=4 * n * count * features * hid,
-            bytes_accessed=2 * features * (n * count + 2 * hid),
+            flops=8 * n * count * features * hid,
+            bytes_accessed=2 * features * (2 * n * count + 2 * hid),
             transcendentals=0,
         ),
         name="weight_grads",
-    )(zs, *ds, *[xs] * n)
+    )(zs, *ds, *x_b, *[x_ac] * n)
 
 
 def home_kernel(code_ref, home_ref, grad_ref, score_ref):
@@ -353,28 +363,32 @@
         ).reshape(rows, width)
 
     rows_a = exchange(pack_call(zs, [chunk], step))
+    packed_b = pack_call(zs, [left, right], step)
     rest_a = shift(right[: 2 * step], -1, Z, nz)
     rest_b = shift(left[2 * step :], 1, Z, nz)
-    packed_b = pack_call(zs, [left, right], step)
     rest_a, rest_b, _ = lax.optimization_barrier((rest_a, rest_b, packed_b))
     packed_b, rows_a = lax.optimization_barrier((packed_b, rows_a))
     rows_b = exchange(packed_b)
     packed_c = pack_call(zs, [rest_a, rest_b], step)
     packed_c, rows_b = lax.optimization_barrier((packed_c, rows_b))
+    x_b = rows_b[:, :features]
+    mid = x_b.shape[0] // 2
+    x_left, x_right = shift(x_b, 1, "x", n), shift(x_b, -1, "x", n)
     rows_c = exchange(packed_c)
-
-    chunks = [rows_a, rows_b, rows_c]
-    x = lax.all_gather(jnp.concatenate([c[:, :features] for c in chunks], axis=0), "x", axis=0)
-
+    x_ac = jnp.concatenate([rows_a[:, :features], rows_c[:, :features]], axis=0)
+    x_ac, rows_c, x_left, x_right = lax.optimization_barrier((x_ac, rows_c, x_left, x_right))
+    x_ac = lax.all_gather(x_ac, "x", axis=0)
+    x_far = [shift(x_right[:mid], -1, "x", n), shift(x_left[mid:], 1, "x", n)]
+
+    chunks = [rows_b, rows_a, rows_c]
     back, d_own, d_left, d_right, d_two, scaled = rows_call(zs, chunks, weights)
     home = lax.all_to_all(
         back.reshape(-1, CAPACITY, back.shape[1]), PLACE, split_axis=0, concat_axis=0, tiled=True
     ).reshape(back.shape)
     ds = [d_own, shift(d_right, 1, "x", n), shift(d_left, -1, "x", n), shift(d_two, 2, "x", n)]
-    grad_gate, grad_up = weights_call(zs, ds, x)
-
     p_own, p_go, p_come, p_right, p_left = down_call(scaled, chunks, features)
     from_left, from_right = shift(p_go, 1, "x", n), shift(p_come, -1, "x", n)
+    from_left, from_right, *ds = lax.optimization_barrier((from_left, from_right, *ds))
     p_right = (p_right.astype(F32) + from_left[:half].astype(F32)).astype(BF)
     p_left = (p_left.astype(F32) + from_right[half:].astype(F32)).astype(BF)
     left_top, right_low = shift(p_right, 1, "x", n), shift(p_left, -1, "x", n)
@@ -385,6 +399,8 @@
         ],
         axis=0,
     ).astype(BF)
+
+    grad_gate, grad_up = weights_call(zs, ds, [x_b, x_left, x_right, *x_far], x_ac)
 
     token_grad, slot_score = home_call(code, home, features)
     return (token_grad, slot_score.T, grad_gate[None], grad_up[None], grad_down[None])

time: 237 us -> 248 us (1.046)
  starting transfers between devices: 65.5 us -> 76 us
  waiting for transfers between devices: 70.2 us -> 63.2 us
  local copies, waits for them, and re-layouts: 11.4 us -> 16.2 us
    ppermute x11 -> x15, starting transfers between devices: 35.4 us -> 45.6 us  [shift(): return lax.ppermute(block, axes, [(i, (i + step) % n) for i in range(n)])]
    all_to_all x3, waiting for transfers between devices: 16.2 us -> 8.47 us  [exchange(): lax.all_to_all(packed.reshape(8, rows // 8, width), YC, split_axis=0, con...]
    ppermute x11 -> x15, waiting for transfers between devices: 49.9 us -> 54 us  [shift(): return lax.ppermute(block, axes, [(i, (i + step) % n) for i in range(n)])]
    all_gather x1, waiting for transfers between devices: 4.1 us -> 0.01 us  [local(): weights = lax.all_gather(joined, 'x', axis=0)]
    unnamed x38 -> x56, local copies, waits for them, and re-layouts: 6.57 us -> 9.45 us
  transfers between devices with their start and end apart: 17 -> 21, of which waited for: 7 -> 10; matrix products, arithmetic and copies ran while one was open for 3% -> 3% of each run, Pallas kernels for 12% -> 7%
where the time goes in v6:
time: 248 us; the launch traced here: 247 us
  starting transfers between devices  76 us (31%)
  waiting for transfers between devices  63.2 us (25%)
  blocking collectives  35.2 us (14%)
  Pallas kernels  32.9 us (13%)
  local copies, waits for them, and re-layouts  16.2 us (7%)
  between operations  14.5 us (6%)
  other arithmetic  9.12 us (4%)
    ppermute x15, waiting for transfers between devices, shift(): return lax.ppermute(block, axes, [(i, (i + step) % n) for i in range(n)])  54 us
    ppermute x15, starting transfers between devices, shift(): return lax.ppermute(block, axes, [(i, (i + step) % n) for i in range(n)])  45.6 us
    all_gather x1, blocking collectives, local(): chunk = lax.all_gather(own, FAR, axis=0, tiled=True)  35.2 us
    all_to_all x1, starting transfers between devices, local(): lax.all_to_all(back.reshape(-1, CAPACITY, back.shape[1]), PLACE, split_ax...  17.8 us
    all_to_all x3, starting transfers between devices, exchange(): lax.all_to_all(packed.reshape(8, rows // 8, width), YC, split_axis=0, con...  12.5 us
    pallas_call x1, Pallas kernels, rows_call(): pl.pallas_call(rows_kernel, out_shape=[jax.ShapeDtypeStruct((count, featu...  12.1 us
    unnamed x56, local copies, waits for them, and re-layouts  9.45 us
    all_to_all x3, waiting for transfers between devices, exchange(): lax.all_to_all(packed.reshape(8, rows // 8, width), YC, split_axis=0, con...  8.47 us
  transfers between devices with their start and end apart: 21, of which 10 were waited for; matrix products, arithmetic and copies ran while one was open for 3% of the time, Pallas kernels for 7%

profile of v6, /device:TPU:6, one launch (start us, length us, event | category | flops | bytes accessed | tf_op | source)
XLA Modules:
  0.0 247.1 jit_solution(10289337715442674248)
XLA Ops:
  7.2 3.3 %pad_maximum_fusion = bf16[576,2048]{1,0:T(8,128)(2,1)} fusion(bf16[192,2048]{1,0:T(8,128)(2,1)} %bitcast.40, bf16[192,2048]{1,0:T(8,128)(2,1)} %bitcast.41, bf16[192,2048]{1,0:T(8,128)(2,1)} %bitcast.42), kind=kLoop, calls=%fused_computation | loop fusion | flops 7077888 | bytes 4718592 | tf_op jit(solution)/shard_map/concatenate | solution.py:352
  12.5 35.2 %all_gather.15.refs_1_ = bf16[64,4224]{1,0:T(8,128)(2,1)S(1)} all-gather(bf16[16,4224]{1,0:T(8,128)(2,1)} %get-tuple-element.39), channel_id=1, replica_groups=mesh['zh'=2,'y'=4,'c'=2,'zq'=2,'zr'=4,'x'=4] {'zh','zq'}, dimensions={0}, use_global_device_ids=true | all-gather | bytes 675840 | tf_op jit(solution)/shard_map/all_gather | solution.py:356
  49.6 3.9 %collective-permute-start.2 = (bf16[64,4224]{1,0:T(8,128)(2,1)S(1)}, bf16[64,4224]{1,0:T(8,128)(2,1)S(1)}, u32[]{:S(2)}, u32[]{:S(2)}) collective-permute-start(bf16[64,4224]{1,0:T(8,128)(2,1)S(1)} %all_gather.15.refs_1_), channel_id=1, source_target_pairs={{0,4},{4,8},{8,12},{12,16},{16,20},{20,24},{24,28},{28,256},{256,2... | collective-permute-start | bytes 1622024 | tf_op jit(solution)/shard_map/ppermute | solution.py:28
  56.5 4.5 %all-to-all-start = ((bf16[8,8,4224]{2,1,0:T(8,128)(2,1)}), bf16[8,8,4224]{2,1,0:T(8,128)(2,1)S(1)}, u32[]{:S(2)}, u32[]{:S(2)}) async-start(bf16[8,8,4224]{2,1,0:T(8,128)(2,1)} %bitcast.39), calls=%async_computation | async-start | bytes 1081344 | tf_op jit(solution)/shard_map/all_to_all | solution.py:361
  64.3 3.2 %pack.3 = bf16[128,4224]{1,0:T(8,128)(2,1)} custom-call(s32[3]{0:T(128)} %pad_add_fusion.refs_0_.zs_ref, bf16[64,4224]{1,0:T(8,128)(2,1)} %copy-done.17, bf16[64,4224]{1,0:T(8,128)(2,1)} %copy-done.19), custom_call_target="tpu_custom_call" | custom-call | tf_op jit(solution)/shard_map/pack/pallas_call | solution.py:126
  67.6 3.9 %all-to-all-done = bf16[8,8,4224]{2,1,0:T(8,128)(2,1)S(1)} async-done(((bf16[8,8,4224]{2,1,0:T(8,128)(2,1)}), bf16[8,8,4224]{2,1,0:T(8,128)(2,1)S(1)}, u32[]{:S(2)}, u32[]{:S(2)}) %all-to-all-start) | async-done | bytes 540704 | tf_op jit(solution)/shard_map/all_to_all | solution.py:361
  71.5 3.6 %all-to-all-start.1 = ((bf16[8,16,4224]{2,1,0:T(8,128)(2,1)}), bf16[8,16,4224]{2,1,0:T(8,128)(2,1)S(1)}, u32[]{:S(2)}, u32[]{:S(2)}) async-start(bf16[8,16,4224]{2,1,0:T(8,128)(2,1)} %bitcast.37), calls=%async_computation.1 | async-start | bytes 2162688 | tf_op jit(solution)/shard_map/all_to_all | solution.py:361
  75.1 3.2 %collective-permute-start.1 = (bf16[32,4224]{1,0:T(8,128)(2,1)S(1)}, bf16[32,4224]{1,0:T(8,128)(2,1)S(1)}, u32[]{:S(2)}, u32[]{:S(2)}) collective-permute-start(bf16[32,4224]{1,0:T(8,128)(2,1)S(1)} %slice.52), channel_id=1, source_target_pairs={{0,284},{4,0},{8,4},{12,8},{16,12},{20,16},{24,20},{28,24},{256,28... | collective-permute-start | bytes 811016 | tf_op jit(solution)/shard_map/ppermute | solution.py:28
  81.0 4.7 %collective-permute-done.1.refs_1_ = bf16[32,4224]{1,0:T(8,128)(2,1)S(1)} collective-permute-done((bf16[32,4224]{1,0:T(8,128)(2,1)S(1)}, bf16[32,4224]{1,0:T(8,128)(2,1)S(1)}, u32[]{:S(2)}, u32[]{:S(2)}) %collective-permute-start.1) | collective-permute-done | bytes 270368 | tf_op jit(solution)/shard_map/ppermute | solution.py:28
  85.7 4.1 %collective-permute-done.3.refs_2_ = bf16[32,4224]{1,0:T(8,128)(2,1)S(1)} collective-permute-done((bf16[32,4224]{1,0:T(8,128)(2,1)S(1)}, bf16[32,4224]{1,0:T(8,128)(2,1)S(1)}, u32[]{:S(2)}, u32[]{:S(2)}) %collective-permute-start.3) | collective-permute-done | bytes 270368 | tf_op jit(solution)/shard_map/ppermute | solution.py:28
  93.0 4.5 %all-to-all-start.2 = ((bf16[8,8,4224]{2,1,0:T(8,128)(2,1)}), bf16[8,8,4224]{2,1,0:T(8,128)(2,1)S(1)}, u32[]{:S(2)}, u32[]{:S(2)}) async-start(bf16[8,8,4224]{2,1,0:T(8,128)(2,1)} %bitcast.38), calls=%async_computation.2 | async-start | bytes 1081344 | tf_op jit(solution)/shard_map/all_to_all | solution.py:361
  99.9 3.5 %collective-permute-start.5 = (bf16[128,2048]{1,0:T(8,128)(2,1)S(1)}, bf16[128,2048]{1,0:T(8,128)(2,1)}, u32[]{:S(2)}, u32[]{:S(2)}) collective-permute-start(bf16[128,2048]{1,0:T(8,128)(2,1)S(1)} %slice.43.refs_4_), channel_id=1, source_target_pairs={{0,3},{1,0},{2,1},{3,2},{4,7},{5,4},{6,5},{7,6},{8,11},{9,8},{10,9... | collective-permute-start | bytes 1572872 | tf_op jit(solution)/shard_map/ppermute | solution.py:28
  103.4 4.6 %all-to-all-done.2 = bf16[8,8,4224]{2,1,0:T(8,128)(2,1)S(1)} async-done(((bf16[8,8,4224]{2,1,0:T(8,128)(2,1)}), bf16[8,8,4224]{2,1,0:T(8,128)(2,1)S(1)}, u32[]{:S(2)}, u32[]{:S(2)}) %all-to-all-start.2) | async-done | bytes 540704 | tf_op jit(solution)/shard_map/all_to_all | solution.py:361
  109.0 14.6 %collective-permute-done.4.refs_5_ = bf16[128,2048]{1,0:T(8,128)(2,1)S(1)} collective-permute-done((bf16[128,2048]{1,0:T(8,128)(2,1)S(1)}, bf16[128,2048]{1,0:T(8,128)(2,1)S(1)}, u32[]{:S(2)}, u32[]{:S(2)}) %collective-permute-start.4) | collective-permute-done | bytes 524320 | tf_op jit(solution)/shard_map/ppermute | solution.py:28
  124.6 12.1 %rows.1 = (bf16[256,2176]{1,0:T(8,128)(2,1)}, bf16[384,256]{1,0:T(8,128)(2,1)}, bf16[384,256]{1,0:T(8,128)(2,1)}, bf16[384,256]{1,0:T(8,128)(2,1)}, bf16[384,256...) custom-call(s32[3]{0:T(128)} %pad_add_fusion.refs_0_.zs_ref, bf16[128,4224]{1,0:T(8,128)(2,1)} %bitcast.29, ...), custom_call_target="tpu_custom_call" | custom-call | flops 4026531840 | bytes 12582912 | tf_op jit(solution)/shard_map/rows/pallas_call | solution.py:203
  139.1 17.8 %all-to-all-start.3 = ((bf16[128,2,2176]{2,1,0:T(2,128)(2,1)}), bf16[128,2,2176]{2,1,0:T(2,128)(2,1)}, u32[]{:S(2)}, u32[]{:S(2)}) async-start(bf16[128,2,2176]{2,1,0:T(2,128)(2,1)} %reshape.71), calls=%async_computation.3 | async-start | bytes 2228224 | tf_op jit(solution)/shard_map/all_to_all | solution.py:385
  163.1 3.5 %collective-permute-start.6 = (bf16[192,2048]{1,0:T(8,128)(2,1)S(1)}, bf16[192,2048]{1,0:T(8,128)(2,1)S(1)}, u32[]{:S(2)}, u32[]{:S(2)}) collective-permute-start(bf16[192,2048]{1,0:T(8,128)(2,1)S(1)} %get-tuple-element.51), channel_id=1, source_target_pairs={{0,1},{1,2},{2,3},{3,0},{4,5},{5,6},{6,7},{7,4},{8,9},{9,10},{10,1... | collective-permute-start | bytes 2359304 | tf_op jit(solution)/shard_map/ppermute | solution.py:28
  169.1 4.6 %collective-permute-start.8 = (bf16[384,256]{1,0:T(8,128)(2,1)}, bf16[384,256]{1,0:T(8,128)(2,1)S(1)}, u32[]{:S(2)}, u32[]{:S(2)}) collective-permute-start(bf16[384,256]{1,0:T(8,128)(2,1)} %get-tuple-element.54), channel_id=1, source_target_pairs={{0,1},{1,2},{2,3},{3,0},{4,5},{5,6},{6,7},{7,4},{8,9},{9,10},{10,1... | collective-permute-start | bytes 589832 | tf_op jit(solution)/shard_map/ppermute | solution.py:28
  175.6 3.6 %collective-permute-start.10 = (bf16[384,256]{1,0:T(8,128)(2,1)}, bf16[384,256]{1,0:T(8,128)(2,1)S(1)}, u32[]{:S(2)}, u32[]{:S(2)}) collective-permute-start(bf16[384,256]{1,0:T(8,128)(2,1)} %get-tuple-element.56), channel_id=1, source_target_pairs={{0,2},{1,3},{2,0},{3,1},{4,6},{5,7},{6,4},{7,5},{8,10},{9,11},{10,... | collective-permute-start | bytes 589832 | tf_op jit(solution)/shard_map/ppermute | solution.py:28
  181.2 17.6 %collective-permute-done.8.refs_1_ = bf16[384,256]{1,0:T(8,128)(2,1)S(1)} collective-permute-done((bf16[384,256]{1,0:T(8,128)(2,1)}, bf16[384,256]{1,0:T(8,128)(2,1)S(1)}, u32[]{:S(2)}, u32[]{:S(2)}) %collective-permute-start.8) | collective-permute-done | bytes 196640 | tf_op jit(solution)/shard_map/ppermute | solution.py:28
  198.8 4.2 %collective-permute-start.11 = (bf16[64,2048]{1,0:T(8,128)(2,1)S(1)}, bf16[64,2048]{1,0:T(8,128)(2,1)S(1)}, u32[]{:S(2)}, u32[]{:S(2)}) collective-permute-start(bf16[64,2048]{1,0:T(8,128)(2,1)S(1)} %slice.44), channel_id=1, source_target_pairs={{0,3},{1,0},{2,1},{3,2},{4,7},{5,4},{6,5},{7,6},{8,11},{9,8},{10,9... | collective-permute-start | bytes 786440 | tf_op jit(solution)/shard_map/ppermute | solution.py:28
  203.0 8.0 %collective-permute-done.9.refs_2_ = bf16[384,256]{1,0:T(8,128)(2,1)S(1)} collective-permute-done((bf16[384,256]{1,0:T(8,128)(2,1)S(1)}, bf16[384,256]{1,0:T(8,128)(2,1)S(1)}, u32[]{:S(2)}, u32[]{:S(2)}) %collective-permute-start.9) | collective-permute-done | bytes 196640 | tf_op jit(solution)/shard_map/ppermute | solution.py:28
  219.5 3.9 %collective-permute-start.14 = (bf16[96,2048]{1,0:T(8,128)(2,1)}, bf16[96,2048]{1,0:T(8,128)(2,1)}, u32[]{:S(2)}, u32[]{:S(2)}) collective-permute-start(bf16[96,2048]{1,0:T(8,128)(2,1)} %add_convert_fusion.1), channel_id=1, source_target_pairs={{0,3},{1,0},{2,1},{3,2},{4,7},{5,4},{6,5},{7,6},{8,11},{9,8},{10,9... | collective-permute-start | bytes 1179656 | tf_op jit(solution)/shard_map/ppermute | solution.py:28
  227.0 6.3 %weight_grads.1 = (bf16[192,2048]{1,0:T(8,128)(2,1)}, bf16[192,2048]{1,0:T(8,128)(2,1)}) custom-call(s32[3]{0:T(128)S(1)} %copy-done.14, bf16[384,256]{1,0:T(8,128)(2,1)S(1)} %copy-done.9, bf16[384,256]{1,0:T(8,128)(2,1)S(1)} %collective-permute-done.8.refs_1_, bf16[384,256]{1,0:T(8,128)(2,1)S(1)} %copy-done.11, bf16[384,256]{1,0:T(8,128)(2,1)S(1)} %copy-done.13, ...), custom_call_target="tpu_custom_call" | custom-call | flops 1610612736 | bytes 5767168 | tf_op jit(solution)/shard_map/weight_grads/pallas_call | solution.py:299
  (101 shorter events, 54.2 us)
Async XLA Ops:
  7.2 117.4 %all-gather.5.cloned.1.call-start = ((), (), s32[]{:S(2)}) async-start(), calls=%async_computation.4 | async-start | bytes 11796480 | tf_op jit(solution)/shard_map/all_gather | solution.py:353
  47.7 13.3 %collective-permute-start = (bf16[64,4224]{1,0:T(8,128)(2,1)S(1)}, bf16[64,4224]{1,0:T(8,128)(2,1)S(1)}, u32[]{:S(2)}, u32[]{:S(2)}) collective-permute-start(bf16[64,4224]{1,0:T(8,128)(2,1)S(1)} %all_gather.15.refs_1_), channel_id=1, source_target_pairs={{0,284},{4,0},{8,4},{12,8},{16,12},{20,16},{24,20},{28,24},{256,28... | collective-permute-start | bytes 1622024 | tf_op jit(solution)/shard_map/ppermute | solution.py:28
  49.6 13.9 %collective-permute-start.2 = (bf16[64,4224]{1,0:T(8,128)(2,1)S(1)}, bf16[64,4224]{1,0:T(8,128)(2,1)S(1)}, u32[]{:S(2)}, u32[]{:S(2)}) collective-permute-start(bf16[64,4224]{1,0:T(8,128)(2,1)S(1)} %all_gather.15.refs_1_), channel_id=1, source_target_pairs={{0,4},{4,8},{8,12},{12,16},{16,20},{20,24},{24,28},{28,256},{256,2... | collective-permute-start | bytes 1622024 | tf_op jit(solution)/shard_map/ppermute | solution.py:28
  56.5 15.0 %all-to-all-start = ((bf16[8,8,4224]{2,1,0:T(8,128)(2,1)}), bf16[8,8,4224]{2,1,0:T(8,128)(2,1)S(1)}, u32[]{:S(2)}, u32[]{:S(2)}) async-start(bf16[8,8,4224]{2,1,0:T(8,128)(2,1)} %bitcast.39), calls=%async_computation | async-start | bytes 1081344 | tf_op jit(solution)/shard_map/all_to_all | solution.py:361
  71.5 21.6 %all-to-all-start.1 = ((bf16[8,16,4224]{2,1,0:T(8,128)(2,1)}), bf16[8,16,4224]{2,1,0:T(8,128)(2,1)S(1)}, u32[]{:S(2)}, u32[]{:S(2)}) async-start(bf16[8,16,4224]{2,1,0:T(8,128)(2,1)} %bitcast.37), calls=%async_computation.1 | async-start | bytes 2162688 | tf_op jit(solution)/shard_map/all_to_all | solution.py:361
  75.1 10.7 %collective-permute-start.1 = (bf16[32,4224]{1,0:T(8,128)(2,1)S(1)}, bf16[32,4224]{1,0:T(8,128)(2,1)S(1)}, u32[]{:S(2)}, u32[]{:S(2)}) collective-permute-start(bf16[32,4224]{1,0:T(8,128)(2,1)S(1)} %slice.52), channel_id=1, source_target_pairs={{0,284},{4,0},{8,4},{12,8},{16,12},{20,16},{24,20},{28,24},{256,28... | collective-permute-start | bytes 811016 | tf_op jit(solution)/shard_map/ppermute | solution.py:28
  78.3 11.6 %collective-permute-start.3 = (bf16[32,4224]{1,0:T(8,128)(2,1)S(1)}, bf16[32,4224]{1,0:T(8,128)(2,1)S(1)}, u32[]{:S(2)}, u32[]{:S(2)}) collective-permute-start(bf16[32,4224]{1,0:T(8,128)(2,1)S(1)} %slice.53), channel_id=1, source_target_pairs={{0,4},{4,8},{8,12},{12,16},{16,20},{20,24},{24,28},{28,256},{256,2... | collective-permute-start | bytes 811016 | tf_op jit(solution)/shard_map/ppermute | solution.py:28
  93.0 15.0 %all-to-all-start.2 = ((bf16[8,8,4224]{2,1,0:T(8,128)(2,1)}), bf16[8,8,4224]{2,1,0:T(8,128)(2,1)S(1)}, u32[]{:S(2)}, u32[]{:S(2)}) async-start(bf16[8,8,4224]{2,1,0:T(8,128)(2,1)} %bitcast.38), calls=%async_computation.2 | async-start | bytes 1081344 | tf_op jit(solution)/shard_map/all_to_all | solution.py:361
  97.5 26.1 %collective-permute-start.4 = (bf16[128,2048]{1,0:T(8,128)(2,1)S(1)}, bf16[128,2048]{1,0:T(8,128)(2,1)S(1)}, u32[]{:S(2)}, u32[]{:S(2)}) collective-permute-start(bf16[128,2048]{1,0:T(8,128)(2,1)S(1)} %slice.43.refs_4_), channel_id=1, source_target_pairs={{0,1},{1,2},{2,3},{3,0},{4,5},{5,6},{6,7},{7,4},{8,9},{9,10},{10,1... | collective-permute-start | bytes 1572872 | tf_op jit(solution)/shard_map/ppermute | solution.py:28
  99.9 24.6 %collective-permute-start.5 = (bf16[128,2048]{1,0:T(8,128)(2,1)S(1)}, bf16[128,2048]{1,0:T(8,128)(2,1)}, u32[]{:S(2)}, u32[]{:S(2)}) collective-permute-start(bf16[128,2048]{1,0:T(8,128)(2,1)S(1)} %slice.43.refs_4_), channel_id=1, source_target_pairs={{0,3},{1,0},{2,1},{3,2},{4,7},{5,4},{6,5},{7,6},{8,11},{9,8},{10,9... | collective-permute-start | bytes 1572872 | tf_op jit(solution)/shard_map/ppermute | solution.py:28
  139.1 96.6 %all-to-all-start.3 = ((bf16[128,2,2176]{2,1,0:T(2,128)(2,1)}), bf16[128,2,2176]{2,1,0:T(2,128)(2,1)}, u32[]{:S(2)}, u32[]{:S(2)}) async-start(bf16[128,2,2176]{2,1,0:T(2,128)(2,1)} %reshape.71), calls=%async_computation.3 | async-start | bytes 2228224 | tf_op jit(solution)/shard_map/all_to_all | solution.py:385
  156.9 66.5 %all-gather.7.cloned.1.call-start = ((), (), s32[]{:S(2)}) async-start(), calls=%async_computation.5 | async-start | bytes 2621440 | tf_op jit(solution)/shard_map/all_gather | solution.py:380
  163.1 60.4 %copy-start.8 = (bf16[128,2048]{1,0:T(8,128)(2,1)S(1)}, bf16[128,2048]{1,0:T(8,128)(2,1)}, u32[]{:S(2)}) copy-start(bf16[128,2048]{1,0:T(8,128)(2,1)} %copy-done.7) | copy-start | bytes 1572868
  163.1 60.4 %copy-start.9 = (bf16[384,256]{1,0:T(8,128)(2,1)S(1)}, bf16[384,256]{1,0:T(8,128)(2,1)}, u32[]{:S(2)}) copy-start(bf16[384,256]{1,0:T(8,128)(2,1)} %get-tuple-element.57.refs_0_) | copy-start | bytes 589828
  163.1 60.4 %copy-start.14 = (s32[3]{0:T(128)S(1)}, s32[3]{0:T(128)}, u32[]{:S(2)}) copy-start(s32[3]{0:T(128)} %pad_add_fusion.refs_0_.zs_ref) | copy-start | bytes 40
  163.1 52.6 %collective-permute-start.6 = (bf16[192,2048]{1,0:T(8,128)(2,1)S(1)}, bf16[192,2048]{1,0:T(8,128)(2,1)S(1)}, u32[]{:S(2)}, u32[]{:S(2)}) collective-permute-start(bf16[192,2048]{1,0:T(8,128)(2,1)S(1)} %get-tuple-element.51), channel_id=1, source_target_pairs={{0,1},{1,2},{2,3},{3,0},{4,5},{5,6},{6,7},{7,4},{8,9},{9,10},{10,1... | collective-permute-start | bytes 2359304 | tf_op jit(solution)/shard_map/ppermute | solution.py:28
  166.6 49.1 %collective-permute-start.7 = (bf16[192,2048]{1,0:T(8,128)(2,1)S(1)}, bf16[192,2048]{1,0:T(8,128)(2,1)S(1)}, u32[]{:S(2)}, u32[]{:S(2)}) collective-permute-start(bf16[192,2048]{1,0:T(8,128)(2,1)S(1)} %get-tuple-element.52), channel_id=1, source_target_pairs={{0,3},{1,0},{2,1},{3,2},{4,7},{5,4},{6,5},{7,6},{8,11},{9,8},{10,9... | collective-permute-start | bytes 2359304 | tf_op jit(solution)/shard_map/ppermute | solution.py:28
  169.1 29.7 %collective-permute-start.8 = (bf16[384,256]{1,0:T(8,128)(2,1)}, bf16[384,256]{1,0:T(8,128)(2,1)S(1)}, u32[]{:S(2)}, u32[]{:S(2)}) collective-permute-start(bf16[384,256]{1,0:T(8,128)(2,1)} %get-tuple-element.54), channel_id=1, source_target_pairs={{0,1},{1,2},{2,3},{3,0},{4,5},{5,6},{6,7},{7,4},{8,9},{9,10},{10,1... | collective-permute-start | bytes 589832 | tf_op jit(solution)/shard_map/ppermute | solution.py:28
  173.7 37.3 %collective-permute-start.9 = (bf16[384,256]{1,0:T(8,128)(2,1)S(1)}, bf16[384,256]{1,0:T(8,128)(2,1)S(1)}, u32[]{:S(2)}, u32[]{:S(2)}) collective-permute-start(bf16[384,256]{1,0:T(8,128)(2,1)S(1)} %copy-done.27), channel_id=1, source_target_pairs={{0,3},{1,0},{2,1},{3,2},{4,7},{5,4},{6,5},{7,6},{8,11},{9,8},{10,9... | collective-permute-start | bytes 589832 | tf_op jit(solution)/shard_map/ppermute | solution.py:28
  175.6 39.4 %collective-permute-start.10 = (bf16[384,256]{1,0:T(8,128)(2,1)}, bf16[384,256]{1,0:T(8,128)(2,1)S(1)}, u32[]{:S(2)}, u32[]{:S(2)}) collective-permute-start(bf16[384,256]{1,0:T(8,128)(2,1)} %get-tuple-element.56), channel_id=1, source_target_pairs={{0,2},{1,3},{2,0},{3,1},{4,6},{5,7},{6,4},{7,5},{8,10},{9,11},{10,... | collective-permute-start | bytes 589832 | tf_op jit(solution)/shard_map/ppermute | solution.py:28
  198.8 24.6 %collective-permute-start.11 = (bf16[64,2048]{1,0:T(8,128)(2,1)S(1)}, bf16[64,2048]{1,0:T(8,128)(2,1)S(1)}, u32[]{:S(2)}, u32[]{:S(2)}) collective-permute-start(bf16[64,2048]{1,0:T(8,128)(2,1)S(1)} %slice.44), channel_id=1, source_target_pairs={{0,3},{1,0},{2,1},{3,2},{4,7},{5,4},{6,5},{7,6},{8,11},{9,8},{10,9... | collective-permute-start | bytes 786440 | tf_op jit(solution)/shard_map/ppermute | solution.py:28
  211.7 11.7 %collective-permute-start.12 = (bf16[64,2048]{1,0:T(8,128)(2,1)S(1)}, bf16[64,2048]{1,0:T(8,128)(2,1)S(1)}, u32[]{:S(2)}, u32[]{:S(2)}) collective-permute-start(bf16[64,2048]{1,0:T(8,128)(2,1)S(1)} %slice.45), channel_id=1, source_target_pairs={{0,1},{1,2},{2,3},{3,0},{4,5},{5,6},{6,7},{7,4},{8,9},{9,10},{10,1... | collective-permute-start | bytes 786440 | tf_op jit(solution)/shard_map/ppermute | solution.py:28
  216.7 16.6 %collective-permute-start.13 = (bf16[96,2048]{1,0:T(8,128)(2,1)}, bf16[96,2048]{1,0:T(8,128)(2,1)}, u32[]{:S(2)}, u32[]{:S(2)}) collective-permute-start(bf16[96,2048]{1,0:T(8,128)(2,1)} %add_convert_fusion.3), channel_id=1, source_target_pairs={{0,1},{1,2},{2,3},{3,0},{4,5},{5,6},{6,7},{7,4},{8,9},{9,10},{10,1... | collective-permute-start | bytes 1179656 | tf_op jit(solution)/shard_map/ppermute | solution.py:28
  219.5 13.8 %collective-permute-start.14 = (bf16[96,2048]{1,0:T(8,128)(2,1)}, bf16[96,2048]{1,0:T(8,128)(2,1)}, u32[]{:S(2)}, u32[]{:S(2)}) collective-permute-start(bf16[96,2048]{1,0:T(8,128)(2,1)} %add_convert_fusion.1), channel_id=1, source_target_pairs={{0,3},{1,0},{2,1},{3,2},{4,7},{5,4},{6,5},{7,6},{8,11},{9,8},{10,9... | collective-permute-start | bytes 1179656 | tf_op jit(solution)/shard_map/ppermute | solution.py:28
  (25 other events, 184.3 us)
Sparse Core Ops, SparseCore 0:
  10.7 111.9 all-gather.4
  159.9 58.9 all-gather.6

commit v7 on v5

--- a/solution.py
+++ b/solution.py
@@ -146,22 +146,25 @@
     return (home == place).astype(BF)
 
 
-def rows_kernel(zs_ref, a_ref, b_ref, c_ref, w_ref, p_ref, *refs):
+def rows_kernel(zs_ref, *refs):
+    (a_ref, b_ref, c_ref, *w_refs), p_ref, refs = refs[:8], refs[8], refs[9:]
     d_refs, s_ref, (gu, dn, rows, d_all, sems) = refs[:4], refs[4], refs[5:]
     hid = dn.shape[1]
     count, width = rows.shape
     features = (width - LANES) // 2
     quarter = count // 4
-    me = zs_ref[2]
-    places = [(me + offset) % 4 for offset in (0, 3, 1, 2)]
     pairs = [
         (a_ref, rows.at[pl.ds(0, quarter)]),
         (b_ref, rows.at[pl.ds(quarter, 2 * quarter)]),
         (c_ref, rows.at[pl.ds(3 * quarter, quarter)]),
     ]
-    for q, place in enumerate(places):
-        pairs.append((w_ref.at[place, pl.ds(0, 2 * hid)], gu.at[pl.ds(q * 2 * hid, 2 * hid)]))
-        pairs.append((w_ref.at[place, pl.ds(2 * hid, hid)], dn.at[q]))
+    for q in range(3):
+        pairs.append((w_refs[q].at[pl.ds(0, 2 * hid)], gu.at[pl.ds(q * 2 * hid, 2 * hid)]))
+        pairs.append((w_refs[q].at[pl.ds(2 * hid, hid)], dn.at[q]))
+    top, first = w_refs[3].shape[0], 6 * hid
+    pairs.append((w_refs[3], gu.at[pl.ds(first, top)]))
+    pairs.append((w_refs[4].at[pl.ds(0, 2 * hid - top)], gu.at[pl.ds(first + top, 2 * hid - top)]))
+    pairs.append((w_refs[4].at[pl.ds(2 * hid - top, hid)], dn.at[3]))
     copies = [pltpu.make_async_copy(s, t, sems.at[i]) for i, (s, t) in enumerate(pairs)]
     for copy in copies:
         copy.start()
@@ -171,8 +174,8 @@
     coef = rows[:, 2 * features :].astype(F32).T[0:1, :]
     score = None
     for q in range(4):
-        copies[3 + 2 * q].wait()
-        copies[4 + 2 * q].wait()
+        for copy in copies[3 + 2 * q : 5 + 2 * q + q // 3]:
+            copy.wait()
         first = q * 2 * hid
         pre = dot(gu[first : first + 2 * hid, :], rows[:, :features], 1, 1)
         back = dot(dn[q], rows[:, features : 2 * features], 1, 1)
@@ -199,7 +202,7 @@
 def rows_call(zs, chunks, weights):
     count = sum(c.shape[0] for c in chunks)
     width = chunks[0].shape[1]
-    n, hid, features = weights.shape[0], weights.shape[1] // 3, weights.shape[2]
+    n, hid, features = 4, weights[0].shape[0] // 3, weights[0].shape[1]
     return pl.pallas_call(
         rows_kernel,
         out_shape=[
@@ -207,14 +210,14 @@
             *[jax.ShapeDtypeStruct((2 * hid, count), BF)] * n,
             jax.ShapeDtypeStruct((n, hid, count), BF),
         ],
-        in_specs=[pl.BlockSpec(memory_space=pltpu.SMEM)] + [pl.BlockSpec(memory_space=pl.ANY)] * 4,
+        in_specs=[pl.BlockSpec(memory_space=pltpu.SMEM)] + [pl.BlockSpec(memory_space=pl.ANY)] * 8,
         out_specs=[vmem()] * (n + 2),
         scratch_shapes=[
             pltpu.VMEM((n * 2 * hid, features), BF),
             pltpu.VMEM((n, hid, features), BF),
             pltpu.VMEM((count, width), BF),
             pltpu.VMEM((n * 2 * hid, count), BF),
-            pltpu.SemaphoreType.DMA((3 + 2 * n,)),
+            pltpu.SemaphoreType.DMA((4 + 2 * n,)),
         ],
         compiler_params=pltpu.CompilerParams(vmem_limit_bytes=56 * MIB),
         cost_estimate=pl.CostEstimate(
@@ -223,7 +226,7 @@
             transcendentals=count * hid * n,
         ),
         name="rows",
-    )(zs, *chunks, weights)
+    )(zs, *chunks, *weights)
 
 
 def down_kernel(s_ref, a_ref, b_ref, c_ref, own_ref, go_ref, come_ref, right_ref, left_ref, rows):
@@ -270,40 +273,42 @@
     )(scaled, *chunks)
 
 
-def weights_kernel(zs_ref, *refs):
-    d_refs, x_refs, (gate_ref, up_ref) = refs[:4], refs[4:8], refs[8:]
+def weights_kernel(*refs):
+    d_refs, x_refs, (gate_ref, up_ref, rows) = refs[:4], refs[4:11], refs[11:]
+    own, left, right, more_left, more_right, last, two = x_refs
     hid = gate_ref.shape[0]
-    total = sum(dot(d[...], x[0], 1, 0) for d, x in zip(d_refs, x_refs)).astype(BF)
+    most, mid = own.shape[0], own.shape[0] // 2
+    for q, (first, end) in enumerate(((own, last), (left, more_left), (right, more_right))):
+        rows[q, :most, :] = first[...]
+        rows[q, most:, :] = end[end.shape[0] - two.shape[0] :, :]
+    rows[3, :mid, :] = more_right[:mid, :]
+    rows[3, mid:most, :] = more_left[:mid, :]
+    rows[3, most:, :] = two[...]
+    total = sum(dot(d[...], rows[q], 1, 0) for q, d in enumerate(d_refs)).astype(BF)
     gate_ref[...] = total[:hid]
     up_ref[...] = total[hid:]
 
 
-def weights_call(zs, ds, xs):
+def weights_call(ds, xs):
     tile = 512
-    n, count, features = xs.shape
-    hid = ds[0].shape[0] // 2
-    whole = [pl.BlockSpec(d.shape, lambda j, zs: (0, 0)) for d in ds]
-    tiled = [
-        pl.BlockSpec((1, count, tile), lambda j, zs, at=at: ((zs[2] + at) % 4, 0, j))
-        for at in (0, 3, 1, 2)
-    ]
+    hid, count, features = ds[0].shape[0] // 2, ds[0].shape[1], xs[0].shape[1]
+    whole = [pl.BlockSpec(d.shape, lambda j: (0, 0)) for d in ds]
+    tiled = [pl.BlockSpec((x.shape[0], tile), lambda j: (0, j)) for x in xs]
     return pl.pallas_call(
         weights_kernel,
-        grid_spec=pltpu.PrefetchScalarGridSpec(
-            num_scalar_prefetch=1,
-            grid=(features // tile,),
-            in_specs=whole + tiled,
-            out_specs=[pl.BlockSpec((hid, tile), lambda j, zs: (0, j))] * 2,
-        ),
+        grid=(features // tile,),
         out_shape=[jax.ShapeDtypeStruct((hid, features), BF)] * 2,
+        in_specs=whole + tiled,
+        out_specs=[pl.BlockSpec((hid, tile), lambda j: (0, j))] * 2,
+        scratch_shapes=[pltpu.VMEM((len(ds), count, tile), BF)],
         compiler_params=pltpu.CompilerParams(vmem_limit_bytes=24 * MIB),
         cost_estimate=pl.CostEstimate(
-            flops=4 * n * count * features * hid,
-            bytes_accessed=2 * features * (n * count + 2 * hid),
+            flops=4 * len(ds) * count * features * hid,
+            bytes_accessed=2 * features * (len(ds) * count + 2 * hid),
             transcendentals=0,
         ),
         name="weight_grads",
-    )(zs, *ds, *[xs] * n)
+    )(*ds, *xs)
 
 
 def home_kernel(code_ref, home_ref, grad_ref, score_ref):
@@ -340,7 +345,8 @@
     half = gate_w.shape[1] // 2
 
     joined = jnp.concatenate([gate_w[0], up_w[0], down_w[0]], axis=0)
-    weights = lax.all_gather(joined, "x", axis=0)
+    part = joined.shape[0] // 2
+    w_left, w_right = shift(joined, 1, "x", n), shift(joined, -1, "x", n)
     own, code = payload_call(tokens, out_grad, expert_ids.T, keep_flags.T, route_weights.T)
 
     chunk = lax.all_gather(own, FAR, axis=0, tiled=True)
@@ -353,9 +359,11 @@
         ).reshape(rows, width)
 
     rows_a = exchange(pack_call(zs, [chunk], step))
+    packed_b = pack_call(zs, [left, right], step)
+    packed_b, w_left, w_right = lax.optimization_barrier((packed_b, w_left, w_right))
+    w_a, w_b = shift(w_right[:part], -1, "x", n), shift(w_left[part:], 1, "x", n)
     rest_a = shift(right[: 2 * step], -1, Z, nz)
     rest_b = shift(left[2 * step :], 1, Z, nz)
-    packed_b = pack_call(zs, [left, right], step)
     rest_a, rest_b, _ = lax.optimization_barrier((rest_a, rest_b, packed_b))
     packed_b, rows_a = lax.optimization_barrier((packed_b, rows_a))
     rows_b = exchange(packed_b)
@@ -364,14 +372,21 @@
     rows_c = exchange(packed_c)
 
     chunks = [rows_a, rows_b, rows_c]
-    x = lax.all_gather(jnp.concatenate([c[:, :features] for c in chunks], axis=0), "x", axis=0)
-
-    back, d_own, d_left, d_right, d_two, scaled = rows_call(zs, chunks, weights)
+    back, d_own, d_left, d_right, d_two, scaled = rows_call(
+        zs, chunks, [joined, w_left, w_right, w_a, w_b]
+    )
+    x_ab = jnp.concatenate([rows_a[:, :features], rows_b[:, :features]], axis=0)
+    x_left, x_right = shift(x_ab, 1, "x", n), shift(x_ab, -1, "x", n)
+    back, x_left, x_right = lax.optimization_barrier((back, x_left, x_right))
     home = lax.all_to_all(
         back.reshape(-1, CAPACITY, back.shape[1]), PLACE, split_axis=0, concat_axis=0, tiled=True
     ).reshape(back.shape)
+    mid = x_ab.shape[0] // 2
+    x_c = rows_c[:, :features]
+    x_two = shift(x_c, 2, "x", n)
+    more_left = shift(jnp.concatenate([x_left[mid:], x_c], axis=0), 1, "x", n)
+    more_right = shift(jnp.concatenate([x_right[:mid], x_c], axis=0), -1, "x", n)
     ds = [d_own, shift(d_right, 1, "x", n), shift(d_left, -1, "x", n), shift(d_two, 2, "x", n)]
-    grad_gate, grad_up = weights_call(zs, ds, x)
 
     p_own, p_go, p_come, p_right, p_left = down_call(scaled, chunks, features)
     from_left, from_right = shift(p_go, 1, "x", n), shift(p_come, -1, "x", n)
@@ -386,6 +401,10 @@
         axis=0,
     ).astype(BF)
 
+    grad_gate, grad_up = weights_call(
+        ds, [x_ab, x_left, x_right, more_left, more_right, x_c, x_two]
+    )
+
     token_grad, slot_score = home_call(code, home, features)
     return (token_grad, slot_score.T, grad_gate[None], grad_up[None], grad_down[None])
 

time: 237 us -> 221 us (0.932)
  starting transfers between devices: 65.5 us -> 95.9 us
  waiting for transfers between devices: 70.2 us -> 42.4 us
  between operations: 14.4 us -> 1.12 us
  blocking collectives: 35.2 us -> 28.5 us
  other arithmetic: 8.53 us -> 4.12 us
  local copies, waits for them, and re-layouts: 11.4 us -> 15 us
    ppermute x11 -> x20, starting transfers between devices: 35.4 us -> 71.9 us  [shift(): return lax.ppermute(block, axes, [(i, (i + step) % n) for i in range(n)])]
    ppermute x11 -> x20, waiting for transfers between devices: 49.9 us -> 31.8 us  [shift(): return lax.ppermute(block, axes, [(i, (i + step) % n) for i in range(n)])]
    all_gather x1, blocking collectives: 35.2 us -> 28.5 us  [local(): chunk = lax.all_gather(own, FAR, axis=0, tiled=True)]
    all_to_all x1, starting transfers between devices: 17.6 us -> 11.5 us  [local(): lax.all_to_all(back.reshape(-1, CAPACITY, back.shape[1]), PLACE, split_ax...]
    slice x3 -> x8, local copies, waits for them, and re-layouts: 0.08 us -> 5.99 us  [the longest x1 2.43 us: local(): w_left[part:]]
    all_to_all x3, waiting for transfers between devices: 16.2 us -> 10.6 us  [exchange(): lax.all_to_all(packed.reshape(8, rows // 8, width), YC, split_axis=0, con...]
    unnamed x38 -> x34, local copies, waits for them, and re-layouts: 6.57 us -> 2.4 us
    all_gather x2 -> x0, waiting for transfers between devices: 4.12 us -> none  [the longest x1 4.1 us: local(): weights = lax.all_gather(joined, 'x', axis=0)]
  transfers between devices with their start and end apart: 17 -> 24, of which waited for: 7 -> 12; matrix products, arithmetic and copies ran while one was open for 3% -> 5% of each run, Pallas kernels for 12% -> 13%
where the time goes in v7:
time: 221 us; the launch traced here: 218 us
  starting transfers between devices  95.9 us (43%)
  waiting for transfers between devices  42.4 us (19%)
  Pallas kernels  31.1 us (14%)
  blocking collectives  28.5 us (13%)
  local copies, waits for them, and re-layouts  15 us (7%)
  other arithmetic  4.12 us (2%)
    ppermute x20, starting transfers between devices, shift(): return lax.ppermute(block, axes, [(i, (i + step) % n) for i in range(n)])  71.9 us
    ppermute x20, waiting for transfers between devices, shift(): return lax.ppermute(block, axes, [(i, (i + step) % n) for i in range(n)])  31.8 us
    all_gather x1, blocking collectives, local(): chunk = lax.all_gather(own, FAR, axis=0, tiled=True)  28.5 us
    all_to_all x3, starting transfers between devices, exchange(): lax.all_to_all(packed.reshape(8, rows // 8, width), YC, split_axis=0, con...  12.5 us
    pallas_call x1, Pallas kernels, rows_call(): pl.pallas_call(rows_kernel, out_shape=[jax.ShapeDtypeStruct((count, featu...  12.1 us
    all_to_all x1, starting transfers between devices, local(): lax.all_to_all(back.reshape(-1, CAPACITY, back.shape[1]), PLACE, split_ax...  11.5 us
    all_to_all x3, waiting for transfers between devices, exchange(): lax.all_to_all(packed.reshape(8, rows // 8, width), YC, split_axis=0, con...  10.6 us
    pallas_call x3, Pallas kernels, pack_call(): pl.pallas_call(body, out_shape=jax.ShapeDtypeStruct((rows, width), BF), i...  7.98 us
  transfers between devices with their start and end apart: 24, of which 12 were waited for; matrix products, arithmetic and copies ran while one was open for 5% of the time, Pallas kernels for 13%

profile of v7, /device:TPU:6, one launch (start us, length us, event | category | flops | bytes accessed | tf_op | source)
XLA Modules:
  0.0 218.2 jit_solution(15974710995610409709)
XLA Ops:
  2.5 7.8 %collective-permute-start.2 = (bf16[576,2048]{1,0:T(8,128)(2,1)S(1)}, bf16[576,2048]{1,0:T(8,128)(2,1)}, u32[]{:S(2)}, u32[]{:S(2)}) collective-permute-start(bf16[576,2048]{1,0:T(8,128)(2,1)S(1)} %pad_maximum_fusion.refs_3_), channel_id=1, source_target_pairs={{0,1},{1,2},{2,3},{3,0},{4,5},{5,6},{6,7},{7,4},{8,9},{9,10},{10,1... | collective-permute-start | bytes 7077896 | tf_op jit(solution)/shard_map/ppermute | solution.py:28
  14.2 28.5 %all_gather.3.refs_1_ = bf16[64,4224]{1,0:T(8,128)(2,1)S(1)} all-gather(bf16[16,4224]{1,0:T(8,128)(2,1)} %get-tuple-element.35), channel_id=1, replica_groups=mesh['zh'=2,'y'=4,'c'=2,'zq'=2,'zr'=4,'x'=4] {'zh','zq'}, dimensions={0}, use_global_device_ids=true | all-gather | bytes 675840 | tf_op jit(solution)/shard_map/all_gather | solution.py:352
  42.7 3.7 %collective-permute-start = (bf16[64,4224]{1,0:T(8,128)(2,1)S(1)}, bf16[64,4224]{1,0:T(8,128)(2,1)}, u32[]{:S(2)}, u32[]{:S(2)}) collective-permute-start(bf16[64,4224]{1,0:T(8,128)(2,1)S(1)} %all_gather.3.refs_1_), channel_id=1, source_target_pairs={{0,4},{4,8},{8,12},{12,16},{16,20},{20,24},{24,28},{28,256},{256,2... | collective-permute-start | bytes 1622024 | tf_op jit(solution)/shard_map/ppermute | solution.py:28
  46.4 3.8 %collective-permute-start.1 = (bf16[64,4224]{1,0:T(8,128)(2,1)S(1)}, bf16[64,4224]{1,0:T(8,128)(2,1)}, u32[]{:S(2)}, u32[]{:S(2)}) collective-permute-start(bf16[64,4224]{1,0:T(8,128)(2,1)S(1)} %all_gather.3.refs_1_), channel_id=1, source_target_pairs={{0,284},{4,0},{8,4},{12,8},{16,12},{20,16},{24,20},{28,24},{256,28... | collective-permute-start | bytes 1622024 | tf_op jit(solution)/shard_map/ppermute | solution.py:28
  53.0 4.5 %all-to-all-start = ((bf16[8,8,4224]{2,1,0:T(8,128)(2,1)}), bf16[8,8,4224]{2,1,0:T(8,128)(2,1)S(1)}, u32[]{:S(2)}, u32[]{:S(2)}) async-start(bf16[8,8,4224]{2,1,0:T(8,128)(2,1)} %bitcast.33), calls=%async_computation | async-start | bytes 1081344 | tf_op jit(solution)/shard_map/all_to_all | solution.py:357
  58.7 3.2 %pack.3 = bf16[128,4224]{1,0:T(8,128)(2,1)} custom-call(s32[3]{0:T(128)} %pad_add_fusion.refs_0_.zs_ref, bf16[64,4224]{1,0:T(8,128)(2,1)} %collective-permute-done.refs_1_, bf16[64,4224]{1,0:T(8,128)(2,1)} %collective-permute-done.1.refs_2_), custom_call_target="tpu_custom_call" | custom-call | tf_op jit(solution)/shard_map/pack/pallas_call | solution.py:126
  61.9 6.1 %all-to-all-done = bf16[8,8,4224]{2,1,0:T(8,128)(2,1)S(1)} async-done(((bf16[8,8,4224]{2,1,0:T(8,128)(2,1)}), bf16[8,8,4224]{2,1,0:T(8,128)(2,1)S(1)}, u32[]{:S(2)}, u32[]{:S(2)}) %all-to-all-start) | async-done | bytes 540704 | tf_op jit(solution)/shard_map/all_to_all | solution.py:357
  68.0 3.6 %all-to-all-start.1 = ((bf16[8,16,4224]{2,1,0:T(8,128)(2,1)}), bf16[8,16,4224]{2,1,0:T(8,128)(2,1)S(1)}, u32[]{:S(2)}, u32[]{:S(2)}) async-start(bf16[8,16,4224]{2,1,0:T(8,128)(2,1)} %bitcast.31), calls=%async_computation.1 | async-start | bytes 2162688 | tf_op jit(solution)/shard_map/all_to_all | solution.py:357
  79.2 4.3 %collective-permute-start.7 = (bf16[288,2048]{1,0:T(8,128)(2,1)}, bf16[288,2048]{1,0:T(8,128)(2,1)}, u32[]{:S(2)}, u32[]{:S(2)}) collective-permute-start(bf16[288,2048]{1,0:T(8,128)(2,1)} %slice.48), channel_id=1, source_target_pairs={{0,1},{1,2},{2,3},{3,0},{4,5},{5,6},{6,7},{7,4},{8,9},{9,10},{10,1... | collective-permute-start | bytes 3538952 | tf_op jit(solution)/shard_map/ppermute | solution.py:28
  84.4 5.2 %collective-permute-start.4 = (bf16[32,4224]{1,0:T(8,128)(2,1)S(1)}, bf16[32,4224]{1,0:T(8,128)(2,1)S(1)}, u32[]{:S(2)}, u32[]{:S(2)}) collective-permute-start(bf16[32,4224]{1,0:T(8,128)(2,1)S(1)} %slice.60), channel_id=1, source_target_pairs={{0,284},{4,0},{8,4},{12,8},{16,12},{20,16},{24,20},{28,24},{256,28... | collective-permute-start | bytes 811016 | tf_op jit(solution)/shard_map/ppermute | solution.py:28
  92.5 2.9 %collective-permute-done.4.refs_1_ = bf16[32,4224]{1,0:T(8,128)(2,1)S(1)} collective-permute-done((bf16[32,4224]{1,0:T(8,128)(2,1)S(1)}, bf16[32,4224]{1,0:T(8,128)(2,1)S(1)}, u32[]{:S(2)}, u32[]{:S(2)}) %collective-permute-start.4) | collective-permute-done | bytes 270368 | tf_op jit(solution)/shard_map/ppermute | solution.py:28
  95.4 6.3 %collective-permute-done.5.refs_2_ = bf16[32,4224]{1,0:T(8,128)(2,1)S(1)} collective-permute-done((bf16[32,4224]{1,0:T(8,128)(2,1)S(1)}, bf16[32,4224]{1,0:T(8,128)(2,1)S(1)}, u32[]{:S(2)}, u32[]{:S(2)}) %collective-permute-start.5) | collective-permute-done | bytes 270368 | tf_op jit(solution)/shard_map/ppermute | solution.py:28
  104.9 4.4 %all-to-all-start.2 = ((bf16[8,8,4224]{2,1,0:T(8,128)(2,1)}), bf16[8,8,4224]{2,1,0:T(8,128)(2,1)S(1)}, u32[]{:S(2)}, u32[]{:S(2)}) async-start(bf16[8,8,4224]{2,1,0:T(8,128)(2,1)} %bitcast.32), calls=%async_computation.2 | async-start | bytes 1081344 | tf_op jit(solution)/shard_map/all_to_all | solution.py:357
  111.7 3.6 %collective-permute-start.9 = (bf16[192,2048]{1,0:T(8,128)(2,1)S(1)}, bf16[192,2048]{1,0:T(8,128)(2,1)S(1)}, u32[]{:S(2)}, u32[]{:S(2)}) collective-permute-start(bf16[192,2048]{1,0:T(8,128)(2,1)S(1)} %pad_maximum_fusion.1.refs_4_), channel_id=1, source_target_pairs={{0,3},{1,0},{2,1},{3,2},{4,7},{5,4},{6,5},{7,6},{8,11},{9,8},{10,9... | collective-permute-start | bytes 2359304 | tf_op jit(solution)/shard_map/ppermute | solution.py:28
  115.4 4.5 %all-to-all-done.2 = bf16[8,8,4224]{2,1,0:T(8,128)(2,1)S(1)} async-done(((bf16[8,8,4224]{2,1,0:T(8,128)(2,1)}), bf16[8,8,4224]{2,1,0:T(8,128)(2,1)S(1)}, u32[]{:S(2)}, u32[]{:S(2)}) %all-to-all-start.2) | async-done | bytes 540704 | tf_op jit(solution)/shard_map/all_to_all | solution.py:357
  120.7 12.1 %rows.1 = (bf16[256,2176]{1,0:T(8,128)(2,1)}, bf16[384,256]{1,0:T(8,128)(2,1)}, bf16[384,256]{1,0:T(8,128)(2,1)}, bf16[384,256]{1,0:T(8,128)(2,1)}, bf16[384,256...) custom-call(s32[3]{0:T(128)} %pad_add_fusion.refs_0_.zs_ref, bf16[64,4224]{1,0:T(8,128)(2,1)} %bitcast.26, ...), custom_call_target="tpu_custom_call" | custom-call | flops 4026531840 | bytes 12582912 | tf_op jit(solution)/shard_map/rows/pallas_call | solution.py:206
  137.7 11.5 %all-to-all-start.3 = ((bf16[128,2,2176]{2,1,0:T(2,128)(2,1)}), bf16[128,2,2176]{2,1,0:T(2,128)(2,1)}, u32[]{:S(2)}, u32[]{:S(2)}) async-start(bf16[128,2,2176]{2,1,0:T(2,128)(2,1)} %reshape.71), calls=%async_computation.3 | async-start | bytes 2228224 | tf_op jit(solution)/shard_map/all_to_all | solution.py:381
  153.7 3.9 %collective-permute-start.18 = (bf16[192,2048]{1,0:T(8,128)(2,1)S(1)}, bf16[192,2048]{1,0:T(8,128)(2,1)S(1)}, u32[]{:S(2)}, u32[]{:S(2)}) collective-permute-start(bf16[192,2048]{1,0:T(8,128)(2,1)S(1)} %get-tuple-element.61), channel_id=1, source_target_pairs={{0,3},{1,0},{2,1},{3,2},{4,7},{5,4},{6,5},{7,6},{8,11},{9,8},{10,9... | collective-permute-start | bytes 2359304 | tf_op jit(solution)/shard_map/ppermute | solution.py:28
  157.7 3.1 %collective-permute-start.10 = (bf16[384,256]{1,0:T(8,128)(2,1)S(1)}, bf16[384,256]{1,0:T(8,128)(2,1)S(1)}, u32[]{:S(2)}, u32[]{:S(2)}) collective-permute-start(bf16[384,256]{1,0:T(8,128)(2,1)S(1)} %copy-done.16), channel_id=1, source_target_pairs={{0,1},{1,2},{2,3},{3,0},{4,5},{5,6},{6,7},{7,4},{8,9},{9,10},{10,1... | collective-permute-start | bytes 589832 | tf_op jit(solution)/shard_map/ppermute | solution.py:28
  167.6 6.6 %collective-permute-done.16 = bf16[192,2048]{1,0:T(8,128)(2,1)S(1)} collective-permute-done((bf16[192,2048]{1,0:T(8,128)(2,1)S(1)}, bf16[192,2048]{1,0:T(8,128)(2,1)S(1)}, u32[]{:S(2)}, u32[]{:S(2)}) %collective-permute-start.16) | collective-permute-done | bytes 786464 | tf_op jit(solution)/shard_map/ppermute | solution.py:28
  181.3 8.7 %collective-permute-start.14 = (bf16[160,2048]{1,0:T(8,128)(2,1)S(1)}, bf16[160,2048]{1,0:T(8,128)(2,1)S(1)}, u32[]{:S(2)}, u32[]{:S(2)}) collective-permute-start(bf16[160,2048]{1,0:T(8,128)(2,1)S(1)} %get-tuple-element.65), channel_id=1, source_target_pairs={{0,3},{1,0},{2,1},{3,2},{4,7},{5,4},{6,5},{7,6},{8,11},{9,8},{10,9... | collective-permute-start | bytes 1966088 | tf_op jit(solution)/shard_map/ppermute | solution.py:28
  192.1 3.9 %collective-permute-start.19 = (bf16[96,2048]{1,0:T(8,128)(2,1)S(1)}, bf16[96,2048]{1,0:T(8,128)(2,1)S(1)}, u32[]{:S(2)}, u32[]{:S(2)}) collective-permute-start(bf16[96,2048]{1,0:T(8,128)(2,1)S(1)} %add_convert_fusion.1), channel_id=1, source_target_pairs={{0,3},{1,0},{2,1},{3,2},{4,7},{5,4},{6,5},{7,6},{8,11},{9,8},{10,9... | collective-permute-start | bytes 1179656 | tf_op jit(solution)/shard_map/ppermute | solution.py:28
  196.0 7.7 %collective-permute-done.13.refs_7_ = bf16[160,2048]{1,0:T(8,128)(2,1)S(1)} collective-permute-done((bf16[160,2048]{1,0:T(8,128)(2,1)S(1)}, bf16[160,2048]{1,0:T(8,128)(2,1)S(1)}, u32[]{:S(2)}, u32[]{:S(2)}) %collective-permute-start.13) | collective-permute-done | bytes 655392 | tf_op jit(solution)/shard_map/ppermute | solution.py:28
  205.2 4.5 %weight_grads.1 = (bf16[192,2048]{1,0:T(8,128)(2,1)}, bf16[192,2048]{1,0:T(8,128)(2,1)}) custom-call(bf16[384,256]{1,0:T(8,128)(2,1)S(1)} %copy-done.9, bf16[384,256]{1,0:T(8,128)(2,1)S(1)} %collective-permute-done.10.refs_1_, bf16[384,256]{1,0:T(8,128)(2,1)S(1)} %collective-permute-done.11.refs_2_, bf16[384,256]{1,0:T(8,128)(2,1)S(1)} %collective-permute-done.12.refs_3_, ...), custom_call_target="tpu_custom_call" | custom-call | flops 1610612736 | bytes 5767168 | tf_op jit(solution)/shard_map/weight_grads/pallas_call | solution.py:297
  (87 shorter events, 62.6 us)
Async XLA Ops:
  2.5 59.4 %collective-permute-start.2 = (bf16[576,2048]{1,0:T(8,128)(2,1)S(1)}, bf16[576,2048]{1,0:T(8,128)(2,1)}, u32[]{:S(2)}, u32[]{:S(2)}) collective-permute-start(bf16[576,2048]{1,0:T(8,128)(2,1)S(1)} %pad_maximum_fusion.refs_3_), channel_id=1, source_target_pairs={{0,1},{1,2},{2,3},{3,0},{4,5},{5,6},{6,7},{7,4},{8,9},{9,10},{10,1... | collective-permute-start | bytes 7077896 | tf_op jit(solution)/shard_map/ppermute | solution.py:28
  10.3 51.6 %collective-permute-start.3 = (bf16[576,2048]{1,0:T(8,128)(2,1)S(1)}, bf16[576,2048]{1,0:T(8,128)(2,1)}, u32[]{:S(2)}, u32[]{:S(2)}) collective-permute-start(bf16[576,2048]{1,0:T(8,128)(2,1)S(1)} %pad_maximum_fusion.refs_3_), channel_id=1, source_target_pairs={{0,3},{1,0},{2,1},{3,2},{4,7},{5,4},{6,5},{7,6},{8,11},{9,8},{10,9... | collective-permute-start | bytes 7077896 | tf_op jit(solution)/shard_map/ppermute | solution.py:28
  42.7 14.9 %collective-permute-start = (bf16[64,4224]{1,0:T(8,128)(2,1)S(1)}, bf16[64,4224]{1,0:T(8,128)(2,1)}, u32[]{:S(2)}, u32[]{:S(2)}) collective-permute-start(bf16[64,4224]{1,0:T(8,128)(2,1)S(1)} %all_gather.3.refs_1_), channel_id=1, source_target_pairs={{0,4},{4,8},{8,12},{12,16},{16,20},{20,24},{24,28},{28,256},{256,2... | collective-permute-start | bytes 1622024 | tf_op jit(solution)/shard_map/ppermute | solution.py:28
  46.4 12.3 %collective-permute-start.1 = (bf16[64,4224]{1,0:T(8,128)(2,1)S(1)}, bf16[64,4224]{1,0:T(8,128)(2,1)}, u32[]{:S(2)}, u32[]{:S(2)}) collective-permute-start(bf16[64,4224]{1,0:T(8,128)(2,1)S(1)} %all_gather.3.refs_1_), channel_id=1, source_target_pairs={{0,284},{4,0},{8,4},{12,8},{16,12},{20,16},{24,20},{28,24},{256,28... | collective-permute-start | bytes 1622024 | tf_op jit(solution)/shard_map/ppermute | solution.py:28
  53.0 15.0 %all-to-all-start = ((bf16[8,8,4224]{2,1,0:T(8,128)(2,1)}), bf16[8,8,4224]{2,1,0:T(8,128)(2,1)S(1)}, u32[]{:S(2)}, u32[]{:S(2)}) async-start(bf16[8,8,4224]{2,1,0:T(8,128)(2,1)} %bitcast.33), calls=%async_computation | async-start | bytes 1081344 | tf_op jit(solution)/shard_map/all_to_all | solution.py:357
  68.0 36.9 %all-to-all-start.1 = ((bf16[8,16,4224]{2,1,0:T(8,128)(2,1)}), bf16[8,16,4224]{2,1,0:T(8,128)(2,1)S(1)}, u32[]{:S(2)}, u32[]{:S(2)}) async-start(bf16[8,16,4224]{2,1,0:T(8,128)(2,1)} %bitcast.31), calls=%async_computation.1 | async-start | bytes 2162688 | tf_op jit(solution)/shard_map/all_to_all | solution.py:357
  74.0 41.4 %collective-permute-start.6 = (bf16[288,2048]{1,0:T(8,128)(2,1)}, bf16[288,2048]{1,0:T(8,128)(2,1)}, u32[]{:S(2)}, u32[]{:S(2)}) collective-permute-start(bf16[288,2048]{1,0:T(8,128)(2,1)} %slice.47), channel_id=1, source_target_pairs={{0,3},{1,0},{2,1},{3,2},{4,7},{5,4},{6,5},{7,6},{8,11},{9,8},{10,9... | collective-permute-start | bytes 3538952 | tf_op jit(solution)/shard_map/ppermute | solution.py:28
  79.2 36.2 %collective-permute-start.7 = (bf16[288,2048]{1,0:T(8,128)(2,1)}, bf16[288,2048]{1,0:T(8,128)(2,1)}, u32[]{:S(2)}, u32[]{:S(2)}) collective-permute-start(bf16[288,2048]{1,0:T(8,128)(2,1)} %slice.48), channel_id=1, source_target_pairs={{0,1},{1,2},{2,3},{3,0},{4,5},{5,6},{6,7},{7,4},{8,9},{9,10},{10,1... | collective-permute-start | bytes 3538952 | tf_op jit(solution)/shard_map/ppermute | solution.py:28
  84.4 11.0 %collective-permute-start.4 = (bf16[32,4224]{1,0:T(8,128)(2,1)S(1)}, bf16[32,4224]{1,0:T(8,128)(2,1)S(1)}, u32[]{:S(2)}, u32[]{:S(2)}) collective-permute-start(bf16[32,4224]{1,0:T(8,128)(2,1)S(1)} %slice.60), channel_id=1, source_target_pairs={{0,284},{4,0},{8,4},{12,8},{16,12},{20,16},{24,20},{28,24},{256,28... | collective-permute-start | bytes 811016 | tf_op jit(solution)/shard_map/ppermute | solution.py:28
  90.6 11.2 %collective-permute-start.5 = (bf16[32,4224]{1,0:T(8,128)(2,1)S(1)}, bf16[32,4224]{1,0:T(8,128)(2,1)S(1)}, u32[]{:S(2)}, u32[]{:S(2)}) collective-permute-start(bf16[32,4224]{1,0:T(8,128)(2,1)S(1)} %slice.61), channel_id=1, source_target_pairs={{0,4},{4,8},{8,12},{12,16},{16,20},{20,24},{24,28},{28,256},{256,2... | collective-permute-start | bytes 811016 | tf_op jit(solution)/shard_map/ppermute | solution.py:28
  104.9 15.0 %all-to-all-start.2 = ((bf16[8,8,4224]{2,1,0:T(8,128)(2,1)}), bf16[8,8,4224]{2,1,0:T(8,128)(2,1)S(1)}, u32[]{:S(2)}, u32[]{:S(2)}) async-start(bf16[8,8,4224]{2,1,0:T(8,128)(2,1)} %bitcast.32), calls=%async_computation.2 | async-start | bytes 1081344 | tf_op jit(solution)/shard_map/all_to_all | solution.py:357
  109.5 23.3 %collective-permute-start.8 = (bf16[192,2048]{1,0:T(8,128)(2,1)S(1)}, bf16[192,2048]{1,0:T(8,128)(2,1)}, u32[]{:S(2)}, u32[]{:S(2)}) collective-permute-start(bf16[192,2048]{1,0:T(8,128)(2,1)S(1)} %pad_maximum_fusion.1.refs_4_), channel_id=1, source_target_pairs={{0,1},{1,2},{2,3},{3,0},{4,5},{5,6},{6,7},{7,4},{8,9},{9,10},{10,1... | collective-permute-start | bytes 2359304 | tf_op jit(solution)/shard_map/ppermute | solution.py:28
  111.7 22.8 %collective-permute-start.9 = (bf16[192,2048]{1,0:T(8,128)(2,1)S(1)}, bf16[192,2048]{1,0:T(8,128)(2,1)S(1)}, u32[]{:S(2)}, u32[]{:S(2)}) collective-permute-start(bf16[192,2048]{1,0:T(8,128)(2,1)S(1)} %pad_maximum_fusion.1.refs_4_), channel_id=1, source_target_pairs={{0,3},{1,0},{2,1},{3,2},{4,7},{5,4},{6,5},{7,6},{8,11},{9,8},{10,9... | collective-permute-start | bytes 2359304 | tf_op jit(solution)/shard_map/ppermute | solution.py:28
  137.7 75.9 %all-to-all-start.3 = ((bf16[128,2,2176]{2,1,0:T(2,128)(2,1)}), bf16[128,2,2176]{2,1,0:T(2,128)(2,1)}, u32[]{:S(2)}, u32[]{:S(2)}) async-start(bf16[128,2,2176]{2,1,0:T(2,128)(2,1)} %reshape.71), calls=%async_computation.3 | async-start | bytes 2228224 | tf_op jit(solution)/shard_map/all_to_all | solution.py:381
  151.6 22.5 %collective-permute-start.16 = (bf16[192,2048]{1,0:T(8,128)(2,1)S(1)}, bf16[192,2048]{1,0:T(8,128)(2,1)S(1)}, u32[]{:S(2)}, u32[]{:S(2)}) collective-permute-start(bf16[192,2048]{1,0:T(8,128)(2,1)S(1)} %get-tuple-element.60), channel_id=1, source_target_pairs={{0,1},{1,2},{2,3},{3,0},{4,5},{5,6},{6,7},{7,4},{8,9},{9,10},{10,1... | collective-permute-start | bytes 2359304 | tf_op jit(solution)/shard_map/ppermute | solution.py:28
  153.7 27.6 %collective-permute-start.18 = (bf16[192,2048]{1,0:T(8,128)(2,1)S(1)}, bf16[192,2048]{1,0:T(8,128)(2,1)S(1)}, u32[]{:S(2)}, u32[]{:S(2)}) collective-permute-start(bf16[192,2048]{1,0:T(8,128)(2,1)S(1)} %get-tuple-element.61), channel_id=1, source_target_pairs={{0,3},{1,0},{2,1},{3,2},{4,7},{5,4},{6,5},{7,6},{8,11},{9,8},{10,9... | collective-permute-start | bytes 2359304 | tf_op jit(solution)/shard_map/ppermute | solution.py:28
  157.7 20.7 %collective-permute-start.10 = (bf16[384,256]{1,0:T(8,128)(2,1)S(1)}, bf16[384,256]{1,0:T(8,128)(2,1)S(1)}, u32[]{:S(2)}, u32[]{:S(2)}) collective-permute-start(bf16[384,256]{1,0:T(8,128)(2,1)S(1)} %copy-done.16), channel_id=1, source_target_pairs={{0,1},{1,2},{2,3},{3,0},{4,5},{5,6},{6,7},{7,4},{8,9},{9,10},{10,1... | collective-permute-start | bytes 589832 | tf_op jit(solution)/shard_map/ppermute | solution.py:28
  160.8 29.3 %collective-permute-start.11 = (bf16[384,256]{1,0:T(8,128)(2,1)S(1)}, bf16[384,256]{1,0:T(8,128)(2,1)S(1)}, u32[]{:S(2)}, u32[]{:S(2)}) collective-permute-start(bf16[384,256]{1,0:T(8,128)(2,1)S(1)} %copy-done.15), channel_id=1, source_target_pairs={{0,3},{1,0},{2,1},{3,2},{4,7},{5,4},{6,5},{7,6},{8,11},{9,8},{10,9... | collective-permute-start | bytes 589832 | tf_op jit(solution)/shard_map/ppermute | solution.py:28
  163.5 32.5 %collective-permute-start.15 = (bf16[64,2048]{1,0:T(8,128)(2,1)S(1)}, bf16[64,2048]{1,0:T(8,128)(2,1)S(1)}, u32[]{:S(2)}, u32[]{:S(2)}) collective-permute-start(bf16[64,2048]{1,0:T(8,128)(2,1)S(1)} %slice.62.refs_9_), channel_id=1, source_target_pairs={{0,2},{1,3},{2,0},{3,1},{4,6},{5,7},{6,4},{7,5},{8,10},{9,11},{10,... | collective-permute-start | bytes 786440 | tf_op jit(solution)/shard_map/ppermute | solution.py:28
  174.1 18.0 %collective-permute-start.12 = (bf16[384,256]{1,0:T(8,128)(2,1)S(1)}, bf16[384,256]{1,0:T(8,128)(2,1)S(1)}, u32[]{:S(2)}, u32[]{:S(2)}) collective-permute-start(bf16[384,256]{1,0:T(8,128)(2,1)S(1)} %copy-done.14), channel_id=1, source_target_pairs={{0,2},{1,3},{2,0},{3,1},{4,6},{5,7},{6,4},{7,5},{8,10},{9,11},{10,... | collective-permute-start | bytes 589832 | tf_op jit(solution)/shard_map/ppermute | solution.py:28
  178.4 25.4 %collective-permute-start.13 = (bf16[160,2048]{1,0:T(8,128)(2,1)S(1)}, bf16[160,2048]{1,0:T(8,128)(2,1)S(1)}, u32[]{:S(2)}, u32[]{:S(2)}) collective-permute-start(bf16[160,2048]{1,0:T(8,128)(2,1)S(1)} %get-tuple-element.66), channel_id=1, source_target_pairs={{0,1},{1,2},{2,3},{3,0},{4,5},{5,6},{6,7},{7,4},{8,9},{9,10},{10,1... | collective-permute-start | bytes 1966088 | tf_op jit(solution)/shard_map/ppermute | solution.py:28
  181.3 23.9 %collective-permute-start.14 = (bf16[160,2048]{1,0:T(8,128)(2,1)S(1)}, bf16[160,2048]{1,0:T(8,128)(2,1)S(1)}, u32[]{:S(2)}, u32[]{:S(2)}) collective-permute-start(bf16[160,2048]{1,0:T(8,128)(2,1)S(1)} %get-tuple-element.65), channel_id=1, source_target_pairs={{0,3},{1,0},{2,1},{3,2},{4,7},{5,4},{6,5},{7,6},{8,11},{9,8},{10,9... | collective-permute-start | bytes 1966088 | tf_op jit(solution)/shard_map/ppermute | solution.py:28
  190.2 19.6 %collective-permute-start.17 = (bf16[96,2048]{1,0:T(8,128)(2,1)S(1)}, bf16[96,2048]{1,0:T(8,128)(2,1)S(1)}, u32[]{:S(2)}, u32[]{:S(2)}) collective-permute-start(bf16[96,2048]{1,0:T(8,128)(2,1)S(1)} %add_convert_fusion.3), channel_id=1, source_target_pairs={{0,1},{1,2},{2,3},{3,0},{4,5},{5,6},{6,7},{7,4},{8,9},{9,10},{10,1... | collective-permute-start | bytes 1179656 | tf_op jit(solution)/shard_map/ppermute | solution.py:28
  192.1 20.2 %collective-permute-start.19 = (bf16[96,2048]{1,0:T(8,128)(2,1)S(1)}, bf16[96,2048]{1,0:T(8,128)(2,1)S(1)}, u32[]{:S(2)}, u32[]{:S(2)}) collective-permute-start(bf16[96,2048]{1,0:T(8,128)(2,1)S(1)} %add_convert_fusion.1), channel_id=1, source_target_pairs={{0,3},{1,0},{2,1},{3,2},{4,7},{5,4},{6,5},{7,6},{8,11},{9,8},{10,9... | collective-permute-start | bytes 1179656 | tf_op jit(solution)/shard_map/ppermute | solution.py:28
  (18 other events, 281.8 us)

commit v8 on v7

--- a/solution.py
+++ b/solution.py
@@ -189,7 +189,14 @@
         d_gate = d_hidden * up_pre * sigma * (1.0 + gate_pre * (1.0 - sigma))
         d_all[first : first + hid, :] = d_gate.astype(BF)
         d_all[first + hid : first + 2 * hid, :] = (d_hidden * active).astype(BF)
-        d_refs[q][...] = d_all[first : first + 2 * hid, :]
+        if q == 0:
+            d_refs[0][...] = d_all[: 2 * hid, :]
+        else:
+            size = d_refs[q].shape[0]
+            for j in range(features // count):
+                d_refs[q][:, j * count : (j + 1) * count] = d_all[
+                    first + j * size : first + (j + 1) * size, :
+                ]
         s_ref[q] = (coef * hidden).astype(BF)
     moved = dot(d_all[...], home, 1, 0).astype(BF)
     tile = 512
@@ -207,7 +214,8 @@
         rows_kernel,
         out_shape=[
             jax.ShapeDtypeStruct((count, features + LANES), BF),
-            *[jax.ShapeDtypeStruct((2 * hid, count), BF)] * n,
+            jax.ShapeDtypeStruct((2 * hid, count), BF),
+            *[jax.ShapeDtypeStruct((2 * hid * count // features, features), BF)] * (n - 1),
             jax.ShapeDtypeStruct((n, hid, count), BF),
         ],
         in_specs=[pl.BlockSpec(memory_space=pltpu.SMEM)] + [pl.BlockSpec(memory_space=pl.ANY)] * 8,
@@ -229,7 +237,9 @@
     )(zs, *chunks, *weights)
 
 
-def down_kernel(s_ref, a_ref, b_ref, c_ref, own_ref, go_ref, come_ref, right_ref, left_ref, rows):
+def down_kernel(
+    s_ref, a_ref, b_ref, c_ref, dl_ref, dr_ref, own_ref, go_ref, come_ref, right_ref, left_ref, rows
+):
     quarter = a_ref.shape[0]
     rows[0:quarter, :] = a_ref[...]
     rows[quarter : 3 * quarter, :] = b_ref[...]
@@ -241,26 +251,31 @@
     right = dot(s_ref[2], grads, 1, 0).astype(BF)
     two = dot(s_ref[3], grads, 1, 0).astype(BF)
     go_ref[:half, :] = two[:half]
-    go_ref[half:, :] = right[half:]
+    go_ref[half : 2 * half, :] = right[half:]
+    go_ref[2 * half :, :] = dr_ref[...]
     come_ref[:half, :] = left[:half]
-    come_ref[half:, :] = two[half:]
+    come_ref[half : 2 * half, :] = two[half:]
+    come_ref[2 * half :, :] = dl_ref[...]
     right_ref[...] = right[:half]
     left_ref[...] = left[half:]
 
 
-def down_call(scaled, chunks, features):
+def down_call(scaled, chunks, d_left, d_right, features):
     tile = 512
     n, hid, count = scaled.shape
     first = features // tile
     tiled = [pl.BlockSpec((c.shape[0], tile), lambda j: (0, first + j)) for c in chunks]
+    extra = d_left.shape[0]
+    tiled += [pl.BlockSpec((extra, tile), lambda j: (0, j))] * 2
     return pl.pallas_call(
         down_kernel,
         grid=(features // tile,),
         out_shape=[jax.ShapeDtypeStruct((hid, features), F32)]
-        + [jax.ShapeDtypeStruct((hid, features), BF)] * 2
+        + [jax.ShapeDtypeStruct((hid + extra, features), BF)] * 2
         + [jax.ShapeDtypeStruct((hid // 2, features), BF)] * 2,
         in_specs=[pl.BlockSpec(scaled.shape, lambda j: (0, 0, 0))] + tiled,
-        out_specs=[pl.BlockSpec((hid, tile), lambda j: (0, j))] * 3
+        out_specs=[pl.BlockSpec((hid, tile), lambda j: (0, j))]
+        + [pl.BlockSpec((hid + extra, tile), lambda j: (0, j))] * 2
         + [pl.BlockSpec((hid // 2, tile), lambda j: (0, j))] * 2,
         scratch_shapes=[pltpu.VMEM((count, tile), BF)],
         compiler_params=pltpu.CompilerParams(vmem_limit_bytes=24 * MIB),
@@ -270,45 +285,59 @@
             transcendentals=0,
         ),
         name="down_parts",
-    )(scaled, *chunks)
+    )(scaled, *chunks, d_left, d_right)
 
 
 def weights_kernel(*refs):
-    d_refs, x_refs, (gate_ref, up_ref, rows) = refs[:4], refs[4:11], refs[11:]
+    d_refs, x_refs, (gate_ref, up_ref, factors, rows) = refs[:4], refs[4:11], refs[11:]
     own, left, right, more_left, more_right, last, two = x_refs
     hid = gate_ref.shape[0]
     most, mid = own.shape[0], own.shape[0] // 2
+    count = rows.shape[1]
+
+    @pl.when(pl.program_id(0) == 0)
+    def _():
+        factors[0] = d_refs[0][...]
+        for q in range(1, 4):
+            size = d_refs[q].shape[0]
+            for j in range(d_refs[q].shape[1] // count):
+                factors[q, j * size : (j + 1) * size, :] = d_refs[q][:, j * count : (j + 1) * count]
+
     for q, (first, end) in enumerate(((own, last), (left, more_left), (right, more_right))):
         rows[q, :most, :] = first[...]
-        rows[q, most:, :] = end[end.shape[0] - two.shape[0] :, :]
+        rows[q, most:, :] = end[end.shape[0] - last.shape[0] :, :]
     rows[3, :mid, :] = more_right[:mid, :]
     rows[3, mid:most, :] = more_left[:mid, :]
-    rows[3, most:, :] = two[...]
-    total = sum(dot(d[...], rows[q], 1, 0) for q, d in enumerate(d_refs)).astype(BF)
+    rows[3, most:, :] = two[two.shape[0] - last.shape[0] :, :]
+    total = sum(dot(factors[q], rows[q], 1, 0) for q in range(4)).astype(BF)
     gate_ref[...] = total[:hid]
     up_ref[...] = total[hid:]
 
 
-def weights_call(ds, xs):
+def weights_call(d_own, from_left, from_right, from_two, xs):
     tile = 512
-    hid, count, features = ds[0].shape[0] // 2, ds[0].shape[1], xs[0].shape[1]
-    whole = [pl.BlockSpec(d.shape, lambda j: (0, 0)) for d in ds]
-    tiled = [pl.BlockSpec((x.shape[0], tile), lambda j: (0, j)) for x in xs]
+    n, (both, count), features = 4, d_own.shape, xs[0].shape[1]
+    hid, size = both // 2, both * count // features
+    last = from_left.shape[0] // size - 1
+    packed = [
+        pl.BlockSpec((size, features), lambda j, at=at: (at, 0)) for at in (last, last, 0)
+    ]
+    tiled = [pl.BlockSpec((x.shape[0], tile), lambda j: (0, j)) for x in [*xs, from_two]]
     return pl.pallas_call(
         weights_kernel,
         grid=(features // tile,),
         out_shape=[jax.ShapeDtypeStruct((hid, features), BF)] * 2,
-        in_specs=whole + tiled,
+        in_specs=[pl.BlockSpec(d_own.shape, lambda j: (0, 0)), *packed, *tiled],
         out_specs=[pl.BlockSpec((hid, tile), lambda j: (0, j))] * 2,
-        scratch_shapes=[pltpu.VMEM((len(ds), count, tile), BF)],
+        scratch_shapes=[pltpu.VMEM((n, both, count), BF), pltpu.VMEM((n, count, tile), BF)],
         compiler_params=pltpu.CompilerParams(vmem_limit_bytes=24 * MIB),
         cost_estimate=pl.CostEstimate(
-            flops=4 * len(ds) * count * features * hid,
-            bytes_accessed=2 * features * (len(ds) * count + 2 * hid),
+            flops=4 * n * count * features * hid,
+            bytes_accessed=2 * features * (n * count + 2 * hid),
             transcendentals=0,
         ),
         name="weight_grads",
-    )(*ds, *xs)
+    )(d_own, from_left, from_right, from_two, *xs, from_two)
 
 
 def home_kernel(code_ref, home_ref, grad_ref, score_ref):
@@ -383,26 +412,24 @@
     ).reshape(back.shape)
     mid = x_ab.shape[0] // 2
     x_c = rows_c[:, :features]
-    x_two = shift(x_c, 2, "x", n)
+    from_two = shift(jnp.concatenate([d_two, x_c], axis=0), 2, "x", n)
     more_left = shift(jnp.concatenate([x_left[mid:], x_c], axis=0), 1, "x", n)
     more_right = shift(jnp.concatenate([x_right[:mid], x_c], axis=0), -1, "x", n)
-    ds = [d_own, shift(d_right, 1, "x", n), shift(d_left, -1, "x", n), shift(d_two, 2, "x", n)]
-
-    p_own, p_go, p_come, p_right, p_left = down_call(scaled, chunks, features)
+
+    p_own, p_go, p_come, p_right, p_left = down_call(scaled, chunks, d_left, d_right, features)
     from_left, from_right = shift(p_go, 1, "x", n), shift(p_come, -1, "x", n)
     p_right = (p_right.astype(F32) + from_left[:half].astype(F32)).astype(BF)
-    p_left = (p_left.astype(F32) + from_right[half:].astype(F32)).astype(BF)
+    p_left = (p_left.astype(F32) + from_right[half : 2 * half].astype(F32)).astype(BF)
     left_top, right_low = shift(p_right, 1, "x", n), shift(p_left, -1, "x", n)
     grad_down = jnp.concatenate(
         [
             p_own[:half] + left_top.astype(F32) + from_right[:half].astype(F32),
-            p_own[half:] + from_left[half:].astype(F32) + right_low.astype(F32),
+            p_own[half:] + from_left[half : 2 * half].astype(F32) + right_low.astype(F32),
         ],
         axis=0,
     ).astype(BF)
-
     grad_gate, grad_up = weights_call(
-        ds, [x_ab, x_left, x_right, more_left, more_right, x_c, x_two]
+        d_own, from_left, from_right, from_two, [x_ab, x_left, x_right, more_left, more_right, x_c]
     )
 
     token_grad, slot_score = home_call(code, home, features)

time: 221 us -> 223 us (level)
  waiting for transfers between devices: 42.4 us -> 57.6 us
  starting transfers between devices: 95.9 us -> 82.4 us
    ppermute x20 -> x17, waiting for transfers between devices: 31.8 us -> 46.9 us  [shift(): return lax.ppermute(block, axes, [(i, (i + step) % n) for i in range(n)])]
    ppermute x20 -> x17, starting transfers between devices: 71.9 us -> 58.4 us  [shift(): return lax.ppermute(block, axes, [(i, (i + step) % n) for i in range(n)])]
    unnamed x34 -> x26, local copies, waits for them, and re-layouts: 2.4 us -> 4.59 us
  transfers between devices with their start and end apart: 24 -> 21, of which waited for: 12 -> 13; matrix products, arithmetic and copies ran while one was open for 5% -> 5% of each run, Pallas kernels for 13% -> 13%
where the time goes in v8:
time: 223 us; the launch traced here: 222 us
  starting transfers between devices  82.4 us (37%)
  waiting for transfers between devices  57.6 us (26%)
  Pallas kernels  31.2 us (14%)
  blocking collectives  28.5 us (13%)
  local copies, waits for them, and re-layouts  17 us (8%)
  other arithmetic  4.05 us (2%)
    ppermute x17, starting transfers between devices, shift(): return lax.ppermute(block, axes, [(i, (i + step) % n) for i in range(n)])  58.4 us
    ppermute x17, waiting for transfers between devices, shift(): return lax.ppermute(block, axes, [(i, (i + step) % n) for i in range(n)])  46.9 us
    all_gather x1, blocking collectives, local(): chunk = lax.all_gather(own, FAR, axis=0, tiled=True)  28.5 us
    all_to_all x3, starting transfers between devices, exchange(): lax.all_to_all(packed.reshape(8, rows // 8, width), YC, split_axis=0, con...  12.5 us
    pallas_call x1, Pallas kernels, rows_call(): pl.pallas_call(rows_kernel, out_shape=[jax.ShapeDtypeStruct((count, featu...  12.1 us
    all_to_all x1, starting transfers between devices, local(): lax.all_to_all(back.reshape(-1, CAPACITY, back.shape[1]), PLACE, split_ax...  11.5 us
    all_to_all x3, waiting for transfers between devices, exchange(): lax.all_to_all(packed.reshape(8, rows // 8, width), YC, split_axis=0, con...  10.7 us
    pallas_call x3, Pallas kernels, pack_call(): pl.pallas_call(body, out_shape=jax.ShapeDtypeStruct((rows, width), BF), i...  8 us
  transfers between devices with their start and end apart: 21, of which 13 were waited for; matrix products, arithmetic and copies ran while one was open for 5% of the time, Pallas kernels for 13%

profile of v8, /device:TPU:6, one launch (start us, length us, event | category | flops | bytes accessed | tf_op | source)
XLA Modules:
  0.0 221.8 jit_solution(12239118936151751350)
XLA Ops:
  2.4 7.8 %collective-permute-start.2 = (bf16[576,2048]{1,0:T(8,128)(2,1)S(1)}, bf16[576,2048]{1,0:T(8,128)(2,1)}, u32[]{:S(2)}, u32[]{:S(2)}) collective-permute-start(bf16[576,2048]{1,0:T(8,128)(2,1)S(1)} %pad_maximum_fusion.refs_3_), channel_id=1, source_target_pairs={{0,1},{1,2},{2,3},{3,0},{4,5},{5,6},{6,7},{7,4},{8,9},{9,10},{10,1... | collective-permute-start | bytes 7077896 | tf_op jit(solution)/shard_map/ppermute | solution.py:28
  14.0 28.5 %all_gather.3.refs_1_ = bf16[64,4224]{1,0:T(8,128)(2,1)S(1)} all-gather(bf16[16,4224]{1,0:T(8,128)(2,1)} %get-tuple-element.35), channel_id=1, replica_groups=mesh['zh'=2,'y'=4,'c'=2,'zq'=2,'zr'=4,'x'=4] {'zh','zq'}, dimensions={0}, use_global_device_ids=true | all-gather | bytes 675840 | tf_op jit(solution)/shard_map/all_gather | solution.py:381
  42.5 3.7 %collective-permute-start = (bf16[64,4224]{1,0:T(8,128)(2,1)S(1)}, bf16[64,4224]{1,0:T(8,128)(2,1)}, u32[]{:S(2)}, u32[]{:S(2)}) collective-permute-start(bf16[64,4224]{1,0:T(8,128)(2,1)S(1)} %all_gather.3.refs_1_), channel_id=1, source_target_pairs={{0,4},{4,8},{8,12},{12,16},{16,20},{20,24},{24,28},{28,256},{256,2... | collective-permute-start | bytes 1622024 | tf_op jit(solution)/shard_map/ppermute | solution.py:28
  46.2 3.8 %collective-permute-start.1 = (bf16[64,4224]{1,0:T(8,128)(2,1)S(1)}, bf16[64,4224]{1,0:T(8,128)(2,1)}, u32[]{:S(2)}, u32[]{:S(2)}) collective-permute-start(bf16[64,4224]{1,0:T(8,128)(2,1)S(1)} %all_gather.3.refs_1_), channel_id=1, source_target_pairs={{0,284},{4,0},{8,4},{12,8},{16,12},{20,16},{24,20},{28,24},{256,28... | collective-permute-start | bytes 1622024 | tf_op jit(solution)/shard_map/ppermute | solution.py:28
  52.9 4.5 %all-to-all-start = ((bf16[8,8,4224]{2,1,0:T(8,128)(2,1)}), bf16[8,8,4224]{2,1,0:T(8,128)(2,1)S(1)}, u32[]{:S(2)}, u32[]{:S(2)}) async-start(bf16[8,8,4224]{2,1,0:T(8,128)(2,1)} %bitcast.30), calls=%async_computation | async-start | bytes 1081344 | tf_op jit(solution)/shard_map/all_to_all | solution.py:386
  58.6 3.2 %pack.3 = bf16[128,4224]{1,0:T(8,128)(2,1)} custom-call(s32[3]{0:T(128)} %pad_add_fusion.refs_0_.zs_ref, bf16[64,4224]{1,0:T(8,128)(2,1)} %collective-permute-done.refs_1_, bf16[64,4224]{1,0:T(8,128)(2,1)} %collective-permute-done.1.refs_2_), custom_call_target="tpu_custom_call" | custom-call | tf_op jit(solution)/shard_map/pack/pallas_call | solution.py:126
  61.8 6.1 %all-to-all-done = bf16[8,8,4224]{2,1,0:T(8,128)(2,1)S(1)} async-done(((bf16[8,8,4224]{2,1,0:T(8,128)(2,1)}), bf16[8,8,4224]{2,1,0:T(8,128)(2,1)S(1)}, u32[]{:S(2)}, u32[]{:S(2)}) %all-to-all-start) | async-done | bytes 540704 | tf_op jit(solution)/shard_map/all_to_all | solution.py:386
  67.9 3.6 %all-to-all-start.1 = ((bf16[8,16,4224]{2,1,0:T(8,128)(2,1)}), bf16[8,16,4224]{2,1,0:T(8,128)(2,1)S(1)}, u32[]{:S(2)}, u32[]{:S(2)}) async-start(bf16[8,16,4224]{2,1,0:T(8,128)(2,1)} %bitcast.28), calls=%async_computation.1 | async-start | bytes 2162688 | tf_op jit(solution)/shard_map/all_to_all | solution.py:386
  79.0 4.3 %collective-permute-start.7 = (bf16[288,2048]{1,0:T(8,128)(2,1)}, bf16[288,2048]{1,0:T(8,128)(2,1)}, u32[]{:S(2)}, u32[]{:S(2)}) collective-permute-start(bf16[288,2048]{1,0:T(8,128)(2,1)} %slice.48), channel_id=1, source_target_pairs={{0,1},{1,2},{2,3},{3,0},{4,5},{5,6},{6,7},{7,4},{8,9},{9,10},{10,1... | collective-permute-start | bytes 3538952 | tf_op jit(solution)/shard_map/ppermute | solution.py:28
  84.3 5.1 %collective-permute-start.4 = (bf16[32,4224]{1,0:T(8,128)(2,1)S(1)}, bf16[32,4224]{1,0:T(8,128)(2,1)S(1)}, u32[]{:S(2)}, u32[]{:S(2)}) collective-permute-start(bf16[32,4224]{1,0:T(8,128)(2,1)S(1)} %slice.60), channel_id=1, source_target_pairs={{0,284},{4,0},{8,4},{12,8},{16,12},{20,16},{24,20},{28,24},{256,28... | collective-permute-start | bytes 811016 | tf_op jit(solution)/shard_map/ppermute | solution.py:28
  95.3 6.3 %collective-permute-done.5.refs_2_ = bf16[32,4224]{1,0:T(8,128)(2,1)S(1)} collective-permute-done((bf16[32,4224]{1,0:T(8,128)(2,1)S(1)}, bf16[32,4224]{1,0:T(8,128)(2,1)S(1)}, u32[]{:S(2)}, u32[]{:S(2)}) %collective-permute-start.5) | collective-permute-done | bytes 270368 | tf_op jit(solution)/shard_map/ppermute | solution.py:28
  104.8 4.4 %all-to-all-start.2 = ((bf16[8,8,4224]{2,1,0:T(8,128)(2,1)}), bf16[8,8,4224]{2,1,0:T(8,128)(2,1)}, u32[]{:S(2)}, u32[]{:S(2)}) async-start(bf16[8,8,4224]{2,1,0:T(8,128)(2,1)} %bitcast.29), calls=%async_computation.2 | async-start | bytes 1081344 | tf_op jit(solution)/shard_map/all_to_all | solution.py:386
  111.6 3.6 %collective-permute-start.9 = (bf16[192,2048]{1,0:T(8,128)(2,1)S(1)}, bf16[192,2048]{1,0:T(8,128)(2,1)S(1)}, u32[]{:S(2)}, u32[]{:S(2)}) collective-permute-start(bf16[192,2048]{1,0:T(8,128)(2,1)S(1)} %pad_maximum_fusion.1.refs_4_), channel_id=1, source_target_pairs={{0,3},{1,0},{2,1},{3,2},{4,7},{5,4},{6,5},{7,6},{8,11},{9,8},{10,9... | collective-permute-start | bytes 2359304 | tf_op jit(solution)/shard_map/ppermute | solution.py:28
  115.2 4.6 %all-to-all-done.2 = bf16[8,8,4224]{2,1,0:T(8,128)(2,1)} async-done(((bf16[8,8,4224]{2,1,0:T(8,128)(2,1)}), bf16[8,8,4224]{2,1,0:T(8,128)(2,1)}, u32[]{:S(2)}, u32[]{:S(2)}) %all-to-all-start.2) | async-done | bytes 540704 | tf_op jit(solution)/shard_map/all_to_all | solution.py:386
  119.8 12.1 %rows.1 = (bf16[256,2176]{1,0:T(8,128)(2,1)}, bf16[384,256]{1,0:T(8,128)(2,1)}, bf16[48,2048]{1,0:T(8,128)(2,1)}, bf16[48,2048]{1,0:T(8,128)(2,1)}, bf16[48,2048...) custom-call(s32[3]{0:T(128)} %pad_add_fusion.refs_0_.zs_ref, bf16[64,4224]{1,0:T(8,128)(2,1)} %bitcast.26, ...), custom_call_target="tpu_custom_call" | custom-call | flops 4026531840 | bytes 12582912 | tf_op jit(solution)/shard_map/rows/pallas_call | solution.py:213
  136.6 11.5 %all-to-all-start.3 = ((bf16[128,2,2176]{2,1,0:T(2,128)(2,1)}), bf16[128,2,2176]{2,1,0:T(2,128)(2,1)}, u32[]{:S(2)}, u32[]{:S(2)}) async-start(bf16[128,2,2176]{2,1,0:T(2,128)(2,1)} %reshape.71), calls=%async_computation.3 | async-start | bytes 2228224 | tf_op jit(solution)/shard_map/all_to_all | solution.py:410
  152.0 3.4 %down_parts.1 = (f32[192,2048]{1,0:T(8,128)S(1)}, bf16[240,2048]{1,0:T(8,128)(2,1)S(1)}, bf16[240,2048]{1,0:T(8,128)(2,1)S(1)}, bf16[96,2048]{1,0:T(8,128)(2,1)S(1)}, bf16[96,2048]{1,0:T(8,128)(2,1)S(1)}) custom-call(bf16[4,192,256]{2,1,0:T(8,128)(2,1)S(1)} %copy-done.5, bf16[64,4224]{1,0:T(8,128)(2,1)S(1)} %bitcast.27, bf16[128,4224]{1,0:T(8,128)(2,1)S(1)} %bitcast.24, ...), custom_call_target="tpu_custom_call" | custom-call | flops 805306368 | bytes 4980736 | tf_op jit(solution)/shard_map/down_parts/pallas_call | solution.py:270
  157.3 3.9 %collective-permute-start.11 = (bf16[240,2048]{1,0:T(8,128)(2,1)S(1)}, bf16[240,2048]{1,0:T(8,128)(2,1)S(1)}, u32[]{:S(2)}, u32[]{:S(2)}) collective-permute-start(bf16[240,2048]{1,0:T(8,128)(2,1)S(1)} %get-tuple-element.54), channel_id=1, source_target_pairs={{0,3},{1,0},{2,1},{3,2},{4,7},{5,4},{6,5},{7,6},{8,11},{9,8},{10,9... | collective-permute-start | bytes 2949128 | tf_op jit(solution)/shard_map/ppermute | solution.py:28
  165.3 4.4 %collective-permute-start.13 = (bf16[160,2048]{1,0:T(8,128)(2,1)S(1)}, bf16[160,2048]{1,0:T(8,128)(2,1)S(1)}, u32[]{:S(2)}, u32[]{:S(2)}) collective-permute-start(bf16[160,2048]{1,0:T(8,128)(2,1)S(1)} %get-tuple-element.66), channel_id=1, source_target_pairs={{0,1},{1,2},{2,3},{3,0},{4,5},{5,6},{6,7},{7,4},{8,9},{9,10},{10,1... | collective-permute-start | bytes 1966088 | tf_op jit(solution)/shard_map/ppermute | solution.py:28
  171.6 10.4 %collective-permute-done.10.refs_1_ = bf16[240,2048]{1,0:T(8,128)(2,1)S(1)} collective-permute-done((bf16[240,2048]{1,0:T(8,128)(2,1)S(1)}, bf16[240,2048]{1,0:T(8,128)(2,1)S(1)}, u32[]{:S(2)}, u32[]{:S(2)}) %collective-permute-start.10) | collective-permute-done | bytes 983072 | tf_op jit(solution)/shard_map/ppermute | solution.py:28
  182.1 4.5 %collective-permute-start.15 = (bf16[96,2048]{1,0:T(8,128)(2,1)S(1)}, bf16[96,2048]{1,0:T(8,128)(2,1)S(1)}, u32[]{:S(2)}, u32[]{:S(2)}) collective-permute-start(bf16[96,2048]{1,0:T(8,128)(2,1)S(1)} %add_convert_fusion.3), channel_id=1, source_target_pairs={{0,1},{1,2},{2,3},{3,0},{4,5},{5,6},{6,7},{7,4},{8,9},{9,10},{10,1... | collective-permute-start | bytes 1179656 | tf_op jit(solution)/shard_map/ppermute | solution.py:28
  186.6 8.3 %collective-permute-done.11.refs_2_ = bf16[240,2048]{1,0:T(8,128)(2,1)S(1)} collective-permute-done((bf16[240,2048]{1,0:T(8,128)(2,1)S(1)}, bf16[240,2048]{1,0:T(8,128)(2,1)S(1)}, u32[]{:S(2)}, u32[]{:S(2)}) %collective-permute-start.11) | collective-permute-done | bytes 983072 | tf_op jit(solution)/shard_map/ppermute | solution.py:28
  197.0 8.9 %collective-permute-done.13.refs_7_ = bf16[160,2048]{1,0:T(8,128)(2,1)S(1)} collective-permute-done((bf16[160,2048]{1,0:T(8,128)(2,1)S(1)}, bf16[160,2048]{1,0:T(8,128)(2,1)S(1)}, u32[]{:S(2)}, u32[]{:S(2)}) %collective-permute-start.13) | collective-permute-done | bytes 655392 | tf_op jit(solution)/shard_map/ppermute | solution.py:28
  209.0 3.5 %weight_grads.1 = (bf16[192,2048]{1,0:T(8,128)(2,1)}, bf16[192,2048]{1,0:T(8,128)(2,1)}) custom-call(bf16[384,256]{1,0:T(8,128)(2,1)S(1)} %copy-done.4, bf16[240,2048]{1,0:T(8,128)(2,1)S(1)} %collective-permute-done.10.refs_1_, bf16[240,2048]{1,0:T(8,128)(2,1)S(1)} %collective-permute-done.11.refs_2_, ...), custom_call_target="tpu_custom_call" | custom-call | flops 1610612736 | bytes 5767168 | tf_op jit(solution)/shard_map/weight_grads/pallas_call | solution.py:326
  (73 shorter events, 60.3 us)
Async XLA Ops:
  2.4 59.4 %copy-start.8 = (bf16[576,2048]{1,0:T(8,128)(2,1)}, bf16[576,2048]{1,0:T(8,128)(2,1)S(1)}, u32[]{:S(2)}) copy-start(bf16[576,2048]{1,0:T(8,128)(2,1)S(1)} %pad_maximum_fusion.refs_3_) | copy-start | bytes 7077892
  2.4 59.4 %collective-permute-start.2 = (bf16[576,2048]{1,0:T(8,128)(2,1)S(1)}, bf16[576,2048]{1,0:T(8,128)(2,1)}, u32[]{:S(2)}, u32[]{:S(2)}) collective-permute-start(bf16[576,2048]{1,0:T(8,128)(2,1)S(1)} %pad_maximum_fusion.refs_3_), channel_id=1, source_target_pairs={{0,1},{1,2},{2,3},{3,0},{4,5},{5,6},{6,7},{7,4},{8,9},{9,10},{10,1... | collective-permute-start | bytes 7077896 | tf_op jit(solution)/shard_map/ppermute | solution.py:28
  10.2 51.6 %collective-permute-start.3 = (bf16[576,2048]{1,0:T(8,128)(2,1)S(1)}, bf16[576,2048]{1,0:T(8,128)(2,1)}, u32[]{:S(2)}, u32[]{:S(2)}) collective-permute-start(bf16[576,2048]{1,0:T(8,128)(2,1)S(1)} %pad_maximum_fusion.refs_3_), channel_id=1, source_target_pairs={{0,3},{1,0},{2,1},{3,2},{4,7},{5,4},{6,5},{7,6},{8,11},{9,8},{10,9... | collective-permute-start | bytes 7077896 | tf_op jit(solution)/shard_map/ppermute | solution.py:28
  42.5 14.9 %collective-permute-start = (bf16[64,4224]{1,0:T(8,128)(2,1)S(1)}, bf16[64,4224]{1,0:T(8,128)(2,1)}, u32[]{:S(2)}, u32[]{:S(2)}) collective-permute-start(bf16[64,4224]{1,0:T(8,128)(2,1)S(1)} %all_gather.3.refs_1_), channel_id=1, source_target_pairs={{0,4},{4,8},{8,12},{12,16},{16,20},{20,24},{24,28},{28,256},{256,2... | collective-permute-start | bytes 1622024 | tf_op jit(solution)/shard_map/ppermute | solution.py:28
  46.2 12.3 %collective-permute-start.1 = (bf16[64,4224]{1,0:T(8,128)(2,1)S(1)}, bf16[64,4224]{1,0:T(8,128)(2,1)}, u32[]{:S(2)}, u32[]{:S(2)}) collective-permute-start(bf16[64,4224]{1,0:T(8,128)(2,1)S(1)} %all_gather.3.refs_1_), channel_id=1, source_target_pairs={{0,284},{4,0},{8,4},{12,8},{16,12},{20,16},{24,20},{28,24},{256,28... | collective-permute-start | bytes 1622024 | tf_op jit(solution)/shard_map/ppermute | solution.py:28
  52.9 15.0 %all-to-all-start = ((bf16[8,8,4224]{2,1,0:T(8,128)(2,1)}), bf16[8,8,4224]{2,1,0:T(8,128)(2,1)S(1)}, u32[]{:S(2)}, u32[]{:S(2)}) async-start(bf16[8,8,4224]{2,1,0:T(8,128)(2,1)} %bitcast.30), calls=%async_computation | async-start | bytes 1081344 | tf_op jit(solution)/shard_map/all_to_all | solution.py:386
  67.9 33.7 %copy-start.2 = (bf16[8,8,4224]{2,1,0:T(8,128)(2,1)}, bf16[8,8,4224]{2,1,0:T(8,128)(2,1)S(1)}, u32[]{:S(2)}) copy-start(bf16[8,8,4224]{2,1,0:T(8,128)(2,1)S(1)} %all-to-all-done) | copy-start | bytes 1622020
  67.9 36.8 %all-to-all-start.1 = ((bf16[8,16,4224]{2,1,0:T(8,128)(2,1)}), bf16[8,16,4224]{2,1,0:T(8,128)(2,1)S(1)}, u32[]{:S(2)}, u32[]{:S(2)}) async-start(bf16[8,16,4224]{2,1,0:T(8,128)(2,1)} %bitcast.28), calls=%async_computation.1 | async-start | bytes 2162688 | tf_op jit(solution)/shard_map/all_to_all | solution.py:386
  73.9 41.3 %collective-permute-start.6 = (bf16[288,2048]{1,0:T(8,128)(2,1)}, bf16[288,2048]{1,0:T(8,128)(2,1)}, u32[]{:S(2)}, u32[]{:S(2)}) collective-permute-start(bf16[288,2048]{1,0:T(8,128)(2,1)} %slice.47), channel_id=1, source_target_pairs={{0,3},{1,0},{2,1},{3,2},{4,7},{5,4},{6,5},{7,6},{8,11},{9,8},{10,9... | collective-permute-start | bytes 3538952 | tf_op jit(solution)/shard_map/ppermute | solution.py:28
  79.0 36.2 %collective-permute-start.7 = (bf16[288,2048]{1,0:T(8,128)(2,1)}, bf16[288,2048]{1,0:T(8,128)(2,1)}, u32[]{:S(2)}, u32[]{:S(2)}) collective-permute-start(bf16[288,2048]{1,0:T(8,128)(2,1)} %slice.48), channel_id=1, source_target_pairs={{0,1},{1,2},{2,3},{3,0},{4,5},{5,6},{6,7},{7,4},{8,9},{9,10},{10,1... | collective-permute-start | bytes 3538952 | tf_op jit(solution)/shard_map/ppermute | solution.py:28
  84.3 11.0 %collective-permute-start.4 = (bf16[32,4224]{1,0:T(8,128)(2,1)S(1)}, bf16[32,4224]{1,0:T(8,128)(2,1)S(1)}, u32[]{:S(2)}, u32[]{:S(2)}) collective-permute-start(bf16[32,4224]{1,0:T(8,128)(2,1)S(1)} %slice.60), channel_id=1, source_target_pairs={{0,284},{4,0},{8,4},{12,8},{16,12},{20,16},{24,20},{28,24},{256,28... | collective-permute-start | bytes 811016 | tf_op jit(solution)/shard_map/ppermute | solution.py:28
  90.4 11.2 %collective-permute-start.5 = (bf16[32,4224]{1,0:T(8,128)(2,1)S(1)}, bf16[32,4224]{1,0:T(8,128)(2,1)S(1)}, u32[]{:S(2)}, u32[]{:S(2)}) collective-permute-start(bf16[32,4224]{1,0:T(8,128)(2,1)S(1)} %slice.61), channel_id=1, source_target_pairs={{0,4},{4,8},{8,12},{12,16},{16,20},{20,24},{24,28},{28,256},{256,2... | collective-permute-start | bytes 811016 | tf_op jit(solution)/shard_map/ppermute | solution.py:28
  104.8 15.1 %all-to-all-start.2 = ((bf16[8,8,4224]{2,1,0:T(8,128)(2,1)}), bf16[8,8,4224]{2,1,0:T(8,128)(2,1)}, u32[]{:S(2)}, u32[]{:S(2)}) async-start(bf16[8,8,4224]{2,1,0:T(8,128)(2,1)} %bitcast.29), calls=%async_computation.2 | async-start | bytes 1081344 | tf_op jit(solution)/shard_map/all_to_all | solution.py:386
  109.3 22.6 %collective-permute-start.8 = (bf16[192,2048]{1,0:T(8,128)(2,1)S(1)}, bf16[192,2048]{1,0:T(8,128)(2,1)S(1)}, u32[]{:S(2)}, u32[]{:S(2)}) collective-permute-start(bf16[192,2048]{1,0:T(8,128)(2,1)S(1)} %pad_maximum_fusion.1.refs_4_), channel_id=1, source_target_pairs={{0,1},{1,2},{2,3},{3,0},{4,5},{5,6},{6,7},{7,4},{8,9},{9,10},{10,1... | collective-permute-start | bytes 2359304 | tf_op jit(solution)/shard_map/ppermute | solution.py:28
  111.6 22.8 %collective-permute-start.9 = (bf16[192,2048]{1,0:T(8,128)(2,1)S(1)}, bf16[192,2048]{1,0:T(8,128)(2,1)S(1)}, u32[]{:S(2)}, u32[]{:S(2)}) collective-permute-start(bf16[192,2048]{1,0:T(8,128)(2,1)S(1)} %pad_maximum_fusion.1.refs_4_), channel_id=1, source_target_pairs={{0,3},{1,0},{2,1},{3,2},{4,7},{5,4},{6,5},{7,6},{8,11},{9,8},{10,9... | collective-permute-start | bytes 2359304 | tf_op jit(solution)/shard_map/ppermute | solution.py:28
  136.6 80.6 %all-to-all-start.3 = ((bf16[128,2,2176]{2,1,0:T(2,128)(2,1)}), bf16[128,2,2176]{2,1,0:T(2,128)(2,1)}, u32[]{:S(2)}, u32[]{:S(2)}) async-start(bf16[128,2,2176]{2,1,0:T(2,128)(2,1)} %reshape.71), calls=%async_computation.3 | async-start | bytes 2228224 | tf_op jit(solution)/shard_map/all_to_all | solution.py:410
  155.4 26.6 %collective-permute-start.10 = (bf16[240,2048]{1,0:T(8,128)(2,1)S(1)}, bf16[240,2048]{1,0:T(8,128)(2,1)S(1)}, u32[]{:S(2)}, u32[]{:S(2)}) collective-permute-start(bf16[240,2048]{1,0:T(8,128)(2,1)S(1)} %get-tuple-element.53), channel_id=1, source_target_pairs={{0,1},{1,2},{2,3},{3,0},{4,5},{5,6},{6,7},{7,4},{8,9},{9,10},{10,1... | collective-permute-start | bytes 2949128 | tf_op jit(solution)/shard_map/ppermute | solution.py:28
  157.3 37.6 %collective-permute-start.11 = (bf16[240,2048]{1,0:T(8,128)(2,1)S(1)}, bf16[240,2048]{1,0:T(8,128)(2,1)S(1)}, u32[]{:S(2)}, u32[]{:S(2)}) collective-permute-start(bf16[240,2048]{1,0:T(8,128)(2,1)S(1)} %get-tuple-element.54), channel_id=1, source_target_pairs={{0,3},{1,0},{2,1},{3,2},{4,7},{5,4},{6,5},{7,6},{8,11},{9,8},{10,9... | collective-permute-start | bytes 2949128 | tf_op jit(solution)/shard_map/ppermute | solution.py:28
  162.3 34.7 %collective-permute-start.12 = (bf16[112,2048]{1,0:T(8,128)(2,1)S(1)}, bf16[112,2048]{1,0:T(8,128)(2,1)S(1)}, u32[]{:S(2)}, u32[]{:S(2)}) collective-permute-start(bf16[112,2048]{1,0:T(8,128)(2,1)S(1)} %pad_maximum_fusion.5), channel_id=1, source_target_pairs={{0,2},{1,3},{2,0},{3,1},{4,6},{5,7},{6,4},{7,5},{8,10},{9,11},{10,... | collective-permute-start | bytes 1376264 | tf_op jit(solution)/shard_map/ppermute | solution.py:28
  165.3 43.7 %copy-start.4 = (bf16[384,256]{1,0:T(8,128)(2,1)S(1)}, bf16[384,256]{1,0:T(8,128)(2,1)}, u32[]{:S(2)}) copy-start(bf16[384,256]{1,0:T(8,128)(2,1)} %get-tuple-element.49.refs_0_) | copy-start | bytes 589828
  165.3 40.6 %collective-permute-start.13 = (bf16[160,2048]{1,0:T(8,128)(2,1)S(1)}, bf16[160,2048]{1,0:T(8,128)(2,1)S(1)}, u32[]{:S(2)}, u32[]{:S(2)}) collective-permute-start(bf16[160,2048]{1,0:T(8,128)(2,1)S(1)} %get-tuple-element.66), channel_id=1, source_target_pairs={{0,1},{1,2},{2,3},{3,0},{4,5},{5,6},{6,7},{7,4},{8,9},{9,10},{10,1... | collective-permute-start | bytes 1966088 | tf_op jit(solution)/shard_map/ppermute | solution.py:28
  169.7 39.3 %collective-permute-start.14 = (bf16[160,2048]{1,0:T(8,128)(2,1)S(1)}, bf16[160,2048]{1,0:T(8,128)(2,1)S(1)}, u32[]{:S(2)}, u32[]{:S(2)}) collective-permute-start(bf16[160,2048]{1,0:T(8,128)(2,1)S(1)} %get-tuple-element.65), channel_id=1, source_target_pairs={{0,3},{1,0},{2,1},{3,2},{4,7},{5,4},{6,5},{7,6},{8,11},{9,8},{10,9... | collective-permute-start | bytes 1966088 | tf_op jit(solution)/shard_map/ppermute | solution.py:28
  182.1 30.8 %collective-permute-start.15 = (bf16[96,2048]{1,0:T(8,128)(2,1)S(1)}, bf16[96,2048]{1,0:T(8,128)(2,1)S(1)}, u32[]{:S(2)}, u32[]{:S(2)}) collective-permute-start(bf16[96,2048]{1,0:T(8,128)(2,1)S(1)} %add_convert_fusion.3), channel_id=1, source_target_pairs={{0,1},{1,2},{2,3},{3,0},{4,5},{5,6},{6,7},{7,4},{8,9},{9,10},{10,1... | collective-permute-start | bytes 1179656 | tf_op jit(solution)/shard_map/ppermute | solution.py:28
  195.1 20.9 %collective-permute-start.16 = (bf16[96,2048]{1,0:T(8,128)(2,1)S(1)}, bf16[96,2048]{1,0:T(8,128)(2,1)S(1)}, u32[]{:S(2)}, u32[]{:S(2)}) collective-permute-start(bf16[96,2048]{1,0:T(8,128)(2,1)S(1)} %add_convert_fusion.1), channel_id=1, source_target_pairs={{0,3},{1,0},{2,1},{3,2},{4,7},{5,4},{6,5},{7,6},{8,11},{9,8},{10,9... | collective-permute-start | bytes 1179656 | tf_op jit(solution)/shard_map/ppermute | solution.py:28
  (10 other events, 45.3 us)

commit v9 on v8

--- a/solution.py
+++ b/solution.py
@@ -238,7 +238,7 @@
 
 
 def down_kernel(
-    s_ref, a_ref, b_ref, c_ref, dl_ref, dr_ref, own_ref, go_ref, come_ref, right_ref, left_ref, rows
+    s_ref, a_ref, b_ref, c_ref, dl_ref, dr_ref, dt_ref, own_ref, go_ref, come_ref, right_ref, left_ref, rows
 ):
     quarter = a_ref.shape[0]
     rows[0:quarter, :] = a_ref[...]
@@ -252,31 +252,33 @@
     two = dot(s_ref[3], grads, 1, 0).astype(BF)
     go_ref[:half, :] = two[:half]
     go_ref[half : 2 * half, :] = right[half:]
-    go_ref[2 * half :, :] = dr_ref[...]
+    end = 2 * half + dr_ref.shape[0]
+    most = go_ref.shape[0] - end
+    go_ref[2 * half : end, :] = dr_ref[...]
+    go_ref[end:, :] = dt_ref[:most, :]
     come_ref[:half, :] = left[:half]
     come_ref[half : 2 * half, :] = two[half:]
-    come_ref[2 * half :, :] = dl_ref[...]
+    come_ref[2 * half : end, :] = dl_ref[...]
+    come_ref[end:, :] = dt_ref[most:, :]
     right_ref[...] = right[:half]
     left_ref[...] = left[half:]
 
 
-def down_call(scaled, chunks, d_left, d_right, features):
+def down_call(scaled, chunks, d_left, d_right, d_two, features):
     tile = 512
     n, hid, count = scaled.shape
     first = features // tile
     tiled = [pl.BlockSpec((c.shape[0], tile), lambda j: (0, first + j)) for c in chunks]
     extra = d_left.shape[0]
-    tiled += [pl.BlockSpec((extra, tile), lambda j: (0, j))] * 2
+    tiled += [pl.BlockSpec((extra, tile), lambda j: (0, j))] * 3
+    sizes = [hid, hid + extra + 2 * extra // 3, hid + extra + extra // 3, hid // 2, hid // 2]
     return pl.pallas_call(
         down_kernel,
         grid=(features // tile,),
         out_shape=[jax.ShapeDtypeStruct((hid, features), F32)]
-        + [jax.ShapeDtypeStruct((hid + extra, features), BF)] * 2
-        + [jax.ShapeDtypeStruct((hid // 2, features), BF)] * 2,
+        + [jax.ShapeDtypeStruct((size, features), BF) for size in sizes[1:]],
         in_specs=[pl.BlockSpec(scaled.shape, lambda j: (0, 0, 0))] + tiled,
-        out_specs=[pl.BlockSpec((hid, tile), lambda j: (0, j))]
-        + [pl.BlockSpec((hid + extra, tile), lambda j: (0, j))] * 2
-        + [pl.BlockSpec((hid // 2, tile), lambda j: (0, j))] * 2,
+        out_specs=[pl.BlockSpec((size, tile), lambda j: (0, j)) for size in sizes],
         scratch_shapes=[pltpu.VMEM((count, tile), BF)],
         compiler_params=pltpu.CompilerParams(vmem_limit_bytes=24 * MIB),
         cost_estimate=pl.CostEstimate(
@@ -285,44 +287,51 @@
             transcendentals=0,
         ),
         name="down_parts",
-    )(scaled, *chunks, d_left, d_right)
+    )(scaled, *chunks, d_left, d_right, d_two)
 
 
 def weights_kernel(*refs):
-    d_refs, x_refs, (gate_ref, up_ref, factors, rows) = refs[:4], refs[4:11], refs[11:]
-    own, left, right, more_left, more_right, last, two = x_refs
+    d_refs, x_refs, (gate_ref, up_ref, factors, rows) = refs[:5], refs[5:13], refs[13:]
+    own, left, right, more_left, more_right, last, two_a, two_b = x_refs
     hid = gate_ref.shape[0]
     most, mid = own.shape[0], own.shape[0] // 2
-    count = rows.shape[1]
+    count, ends = rows.shape[1], last.shape[0]
+    size = d_refs[1].shape[0]
+    top = d_refs[3].shape[0]
 
     @pl.when(pl.program_id(0) == 0)
     def _():
         factors[0] = d_refs[0][...]
-        for q in range(1, 4):
-            size = d_refs[q].shape[0]
-            for j in range(d_refs[q].shape[1] // count):
-                factors[q, j * size : (j + 1) * size, :] = d_refs[q][:, j * count : (j + 1) * count]
+        for j in range(d_refs[1].shape[1] // count):
+            part, at = slice(j * count, (j + 1) * count), j * size
+            for q in (1, 2):
+                factors[q, at : at + size, :] = d_refs[q][:, part]
+            factors[3, at : at + top, :] = d_refs[3][:, part]
+            factors[3, at + top : at + size, :] = d_refs[4][:, part]
 
     for q, (first, end) in enumerate(((own, last), (left, more_left), (right, more_right))):
         rows[q, :most, :] = first[...]
-        rows[q, most:, :] = end[end.shape[0] - last.shape[0] :, :]
+        rows[q, most:, :] = end[end.shape[0] - ends :, :]
     rows[3, :mid, :] = more_right[:mid, :]
     rows[3, mid:most, :] = more_left[:mid, :]
-    rows[3, most:, :] = two[two.shape[0] - last.shape[0] :, :]
+    rows[3, most : most + ends // 2, :] = two_a[two_a.shape[0] - ends // 2 :, :]
+    rows[3, most + ends // 2 :, :] = two_b[two_b.shape[0] - ends // 2 :, :]
     total = sum(dot(factors[q], rows[q], 1, 0) for q in range(4)).astype(BF)
     gate_ref[...] = total[:hid]
     up_ref[...] = total[hid:]
 
 
-def weights_call(d_own, from_left, from_right, from_two, xs):
+def weights_call(d_own, from_left, from_right, two_a, two_b, half, xs):
     tile = 512
     n, (both, count), features = 4, d_own.shape, xs[0].shape[1]
     hid, size = both // 2, both * count // features
-    last = from_left.shape[0] // size - 1
-    packed = [
-        pl.BlockSpec((size, features), lambda j, at=at: (at, 0)) for at in (last, last, 0)
-    ]
-    tiled = [pl.BlockSpec((x.shape[0], tile), lambda j: (0, j)) for x in [*xs, from_two]]
+    top, low = 2 * size // 3, size // 3
+
+    def piece(rows, first):
+        return pl.BlockSpec((rows, features), lambda j: (first // rows, 0))
+
+    packed = [piece(size, 2 * half), piece(size, 2 * half), piece(top, half), piece(low, half)]
+    tiled = [pl.BlockSpec((x.shape[0], tile), lambda j: (0, j)) for x in [*xs, two_a, two_b]]
     return pl.pallas_call(
         weights_kernel,
         grid=(features // tile,),
@@ -337,7 +346,7 @@
             transcendentals=0,
         ),
         name="weight_grads",
-    )(d_own, from_left, from_right, from_two, *xs, from_two)
+    )(d_own, from_left, from_right, two_a, two_b, *xs, two_a, two_b)
 
 
 def home_kernel(code_ref, home_ref, grad_ref, score_ref):
@@ -412,25 +421,35 @@
     ).reshape(back.shape)
     mid = x_ab.shape[0] // 2
     x_c = rows_c[:, :features]
-    from_two = shift(jnp.concatenate([d_two, x_c], axis=0), 2, "x", n)
     more_left = shift(jnp.concatenate([x_left[mid:], x_c], axis=0), 1, "x", n)
     more_right = shift(jnp.concatenate([x_right[:mid], x_c], axis=0), -1, "x", n)
 
-    p_own, p_go, p_come, p_right, p_left = down_call(scaled, chunks, d_left, d_right, features)
+    scaled, more_left, more_right = lax.optimization_barrier((scaled, more_left, more_right))
+    p_own, p_go, p_come, p_right, p_left = down_call(
+        scaled, chunks, d_left, d_right, d_two, features
+    )
     from_left, from_right = shift(p_go, 1, "x", n), shift(p_come, -1, "x", n)
+    passed = 2 * half + d_left.shape[0]
+    last = x_c.shape[0] // 2
     p_right = (p_right.astype(F32) + from_left[:half].astype(F32)).astype(BF)
     p_left = (p_left.astype(F32) + from_right[half : 2 * half].astype(F32)).astype(BF)
-    left_top, right_low = shift(p_right, 1, "x", n), shift(p_left, -1, "x", n)
+    two_a = shift(
+        jnp.concatenate([p_right, from_left[passed:], more_left[mid : mid + last]], axis=0),
+        1, "x", n,
+    )
+    two_b = shift(
+        jnp.concatenate([p_left, from_right[passed:], more_right[mid + last :]], axis=0),
+        -1, "x", n,
+    )
     grad_down = jnp.concatenate(
         [
-            p_own[:half] + left_top.astype(F32) + from_right[:half].astype(F32),
-            p_own[half:] + from_left[half : 2 * half].astype(F32) + right_low.astype(F32),
+            p_own[:half] + two_a[:half].astype(F32) + from_right[:half].astype(F32),
+            p_own[half:] + from_left[half : 2 * half].astype(F32) + two_b[:half].astype(F32),
         ],
         axis=0,
     ).astype(BF)
-    grad_gate, grad_up = weights_call(
-        d_own, from_left, from_right, from_two, [x_ab, x_left, x_right, more_left, more_right, x_c]
-    )
+    xs = [x_ab, x_left, x_right, more_left, more_right, x_c]
+    grad_gate, grad_up = weights_call(d_own, from_left, from_right, two_a, two_b, half, xs)
 
     token_grad, slot_score = home_call(code, home, features)
     return (token_grad, slot_score.T, grad_gate[None], grad_up[None], grad_down[None])

time: 223 us -> 226 us (1.013)
    ppermute x17 -> x16, waiting for transfers between devices: 46.9 us -> 48.5 us  [shift(): return lax.ppermute(block, axes, [(i, (i + step) % n) for i in range(n)])]
    ppermute x17 -> x16, starting transfers between devices: 58.4 us -> 57.6 us  [shift(): return lax.ppermute(block, axes, [(i, (i + step) % n) for i in range(n)])]
    unnamed x26 -> x36, local copies, waits for them, and re-layouts: 4.59 us -> 4.36 us
  transfers between devices with their start and end apart: 21 -> 20, of which waited for: 13 -> 11; matrix products, arithmetic and copies ran while one was open for 5% -> 5% of each run, Pallas kernels for 13% -> 13%
where the time goes in v9:
time: 226 us; the launch traced here: 225 us
  starting transfers between devices  81.6 us (36%)
  waiting for transfers between devices  59.2 us (26%)
  Pallas kernels  31.5 us (14%)
  blocking collectives  28.5 us (13%)
  local copies, waits for them, and re-layouts  17.9 us (8%)
  other arithmetic  5.22 us (2%)
    ppermute x16, starting transfers between devices, shift(): return lax.ppermute(block, axes, [(i, (i + step) % n) for i in range(n)])  57.6 us
    ppermute x16, waiting for transfers between devices, shift(): return lax.ppermute(block, axes, [(i, (i + step) % n) for i in range(n)])  48.5 us
    all_gather x1, blocking collectives, local(): chunk = lax.all_gather(own, FAR, axis=0, tiled=True)  28.5 us
    all_to_all x3, starting transfers between devices, exchange(): lax.all_to_all(packed.reshape(8, rows // 8, width), YC, split_axis=0, con...  12.5 us
    pallas_call x1, Pallas kernels, rows_call(): pl.pallas_call(rows_kernel, out_shape=[jax.ShapeDtypeStruct((count, featu...  12.1 us
    all_to_all x1, starting transfers between devices, local(): lax.all_to_all(back.reshape(-1, CAPACITY, back.shape[1]), PLACE, split_ax...  11.5 us
    all_to_all x3, waiting for transfers between devices, exchange(): lax.all_to_all(packed.reshape(8, rows // 8, width), YC, split_axis=0, con...  10.7 us
    pallas_call x3, Pallas kernels, pack_call(): pl.pallas_call(body, out_shape=jax.ShapeDtypeStruct((rows, width), BF), i...  7.91 us
  transfers between devices with their start and end apart: 20, of which 11 were waited for; matrix products, arithmetic and copies ran while one was open for 5% of the time, Pallas kernels for 13%

profile of v9, /device:TPU:6, one launch (start us, length us, event | category | flops | bytes accessed | tf_op | source)
XLA Modules:
  0.0 225.0 jit_solution(3260571121799507435)
XLA Ops:
  2.4 7.8 %collective-permute-start.2 = (bf16[576,2048]{1,0:T(8,128)(2,1)S(1)}, bf16[576,2048]{1,0:T(8,128)(2,1)}, u32[]{:S(2)}, u32[]{:S(2)}) collective-permute-start(bf16[576,2048]{1,0:T(8,128)(2,1)S(1)} %pad_maximum_fusion.refs_3_), channel_id=1, source_target_pairs={{0,1},{1,2},{2,3},{3,0},{4,5},{5,6},{6,7},{7,4},{8,9},{9,10},{10,1... | collective-permute-start | bytes 7077896 | tf_op jit(solution)/shard_map/ppermute | solution.py:28
  14.0 28.5 %all_gather.3.refs_1_ = bf16[64,4224]{1,0:T(8,128)(2,1)S(1)} all-gather(bf16[16,4224]{1,0:T(8,128)(2,1)} %get-tuple-element.38), channel_id=1, replica_groups=mesh['zh'=2,'y'=4,'c'=2,'zq'=2,'zr'=4,'x'=4] {'zh','zq'}, dimensions={0}, use_global_device_ids=true | all-gather | bytes 675840 | tf_op jit(solution)/shard_map/all_gather | solution.py:390
  42.5 3.7 %collective-permute-start = (bf16[64,4224]{1,0:T(8,128)(2,1)S(1)}, bf16[64,4224]{1,0:T(8,128)(2,1)}, u32[]{:S(2)}, u32[]{:S(2)}) collective-permute-start(bf16[64,4224]{1,0:T(8,128)(2,1)S(1)} %all_gather.3.refs_1_), channel_id=1, source_target_pairs={{0,4},{4,8},{8,12},{12,16},{16,20},{20,24},{24,28},{28,256},{256,2... | collective-permute-start | bytes 1622024 | tf_op jit(solution)/shard_map/ppermute | solution.py:28
  46.2 3.8 %collective-permute-start.1 = (bf16[64,4224]{1,0:T(8,128)(2,1)S(1)}, bf16[64,4224]{1,0:T(8,128)(2,1)}, u32[]{:S(2)}, u32[]{:S(2)}) collective-permute-start(bf16[64,4224]{1,0:T(8,128)(2,1)S(1)} %all_gather.3.refs_1_), channel_id=1, source_target_pairs={{0,284},{4,0},{8,4},{12,8},{16,12},{20,16},{24,20},{28,24},{256,28... | collective-permute-start | bytes 1622024 | tf_op jit(solution)/shard_map/ppermute | solution.py:28
  52.9 4.5 %all-to-all-start = ((bf16[8,8,4224]{2,1,0:T(8,128)(2,1)}), bf16[8,8,4224]{2,1,0:T(8,128)(2,1)S(1)}, u32[]{:S(2)}, u32[]{:S(2)}) async-start(bf16[8,8,4224]{2,1,0:T(8,128)(2,1)} %bitcast.33), calls=%async_computation | async-start | bytes 1081344 | tf_op jit(solution)/shard_map/all_to_all | solution.py:395
  58.6 3.1 %pack.3 = bf16[128,4224]{1,0:T(8,128)(2,1)} custom-call(s32[3]{0:T(128)} %pad_add_fusion.refs_0_.zs_ref, bf16[64,4224]{1,0:T(8,128)(2,1)} %collective-permute-done.refs_1_, bf16[64,4224]{1,0:T(8,128)(2,1)} %collective-permute-done.1.refs_2_), custom_call_target="tpu_custom_call" | custom-call | tf_op jit(solution)/shard_map/pack/pallas_call | solution.py:126
  61.7 6.2 %all-to-all-done = bf16[8,8,4224]{2,1,0:T(8,128)(2,1)S(1)} async-done(((bf16[8,8,4224]{2,1,0:T(8,128)(2,1)}), bf16[8,8,4224]{2,1,0:T(8,128)(2,1)S(1)}, u32[]{:S(2)}, u32[]{:S(2)}) %all-to-all-start) | async-done | bytes 540704 | tf_op jit(solution)/shard_map/all_to_all | solution.py:395
  67.9 3.6 %all-to-all-start.1 = ((bf16[8,16,4224]{2,1,0:T(8,128)(2,1)}), bf16[8,16,4224]{2,1,0:T(8,128)(2,1)S(1)}, u32[]{:S(2)}, u32[]{:S(2)}) async-start(bf16[8,16,4224]{2,1,0:T(8,128)(2,1)} %bitcast.31), calls=%async_computation.1 | async-start | bytes 2162688 | tf_op jit(solution)/shard_map/all_to_all | solution.py:395
  73.9 2.7 %collective-permute-start.6 = (bf16[288,2048]{1,0:T(8,128)(2,1)}, bf16[288,2048]{1,0:T(8,128)(2,1)}, u32[]{:S(2)}, u32[]{:S(2)}) collective-permute-start(bf16[288,2048]{1,0:T(8,128)(2,1)} %slice.65), channel_id=1, source_target_pairs={{0,3},{1,0},{2,1},{3,2},{4,7},{5,4},{6,5},{7,6},{8,11},{9,8},{10,9... | collective-permute-start | bytes 3538952 | tf_op jit(solution)/shard_map/ppermute | solution.py:28
  79.0 4.3 %collective-permute-start.7 = (bf16[288,2048]{1,0:T(8,128)(2,1)}, bf16[288,2048]{1,0:T(8,128)(2,1)}, u32[]{:S(2)}, u32[]{:S(2)}) collective-permute-start(bf16[288,2048]{1,0:T(8,128)(2,1)} %slice.66), channel_id=1, source_target_pairs={{0,1},{1,2},{2,3},{3,0},{4,5},{5,6},{6,7},{7,4},{8,9},{9,10},{10,1... | collective-permute-start | bytes 3538952 | tf_op jit(solution)/shard_map/ppermute | solution.py:28
  84.3 5.1 %collective-permute-start.4 = (bf16[32,4224]{1,0:T(8,128)(2,1)S(1)}, bf16[32,4224]{1,0:T(8,128)(2,1)S(1)}, u32[]{:S(2)}, u32[]{:S(2)}) collective-permute-start(bf16[32,4224]{1,0:T(8,128)(2,1)S(1)} %slice.84), channel_id=1, source_target_pairs={{0,284},{4,0},{8,4},{12,8},{16,12},{20,16},{24,20},{28,24},{256,28... | collective-permute-start | bytes 811016 | tf_op jit(solution)/shard_map/ppermute | solution.py:28
  92.4 2.9 %collective-permute-done.4.refs_1_ = bf16[32,4224]{1,0:T(8,128)(2,1)S(1)} collective-permute-done((bf16[32,4224]{1,0:T(8,128)(2,1)S(1)}, bf16[32,4224]{1,0:T(8,128)(2,1)S(1)}, u32[]{:S(2)}, u32[]{:S(2)}) %collective-permute-start.4) | collective-permute-done | bytes 270368 | tf_op jit(solution)/shard_map/ppermute | solution.py:28
  95.3 6.3 %collective-permute-done.5.refs_2_ = bf16[32,4224]{1,0:T(8,128)(2,1)S(1)} collective-permute-done((bf16[32,4224]{1,0:T(8,128)(2,1)S(1)}, bf16[32,4224]{1,0:T(8,128)(2,1)S(1)}, u32[]{:S(2)}, u32[]{:S(2)}) %collective-permute-start.5) | collective-permute-done | bytes 270368 | tf_op jit(solution)/shard_map/ppermute | solution.py:28
  104.8 4.4 %all-to-all-start.2 = ((bf16[8,8,4224]{2,1,0:T(8,128)(2,1)}), bf16[8,8,4224]{2,1,0:T(8,128)(2,1)S(1)}, u32[]{:S(2)}, u32[]{:S(2)}) async-start(bf16[8,8,4224]{2,1,0:T(8,128)(2,1)} %bitcast.32), calls=%async_computation.2 | async-start | bytes 1081344 | tf_op jit(solution)/shard_map/all_to_all | solution.py:395
  111.6 3.6 %collective-permute-start.9 = (bf16[192,2048]{1,0:T(8,128)(2,1)S(1)}, bf16[192,2048]{1,0:T(8,128)(2,1)S(1)}, u32[]{:S(2)}, u32[]{:S(2)}) collective-permute-start(bf16[192,2048]{1,0:T(8,128)(2,1)S(1)} %pad_maximum_fusion.1.refs_5_), channel_id=1, source_target_pairs={{0,3},{1,0},{2,1},{3,2},{4,7},{5,4},{6,5},{7,6},{8,11},{9,8},{10,9... | collective-permute-start | bytes 2359304 | tf_op jit(solution)/shard_map/ppermute | solution.py:28
  115.2 4.5 %all-to-all-done.2 = bf16[8,8,4224]{2,1,0:T(8,128)(2,1)S(1)} async-done(((bf16[8,8,4224]{2,1,0:T(8,128)(2,1)}), bf16[8,8,4224]{2,1,0:T(8,128)(2,1)S(1)}, u32[]{:S(2)}, u32[]{:S(2)}) %all-to-all-start.2) | async-done | bytes 540704 | tf_op jit(solution)/shard_map/all_to_all | solution.py:395
  120.6 12.1 %rows.1 = (bf16[256,2176]{1,0:T(8,128)(2,1)}, bf16[384,256]{1,0:T(8,128)(2,1)}, bf16[48,2048]{1,0:T(8,128)(2,1)}, bf16[48,2048]{1,0:T(8,128)(2,1)}, bf16[48,2048...) custom-call(s32[3]{0:T(128)} %pad_add_fusion.refs_0_.zs_ref, bf16[64,4224]{1,0:T(8,128)(2,1)} %bitcast.26, ...), custom_call_target="tpu_custom_call" | custom-call | flops 4026531840 | bytes 12582912 | tf_op jit(solution)/shard_map/rows/pallas_call | solution.py:213
  138.8 3.9 %collective-permute-start.11 = (bf16[160,2048]{1,0:T(8,128)(2,1)}, bf16[160,2048]{1,0:T(8,128)(2,1)}, u32[]{:S(2)}, u32[]{:S(2)}) collective-permute-start(bf16[160,2048]{1,0:T(8,128)(2,1)} %get-tuple-element.71), channel_id=1, source_target_pairs={{0,3},{1,0},{2,1},{3,2},{4,7},{5,4},{6,5},{7,6},{8,11},{9,8},{10,9... | collective-permute-start | bytes 1966088 | tf_op jit(solution)/shard_map/ppermute | solution.py:28
  144.1 11.5 %all-to-all-start.3 = ((bf16[128,2,2176]{2,1,0:T(2,128)(2,1)}), bf16[128,2,2176]{2,1,0:T(2,128)(2,1)}, u32[]{:S(2)}, u32[]{:S(2)}) async-start(bf16[128,2,2176]{2,1,0:T(2,128)(2,1)} %reshape.71), calls=%async_computation.3 | async-start | bytes 2228224 | tf_op jit(solution)/shard_map/all_to_all | solution.py:419
  166.0 4.6 %collective-permute-start.12 = (bf16[272,2048]{1,0:T(8,128)(2,1)S(1)}, bf16[272,2048]{1,0:T(8,128)(2,1)S(1)}, u32[]{:S(2)}, u32[]{:S(2)}) collective-permute-start(bf16[272,2048]{1,0:T(8,128)(2,1)S(1)} %get-tuple-element.60), channel_id=1, source_target_pairs={{0,1},{1,2},{2,3},{3,0},{4,5},{5,6},{6,7},{7,4},{8,9},{9,10},{10,1... | collective-permute-start | bytes 3342344 | tf_op jit(solution)/shard_map/ppermute | solution.py:28
  172.5 17.7 %collective-permute-done.13.refs_2_ = bf16[256,2048]{1,0:T(8,128)(2,1)S(1)} collective-permute-done((bf16[256,2048]{1,0:T(8,128)(2,1)S(1)}, bf16[256,2048]{1,0:T(8,128)(2,1)S(1)}, u32[]{:S(2)}, u32[]{:S(2)}) %collective-permute-start.13) | collective-permute-done | bytes 1048608 | tf_op jit(solution)/shard_map/ppermute | solution.py:28
  193.0 5.7 %collective-permute-start.14 = (bf16[160,2048]{1,0:T(8,128)(2,1)S(1)}, bf16[160,2048]{1,0:T(8,128)(2,1)S(1)}, u32[]{:S(2)}, u32[]{:S(2)}) collective-permute-start(bf16[160,2048]{1,0:T(8,128)(2,1)S(1)} %pad_maximum_fusion.5), channel_id=1, source_target_pairs={{0,1},{1,2},{2,3},{3,0},{4,5},{5,6},{6,7},{7,4},{8,9},{9,10},{10,1... | collective-permute-start | bytes 1966088 | tf_op jit(solution)/shard_map/ppermute | solution.py:28
  200.7 13.5 %collective-permute-done.15.refs_4_.refs_12_ = bf16[144,2048]{1,0:T(8,128)(2,1)S(1)} collective-permute-done((bf16[144,2048]{1,0:T(8,128)(2,1)S(1)}, bf16[144,2048]{1,0:T(8,128)(2,1)S(1)}, u32[]{:S(2)}, u32[]{:S(2)}) %collective-permute-start.15) | collective-permute-done | bytes 589856 | tf_op jit(solution)/shard_map/ppermute | solution.py:28
  214.2 4.9 %weight_grads.1 = (bf16[192,2048]{1,0:T(8,128)(2,1)}, bf16[192,2048]{1,0:T(8,128)(2,1)}) custom-call(bf16[384,256]{1,0:T(8,128)(2,1)S(1)} %copy-done.12, bf16[272,2048]{1,0:T(8,128)(2,1)S(1)} %collective-permute-done.12.refs_1_, bf16[256,2048]{1,0:T(8,128)(2,1)S(1)} %collective-permute-done.13.refs_2_, ...), custom_call_target="tpu_custom_call" | custom-call | flops 1610612736 | bytes 5767168 | tf_op jit(solution)/shard_map/weight_grads/pallas_call | solution.py:335
  (86 shorter events, 54.8 us)
Async XLA Ops:
  2.4 50.5 %copy-start.13 = (bf16[576,2048]{1,0:T(8,128)(2,1)}, bf16[576,2048]{1,0:T(8,128)(2,1)S(1)}, u32[]{:S(2)}) copy-start(bf16[576,2048]{1,0:T(8,128)(2,1)S(1)} %pad_maximum_fusion.refs_3_) | copy-start | bytes 7077892
  2.4 59.3 %collective-permute-start.2 = (bf16[576,2048]{1,0:T(8,128)(2,1)S(1)}, bf16[576,2048]{1,0:T(8,128)(2,1)}, u32[]{:S(2)}, u32[]{:S(2)}) collective-permute-start(bf16[576,2048]{1,0:T(8,128)(2,1)S(1)} %pad_maximum_fusion.refs_3_), channel_id=1, source_target_pairs={{0,1},{1,2},{2,3},{3,0},{4,5},{5,6},{6,7},{7,4},{8,9},{9,10},{10,1... | collective-permute-start | bytes 7077896 | tf_op jit(solution)/shard_map/ppermute | solution.py:28
  10.2 51.5 %collective-permute-start.3 = (bf16[576,2048]{1,0:T(8,128)(2,1)S(1)}, bf16[576,2048]{1,0:T(8,128)(2,1)}, u32[]{:S(2)}, u32[]{:S(2)}) collective-permute-start(bf16[576,2048]{1,0:T(8,128)(2,1)S(1)} %pad_maximum_fusion.refs_3_), channel_id=1, source_target_pairs={{0,3},{1,0},{2,1},{3,2},{4,7},{5,4},{6,5},{7,6},{8,11},{9,8},{10,9... | collective-permute-start | bytes 7077896 | tf_op jit(solution)/shard_map/ppermute | solution.py:28
  42.5 14.9 %collective-permute-start = (bf16[64,4224]{1,0:T(8,128)(2,1)S(1)}, bf16[64,4224]{1,0:T(8,128)(2,1)}, u32[]{:S(2)}, u32[]{:S(2)}) collective-permute-start(bf16[64,4224]{1,0:T(8,128)(2,1)S(1)} %all_gather.3.refs_1_), channel_id=1, source_target_pairs={{0,4},{4,8},{8,12},{12,16},{16,20},{20,24},{24,28},{28,256},{256,2... | collective-permute-start | bytes 1622024 | tf_op jit(solution)/shard_map/ppermute | solution.py:28
  46.2 12.3 %collective-permute-start.1 = (bf16[64,4224]{1,0:T(8,128)(2,1)S(1)}, bf16[64,4224]{1,0:T(8,128)(2,1)}, u32[]{:S(2)}, u32[]{:S(2)}) collective-permute-start(bf16[64,4224]{1,0:T(8,128)(2,1)S(1)} %all_gather.3.refs_1_), channel_id=1, source_target_pairs={{0,284},{4,0},{8,4},{12,8},{16,12},{20,16},{24,20},{28,24},{256,28... | collective-permute-start | bytes 1622024 | tf_op jit(solution)/shard_map/ppermute | solution.py:28
  52.9 15.0 %all-to-all-start = ((bf16[8,8,4224]{2,1,0:T(8,128)(2,1)}), bf16[8,8,4224]{2,1,0:T(8,128)(2,1)S(1)}, u32[]{:S(2)}, u32[]{:S(2)}) async-start(bf16[8,8,4224]{2,1,0:T(8,128)(2,1)} %bitcast.33), calls=%async_computation | async-start | bytes 1081344 | tf_op jit(solution)/shard_map/all_to_all | solution.py:395
  67.9 33.7 %copy-start.2 = (bf16[8,8,4224]{2,1,0:T(8,128)(2,1)}, bf16[8,8,4224]{2,1,0:T(8,128)(2,1)S(1)}, u32[]{:S(2)}) copy-start(bf16[8,8,4224]{2,1,0:T(8,128)(2,1)S(1)} %all-to-all-done) | copy-start | bytes 1622020
  67.9 36.9 %all-to-all-start.1 = ((bf16[8,16,4224]{2,1,0:T(8,128)(2,1)}), bf16[8,16,4224]{2,1,0:T(8,128)(2,1)S(1)}, u32[]{:S(2)}, u32[]{:S(2)}) async-start(bf16[8,16,4224]{2,1,0:T(8,128)(2,1)} %bitcast.31), calls=%async_computation.1 | async-start | bytes 2162688 | tf_op jit(solution)/shard_map/all_to_all | solution.py:395
  73.9 45.9 %collective-permute-start.6 = (bf16[288,2048]{1,0:T(8,128)(2,1)}, bf16[288,2048]{1,0:T(8,128)(2,1)}, u32[]{:S(2)}, u32[]{:S(2)}) collective-permute-start(bf16[288,2048]{1,0:T(8,128)(2,1)} %slice.65), channel_id=1, source_target_pairs={{0,3},{1,0},{2,1},{3,2},{4,7},{5,4},{6,5},{7,6},{8,11},{9,8},{10,9... | collective-permute-start | bytes 3538952 | tf_op jit(solution)/shard_map/ppermute | solution.py:28
  79.0 40.8 %collective-permute-start.7 = (bf16[288,2048]{1,0:T(8,128)(2,1)}, bf16[288,2048]{1,0:T(8,128)(2,1)}, u32[]{:S(2)}, u32[]{:S(2)}) collective-permute-start(bf16[288,2048]{1,0:T(8,128)(2,1)} %slice.66), channel_id=1, source_target_pairs={{0,1},{1,2},{2,3},{3,0},{4,5},{5,6},{6,7},{7,4},{8,9},{9,10},{10,1... | collective-permute-start | bytes 3538952 | tf_op jit(solution)/shard_map/ppermute | solution.py:28
  84.3 11.0 %collective-permute-start.4 = (bf16[32,4224]{1,0:T(8,128)(2,1)S(1)}, bf16[32,4224]{1,0:T(8,128)(2,1)S(1)}, u32[]{:S(2)}, u32[]{:S(2)}) collective-permute-start(bf16[32,4224]{1,0:T(8,128)(2,1)S(1)} %slice.84), channel_id=1, source_target_pairs={{0,284},{4,0},{8,4},{12,8},{16,12},{20,16},{24,20},{28,24},{256,28... | collective-permute-start | bytes 811016 | tf_op jit(solution)/shard_map/ppermute | solution.py:28
  90.4 11.2 %collective-permute-start.5 = (bf16[32,4224]{1,0:T(8,128)(2,1)S(1)}, bf16[32,4224]{1,0:T(8,128)(2,1)S(1)}, u32[]{:S(2)}, u32[]{:S(2)}) collective-permute-start(bf16[32,4224]{1,0:T(8,128)(2,1)S(1)} %slice.85), channel_id=1, source_target_pairs={{0,4},{4,8},{8,12},{12,16},{16,20},{20,24},{24,28},{28,256},{256,2... | collective-permute-start | bytes 811016 | tf_op jit(solution)/shard_map/ppermute | solution.py:28
  104.8 15.0 %all-to-all-start.2 = ((bf16[8,8,4224]{2,1,0:T(8,128)(2,1)}), bf16[8,8,4224]{2,1,0:T(8,128)(2,1)S(1)}, u32[]{:S(2)}, u32[]{:S(2)}) async-start(bf16[8,8,4224]{2,1,0:T(8,128)(2,1)} %bitcast.32), calls=%async_computation.2 | async-start | bytes 1081344 | tf_op jit(solution)/shard_map/all_to_all | solution.py:395
  109.4 23.3 %collective-permute-start.8 = (bf16[192,2048]{1,0:T(8,128)(2,1)S(1)}, bf16[192,2048]{1,0:T(8,128)(2,1)}, u32[]{:S(2)}, u32[]{:S(2)}) collective-permute-start(bf16[192,2048]{1,0:T(8,128)(2,1)S(1)} %pad_maximum_fusion.1.refs_5_), channel_id=1, source_target_pairs={{0,1},{1,2},{2,3},{3,0},{4,5},{5,6},{6,7},{7,4},{8,9},{9,10},{10,1... | collective-permute-start | bytes 2359304 | tf_op jit(solution)/shard_map/ppermute | solution.py:28
  111.6 22.8 %collective-permute-start.9 = (bf16[192,2048]{1,0:T(8,128)(2,1)S(1)}, bf16[192,2048]{1,0:T(8,128)(2,1)S(1)}, u32[]{:S(2)}, u32[]{:S(2)}) collective-permute-start(bf16[192,2048]{1,0:T(8,128)(2,1)S(1)} %pad_maximum_fusion.1.refs_5_), channel_id=1, source_target_pairs={{0,3},{1,0},{2,1},{3,2},{4,7},{5,4},{6,5},{7,6},{8,11},{9,8},{10,9... | collective-permute-start | bytes 2359304 | tf_op jit(solution)/shard_map/ppermute | solution.py:28
  136.9 18.7 %collective-permute-start.10 = (bf16[160,2048]{1,0:T(8,128)(2,1)}, bf16[160,2048]{1,0:T(8,128)(2,1)}, u32[]{:S(2)}, u32[]{:S(2)}) collective-permute-start(bf16[160,2048]{1,0:T(8,128)(2,1)} %get-tuple-element.72), channel_id=1, source_target_pairs={{0,1},{1,2},{2,3},{3,0},{4,5},{5,6},{6,7},{7,4},{8,9},{9,10},{10,1... | collective-permute-start | bytes 1966088 | tf_op jit(solution)/shard_map/ppermute | solution.py:28
  138.8 19.5 %collective-permute-start.11 = (bf16[160,2048]{1,0:T(8,128)(2,1)}, bf16[160,2048]{1,0:T(8,128)(2,1)}, u32[]{:S(2)}, u32[]{:S(2)}) collective-permute-start(bf16[160,2048]{1,0:T(8,128)(2,1)} %get-tuple-element.71), channel_id=1, source_target_pairs={{0,3},{1,0},{2,1},{3,2},{4,7},{5,4},{6,5},{7,6},{8,11},{9,8},{10,9... | collective-permute-start | bytes 1966088 | tf_op jit(solution)/shard_map/ppermute | solution.py:28
  144.1 76.4 %all-to-all-start.3 = ((bf16[128,2,2176]{2,1,0:T(2,128)(2,1)}), bf16[128,2,2176]{2,1,0:T(2,128)(2,1)}, u32[]{:S(2)}, u32[]{:S(2)}) async-start(bf16[128,2,2176]{2,1,0:T(2,128)(2,1)} %reshape.71), calls=%async_computation.3 | async-start | bytes 2228224 | tf_op jit(solution)/shard_map/all_to_all | solution.py:419
  163.5 26.6 %collective-permute-start.13 = (bf16[256,2048]{1,0:T(8,128)(2,1)S(1)}, bf16[256,2048]{1,0:T(8,128)(2,1)S(1)}, u32[]{:S(2)}, u32[]{:S(2)}) collective-permute-start(bf16[256,2048]{1,0:T(8,128)(2,1)S(1)} %get-tuple-element.61), channel_id=1, source_target_pairs={{0,3},{1,0},{2,1},{3,2},{4,7},{5,4},{6,5},{7,6},{8,11},{9,8},{10,9... | collective-permute-start | bytes 3145736 | tf_op jit(solution)/shard_map/ppermute | solution.py:28
  166.0 26.8 %collective-permute-start.12 = (bf16[272,2048]{1,0:T(8,128)(2,1)S(1)}, bf16[272,2048]{1,0:T(8,128)(2,1)S(1)}, u32[]{:S(2)}, u32[]{:S(2)}) collective-permute-start(bf16[272,2048]{1,0:T(8,128)(2,1)S(1)} %get-tuple-element.60), channel_id=1, source_target_pairs={{0,1},{1,2},{2,3},{3,0},{4,5},{5,6},{6,7},{7,4},{8,9},{9,10},{10,1... | collective-permute-start | bytes 3342344 | tf_op jit(solution)/shard_map/ppermute | solution.py:28
  192.9 21.3 %copy-start.7 = (bf16[192,2048]{1,0:T(8,128)(2,1)S(1)}, bf16[192,2048]{1,0:T(8,128)(2,1)}, u32[]{:S(2)}) copy-start(bf16[192,2048]{1,0:T(8,128)(2,1)} %copy-done.6) | copy-start | bytes 2359300
  192.9 21.3 %copy-start.12 = (bf16[384,256]{1,0:T(8,128)(2,1)S(1)}, bf16[384,256]{1,0:T(8,128)(2,1)}, u32[]{:S(2)}) copy-start(bf16[384,256]{1,0:T(8,128)(2,1)} %get-tuple-element.52.refs_0_) | copy-start | bytes 589828
  193.0 21.2 %collective-permute-start.14 = (bf16[160,2048]{1,0:T(8,128)(2,1)S(1)}, bf16[160,2048]{1,0:T(8,128)(2,1)S(1)}, u32[]{:S(2)}, u32[]{:S(2)}) collective-permute-start(bf16[160,2048]{1,0:T(8,128)(2,1)S(1)} %pad_maximum_fusion.5), channel_id=1, source_target_pairs={{0,1},{1,2},{2,3},{3,0},{4,5},{5,6},{6,7},{7,4},{8,9},{9,10},{10,1... | collective-permute-start | bytes 1966088 | tf_op jit(solution)/shard_map/ppermute | solution.py:28
  198.8 15.4 %collective-permute-start.15 = (bf16[144,2048]{1,0:T(8,128)(2,1)S(1)}, bf16[144,2048]{1,0:T(8,128)(2,1)S(1)}, u32[]{:S(2)}, u32[]{:S(2)}) collective-permute-start(bf16[144,2048]{1,0:T(8,128)(2,1)S(1)} %pad_maximum_fusion.6), channel_id=1, source_target_pairs={{0,3},{1,0},{2,1},{3,2},{4,7},{5,4},{6,5},{7,6},{8,11},{9,8},{10,9... | collective-permute-start | bytes 1769480 | tf_op jit(solution)/shard_map/ppermute | solution.py:28
  (14 other events, 91.3 us)

commit v10 on v9

--- a/solution.py
+++ b/solution.py
@@ -147,8 +147,9 @@
 
 
 def rows_kernel(zs_ref, *refs):
-    (a_ref, b_ref, c_ref, *w_refs), p_ref, refs = refs[:8], refs[8], refs[9:]
-    d_refs, s_ref, (gu, dn, rows, d_all, sems) = refs[:4], refs[4], refs[5:]
+    (a_ref, b_ref, c_ref, *w_refs), refs = refs[:8], refs[8:]
+    p_ref, d_ref, s_ref, go_ref, come_ref, right_ref, left_ref = refs[:7]
+    gu, dn, rows, d_all, s_all, sems = refs[7:]
     hid = dn.shape[1]
     count, width = rows.shape
     features = (width - LANES) // 2
@@ -189,42 +190,63 @@
         d_gate = d_hidden * up_pre * sigma * (1.0 + gate_pre * (1.0 - sigma))
         d_all[first : first + hid, :] = d_gate.astype(BF)
         d_all[first + hid : first + 2 * hid, :] = (d_hidden * active).astype(BF)
-        if q == 0:
-            d_refs[0][...] = d_all[: 2 * hid, :]
-        else:
-            size = d_refs[q].shape[0]
-            for j in range(features // count):
-                d_refs[q][:, j * count : (j + 1) * count] = d_all[
-                    first + j * size : first + (j + 1) * size, :
-                ]
-        s_ref[q] = (coef * hidden).astype(BF)
+        s_all[q] = (coef * hidden).astype(BF)
     moved = dot(d_all[...], home, 1, 0).astype(BF)
     tile = 512
     for j in range(0, features, tile):
         p_ref[:, j : j + tile] = dot(moved, gu[:, j : j + tile], 0, 0).astype(BF)
     score = dot(jnp.broadcast_to(score, (LANES, count)).astype(BF), home, 1, 0)
     p_ref[:, features:] = score.T.astype(BF)
+    d_ref[...] = d_all[: 2 * hid, :]
+    s_ref[...] = s_all[0]
+    half, size = hid // 2, 2 * hid * count // features
+    most, end = 2 * size // 3, hid + size
+    for j in range(features // count):
+        part, at = slice(j * count, (j + 1) * count), j * size
+        left, right, two = 2 * hid + at, 4 * hid + at, 6 * hid + at
+        come_ref[hid:end, part] = d_all[left : left + size, :]
+        go_ref[hid:end, part] = d_all[right : right + size, :]
+        go_ref[end : end + most, part] = d_all[two : two + most, :]
+        come_ref[end : end + size - most, part] = d_all[two + most : two + size, :]
+    go_ref[end + most :, :] = rows[3 * quarter :, :features]
+    come_ref[end + size - most :, :] = rows[3 * quarter :, :features]
+    for j in range(0, features, tile):
+        part = slice(j, j + tile)
+        grads = rows[:, features + j : features + j + tile]
+        left, right, two = [dot(s_all[q], grads, 1, 0).astype(BF) for q in (1, 2, 3)]
+        go_ref[:half, part] = two[:half]
+        go_ref[half:hid, part] = right[half:]
+        come_ref[:half, part] = left[:half]
+        come_ref[half:hid, part] = two[half:]
+        right_ref[:, part] = right[:half]
+        left_ref[:, part] = left[half:]
 
 
 def rows_call(zs, chunks, weights):
     count = sum(c.shape[0] for c in chunks)
     width = chunks[0].shape[1]
     n, hid, features = 4, weights[0].shape[0] // 3, weights[0].shape[1]
+    size, last = 2 * hid * count // features, count // 4
+    fixed = hid + size + last
     return pl.pallas_call(
         rows_kernel,
         out_shape=[
             jax.ShapeDtypeStruct((count, features + LANES), BF),
             jax.ShapeDtypeStruct((2 * hid, count), BF),
-            *[jax.ShapeDtypeStruct((2 * hid * count // features, features), BF)] * (n - 1),
-            jax.ShapeDtypeStruct((n, hid, count), BF),
+            jax.ShapeDtypeStruct((hid, count), BF),
+            jax.ShapeDtypeStruct((fixed + 2 * size // 3, features), BF),
+            jax.ShapeDtypeStruct((fixed + size // 3, features), BF),
+            jax.ShapeDtypeStruct((hid // 2, features), BF),
+            jax.ShapeDtypeStruct((hid // 2, features), BF),
         ],
         in_specs=[pl.BlockSpec(memory_space=pltpu.SMEM)] + [pl.BlockSpec(memory_space=pl.ANY)] * 8,
-        out_specs=[vmem()] * (n + 2),
+        out_specs=[vmem()] * 7,
         scratch_shapes=[
             pltpu.VMEM((n * 2 * hid, features), BF),
             pltpu.VMEM((n, hid, features), BF),
             pltpu.VMEM((count, width), BF),
             pltpu.VMEM((n * 2 * hid, count), BF),
+            pltpu.VMEM((n, hid, count), BF),
             pltpu.SemaphoreType.DMA((4 + 2 * n,)),
         ],
         compiler_params=pltpu.CompilerParams(vmem_limit_bytes=56 * MIB),
@@ -237,67 +259,15 @@
     )(zs, *chunks, *weights)
 
 
-def down_kernel(
-    s_ref, a_ref, b_ref, c_ref, dl_ref, dr_ref, dt_ref, own_ref, go_ref, come_ref, right_ref, left_ref, rows
-):
-    quarter = a_ref.shape[0]
-    rows[0:quarter, :] = a_ref[...]
-    rows[quarter : 3 * quarter, :] = b_ref[...]
-    rows[3 * quarter :, :] = c_ref[...]
-    grads = rows[...]
-    half = right_ref.shape[0]
-    own_ref[...] = dot(s_ref[0], grads, 1, 0)
-    left = dot(s_ref[1], grads, 1, 0).astype(BF)
-    right = dot(s_ref[2], grads, 1, 0).astype(BF)
-    two = dot(s_ref[3], grads, 1, 0).astype(BF)
-    go_ref[:half, :] = two[:half]
-    go_ref[half : 2 * half, :] = right[half:]
-    end = 2 * half + dr_ref.shape[0]
-    most = go_ref.shape[0] - end
-    go_ref[2 * half : end, :] = dr_ref[...]
-    go_ref[end:, :] = dt_ref[:most, :]
-    come_ref[:half, :] = left[:half]
-    come_ref[half : 2 * half, :] = two[half:]
-    come_ref[2 * half : end, :] = dl_ref[...]
-    come_ref[end:, :] = dt_ref[most:, :]
-    right_ref[...] = right[:half]
-    left_ref[...] = left[half:]
-
-
-def down_call(scaled, chunks, d_left, d_right, d_two, features):
-    tile = 512
-    n, hid, count = scaled.shape
-    first = features // tile
-    tiled = [pl.BlockSpec((c.shape[0], tile), lambda j: (0, first + j)) for c in chunks]
-    extra = d_left.shape[0]
-    tiled += [pl.BlockSpec((extra, tile), lambda j: (0, j))] * 3
-    sizes = [hid, hid + extra + 2 * extra // 3, hid + extra + extra // 3, hid // 2, hid // 2]
-    return pl.pallas_call(
-        down_kernel,
-        grid=(features // tile,),
-        out_shape=[jax.ShapeDtypeStruct((hid, features), F32)]
-        + [jax.ShapeDtypeStruct((size, features), BF) for size in sizes[1:]],
-        in_specs=[pl.BlockSpec(scaled.shape, lambda j: (0, 0, 0))] + tiled,
-        out_specs=[pl.BlockSpec((size, tile), lambda j: (0, j)) for size in sizes],
-        scratch_shapes=[pltpu.VMEM((count, tile), BF)],
-        compiler_params=pltpu.CompilerParams(vmem_limit_bytes=24 * MIB),
-        cost_estimate=pl.CostEstimate(
-            flops=2 * n * count * features * hid,
-            bytes_accessed=2 * features * (count + 5 * hid),
-            transcendentals=0,
-        ),
-        name="down_parts",
-    )(scaled, *chunks, d_left, d_right, d_two)
-
-
 def weights_kernel(*refs):
-    d_refs, x_refs, (gate_ref, up_ref, factors, rows) = refs[:5], refs[5:13], refs[13:]
-    own, left, right, more_left, more_right, last, two_a, two_b = x_refs
+    s_ref, d_refs, g_refs, x_refs = refs[0], refs[1:6], refs[6:9], refs[9:17]
+    gate_ref, up_ref, down_ref, factors, rows, grads = refs[17:]
+    own, left, right, last, from_left, from_right, two_a, two_b = x_refs
     hid = gate_ref.shape[0]
-    most, mid = own.shape[0], own.shape[0] // 2
-    count, ends = rows.shape[1], last.shape[0]
-    size = d_refs[1].shape[0]
-    top = d_refs[3].shape[0]
+    most, half, ends = own.shape[0], hid // 2, last.shape[0]
+    mid, cut = most // 2, ends // 2
+    count = rows.shape[1]
+    size, top = d_refs[1].shape[0], d_refs[3].shape[0]
 
     @pl.when(pl.program_id(0) == 0)
     def _():
@@ -309,44 +279,68 @@
             factors[3, at : at + top, :] = d_refs[3][:, part]
             factors[3, at + top : at + size, :] = d_refs[4][:, part]
 
-    for q, (first, end) in enumerate(((own, last), (left, more_left), (right, more_right))):
+    for q, (first, end) in enumerate(((own, last), (left, from_left), (right, from_right))):
         rows[q, :most, :] = first[...]
         rows[q, most:, :] = end[end.shape[0] - ends :, :]
-    rows[3, :mid, :] = more_right[:mid, :]
-    rows[3, mid:most, :] = more_left[:mid, :]
-    rows[3, most : most + ends // 2, :] = two_a[two_a.shape[0] - ends // 2 :, :]
-    rows[3, most + ends // 2 :, :] = two_b[two_b.shape[0] - ends // 2 :, :]
+    far_a, far_b = half + top, half + size - top
+    rows[3, :mid, :] = two_b[far_b : far_b + mid, :]
+    rows[3, mid:most, :] = two_a[far_a : far_a + mid, :]
+    rows[3, most : most + cut, :] = two_a[far_a + mid :, :]
+    rows[3, most + cut :, :] = two_b[far_b + mid :, :]
     total = sum(dot(factors[q], rows[q], 1, 0) for q in range(4)).astype(BF)
     gate_ref[...] = total[:hid]
     up_ref[...] = total[hid:]
 
-
-def weights_call(d_own, from_left, from_right, two_a, two_b, half, xs):
+    at = 0
+    for ref in g_refs:
+        grads[at : at + ref.shape[0], :] = ref[...]
+        at += ref.shape[0]
+    down = dot(s_ref[...], grads[...], 1, 0)
+    upper = two_a[:half, :].astype(F32) + from_right[:half, :].astype(F32)
+    lower = from_left[half:hid, :].astype(F32) + two_b[:half, :].astype(F32)
+    down_ref[:half, :] = (down[:half] + upper).astype(BF)
+    down_ref[half:, :] = (down[half:] + lower).astype(BF)
+
+
+def weights_call(scaled, d_own, chunks, x_ab, x_left, x_right, x_c, messages):
     tile = 512
-    n, (both, count), features = 4, d_own.shape, xs[0].shape[1]
+    from_left, from_right, two_a, two_b = messages
+    n, (both, count), features = 4, d_own.shape, x_ab.shape[1]
     hid, size = both // 2, both * count // features
     top, low = 2 * size // 3, size // 3
 
     def piece(rows, first):
         return pl.BlockSpec((rows, features), lambda j: (first // rows, 0))
 
-    packed = [piece(size, 2 * half), piece(size, 2 * half), piece(top, half), piece(low, half)]
-    tiled = [pl.BlockSpec((x.shape[0], tile), lambda j: (0, j)) for x in [*xs, two_a, two_b]]
+    packed = [piece(size, hid), piece(size, hid), piece(top, hid // 2), piece(low, hid // 2)]
+    skip = features // tile
+    grads = [pl.BlockSpec((c.shape[0], tile), lambda j: (0, skip + j)) for c in chunks]
+    tiled = [x_ab, x_left, x_right, x_c, *messages]
     return pl.pallas_call(
         weights_kernel,
         grid=(features // tile,),
-        out_shape=[jax.ShapeDtypeStruct((hid, features), BF)] * 2,
-        in_specs=[pl.BlockSpec(d_own.shape, lambda j: (0, 0)), *packed, *tiled],
-        out_specs=[pl.BlockSpec((hid, tile), lambda j: (0, j))] * 2,
-        scratch_shapes=[pltpu.VMEM((n, both, count), BF), pltpu.VMEM((n, count, tile), BF)],
-        compiler_params=pltpu.CompilerParams(vmem_limit_bytes=24 * MIB),
+        out_shape=[jax.ShapeDtypeStruct((hid, features), BF)] * 3,
+        in_specs=[
+            pl.BlockSpec(scaled.shape, lambda j: (0, 0)),
+            pl.BlockSpec(d_own.shape, lambda j: (0, 0)),
+            *packed,
+            *grads,
+            *[pl.BlockSpec((x.shape[0], tile), lambda j: (0, j)) for x in tiled],
+        ],
+        out_specs=[pl.BlockSpec((hid, tile), lambda j: (0, j))] * 3,
+        scratch_shapes=[
+            pltpu.VMEM((n, both, count), BF),
+            pltpu.VMEM((n, count, tile), BF),
+            pltpu.VMEM((count, tile), BF),
+        ],
+        compiler_params=pltpu.CompilerParams(vmem_limit_bytes=32 * MIB),
         cost_estimate=pl.CostEstimate(
-            flops=4 * n * count * features * hid,
-            bytes_accessed=2 * features * (n * count + 2 * hid),
+            flops=40 * n * count * features * hid,
+            bytes_accessed=2 * features * (2 * n * count + 3 * hid),
             transcendentals=0,
         ),
         name="weight_grads",
-    )(d_own, from_left, from_right, two_a, two_b, *xs, two_a, two_b)
+    )(scaled, d_own, *messages, *chunks, *tiled)
 
 
 def home_kernel(code_ref, home_ref, grad_ref, score_ref):
@@ -410,46 +404,48 @@
     rows_c = exchange(packed_c)
 
     chunks = [rows_a, rows_b, rows_c]
-    back, d_own, d_left, d_right, d_two, scaled = rows_call(
+    back, d_own, scaled, go, come, p_right, p_left = rows_call(
         zs, chunks, [joined, w_left, w_right, w_a, w_b]
     )
     x_ab = jnp.concatenate([rows_a[:, :features], rows_b[:, :features]], axis=0)
     x_left, x_right = shift(x_ab, 1, "x", n), shift(x_ab, -1, "x", n)
-    back, x_left, x_right = lax.optimization_barrier((back, x_left, x_right))
+    go, come, x_left, x_right = lax.optimization_barrier((go, come, x_left, x_right))
     home = lax.all_to_all(
         back.reshape(-1, CAPACITY, back.shape[1]), PLACE, split_axis=0, concat_axis=0, tiled=True
     ).reshape(back.shape)
-    mid = x_ab.shape[0] // 2
-    x_c = rows_c[:, :features]
-    more_left = shift(jnp.concatenate([x_left[mid:], x_c], axis=0), 1, "x", n)
-    more_right = shift(jnp.concatenate([x_right[:mid], x_c], axis=0), -1, "x", n)
-
-    scaled, more_left, more_right = lax.optimization_barrier((scaled, more_left, more_right))
-    p_own, p_go, p_come, p_right, p_left = down_call(
-        scaled, chunks, d_left, d_right, d_two, features
-    )
-    from_left, from_right = shift(p_go, 1, "x", n), shift(p_come, -1, "x", n)
-    passed = 2 * half + d_left.shape[0]
-    last = x_c.shape[0] // 2
-    p_right = (p_right.astype(F32) + from_left[:half].astype(F32)).astype(BF)
-    p_left = (p_left.astype(F32) + from_right[half : 2 * half].astype(F32)).astype(BF)
+
+    from_left, from_right = shift(go, 1, "x", n), shift(come, -1, "x", n)
+    hid, mid, cut = 2 * half, x_ab.shape[0] // 2, rows_c.shape[0] // 2
+    at = hid + d_own.size // go.shape[1]
+    end_a, end_b = go.shape[0] - 2 * cut, come.shape[0] - 2 * cut
     two_a = shift(
-        jnp.concatenate([p_right, from_left[passed:], more_left[mid : mid + last]], axis=0),
+        jnp.concatenate(
+            [
+                (p_right.astype(F32) + from_left[:half].astype(F32)).astype(BF),
+                from_left[at:end_a],
+                x_left[mid:],
+                from_left[end_a : end_a + cut],
+            ],
+            axis=0,
+        ),
         1, "x", n,
     )
     two_b = shift(
-        jnp.concatenate([p_left, from_right[passed:], more_right[mid + last :]], axis=0),
+        jnp.concatenate(
+            [
+                (p_left.astype(F32) + from_right[half:hid].astype(F32)).astype(BF),
+                from_right[at:end_b],
+                x_right[:mid],
+                from_right[end_b + cut :],
+            ],
+            axis=0,
+        ),
         -1, "x", n,
     )
-    grad_down = jnp.concatenate(
-        [
-            p_own[:half] + two_a[:half].astype(F32) + from_right[:half].astype(F32),
-            p_own[half:] + from_left[half : 2 * half].astype(F32) + two_b[:half].astype(F32),
-        ],
-        axis=0,
-    ).astype(BF)
-    xs = [x_ab, x_left, x_right, more_left, more_right, x_c]
-    grad_gate, grad_up = weights_call(d_own, from_left, from_right, two_a, two_b, half, xs)
+    grad_gate, grad_up, grad_down = weights_call(
+        scaled, d_own, chunks, x_ab, x_left, x_right, rows_c[:, :features],
+        [from_left, from_right, two_a, two_b],
+    )
 
     token_grad, slot_score = home_call(code, home, features)
     return (token_grad, slot_score.T, grad_gate[None], grad_up[None], grad_down[None])

time: 226 us -> 220 us (0.973)
  starting transfers between devices: 81.6 us -> 75.6 us
  local copies, waits for them, and re-layouts: 17.9 us -> 15 us
  waiting for transfers between devices: 59.2 us -> 61.6 us
    all_to_all x1, waiting for transfers between devices: 0.01 us -> 6.47 us  [local(): lax.all_to_all(back.reshape(-1, CAPACITY, back.shape[1]), PLACE, split_ax...]
    ppermute x16 -> x14, starting transfers between devices: 57.6 us -> 51.9 us  [shift(): return lax.ppermute(block, axes, [(i, (i + step) % n) for i in range(n)])]
    ppermute x16 -> x14, waiting for transfers between devices: 48.5 us -> 45.4 us  [shift(): return lax.ppermute(block, axes, [(i, (i + step) % n) for i in range(n)])]
    concatenate x5 -> x2, other arithmetic: 2.6 us -> 0.16 us  [the longest x1 0.09 us: local(): jnp.concatenate([(p_left.astype(F32) + from_right[half:hid].astype(F32))....]
    pallas_call x1 -> x0, Pallas kernels: 2.37 us -> none  [down_call(): pl.pallas_call(down_kernel, grid=(features // tile,), out_shape=[jax.Shap...]
  transfers between devices with their start and end apart: 20 -> 18, of which waited for: 11 -> 9; matrix products, arithmetic and copies ran while one was open for 5% -> 6% of each run, Pallas kernels for 13% -> 13%
where the time goes in v10:
time: 220 us; the launch traced here: 219 us
  starting transfers between devices  75.6 us (34%)
  waiting for transfers between devices  61.6 us (28%)
  Pallas kernels  31.4 us (14%)
  blocking collectives  28.5 us (13%)
  local copies, waits for them, and re-layouts  15 us (7%)
  other arithmetic  5.38 us (2%)
    ppermute x14, starting transfers between devices, shift(): return lax.ppermute(block, axes, [(i, (i + step) % n) for i in range(n)])  51.9 us
    ppermute x14, waiting for transfers between devices, shift(): return lax.ppermute(block, axes, [(i, (i + step) % n) for i in range(n)])  45.4 us
    all_gather x1, blocking collectives, local(): chunk = lax.all_gather(own, FAR, axis=0, tiled=True)  28.5 us
    pallas_call x1, Pallas kernels, rows_call(): pl.pallas_call(rows_kernel, out_shape=[jax.ShapeDtypeStruct((count, featu...  13.8 us
    all_to_all x3, starting transfers between devices, exchange(): lax.all_to_all(packed.reshape(8, rows // 8, width), YC, split_axis=0, con...  12.5 us
    all_to_all x1, starting transfers between devices, local(): lax.all_to_all(back.reshape(-1, CAPACITY, back.shape[1]), PLACE, split_ax...  11.2 us
    all_to_all x3, waiting for transfers between devices, exchange(): lax.all_to_all(packed.reshape(8, rows // 8, width), YC, split_axis=0, con...  9.73 us
    pallas_call x3, Pallas kernels, pack_call(): pl.pallas_call(body, out_shape=jax.ShapeDtypeStruct((rows, width), BF), i...  7.97 us
  transfers between devices with their start and end apart: 18, of which 9 were waited for; matrix products, arithmetic and copies ran while one was open for 6% of the time, Pallas kernels for 13%

profile of v10, /device:TPU:6, one launch (start us, length us, event | category | flops | bytes accessed | tf_op | source)
XLA Modules:
  0.0 218.6 jit_solution(609860275459998553)
XLA Ops:
  0.6 3.3 %pad_maximum_fusion.refs_3_ = bf16[576,2048]{1,0:T(8,128)(2,1)} fusion(bf16[192,2048]{1,0:T(8,128)(2,1)} %bitcast.31, bf16[192,2048]{1,0:T(8,128)(2,1)} %bitcast.32, bf16[192,2048]{1,0:T(8,128)(2,1)} %bitcast.33), kind=kLoop, calls=%fused_computation | loop fusion | flops 7077888 | bytes 4718592 | tf_op jit(solution)/shard_map/concatenate | solution.py:379
  4.0 7.7 %collective-permute-start.2 = (bf16[576,2048]{1,0:T(8,128)(2,1)}, bf16[576,2048]{1,0:T(8,128)(2,1)}, u32[]{:S(2)}, u32[]{:S(2)}) collective-permute-start(bf16[576,2048]{1,0:T(8,128)(2,1)} %pad_maximum_fusion.refs_3_), channel_id=1, source_target_pairs={{0,1},{1,2},{2,3},{3,0},{4,5},{5,6},{6,7},{7,4},{8,9},{9,10},{10,1... | collective-permute-start | bytes 7077896 | tf_op jit(solution)/shard_map/ppermute | solution.py:28
  15.6 28.5 %all_gather.3.refs_1_ = bf16[64,4224]{1,0:T(8,128)(2,1)S(1)} all-gather(bf16[16,4224]{1,0:T(8,128)(2,1)} %get-tuple-element.33), channel_id=1, replica_groups=mesh['zh'=2,'y'=4,'c'=2,'zq'=2,'zr'=4,'x'=4] {'zh','zq'}, dimensions={0}, use_global_device_ids=true | all-gather | bytes 675840 | tf_op jit(solution)/shard_map/all_gather | solution.py:384
  44.1 3.7 %collective-permute-start = (bf16[64,4224]{1,0:T(8,128)(2,1)S(1)}, bf16[64,4224]{1,0:T(8,128)(2,1)S(1)}, u32[]{:S(2)}, u32[]{:S(2)}) collective-permute-start(bf16[64,4224]{1,0:T(8,128)(2,1)S(1)} %all_gather.3.refs_1_), channel_id=1, source_target_pairs={{0,4},{4,8},{8,12},{12,16},{16,20},{20,24},{24,28},{28,256},{256,2... | collective-permute-start | bytes 1622024 | tf_op jit(solution)/shard_map/ppermute | solution.py:28
  47.8 3.7 %collective-permute-start.1 = (bf16[64,4224]{1,0:T(8,128)(2,1)S(1)}, bf16[64,4224]{1,0:T(8,128)(2,1)S(1)}, u32[]{:S(2)}, u32[]{:S(2)}) collective-permute-start(bf16[64,4224]{1,0:T(8,128)(2,1)S(1)} %all_gather.3.refs_1_), channel_id=1, source_target_pairs={{0,284},{4,0},{8,4},{12,8},{16,12},{20,16},{24,20},{28,24},{256,28... | collective-permute-start | bytes 1622024 | tf_op jit(solution)/shard_map/ppermute | solution.py:28
  54.5 4.5 %all-to-all-start = ((bf16[8,8,4224]{2,1,0:T(8,128)(2,1)}), bf16[8,8,4224]{2,1,0:T(8,128)(2,1)S(1)}, u32[]{:S(2)}, u32[]{:S(2)}) async-start(bf16[8,8,4224]{2,1,0:T(8,128)(2,1)} %bitcast.30), calls=%async_computation | async-start | bytes 1081344 | tf_op jit(solution)/shard_map/all_to_all | solution.py:389
  60.9 3.2 %pack.3 = bf16[128,4224]{1,0:T(8,128)(2,1)} custom-call(s32[3]{0:T(128)} %pad_add_fusion.refs_0_.zs_ref, bf16[64,4224]{1,0:T(8,128)(2,1)} %copy-done.11, bf16[64,4224]{1,0:T(8,128)(2,1)} %copy-done.13), custom_call_target="tpu_custom_call" | custom-call | tf_op jit(solution)/shard_map/pack/pallas_call | solution.py:126
  64.1 5.4 %all-to-all-done = bf16[8,8,4224]{2,1,0:T(8,128)(2,1)S(1)} async-done(((bf16[8,8,4224]{2,1,0:T(8,128)(2,1)}), bf16[8,8,4224]{2,1,0:T(8,128)(2,1)S(1)}, u32[]{:S(2)}, u32[]{:S(2)}) %all-to-all-start) | async-done | bytes 540704 | tf_op jit(solution)/shard_map/all_to_all | solution.py:389
  69.5 3.6 %all-to-all-start.1 = ((bf16[8,16,4224]{2,1,0:T(8,128)(2,1)}), bf16[8,16,4224]{2,1,0:T(8,128)(2,1)S(1)}, u32[]{:S(2)}, u32[]{:S(2)}) async-start(bf16[8,16,4224]{2,1,0:T(8,128)(2,1)} %bitcast.28), calls=%async_computation.1 | async-start | bytes 2162688 | tf_op jit(solution)/shard_map/all_to_all | solution.py:389
  81.0 4.3 %collective-permute-start.7 = (bf16[288,2048]{1,0:T(8,128)(2,1)}, bf16[288,2048]{1,0:T(8,128)(2,1)}, u32[]{:S(2)}, u32[]{:S(2)}) collective-permute-start(bf16[288,2048]{1,0:T(8,128)(2,1)} %slice.48), channel_id=1, source_target_pairs={{0,1},{1,2},{2,3},{3,0},{4,5},{5,6},{6,7},{7,4},{8,9},{9,10},{10,1... | collective-permute-start | bytes 3538952 | tf_op jit(solution)/shard_map/ppermute | solution.py:28
  85.3 5.2 %collective-permute-start.4 = (bf16[32,4224]{1,0:T(8,128)(2,1)S(1)}, bf16[32,4224]{1,0:T(8,128)(2,1)S(1)}, u32[]{:S(2)}, u32[]{:S(2)}) collective-permute-start(bf16[32,4224]{1,0:T(8,128)(2,1)S(1)} %slice.60), channel_id=1, source_target_pairs={{0,284},{4,0},{8,4},{12,8},{16,12},{20,16},{24,20},{28,24},{256,28... | collective-permute-start | bytes 811016 | tf_op jit(solution)/shard_map/ppermute | solution.py:28
  92.6 3.9 %collective-permute-done.4.refs_1_ = bf16[32,4224]{1,0:T(8,128)(2,1)S(1)} collective-permute-done((bf16[32,4224]{1,0:T(8,128)(2,1)S(1)}, bf16[32,4224]{1,0:T(8,128)(2,1)S(1)}, u32[]{:S(2)}, u32[]{:S(2)}) %collective-permute-start.4) | collective-permute-done | bytes 270368 | tf_op jit(solution)/shard_map/ppermute | solution.py:28
  96.4 5.4 %collective-permute-done.5.refs_2_ = bf16[32,4224]{1,0:T(8,128)(2,1)S(1)} collective-permute-done((bf16[32,4224]{1,0:T(8,128)(2,1)S(1)}, bf16[32,4224]{1,0:T(8,128)(2,1)S(1)}, u32[]{:S(2)}, u32[]{:S(2)}) %collective-permute-start.5) | collective-permute-done | bytes 270368 | tf_op jit(solution)/shard_map/ppermute | solution.py:28
  105.0 4.4 %all-to-all-start.2 = ((bf16[8,8,4224]{2,1,0:T(8,128)(2,1)}), bf16[8,8,4224]{2,1,0:T(8,128)(2,1)S(1)}, u32[]{:S(2)}, u32[]{:S(2)}) async-start(bf16[8,8,4224]{2,1,0:T(8,128)(2,1)} %bitcast.29), calls=%async_computation.2 | async-start | bytes 1081344 | tf_op jit(solution)/shard_map/all_to_all | solution.py:389
  111.7 3.8 %collective-permute-start.9 = (bf16[192,2048]{1,0:T(8,128)(2,1)S(1)}, bf16[192,2048]{1,0:T(8,128)(2,1)}, u32[]{:S(2)}, u32[]{:S(2)}) collective-permute-start(bf16[192,2048]{1,0:T(8,128)(2,1)S(1)} %pad_maximum_fusion.3.refs_9_), channel_id=1, source_target_pairs={{0,3},{1,0},{2,1},{3,2},{4,7},{5,4},{6,5},{7,6},{8,11},{9,8},{10,9... | collective-permute-start | bytes 2359304 | tf_op jit(solution)/shard_map/ppermute | solution.py:28
  115.6 4.3 %all-to-all-done.2 = bf16[8,8,4224]{2,1,0:T(8,128)(2,1)S(1)} async-done(((bf16[8,8,4224]{2,1,0:T(8,128)(2,1)}), bf16[8,8,4224]{2,1,0:T(8,128)(2,1)S(1)}, u32[]{:S(2)}, u32[]{:S(2)}) %all-to-all-start.2) | async-done | bytes 540704 | tf_op jit(solution)/shard_map/all_to_all | solution.py:389
  120.7 13.8 %rows.1 = (bf16[256,2176]{1,0:T(8,128)(2,1)}, bf16[384,256]{1,0:T(8,128)(2,1)}, bf16[192,256]{1,0:T(8,128)(2,1)}, bf16[336,2048]{1,0:T(8,128)(2,1)}, bf16[320,20...) custom-call(s32[3]{0:T(128)} %pad_add_fusion.refs_0_.zs_ref, bf16[64,4224]{1,0:T(8,128)(2,1)} %bitcast.23, ...), custom_call_target="tpu_custom_call" | custom-call | flops 4026531840 | bytes 12582912 | tf_op jit(solution)/shard_map/rows/pallas_call | solution.py:231
  137.1 4.6 %collective-permute-start.10 = (bf16[336,2048]{1,0:T(8,128)(2,1)}, bf16[336,2048]{1,0:T(8,128)(2,1)S(1)}, u32[]{:S(2)}, u32[]{:S(2)}) collective-permute-start(bf16[336,2048]{1,0:T(8,128)(2,1)} %get-tuple-element.50), channel_id=1, source_target_pairs={{0,1},{1,2},{2,3},{3,0},{4,5},{5,6},{6,7},{7,4},{8,9},{9,10},{10,1... | collective-permute-start | bytes 4128776 | tf_op jit(solution)/shard_map/ppermute | solution.py:28
  144.0 11.2 %all-to-all-start.3 = ((bf16[128,2,2176]{2,1,0:T(2,128)(2,1)}), bf16[128,2,2176]{2,1,0:T(2,128)(2,1)}, u32[]{:S(2)}, u32[]{:S(2)}) async-start(bf16[128,2,2176]{2,1,0:T(2,128)(2,1)} %reshape.40), calls=%async_computation.3 | async-start | bytes 2228224 | tf_op jit(solution)/shard_map/all_to_all | solution.py:413
  156.4 12.0 %collective-permute-done.11.refs_3_.refs_14_ = bf16[320,2048]{1,0:T(8,128)(2,1)} collective-permute-done((bf16[320,2048]{1,0:T(8,128)(2,1)}, bf16[320,2048]{1,0:T(8,128)(2,1)}, u32[]{:S(2)}, u32[]{:S(2)}) %collective-permute-start.11) | collective-permute-done | bytes 1310752 | tf_op jit(solution)/shard_map/ppermute | solution.py:28
  171.5 5.5 %collective-permute-start.12 = (bf16[256,2048]{1,0:T(8,128)(2,1)S(1)}, bf16[256,2048]{1,0:T(8,128)(2,1)S(1)}, u32[]{:S(2)}, u32[]{:S(2)}) collective-permute-start(bf16[256,2048]{1,0:T(8,128)(2,1)S(1)} %pad_maximum_fusion.1), channel_id=1, source_target_pairs={{0,1},{1,2},{2,3},{3,0},{4,5},{5,6},{6,7},{7,4},{8,9},{9,10},{10,1... | collective-permute-start | bytes 3145736 | tf_op jit(solution)/shard_map/ppermute | solution.py:28
  179.0 23.0 %collective-permute-done.13.refs_5_.refs_16_ = bf16[240,2048]{1,0:T(8,128)(2,1)S(1)} collective-permute-done((bf16[240,2048]{1,0:T(8,128)(2,1)S(1)}, bf16[240,2048]{1,0:T(8,128)(2,1)S(1)}, u32[]{:S(2)}, u32[]{:S(2)}) %collective-permute-start.13) | collective-permute-done | bytes 983072 | tf_op jit(solution)/shard_map/ppermute | solution.py:28
  202.1 5.5 %weight_grads.1 = (bf16[192,2048]{1,0:T(8,128)(2,1)}, bf16[192,2048]{1,0:T(8,128)(2,1)}, bf16[192,2048]{1,0:T(8,128)(2,1)}) custom-call(bf16[192,256]{1,0:T(8,128)(2,1)S(1)} %copy-done.9, bf16[384,256]{1,0:T(8,128)(2,1)S(1)} %copy-done.8, bf16[336,2048]{1,0:T(8,128)(2,1)S(1)} %collective-permute-done.10.refs_2_.refs_13_, ...), custom_call_target="tpu_custom_call" | custom-call | flops 16106127360 | bytes 10747904 | tf_op jit(solution)/shard_map/weight_grads/pallas_call | solution.py:319
  207.6 6.5 %all-to-all-done.3 = bf16[128,2,2176]{2,1,0:T(2,128)(2,1)} async-done(((bf16[128,2,2176]{2,1,0:T(2,128)(2,1)}), bf16[128,2,2176]{2,1,0:T(2,128)(2,1)}, u32[]{:S(2)}, u32[]{:S(2)}) %all-to-all-start.3) | async-done | bytes 1114144 | tf_op jit(solution)/shard_map/all_to_all | solution.py:413
  (80 shorter events, 40.5 us)
Async XLA Ops:
  4.0 60.2 %collective-permute-start.2 = (bf16[576,2048]{1,0:T(8,128)(2,1)}, bf16[576,2048]{1,0:T(8,128)(2,1)}, u32[]{:S(2)}, u32[]{:S(2)}) collective-permute-start(bf16[576,2048]{1,0:T(8,128)(2,1)} %pad_maximum_fusion.refs_3_), channel_id=1, source_target_pairs={{0,1},{1,2},{2,3},{3,0},{4,5},{5,6},{6,7},{7,4},{8,9},{9,10},{10,1... | collective-permute-start | bytes 7077896 | tf_op jit(solution)/shard_map/ppermute | solution.py:28
  11.7 52.4 %collective-permute-start.3 = (bf16[576,2048]{1,0:T(8,128)(2,1)}, bf16[576,2048]{1,0:T(8,128)(2,1)}, u32[]{:S(2)}, u32[]{:S(2)}) collective-permute-start(bf16[576,2048]{1,0:T(8,128)(2,1)} %pad_maximum_fusion.refs_3_), channel_id=1, source_target_pairs={{0,3},{1,0},{2,1},{3,2},{4,7},{5,4},{6,5},{7,6},{8,11},{9,8},{10,9... | collective-permute-start | bytes 7077896 | tf_op jit(solution)/shard_map/ppermute | solution.py:28
  44.1 14.9 %collective-permute-start = (bf16[64,4224]{1,0:T(8,128)(2,1)S(1)}, bf16[64,4224]{1,0:T(8,128)(2,1)S(1)}, u32[]{:S(2)}, u32[]{:S(2)}) collective-permute-start(bf16[64,4224]{1,0:T(8,128)(2,1)S(1)} %all_gather.3.refs_1_), channel_id=1, source_target_pairs={{0,4},{4,8},{8,12},{12,16},{16,20},{20,24},{24,28},{28,256},{256,2... | collective-permute-start | bytes 1622024 | tf_op jit(solution)/shard_map/ppermute | solution.py:28
  47.8 12.3 %collective-permute-start.1 = (bf16[64,4224]{1,0:T(8,128)(2,1)S(1)}, bf16[64,4224]{1,0:T(8,128)(2,1)S(1)}, u32[]{:S(2)}, u32[]{:S(2)}) collective-permute-start(bf16[64,4224]{1,0:T(8,128)(2,1)S(1)} %all_gather.3.refs_1_), channel_id=1, source_target_pairs={{0,284},{4,0},{8,4},{12,8},{16,12},{20,16},{24,20},{28,24},{256,28... | collective-permute-start | bytes 1622024 | tf_op jit(solution)/shard_map/ppermute | solution.py:28
  54.5 15.0 %all-to-all-start = ((bf16[8,8,4224]{2,1,0:T(8,128)(2,1)}), bf16[8,8,4224]{2,1,0:T(8,128)(2,1)S(1)}, u32[]{:S(2)}, u32[]{:S(2)}) async-start(bf16[8,8,4224]{2,1,0:T(8,128)(2,1)} %bitcast.30), calls=%async_computation | async-start | bytes 1081344 | tf_op jit(solution)/shard_map/all_to_all | solution.py:389
  69.5 32.3 %copy-start.2 = (bf16[8,8,4224]{2,1,0:T(8,128)(2,1)}, bf16[8,8,4224]{2,1,0:T(8,128)(2,1)S(1)}, u32[]{:S(2)}) copy-start(bf16[8,8,4224]{2,1,0:T(8,128)(2,1)S(1)} %all-to-all-done) | copy-start | bytes 1622020
  69.5 35.5 %all-to-all-start.1 = ((bf16[8,16,4224]{2,1,0:T(8,128)(2,1)}), bf16[8,16,4224]{2,1,0:T(8,128)(2,1)S(1)}, u32[]{:S(2)}, u32[]{:S(2)}) async-start(bf16[8,16,4224]{2,1,0:T(8,128)(2,1)} %bitcast.28), calls=%async_computation.1 | async-start | bytes 2162688 | tf_op jit(solution)/shard_map/all_to_all | solution.py:389
  75.7 39.9 %collective-permute-start.6 = (bf16[288,2048]{1,0:T(8,128)(2,1)}, bf16[288,2048]{1,0:T(8,128)(2,1)}, u32[]{:S(2)}, u32[]{:S(2)}) collective-permute-start(bf16[288,2048]{1,0:T(8,128)(2,1)} %slice.47), channel_id=1, source_target_pairs={{0,3},{1,0},{2,1},{3,2},{4,7},{5,4},{6,5},{7,6},{8,11},{9,8},{10,9... | collective-permute-start | bytes 3538952 | tf_op jit(solution)/shard_map/ppermute | solution.py:28
  81.0 34.6 %collective-permute-start.7 = (bf16[288,2048]{1,0:T(8,128)(2,1)}, bf16[288,2048]{1,0:T(8,128)(2,1)}, u32[]{:S(2)}, u32[]{:S(2)}) collective-permute-start(bf16[288,2048]{1,0:T(8,128)(2,1)} %slice.48), channel_id=1, source_target_pairs={{0,1},{1,2},{2,3},{3,0},{4,5},{5,6},{6,7},{7,4},{8,9},{9,10},{10,1... | collective-permute-start | bytes 3538952 | tf_op jit(solution)/shard_map/ppermute | solution.py:28
  85.3 11.1 %collective-permute-start.4 = (bf16[32,4224]{1,0:T(8,128)(2,1)S(1)}, bf16[32,4224]{1,0:T(8,128)(2,1)S(1)}, u32[]{:S(2)}, u32[]{:S(2)}) collective-permute-start(bf16[32,4224]{1,0:T(8,128)(2,1)S(1)} %slice.60), channel_id=1, source_target_pairs={{0,284},{4,0},{8,4},{12,8},{16,12},{20,16},{24,20},{28,24},{256,28... | collective-permute-start | bytes 811016 | tf_op jit(solution)/shard_map/ppermute | solution.py:28
  90.6 11.2 %collective-permute-start.5 = (bf16[32,4224]{1,0:T(8,128)(2,1)S(1)}, bf16[32,4224]{1,0:T(8,128)(2,1)S(1)}, u32[]{:S(2)}, u32[]{:S(2)}) collective-permute-start(bf16[32,4224]{1,0:T(8,128)(2,1)S(1)} %slice.61), channel_id=1, source_target_pairs={{0,4},{4,8},{8,12},{12,16},{16,20},{20,24},{24,28},{28,256},{256,2... | collective-permute-start | bytes 811016 | tf_op jit(solution)/shard_map/ppermute | solution.py:28
  105.0 15.0 %all-to-all-start.2 = ((bf16[8,8,4224]{2,1,0:T(8,128)(2,1)}), bf16[8,8,4224]{2,1,0:T(8,128)(2,1)S(1)}, u32[]{:S(2)}, u32[]{:S(2)}) async-start(bf16[8,8,4224]{2,1,0:T(8,128)(2,1)} %bitcast.29), calls=%async_computation.2 | async-start | bytes 1081344 | tf_op jit(solution)/shard_map/all_to_all | solution.py:389
  109.5 25.0 %collective-permute-start.8 = (bf16[192,2048]{1,0:T(8,128)(2,1)S(1)}, bf16[192,2048]{1,0:T(8,128)(2,1)S(1)}, u32[]{:S(2)}, u32[]{:S(2)}) collective-permute-start(bf16[192,2048]{1,0:T(8,128)(2,1)S(1)} %pad_maximum_fusion.3.refs_9_), channel_id=1, source_target_pairs={{0,1},{1,2},{2,3},{3,0},{4,5},{5,6},{6,7},{7,4},{8,9},{9,10},{10,1... | collective-permute-start | bytes 2359304 | tf_op jit(solution)/shard_map/ppermute | solution.py:28
  111.7 22.9 %collective-permute-start.9 = (bf16[192,2048]{1,0:T(8,128)(2,1)S(1)}, bf16[192,2048]{1,0:T(8,128)(2,1)}, u32[]{:S(2)}, u32[]{:S(2)}) collective-permute-start(bf16[192,2048]{1,0:T(8,128)(2,1)S(1)} %pad_maximum_fusion.3.refs_9_), channel_id=1, source_target_pairs={{0,3},{1,0},{2,1},{3,2},{4,7},{5,4},{6,5},{7,6},{8,11},{9,8},{10,9... | collective-permute-start | bytes 2359304 | tf_op jit(solution)/shard_map/ppermute | solution.py:28
  134.6 33.7 %collective-permute-start.11 = (bf16[320,2048]{1,0:T(8,128)(2,1)}, bf16[320,2048]{1,0:T(8,128)(2,1)}, u32[]{:S(2)}, u32[]{:S(2)}) collective-permute-start(bf16[320,2048]{1,0:T(8,128)(2,1)} %get-tuple-element.51), channel_id=1, source_target_pairs={{0,3},{1,0},{2,1},{3,2},{4,7},{5,4},{6,5},{7,6},{8,11},{9,8},{10,9... | collective-permute-start | bytes 3932168 | tf_op jit(solution)/shard_map/ppermute | solution.py:28
  137.1 34.1 %collective-permute-start.10 = (bf16[336,2048]{1,0:T(8,128)(2,1)}, bf16[336,2048]{1,0:T(8,128)(2,1)S(1)}, u32[]{:S(2)}, u32[]{:S(2)}) collective-permute-start(bf16[336,2048]{1,0:T(8,128)(2,1)} %get-tuple-element.50), channel_id=1, source_target_pairs={{0,1},{1,2},{2,3},{3,0},{4,5},{5,6},{6,7},{7,4},{8,9},{9,10},{10,1... | collective-permute-start | bytes 4128776 | tf_op jit(solution)/shard_map/ppermute | solution.py:28
  144.0 70.0 %all-to-all-start.3 = ((bf16[128,2,2176]{2,1,0:T(2,128)(2,1)}), bf16[128,2,2176]{2,1,0:T(2,128)(2,1)}, u32[]{:S(2)}, u32[]{:S(2)}) async-start(bf16[128,2,2176]{2,1,0:T(2,128)(2,1)} %reshape.40), calls=%async_computation.3 | async-start | bytes 2228224 | tf_op jit(solution)/shard_map/all_to_all | solution.py:413
  171.3 30.7 %copy-start.1 = (bf16[8,16,4224]{2,1,0:T(8,128)(2,1)S(1)}, bf16[8,16,4224]{2,1,0:T(8,128)(2,1)}, u32[]{:S(2)}) copy-start(bf16[8,16,4224]{2,1,0:T(8,128)(2,1)} %copy-done) | copy-start | bytes 3244036
  171.4 30.7 %copy-start.3 = (bf16[8,8,4224]{2,1,0:T(8,128)(2,1)S(1)}, bf16[8,8,4224]{2,1,0:T(8,128)(2,1)}, u32[]{:S(2)}) copy-start(bf16[8,8,4224]{2,1,0:T(8,128)(2,1)} %copy-done.2) | copy-start | bytes 1622020
  171.4 30.7 %copy-start.7 = (bf16[192,2048]{1,0:T(8,128)(2,1)S(1)}, bf16[192,2048]{1,0:T(8,128)(2,1)}, u32[]{:S(2)}) copy-start(bf16[192,2048]{1,0:T(8,128)(2,1)} %copy-done.6) | copy-start | bytes 2359300
  171.4 30.7 %copy-start.8 = (bf16[384,256]{1,0:T(8,128)(2,1)S(1)}, bf16[384,256]{1,0:T(8,128)(2,1)}, u32[]{:S(2)}) copy-start(bf16[384,256]{1,0:T(8,128)(2,1)} %get-tuple-element.47.refs_1_) | copy-start | bytes 589828
  171.4 30.7 %copy-start.9 = (bf16[192,256]{1,0:T(8,128)(2,1)S(1)}, bf16[192,256]{1,0:T(8,128)(2,1)}, u32[]{:S(2)}) copy-start(bf16[192,256]{1,0:T(8,128)(2,1)} %get-tuple-element.46.refs_0_) | copy-start | bytes 294916
  171.5 30.6 %collective-permute-start.12 = (bf16[256,2048]{1,0:T(8,128)(2,1)S(1)}, bf16[256,2048]{1,0:T(8,128)(2,1)S(1)}, u32[]{:S(2)}, u32[]{:S(2)}) collective-permute-start(bf16[256,2048]{1,0:T(8,128)(2,1)S(1)} %pad_maximum_fusion.1), channel_id=1, source_target_pairs={{0,1},{1,2},{2,3},{3,0},{4,5},{5,6},{6,7},{7,4},{8,9},{9,10},{10,1... | collective-permute-start | bytes 3145736 | tf_op jit(solution)/shard_map/ppermute | solution.py:28
  177.1 25.0 %collective-permute-start.13 = (bf16[240,2048]{1,0:T(8,128)(2,1)S(1)}, bf16[240,2048]{1,0:T(8,128)(2,1)S(1)}, u32[]{:S(2)}, u32[]{:S(2)}) collective-permute-start(bf16[240,2048]{1,0:T(8,128)(2,1)S(1)} %pad_maximum_fusion.2), channel_id=1, source_target_pairs={{0,3},{1,0},{2,1},{3,2},{4,7},{5,4},{6,5},{7,6},{8,11},{9,8},{10,9... | collective-permute-start | bytes 2949128 | tf_op jit(solution)/shard_map/ppermute | solution.py:28
  (14 other events, 134.4 us)

commit v11 on v10

--- a/solution.py
+++ b/solution.py
@@ -130,6 +130,34 @@
         out_specs=vmem(),
         name="pack",
     )(zs, *blocks)
+
+
+def halves_kernel(*refs):
+    n = len(refs) // 2
+    sources, targets, sems = refs[:n], refs[n : 2 * n], refs[-1]
+    copies = []
+    for i, (source, target) in enumerate(zip(sources, targets)):
+        size = target.shape[0]
+        first = size if i % 2 == 0 else 0
+        copies.append(pltpu.make_async_copy(source.at[pl.ds(first, size)], target, sems.at[i]))
+    for copy in copies:
+        copy.start()
+    for copy in copies:
+        copy.wait()
+
+
+def halves_call(*blocks):
+    return pl.pallas_call(
+        halves_kernel,
+        out_shape=[jax.ShapeDtypeStruct((b.shape[0] // 2, b.shape[1]), BF) for b in blocks],
+        in_specs=[pl.BlockSpec(memory_space=pl.ANY)] * len(blocks),
+        out_specs=[pl.BlockSpec(memory_space=pl.ANY)] * len(blocks),
+        scratch_shapes=[pltpu.SemaphoreType.DMA((len(blocks),))],
+        cost_estimate=pl.CostEstimate(
+            flops=0, bytes_accessed=2 * sum(b.size for b in blocks), transcendentals=0
+        ),
+        name="halves",
+    )(*blocks)
 
 
 def homes(z, rows):
@@ -377,7 +405,6 @@
     half = gate_w.shape[1] // 2
 
     joined = jnp.concatenate([gate_w[0], up_w[0], down_w[0]], axis=0)
-    part = joined.shape[0] // 2
     w_left, w_right = shift(joined, 1, "x", n), shift(joined, -1, "x", n)
     own, code = payload_call(tokens, out_grad, expert_ids.T, keep_flags.T, route_weights.T)
 
@@ -393,9 +420,9 @@
     rows_a = exchange(pack_call(zs, [chunk], step))
     packed_b = pack_call(zs, [left, right], step)
     packed_b, w_left, w_right = lax.optimization_barrier((packed_b, w_left, w_right))
-    w_a, w_b = shift(w_right[:part], -1, "x", n), shift(w_left[part:], 1, "x", n)
-    rest_a = shift(right[: 2 * step], -1, Z, nz)
-    rest_b = shift(left[2 * step :], 1, Z, nz)
+    w_low, w_top, low, top = halves_call(w_left, w_right, left, right)
+    w_a, w_b = shift(w_top, -1, "x", n), shift(w_low, 1, "x", n)
+    rest_a, rest_b = shift(top, -1, Z, nz), shift(low, 1, Z, nz)
     rest_a, rest_b, _ = lax.optimization_barrier((rest_a, rest_b, packed_b))
     packed_b, rows_a = lax.optimization_barrier((packed_b, rows_a))
     rows_b = exchange(packed_b)

time: 220 us -> 304 us (1.38)
  Pallas kernels: 31.4 us -> 120 us
  local copies, waits for them, and re-layouts: 15 us -> 9.98 us
    pallas_call x0 -> x1, Pallas kernels: none -> 89 us  [halves_call(): pl.pallas_call(halves_kernel, out_shape=[jax.ShapeDtypeStruct((b.shape[0]...]
    slice x4 -> x0, local copies, waits for them, and re-layouts: 5.05 us -> none  [the longest x1 2.58 us: local(): w_right[:part]]
  transfers between devices with their start and end apart: 18 -> 18, of which waited for: 9 -> 9; matrix products, arithmetic and copies ran while one was open for 6% -> 2% of each run, Pallas kernels for 13% -> 39%
where the time goes in v11:
time: 304 us; the launch traced here: 303 us
  Pallas kernels  120 us (39%)
  starting transfers between devices  75.7 us (25%)
  waiting for transfers between devices  61.8 us (20%)
  blocking collectives  28.5 us (9%)
  local copies, waits for them, and re-layouts  9.98 us (3%)
  other arithmetic  5.35 us (2%)
    pallas_call x1, Pallas kernels, halves_call(): pl.pallas_call(halves_kernel, out_shape=[jax.ShapeDtypeStruct((b.shape[0]...  89 us
    ppermute x14, starting transfers between devices, shift(): return lax.ppermute(block, axes, [(i, (i + step) % n) for i in range(n)])  52 us
    ppermute x14, waiting for transfers between devices, shift(): return lax.ppermute(block, axes, [(i, (i + step) % n) for i in range(n)])  45.4 us
    all_gather x1, blocking collectives, local(): chunk = lax.all_gather(own, FAR, axis=0, tiled=True)  28.5 us
    pallas_call x1, Pallas kernels, rows_call(): pl.pallas_call(rows_kernel, out_shape=[jax.ShapeDtypeStruct((count, featu...  13.8 us
    all_to_all x3, starting transfers between devices, exchange(): lax.all_to_all(packed.reshape(8, rows // 8, width), YC, split_axis=0, con...  12.5 us
    all_to_all x1, starting transfers between devices, local(): lax.all_to_all(back.reshape(-1, CAPACITY, back.shape[1]), PLACE, split_ax...  11.2 us
    all_to_all x3, waiting for transfers between devices, exchange(): lax.all_to_all(packed.reshape(8, rows // 8, width), YC, split_axis=0, con...  9.88 us
  transfers between devices with their start and end apart: 18, of which 9 were waited for; matrix products, arithmetic and copies ran while one was open for 2% of the time, Pallas kernels for 39%

profile of v11, /device:TPU:6, one launch (start us, length us, event | category | flops | bytes accessed | tf_op | source)
XLA Modules:
  0.0 302.8 jit_solution(20564274504067154)
XLA Ops:
  0.6 3.3 %pad_maximum_fusion.refs_3_ = bf16[576,2048]{1,0:T(8,128)(2,1)} fusion(bf16[192,2048]{1,0:T(8,128)(2,1)} %bitcast.31, bf16[192,2048]{1,0:T(8,128)(2,1)} %bitcast.32, bf16[192,2048]{1,0:T(8,128)(2,1)} %bitcast.33), kind=kLoop, calls=%fused_computation | loop fusion | flops 7077888 | bytes 4718592 | tf_op jit(solution)/shard_map/concatenate | solution.py:407
  4.0 7.7 %collective-permute-start.2 = (bf16[576,2048]{1,0:T(8,128)(2,1)}, bf16[576,2048]{1,0:T(8,128)(2,1)}, u32[]{:S(2)}, u32[]{:S(2)}) collective-permute-start(bf16[576,2048]{1,0:T(8,128)(2,1)} %pad_maximum_fusion.refs_3_), channel_id=1, source_target_pairs={{0,1},{1,2},{2,3},{3,0},{4,5},{5,6},{6,7},{7,4},{8,9},{9,10},{10,1... | collective-permute-start | bytes 7077896 | tf_op jit(solution)/shard_map/ppermute | solution.py:28
  15.6 28.5 %all_gather.3.refs_1_ = bf16[64,4224]{1,0:T(8,128)(2,1)S(1)} all-gather(bf16[16,4224]{1,0:T(8,128)(2,1)} %get-tuple-element.37), channel_id=1, replica_groups=mesh['zh'=2,'y'=4,'c'=2,'zq'=2,'zr'=4,'x'=4] {'zh','zq'}, dimensions={0}, use_global_device_ids=true | all-gather | bytes 675840 | tf_op jit(solution)/shard_map/all_gather | solution.py:411
  44.1 3.7 %collective-permute-start = (bf16[64,4224]{1,0:T(8,128)(2,1)S(1)}, bf16[64,4224]{1,0:T(8,128)(2,1)S(1)}, u32[]{:S(2)}, u32[]{:S(2)}) collective-permute-start(bf16[64,4224]{1,0:T(8,128)(2,1)S(1)} %all_gather.3.refs_1_), channel_id=1, source_target_pairs={{0,4},{4,8},{8,12},{12,16},{16,20},{20,24},{24,28},{28,256},{256,2... | collective-permute-start | bytes 1622024 | tf_op jit(solution)/shard_map/ppermute | solution.py:28
  47.8 3.7 %collective-permute-start.1 = (bf16[64,4224]{1,0:T(8,128)(2,1)S(1)}, bf16[64,4224]{1,0:T(8,128)(2,1)S(1)}, u32[]{:S(2)}, u32[]{:S(2)}) collective-permute-start(bf16[64,4224]{1,0:T(8,128)(2,1)S(1)} %all_gather.3.refs_1_), channel_id=1, source_target_pairs={{0,284},{4,0},{8,4},{12,8},{16,12},{20,16},{24,20},{28,24},{256,28... | collective-permute-start | bytes 1622024 | tf_op jit(solution)/shard_map/ppermute | solution.py:28
  54.5 4.5 %all-to-all-start = ((bf16[8,8,4224]{2,1,0:T(8,128)(2,1)}), bf16[8,8,4224]{2,1,0:T(8,128)(2,1)S(1)}, u32[]{:S(2)}, u32[]{:S(2)}) async-start(bf16[8,8,4224]{2,1,0:T(8,128)(2,1)} %bitcast.30), calls=%async_computation | async-start | bytes 1081344 | tf_op jit(solution)/shard_map/all_to_all | solution.py:416
  64.1 5.3 %all-to-all-done = bf16[8,8,4224]{2,1,0:T(8,128)(2,1)S(1)} async-done(((bf16[8,8,4224]{2,1,0:T(8,128)(2,1)}), bf16[8,8,4224]{2,1,0:T(8,128)(2,1)S(1)}, u32[]{:S(2)}, u32[]{:S(2)}) %all-to-all-start) | async-done | bytes 540704 | tf_op jit(solution)/shard_map/all_to_all | solution.py:416
  69.5 3.6 %all-to-all-start.1 = ((bf16[8,16,4224]{2,1,0:T(8,128)(2,1)}), bf16[8,16,4224]{2,1,0:T(8,128)(2,1)S(1)}, u32[]{:S(2)}, u32[]{:S(2)}) async-start(bf16[8,16,4224]{2,1,0:T(8,128)(2,1)} %bitcast.28), calls=%async_computation.1 | async-start | bytes 2162688 | tf_op jit(solution)/shard_map/all_to_all | solution.py:416
  73.0 89.0 %halves.1 = (bf16[288,2048]{1,0:T(8,128)(2,1)}, bf16[288,2048]{1,0:T(8,128)(2,1)}, bf16[32,4224]{1,0:T(8,128)(2,1)}, bf16[32,4224]{1,0:T(8,128)(2,1)}) custom-call(bf16[576,2048]{1,0:T(8,128)(2,1)} %collective-permute-done.2.refs_0_.refs_4_, bf16[576,2048]{1,0:T(8,128)(2,1)} %collective-permute-done.3.refs_1_.refs_5_, bf16[64,4224]{1,0:T(8,128)(2,1)} %copy-done.11, ...), custom_call_target="tpu_custom_call" | custom-call | bytes 5799936 | tf_op jit(solution)/shard_map/halves/pallas_call | solution.py:150
  164.8 4.3 %collective-permute-start.7 = (bf16[288,2048]{1,0:T(8,128)(2,1)}, bf16[288,2048]{1,0:T(8,128)(2,1)}, u32[]{:S(2)}, u32[]{:S(2)}) collective-permute-start(bf16[288,2048]{1,0:T(8,128)(2,1)} %get-tuple-element.50), channel_id=1, source_target_pairs={{0,1},{1,2},{2,3},{3,0},{4,5},{5,6},{6,7},{7,4},{8,9},{9,10},{10,1... | collective-permute-start | bytes 3538952 | tf_op jit(solution)/shard_map/ppermute | solution.py:28
  169.1 5.3 %collective-permute-start.4 = (bf16[32,4224]{1,0:T(8,128)(2,1)}, bf16[32,4224]{1,0:T(8,128)(2,1)S(1)}, u32[]{:S(2)}, u32[]{:S(2)}) collective-permute-start(bf16[32,4224]{1,0:T(8,128)(2,1)} %get-tuple-element.42), channel_id=1, source_target_pairs={{0,284},{4,0},{8,4},{12,8},{16,12},{20,16},{24,20},{28,24},{256,28... | collective-permute-start | bytes 811016 | tf_op jit(solution)/shard_map/ppermute | solution.py:28
  176.4 4.2 %collective-permute-done.4.refs_1_ = bf16[32,4224]{1,0:T(8,128)(2,1)S(1)} collective-permute-done((bf16[32,4224]{1,0:T(8,128)(2,1)}, bf16[32,4224]{1,0:T(8,128)(2,1)S(1)}, u32[]{:S(2)}, u32[]{:S(2)}) %collective-permute-start.4) | collective-permute-done | bytes 270368 | tf_op jit(solution)/shard_map/ppermute | solution.py:28
  180.6 5.2 %collective-permute-done.5.refs_2_ = bf16[32,4224]{1,0:T(8,128)(2,1)S(1)} collective-permute-done((bf16[32,4224]{1,0:T(8,128)(2,1)}, bf16[32,4224]{1,0:T(8,128)(2,1)S(1)}, u32[]{:S(2)}, u32[]{:S(2)}) %collective-permute-start.5) | collective-permute-done | bytes 270368 | tf_op jit(solution)/shard_map/ppermute | solution.py:28
  189.0 4.4 %all-to-all-start.2 = ((bf16[8,8,4224]{2,1,0:T(8,128)(2,1)}), bf16[8,8,4224]{2,1,0:T(8,128)(2,1)S(1)}, u32[]{:S(2)}, u32[]{:S(2)}) async-start(bf16[8,8,4224]{2,1,0:T(8,128)(2,1)} %bitcast.29), calls=%async_computation.2 | async-start | bytes 1081344 | tf_op jit(solution)/shard_map/all_to_all | solution.py:416
  195.8 3.6 %collective-permute-start.9 = (bf16[192,2048]{1,0:T(8,128)(2,1)S(1)}, bf16[192,2048]{1,0:T(8,128)(2,1)}, u32[]{:S(2)}, u32[]{:S(2)}) collective-permute-start(bf16[192,2048]{1,0:T(8,128)(2,1)S(1)} %pad_maximum_fusion.3.refs_9_), channel_id=1, source_target_pairs={{0,3},{1,0},{2,1},{3,2},{4,7},{5,4},{6,5},{7,6},{8,11},{9,8},{10,9... | collective-permute-start | bytes 2359304 | tf_op jit(solution)/shard_map/ppermute | solution.py:28
  199.4 4.5 %all-to-all-done.2 = bf16[8,8,4224]{2,1,0:T(8,128)(2,1)S(1)} async-done(((bf16[8,8,4224]{2,1,0:T(8,128)(2,1)}), bf16[8,8,4224]{2,1,0:T(8,128)(2,1)S(1)}, u32[]{:S(2)}, u32[]{:S(2)}) %all-to-all-start.2) | async-done | bytes 540704 | tf_op jit(solution)/shard_map/all_to_all | solution.py:416
  204.8 13.8 %rows.1 = (bf16[256,2176]{1,0:T(8,128)(2,1)}, bf16[384,256]{1,0:T(8,128)(2,1)}, bf16[192,256]{1,0:T(8,128)(2,1)}, bf16[336,2048]{1,0:T(8,128)(2,1)}, bf16[320,20...) custom-call(s32[3]{0:T(128)} %pad_add_fusion.refs_0_.zs_ref, bf16[64,4224]{1,0:T(8,128)(2,1)} %bitcast.23, ...), custom_call_target="tpu_custom_call" | custom-call | flops 4026531840 | bytes 12582912 | tf_op jit(solution)/shard_map/rows/pallas_call | solution.py:259
  221.2 4.6 %collective-permute-start.10 = (bf16[336,2048]{1,0:T(8,128)(2,1)}, bf16[336,2048]{1,0:T(8,128)(2,1)S(1)}, u32[]{:S(2)}, u32[]{:S(2)}) collective-permute-start(bf16[336,2048]{1,0:T(8,128)(2,1)} %get-tuple-element.58), channel_id=1, source_target_pairs={{0,1},{1,2},{2,3},{3,0},{4,5},{5,6},{6,7},{7,4},{8,9},{9,10},{10,1... | collective-permute-start | bytes 4128776 | tf_op jit(solution)/shard_map/ppermute | solution.py:28
  228.2 11.2 %all-to-all-start.3 = ((bf16[128,2,2176]{2,1,0:T(2,128)(2,1)}), bf16[128,2,2176]{2,1,0:T(2,128)(2,1)}, u32[]{:S(2)}, u32[]{:S(2)}) async-start(bf16[128,2,2176]{2,1,0:T(2,128)(2,1)} %reshape.40), calls=%async_computation.3 | async-start | bytes 2228224 | tf_op jit(solution)/shard_map/all_to_all | solution.py:440
  240.5 11.8 %collective-permute-done.11.refs_3_.refs_14_ = bf16[320,2048]{1,0:T(8,128)(2,1)} collective-permute-done((bf16[320,2048]{1,0:T(8,128)(2,1)}, bf16[320,2048]{1,0:T(8,128)(2,1)}, u32[]{:S(2)}, u32[]{:S(2)}) %collective-permute-start.11) | collective-permute-done | bytes 1310752 | tf_op jit(solution)/shard_map/ppermute | solution.py:28
  255.5 5.6 %collective-permute-start.12 = (bf16[256,2048]{1,0:T(8,128)(2,1)S(1)}, bf16[256,2048]{1,0:T(8,128)(2,1)S(1)}, u32[]{:S(2)}, u32[]{:S(2)}) collective-permute-start(bf16[256,2048]{1,0:T(8,128)(2,1)S(1)} %pad_maximum_fusion.1), channel_id=1, source_target_pairs={{0,1},{1,2},{2,3},{3,0},{4,5},{5,6},{6,7},{7,4},{8,9},{9,10},{10,1... | collective-permute-start | bytes 3145736 | tf_op jit(solution)/shard_map/ppermute | solution.py:28
  263.2 23.0 %collective-permute-done.13.refs_5_.refs_16_ = bf16[240,2048]{1,0:T(8,128)(2,1)S(1)} collective-permute-done((bf16[240,2048]{1,0:T(8,128)(2,1)S(1)}, bf16[240,2048]{1,0:T(8,128)(2,1)S(1)}, u32[]{:S(2)}, u32[]{:S(2)}) %collective-permute-start.13) | collective-permute-done | bytes 983072 | tf_op jit(solution)/shard_map/ppermute | solution.py:28
  286.3 5.5 %weight_grads.1 = (bf16[192,2048]{1,0:T(8,128)(2,1)}, bf16[192,2048]{1,0:T(8,128)(2,1)}, bf16[192,2048]{1,0:T(8,128)(2,1)}) custom-call(bf16[192,256]{1,0:T(8,128)(2,1)S(1)} %copy-done.9, bf16[384,256]{1,0:T(8,128)(2,1)S(1)} %copy-done.8, bf16[336,2048]{1,0:T(8,128)(2,1)S(1)} %collective-permute-done.10.refs_2_.refs_13_, ...), custom_call_target="tpu_custom_call" | custom-call | flops 16106127360 | bytes 10747904 | tf_op jit(solution)/shard_map/weight_grads/pallas_call | solution.py:347
  291.7 6.5 %all-to-all-done.3 = bf16[128,2,2176]{2,1,0:T(2,128)(2,1)} async-done(((bf16[128,2,2176]{2,1,0:T(2,128)(2,1)}), bf16[128,2,2176]{2,1,0:T(2,128)(2,1)}, u32[]{:S(2)}, u32[]{:S(2)}) %all-to-all-start.3) | async-done | bytes 1114144 | tf_op jit(solution)/shard_map/all_to_all | solution.py:440
  (73 shorter events, 38.7 us)
Async XLA Ops:
  4.0 60.1 %collective-permute-start.2 = (bf16[576,2048]{1,0:T(8,128)(2,1)}, bf16[576,2048]{1,0:T(8,128)(2,1)}, u32[]{:S(2)}, u32[]{:S(2)}) collective-permute-start(bf16[576,2048]{1,0:T(8,128)(2,1)} %pad_maximum_fusion.refs_3_), channel_id=1, source_target_pairs={{0,1},{1,2},{2,3},{3,0},{4,5},{5,6},{6,7},{7,4},{8,9},{9,10},{10,1... | collective-permute-start | bytes 7077896 | tf_op jit(solution)/shard_map/ppermute | solution.py:28
  11.7 52.4 %collective-permute-start.3 = (bf16[576,2048]{1,0:T(8,128)(2,1)}, bf16[576,2048]{1,0:T(8,128)(2,1)}, u32[]{:S(2)}, u32[]{:S(2)}) collective-permute-start(bf16[576,2048]{1,0:T(8,128)(2,1)} %pad_maximum_fusion.refs_3_), channel_id=1, source_target_pairs={{0,3},{1,0},{2,1},{3,2},{4,7},{5,4},{6,5},{7,6},{8,11},{9,8},{10,9... | collective-permute-start | bytes 7077896 | tf_op jit(solution)/shard_map/ppermute | solution.py:28
  44.1 14.8 %collective-permute-start = (bf16[64,4224]{1,0:T(8,128)(2,1)S(1)}, bf16[64,4224]{1,0:T(8,128)(2,1)S(1)}, u32[]{:S(2)}, u32[]{:S(2)}) collective-permute-start(bf16[64,4224]{1,0:T(8,128)(2,1)S(1)} %all_gather.3.refs_1_), channel_id=1, source_target_pairs={{0,4},{4,8},{8,12},{12,16},{16,20},{20,24},{24,28},{28,256},{256,2... | collective-permute-start | bytes 1622024 | tf_op jit(solution)/shard_map/ppermute | solution.py:28
  47.8 12.3 %collective-permute-start.1 = (bf16[64,4224]{1,0:T(8,128)(2,1)S(1)}, bf16[64,4224]{1,0:T(8,128)(2,1)S(1)}, u32[]{:S(2)}, u32[]{:S(2)}) collective-permute-start(bf16[64,4224]{1,0:T(8,128)(2,1)S(1)} %all_gather.3.refs_1_), channel_id=1, source_target_pairs={{0,284},{4,0},{8,4},{12,8},{16,12},{20,16},{24,20},{28,24},{256,28... | collective-permute-start | bytes 1622024 | tf_op jit(solution)/shard_map/ppermute | solution.py:28
  54.5 15.0 %all-to-all-start = ((bf16[8,8,4224]{2,1,0:T(8,128)(2,1)}), bf16[8,8,4224]{2,1,0:T(8,128)(2,1)S(1)}, u32[]{:S(2)}, u32[]{:S(2)}) async-start(bf16[8,8,4224]{2,1,0:T(8,128)(2,1)} %bitcast.30), calls=%async_computation | async-start | bytes 1081344 | tf_op jit(solution)/shard_map/all_to_all | solution.py:416
  69.5 106.9 %copy-start.2 = (bf16[8,8,4224]{2,1,0:T(8,128)(2,1)}, bf16[8,8,4224]{2,1,0:T(8,128)(2,1)S(1)}, u32[]{:S(2)}) copy-start(bf16[8,8,4224]{2,1,0:T(8,128)(2,1)S(1)} %all-to-all-done) | copy-start | bytes 1622020
  69.5 119.5 %all-to-all-start.1 = ((bf16[8,16,4224]{2,1,0:T(8,128)(2,1)}), bf16[8,16,4224]{2,1,0:T(8,128)(2,1)S(1)}, u32[]{:S(2)}, u32[]{:S(2)}) async-start(bf16[8,16,4224]{2,1,0:T(8,128)(2,1)} %bitcast.28), calls=%async_computation.1 | async-start | bytes 2162688 | tf_op jit(solution)/shard_map/all_to_all | solution.py:416
  162.0 37.4 %collective-permute-start.6 = (bf16[288,2048]{1,0:T(8,128)(2,1)}, bf16[288,2048]{1,0:T(8,128)(2,1)}, u32[]{:S(2)}, u32[]{:S(2)}) collective-permute-start(bf16[288,2048]{1,0:T(8,128)(2,1)} %get-tuple-element.49), channel_id=1, source_target_pairs={{0,3},{1,0},{2,1},{3,2},{4,7},{5,4},{6,5},{7,6},{8,11},{9,8},{10,9... | collective-permute-start | bytes 3538952 | tf_op jit(solution)/shard_map/ppermute | solution.py:28
  164.8 34.6 %collective-permute-start.7 = (bf16[288,2048]{1,0:T(8,128)(2,1)}, bf16[288,2048]{1,0:T(8,128)(2,1)}, u32[]{:S(2)}, u32[]{:S(2)}) collective-permute-start(bf16[288,2048]{1,0:T(8,128)(2,1)} %get-tuple-element.50), channel_id=1, source_target_pairs={{0,1},{1,2},{2,3},{3,0},{4,5},{5,6},{6,7},{7,4},{8,9},{9,10},{10,1... | collective-permute-start | bytes 3538952 | tf_op jit(solution)/shard_map/ppermute | solution.py:28
  169.1 11.5 %collective-permute-start.4 = (bf16[32,4224]{1,0:T(8,128)(2,1)}, bf16[32,4224]{1,0:T(8,128)(2,1)S(1)}, u32[]{:S(2)}, u32[]{:S(2)}) collective-permute-start(bf16[32,4224]{1,0:T(8,128)(2,1)} %get-tuple-element.42), channel_id=1, source_target_pairs={{0,284},{4,0},{8,4},{12,8},{16,12},{20,16},{24,20},{28,24},{256,28... | collective-permute-start | bytes 811016 | tf_op jit(solution)/shard_map/ppermute | solution.py:28
  174.4 11.4 %collective-permute-start.5 = (bf16[32,4224]{1,0:T(8,128)(2,1)}, bf16[32,4224]{1,0:T(8,128)(2,1)S(1)}, u32[]{:S(2)}, u32[]{:S(2)}) collective-permute-start(bf16[32,4224]{1,0:T(8,128)(2,1)} %get-tuple-element.43), channel_id=1, source_target_pairs={{0,4},{4,8},{8,12},{12,16},{16,20},{20,24},{24,28},{28,256},{256,2... | collective-permute-start | bytes 811016 | tf_op jit(solution)/shard_map/ppermute | solution.py:28
  189.0 15.0 %all-to-all-start.2 = ((bf16[8,8,4224]{2,1,0:T(8,128)(2,1)}), bf16[8,8,4224]{2,1,0:T(8,128)(2,1)S(1)}, u32[]{:S(2)}, u32[]{:S(2)}) async-start(bf16[8,8,4224]{2,1,0:T(8,128)(2,1)} %bitcast.29), calls=%async_computation.2 | async-start | bytes 1081344 | tf_op jit(solution)/shard_map/all_to_all | solution.py:416
  193.5 25.0 %collective-permute-start.8 = (bf16[192,2048]{1,0:T(8,128)(2,1)S(1)}, bf16[192,2048]{1,0:T(8,128)(2,1)S(1)}, u32[]{:S(2)}, u32[]{:S(2)}) collective-permute-start(bf16[192,2048]{1,0:T(8,128)(2,1)S(1)} %pad_maximum_fusion.3.refs_9_), channel_id=1, source_target_pairs={{0,1},{1,2},{2,3},{3,0},{4,5},{5,6},{6,7},{7,4},{8,9},{9,10},{10,1... | collective-permute-start | bytes 2359304 | tf_op jit(solution)/shard_map/ppermute | solution.py:28
  195.8 22.9 %collective-permute-start.9 = (bf16[192,2048]{1,0:T(8,128)(2,1)S(1)}, bf16[192,2048]{1,0:T(8,128)(2,1)}, u32[]{:S(2)}, u32[]{:S(2)}) collective-permute-start(bf16[192,2048]{1,0:T(8,128)(2,1)S(1)} %pad_maximum_fusion.3.refs_9_), channel_id=1, source_target_pairs={{0,3},{1,0},{2,1},{3,2},{4,7},{5,4},{6,5},{7,6},{8,11},{9,8},{10,9... | collective-permute-start | bytes 2359304 | tf_op jit(solution)/shard_map/ppermute | solution.py:28
  218.6 33.7 %collective-permute-start.11 = (bf16[320,2048]{1,0:T(8,128)(2,1)}, bf16[320,2048]{1,0:T(8,128)(2,1)}, u32[]{:S(2)}, u32[]{:S(2)}) collective-permute-start(bf16[320,2048]{1,0:T(8,128)(2,1)} %get-tuple-element.59), channel_id=1, source_target_pairs={{0,3},{1,0},{2,1},{3,2},{4,7},{5,4},{6,5},{7,6},{8,11},{9,8},{10,9... | collective-permute-start | bytes 3932168 | tf_op jit(solution)/shard_map/ppermute | solution.py:28
  221.2 33.9 %collective-permute-start.10 = (bf16[336,2048]{1,0:T(8,128)(2,1)}, bf16[336,2048]{1,0:T(8,128)(2,1)S(1)}, u32[]{:S(2)}, u32[]{:S(2)}) collective-permute-start(bf16[336,2048]{1,0:T(8,128)(2,1)} %get-tuple-element.58), channel_id=1, source_target_pairs={{0,1},{1,2},{2,3},{3,0},{4,5},{5,6},{6,7},{7,4},{8,9},{9,10},{10,1... | collective-permute-start | bytes 4128776 | tf_op jit(solution)/shard_map/ppermute | solution.py:28
  228.2 70.0 %all-to-all-start.3 = ((bf16[128,2,2176]{2,1,0:T(2,128)(2,1)}), bf16[128,2,2176]{2,1,0:T(2,128)(2,1)}, u32[]{:S(2)}, u32[]{:S(2)}) async-start(bf16[128,2,2176]{2,1,0:T(2,128)(2,1)} %reshape.40), calls=%async_computation.3 | async-start | bytes 2228224 | tf_op jit(solution)/shard_map/all_to_all | solution.py:440
  255.4 30.9 %copy-start.1 = (bf16[8,16,4224]{2,1,0:T(8,128)(2,1)S(1)}, bf16[8,16,4224]{2,1,0:T(8,128)(2,1)}, u32[]{:S(2)}) copy-start(bf16[8,16,4224]{2,1,0:T(8,128)(2,1)} %copy-done) | copy-start | bytes 3244036
  255.4 30.9 %copy-start.3 = (bf16[8,8,4224]{2,1,0:T(8,128)(2,1)S(1)}, bf16[8,8,4224]{2,1,0:T(8,128)(2,1)}, u32[]{:S(2)}) copy-start(bf16[8,8,4224]{2,1,0:T(8,128)(2,1)} %copy-done.2) | copy-start | bytes 1622020
  255.4 30.9 %copy-start.7 = (bf16[192,2048]{1,0:T(8,128)(2,1)S(1)}, bf16[192,2048]{1,0:T(8,128)(2,1)}, u32[]{:S(2)}) copy-start(bf16[192,2048]{1,0:T(8,128)(2,1)} %copy-done.6) | copy-start | bytes 2359300
  255.4 30.9 %copy-start.8 = (bf16[384,256]{1,0:T(8,128)(2,1)S(1)}, bf16[384,256]{1,0:T(8,128)(2,1)}, u32[]{:S(2)}) copy-start(bf16[384,256]{1,0:T(8,128)(2,1)} %get-tuple-element.55.refs_1_) | copy-start | bytes 589828
  255.4 30.9 %copy-start.9 = (bf16[192,256]{1,0:T(8,128)(2,1)S(1)}, bf16[192,256]{1,0:T(8,128)(2,1)}, u32[]{:S(2)}) copy-start(bf16[192,256]{1,0:T(8,128)(2,1)} %get-tuple-element.54.refs_0_) | copy-start | bytes 294916
  255.5 30.7 %collective-permute-start.12 = (bf16[256,2048]{1,0:T(8,128)(2,1)S(1)}, bf16[256,2048]{1,0:T(8,128)(2,1)S(1)}, u32[]{:S(2)}, u32[]{:S(2)}) collective-permute-start(bf16[256,2048]{1,0:T(8,128)(2,1)S(1)} %pad_maximum_fusion.1), channel_id=1, source_target_pairs={{0,1},{1,2},{2,3},{3,0},{4,5},{5,6},{6,7},{7,4},{8,9},{9,10},{10,1... | collective-permute-start | bytes 3145736 | tf_op jit(solution)/shard_map/ppermute | solution.py:28
  261.2 25.0 %collective-permute-start.13 = (bf16[240,2048]{1,0:T(8,128)(2,1)S(1)}, bf16[240,2048]{1,0:T(8,128)(2,1)S(1)}, u32[]{:S(2)}, u32[]{:S(2)}) collective-permute-start(bf16[240,2048]{1,0:T(8,128)(2,1)S(1)} %pad_maximum_fusion.2), channel_id=1, source_target_pairs={{0,3},{1,0},{2,1},{3,2},{4,7},{5,4},{6,5},{7,6},{8,11},{9,8},{10,9... | collective-permute-start | bytes 2949128 | tf_op jit(solution)/shard_map/ppermute | solution.py:28
  (12 other events, 106.9 us)

commit v12 on v11

--- a/solution.py
+++ b/solution.py
@@ -151,7 +151,7 @@
         halves_kernel,
         out_shape=[jax.ShapeDtypeStruct((b.shape[0] // 2, b.shape[1]), BF) for b in blocks],
         in_specs=[pl.BlockSpec(memory_space=pl.ANY)] * len(blocks),
-        out_specs=[pl.BlockSpec(memory_space=pl.ANY)] * len(blocks),
+        out_specs=[vmem()] * len(blocks),
         scratch_shapes=[pltpu.SemaphoreType.DMA((len(blocks),))],
         cost_estimate=pl.CostEstimate(
             flops=0, bytes_accessed=2 * sum(b.size for b in blocks), transcendentals=0

time: 304 us -> 219 us (0.72)
  Pallas kernels: 120 us -> 34.8 us
    pallas_call x1, Pallas kernels: 89 us -> 3.44 us  [halves_call(): pl.pallas_call(halves_kernel, out_shape=[jax.ShapeDtypeStruct((b.shape[0]...]
  transfers between devices with their start and end apart: 18 -> 18, of which waited for: 9 -> 9; matrix products, arithmetic and copies ran while one was open for 2% -> 3% of each run, Pallas kernels for 39% -> 15%
where the time goes in v12:
time: 219 us; the launch traced here: 217 us
  starting transfers between devices  75.7 us (35%)
  waiting for transfers between devices  61.8 us (28%)
  Pallas kernels  34.8 us (16%)
  blocking collectives  28.5 us (13%)
  local copies, waits for them, and re-layouts  9.98 us (5%)
  other arithmetic  5.35 us (2%)
    ppermute x14, starting transfers between devices, shift(): return lax.ppermute(block, axes, [(i, (i + step) % n) for i in range(n)])  52 us
    ppermute x14, waiting for transfers between devices, shift(): return lax.ppermute(block, axes, [(i, (i + step) % n) for i in range(n)])  45.4 us
    all_gather x1, blocking collectives, local(): chunk = lax.all_gather(own, FAR, axis=0, tiled=True)  28.5 us
    pallas_call x1, Pallas kernels, rows_call(): pl.pallas_call(rows_kernel, out_shape=[jax.ShapeDtypeStruct((count, featu...  13.8 us
    all_to_all x3, starting transfers between devices, exchange(): lax.all_to_all(packed.reshape(8, rows // 8, width), YC, split_axis=0, con...  12.5 us
    all_to_all x1, starting transfers between devices, local(): lax.all_to_all(back.reshape(-1, CAPACITY, back.shape[1]), PLACE, split_ax...  11.2 us
    all_to_all x3, waiting for transfers between devices, exchange(): lax.all_to_all(packed.reshape(8, rows // 8, width), YC, split_axis=0, con...  9.88 us
    pallas_call x3, Pallas kernels, pack_call(): pl.pallas_call(body, out_shape=jax.ShapeDtypeStruct((rows, width), BF), i...  7.97 us
  transfers between devices with their start and end apart: 18, of which 9 were waited for; matrix products, arithmetic and copies ran while one was open for 3% of the time, Pallas kernels for 15%

profile of v12, /device:TPU:6, one launch (start us, length us, event | category | flops | bytes accessed | tf_op | source)
XLA Modules:
  0.0 217.2 jit_solution(15141731478291137963)
XLA Ops:
  0.6 3.3 %pad_maximum_fusion.refs_3_ = bf16[576,2048]{1,0:T(8,128)(2,1)} fusion(bf16[192,2048]{1,0:T(8,128)(2,1)} %bitcast.31, bf16[192,2048]{1,0:T(8,128)(2,1)} %bitcast.32, bf16[192,2048]{1,0:T(8,128)(2,1)} %bitcast.33), kind=kLoop, calls=%fused_computation | loop fusion | flops 7077888 | bytes 4718592 | tf_op jit(solution)/shard_map/concatenate | solution.py:407
  4.0 7.7 %collective-permute-start.2 = (bf16[576,2048]{1,0:T(8,128)(2,1)}, bf16[576,2048]{1,0:T(8,128)(2,1)}, u32[]{:S(2)}, u32[]{:S(2)}) collective-permute-start(bf16[576,2048]{1,0:T(8,128)(2,1)} %pad_maximum_fusion.refs_3_), channel_id=1, source_target_pairs={{0,1},{1,2},{2,3},{3,0},{4,5},{5,6},{6,7},{7,4},{8,9},{9,10},{10,1... | collective-permute-start | bytes 7077896 | tf_op jit(solution)/shard_map/ppermute | solution.py:28
  15.6 28.5 %all_gather.3.refs_1_ = bf16[64,4224]{1,0:T(8,128)(2,1)S(1)} all-gather(bf16[16,4224]{1,0:T(8,128)(2,1)} %get-tuple-element.37), channel_id=1, replica_groups=mesh['zh'=2,'y'=4,'c'=2,'zq'=2,'zr'=4,'x'=4] {'zh','zq'}, dimensions={0}, use_global_device_ids=true | all-gather | bytes 675840 | tf_op jit(solution)/shard_map/all_gather | solution.py:411
  44.1 3.7 %collective-permute-start = (bf16[64,4224]{1,0:T(8,128)(2,1)S(1)}, bf16[64,4224]{1,0:T(8,128)(2,1)S(1)}, u32[]{:S(2)}, u32[]{:S(2)}) collective-permute-start(bf16[64,4224]{1,0:T(8,128)(2,1)S(1)} %all_gather.3.refs_1_), channel_id=1, source_target_pairs={{0,4},{4,8},{8,12},{12,16},{16,20},{20,24},{24,28},{28,256},{256,2... | collective-permute-start | bytes 1622024 | tf_op jit(solution)/shard_map/ppermute | solution.py:28
  47.8 3.7 %collective-permute-start.1 = (bf16[64,4224]{1,0:T(8,128)(2,1)S(1)}, bf16[64,4224]{1,0:T(8,128)(2,1)S(1)}, u32[]{:S(2)}, u32[]{:S(2)}) collective-permute-start(bf16[64,4224]{1,0:T(8,128)(2,1)S(1)} %all_gather.3.refs_1_), channel_id=1, source_target_pairs={{0,284},{4,0},{8,4},{12,8},{16,12},{20,16},{24,20},{28,24},{256,28... | collective-permute-start | bytes 1622024 | tf_op jit(solution)/shard_map/ppermute | solution.py:28
  54.5 4.5 %all-to-all-start = ((bf16[8,8,4224]{2,1,0:T(8,128)(2,1)}), bf16[8,8,4224]{2,1,0:T(8,128)(2,1)S(1)}, u32[]{:S(2)}, u32[]{:S(2)}) async-start(bf16[8,8,4224]{2,1,0:T(8,128)(2,1)} %bitcast.30), calls=%async_computation | async-start | bytes 1081344 | tf_op jit(solution)/shard_map/all_to_all | solution.py:416
  64.1 5.3 %all-to-all-done = bf16[8,8,4224]{2,1,0:T(8,128)(2,1)S(1)} async-done(((bf16[8,8,4224]{2,1,0:T(8,128)(2,1)}), bf16[8,8,4224]{2,1,0:T(8,128)(2,1)S(1)}, u32[]{:S(2)}, u32[]{:S(2)}) %all-to-all-start) | async-done | bytes 540704 | tf_op jit(solution)/shard_map/all_to_all | solution.py:416
  69.5 3.6 %all-to-all-start.1 = ((bf16[8,16,4224]{2,1,0:T(8,128)(2,1)}), bf16[8,16,4224]{2,1,0:T(8,128)(2,1)S(1)}, u32[]{:S(2)}, u32[]{:S(2)}) async-start(bf16[8,16,4224]{2,1,0:T(8,128)(2,1)} %bitcast.28), calls=%async_computation.1 | async-start | bytes 2162688 | tf_op jit(solution)/shard_map/all_to_all | solution.py:416
  73.0 3.4 %halves.1 = (bf16[288,2048]{1,0:T(8,128)(2,1)}, bf16[288,2048]{1,0:T(8,128)(2,1)}, bf16[32,4224]{1,0:T(8,128)(2,1)}, bf16[32,4224]{1,0:T(8,128)(2,1)}) custom-call(bf16[576,2048]{1,0:T(8,128)(2,1)} %collective-permute-done.2.refs_0_.refs_4_, bf16[576,2048]{1,0:T(8,128)(2,1)} %collective-permute-done.3.refs_1_.refs_5_, bf16[64,4224]{1,0:T(8,128)(2,1)} %copy-done.11, ...), custom_call_target="tpu_custom_call" | custom-call | bytes 5799936 | tf_op jit(solution)/shard_map/halves/pallas_call | solution.py:150
  79.2 4.3 %collective-permute-start.7 = (bf16[288,2048]{1,0:T(8,128)(2,1)}, bf16[288,2048]{1,0:T(8,128)(2,1)}, u32[]{:S(2)}, u32[]{:S(2)}) collective-permute-start(bf16[288,2048]{1,0:T(8,128)(2,1)} %get-tuple-element.50), channel_id=1, source_target_pairs={{0,1},{1,2},{2,3},{3,0},{4,5},{5,6},{6,7},{7,4},{8,9},{9,10},{10,1... | collective-permute-start | bytes 3538952 | tf_op jit(solution)/shard_map/ppermute | solution.py:28
  83.5 5.3 %collective-permute-start.4 = (bf16[32,4224]{1,0:T(8,128)(2,1)}, bf16[32,4224]{1,0:T(8,128)(2,1)S(1)}, u32[]{:S(2)}, u32[]{:S(2)}) collective-permute-start(bf16[32,4224]{1,0:T(8,128)(2,1)} %get-tuple-element.42), channel_id=1, source_target_pairs={{0,284},{4,0},{8,4},{12,8},{16,12},{20,16},{24,20},{28,24},{256,28... | collective-permute-start | bytes 811016 | tf_op jit(solution)/shard_map/ppermute | solution.py:28
  90.8 4.2 %collective-permute-done.4.refs_1_ = bf16[32,4224]{1,0:T(8,128)(2,1)S(1)} collective-permute-done((bf16[32,4224]{1,0:T(8,128)(2,1)}, bf16[32,4224]{1,0:T(8,128)(2,1)S(1)}, u32[]{:S(2)}, u32[]{:S(2)}) %collective-permute-start.4) | collective-permute-done | bytes 270368 | tf_op jit(solution)/shard_map/ppermute | solution.py:28
  95.0 5.2 %collective-permute-done.5.refs_2_ = bf16[32,4224]{1,0:T(8,128)(2,1)S(1)} collective-permute-done((bf16[32,4224]{1,0:T(8,128)(2,1)}, bf16[32,4224]{1,0:T(8,128)(2,1)S(1)}, u32[]{:S(2)}, u32[]{:S(2)}) %collective-permute-start.5) | collective-permute-done | bytes 270368 | tf_op jit(solution)/shard_map/ppermute | solution.py:28
  103.4 4.4 %all-to-all-start.2 = ((bf16[8,8,4224]{2,1,0:T(8,128)(2,1)}), bf16[8,8,4224]{2,1,0:T(8,128)(2,1)S(1)}, u32[]{:S(2)}, u32[]{:S(2)}) async-start(bf16[8,8,4224]{2,1,0:T(8,128)(2,1)} %bitcast.29), calls=%async_computation.2 | async-start | bytes 1081344 | tf_op jit(solution)/shard_map/all_to_all | solution.py:416
  110.2 3.6 %collective-permute-start.9 = (bf16[192,2048]{1,0:T(8,128)(2,1)S(1)}, bf16[192,2048]{1,0:T(8,128)(2,1)}, u32[]{:S(2)}, u32[]{:S(2)}) collective-permute-start(bf16[192,2048]{1,0:T(8,128)(2,1)S(1)} %pad_maximum_fusion.3.refs_9_), channel_id=1, source_target_pairs={{0,3},{1,0},{2,1},{3,2},{4,7},{5,4},{6,5},{7,6},{8,11},{9,8},{10,9... | collective-permute-start | bytes 2359304 | tf_op jit(solution)/shard_map/ppermute | solution.py:28
  113.9 4.5 %all-to-all-done.2 = bf16[8,8,4224]{2,1,0:T(8,128)(2,1)S(1)} async-done(((bf16[8,8,4224]{2,1,0:T(8,128)(2,1)}), bf16[8,8,4224]{2,1,0:T(8,128)(2,1)S(1)}, u32[]{:S(2)}, u32[]{:S(2)}) %all-to-all-start.2) | async-done | bytes 540704 | tf_op jit(solution)/shard_map/all_to_all | solution.py:416
  119.2 13.8 %rows.1 = (bf16[256,2176]{1,0:T(8,128)(2,1)}, bf16[384,256]{1,0:T(8,128)(2,1)}, bf16[192,256]{1,0:T(8,128)(2,1)}, bf16[336,2048]{1,0:T(8,128)(2,1)}, bf16[320,20...) custom-call(s32[3]{0:T(128)} %pad_add_fusion.refs_0_.zs_ref, bf16[64,4224]{1,0:T(8,128)(2,1)} %bitcast.23, ...), custom_call_target="tpu_custom_call" | custom-call | flops 4026531840 | bytes 12582912 | tf_op jit(solution)/shard_map/rows/pallas_call | solution.py:259
  135.7 4.6 %collective-permute-start.10 = (bf16[336,2048]{1,0:T(8,128)(2,1)}, bf16[336,2048]{1,0:T(8,128)(2,1)S(1)}, u32[]{:S(2)}, u32[]{:S(2)}) collective-permute-start(bf16[336,2048]{1,0:T(8,128)(2,1)} %get-tuple-element.58), channel_id=1, source_target_pairs={{0,1},{1,2},{2,3},{3,0},{4,5},{5,6},{6,7},{7,4},{8,9},{9,10},{10,1... | collective-permute-start | bytes 4128776 | tf_op jit(solution)/shard_map/ppermute | solution.py:28
  142.6 11.2 %all-to-all-start.3 = ((bf16[128,2,2176]{2,1,0:T(2,128)(2,1)}), bf16[128,2,2176]{2,1,0:T(2,128)(2,1)}, u32[]{:S(2)}, u32[]{:S(2)}) async-start(bf16[128,2,2176]{2,1,0:T(2,128)(2,1)} %reshape.40), calls=%async_computation.3 | async-start | bytes 2228224 | tf_op jit(solution)/shard_map/all_to_all | solution.py:440
  155.0 11.8 %collective-permute-done.11.refs_3_.refs_14_ = bf16[320,2048]{1,0:T(8,128)(2,1)} collective-permute-done((bf16[320,2048]{1,0:T(8,128)(2,1)}, bf16[320,2048]{1,0:T(8,128)(2,1)}, u32[]{:S(2)}, u32[]{:S(2)}) %collective-permute-start.11) | collective-permute-done | bytes 1310752 | tf_op jit(solution)/shard_map/ppermute | solution.py:28
  169.9 5.6 %collective-permute-start.12 = (bf16[256,2048]{1,0:T(8,128)(2,1)S(1)}, bf16[256,2048]{1,0:T(8,128)(2,1)S(1)}, u32[]{:S(2)}, u32[]{:S(2)}) collective-permute-start(bf16[256,2048]{1,0:T(8,128)(2,1)S(1)} %pad_maximum_fusion.1), channel_id=1, source_target_pairs={{0,1},{1,2},{2,3},{3,0},{4,5},{5,6},{6,7},{7,4},{8,9},{9,10},{10,1... | collective-permute-start | bytes 3145736 | tf_op jit(solution)/shard_map/ppermute | solution.py:28
  177.7 23.0 %collective-permute-done.13.refs_5_.refs_16_ = bf16[240,2048]{1,0:T(8,128)(2,1)S(1)} collective-permute-done((bf16[240,2048]{1,0:T(8,128)(2,1)S(1)}, bf16[240,2048]{1,0:T(8,128)(2,1)S(1)}, u32[]{:S(2)}, u32[]{:S(2)}) %collective-permute-start.13) | collective-permute-done | bytes 983072 | tf_op jit(solution)/shard_map/ppermute | solution.py:28
  200.7 5.5 %weight_grads.1 = (bf16[192,2048]{1,0:T(8,128)(2,1)}, bf16[192,2048]{1,0:T(8,128)(2,1)}, bf16[192,2048]{1,0:T(8,128)(2,1)}) custom-call(bf16[192,256]{1,0:T(8,128)(2,1)S(1)} %copy-done.9, bf16[384,256]{1,0:T(8,128)(2,1)S(1)} %copy-done.8, bf16[336,2048]{1,0:T(8,128)(2,1)S(1)} %collective-permute-done.10.refs_2_.refs_13_, ...), custom_call_target="tpu_custom_call" | custom-call | flops 16106127360 | bytes 10747904 | tf_op jit(solution)/shard_map/weight_grads/pallas_call | solution.py:347
  206.2 6.4 %all-to-all-done.3 = bf16[128,2,2176]{2,1,0:T(2,128)(2,1)} async-done(((bf16[128,2,2176]{2,1,0:T(2,128)(2,1)}), bf16[128,2,2176]{2,1,0:T(2,128)(2,1)}, u32[]{:S(2)}, u32[]{:S(2)}) %all-to-all-start.3) | async-done | bytes 1114144 | tf_op jit(solution)/shard_map/all_to_all | solution.py:440
  (73 shorter events, 38.7 us)
Async XLA Ops:
  4.0 60.1 %collective-permute-start.2 = (bf16[576,2048]{1,0:T(8,128)(2,1)}, bf16[576,2048]{1,0:T(8,128)(2,1)}, u32[]{:S(2)}, u32[]{:S(2)}) collective-permute-start(bf16[576,2048]{1,0:T(8,128)(2,1)} %pad_maximum_fusion.refs_3_), channel_id=1, source_target_pairs={{0,1},{1,2},{2,3},{3,0},{4,5},{5,6},{6,7},{7,4},{8,9},{9,10},{10,1... | collective-permute-start | bytes 7077896 | tf_op jit(solution)/shard_map/ppermute | solution.py:28
  11.7 52.4 %collective-permute-start.3 = (bf16[576,2048]{1,0:T(8,128)(2,1)}, bf16[576,2048]{1,0:T(8,128)(2,1)}, u32[]{:S(2)}, u32[]{:S(2)}) collective-permute-start(bf16[576,2048]{1,0:T(8,128)(2,1)} %pad_maximum_fusion.refs_3_), channel_id=1, source_target_pairs={{0,3},{1,0},{2,1},{3,2},{4,7},{5,4},{6,5},{7,6},{8,11},{9,8},{10,9... | collective-permute-start | bytes 7077896 | tf_op jit(solution)/shard_map/ppermute | solution.py:28
  44.1 14.8 %collective-permute-start = (bf16[64,4224]{1,0:T(8,128)(2,1)S(1)}, bf16[64,4224]{1,0:T(8,128)(2,1)S(1)}, u32[]{:S(2)}, u32[]{:S(2)}) collective-permute-start(bf16[64,4224]{1,0:T(8,128)(2,1)S(1)} %all_gather.3.refs_1_), channel_id=1, source_target_pairs={{0,4},{4,8},{8,12},{12,16},{16,20},{20,24},{24,28},{28,256},{256,2... | collective-permute-start | bytes 1622024 | tf_op jit(solution)/shard_map/ppermute | solution.py:28
  47.8 12.3 %collective-permute-start.1 = (bf16[64,4224]{1,0:T(8,128)(2,1)S(1)}, bf16[64,4224]{1,0:T(8,128)(2,1)S(1)}, u32[]{:S(2)}, u32[]{:S(2)}) collective-permute-start(bf16[64,4224]{1,0:T(8,128)(2,1)S(1)} %all_gather.3.refs_1_), channel_id=1, source_target_pairs={{0,284},{4,0},{8,4},{12,8},{16,12},{20,16},{24,20},{28,24},{256,28... | collective-permute-start | bytes 1622024 | tf_op jit(solution)/shard_map/ppermute | solution.py:28
  54.5 15.0 %all-to-all-start = ((bf16[8,8,4224]{2,1,0:T(8,128)(2,1)}), bf16[8,8,4224]{2,1,0:T(8,128)(2,1)S(1)}, u32[]{:S(2)}, u32[]{:S(2)}) async-start(bf16[8,8,4224]{2,1,0:T(8,128)(2,1)} %bitcast.30), calls=%async_computation | async-start | bytes 1081344 | tf_op jit(solution)/shard_map/all_to_all | solution.py:416
  69.5 21.3 %copy-start.2 = (bf16[8,8,4224]{2,1,0:T(8,128)(2,1)}, bf16[8,8,4224]{2,1,0:T(8,128)(2,1)S(1)}, u32[]{:S(2)}) copy-start(bf16[8,8,4224]{2,1,0:T(8,128)(2,1)S(1)} %all-to-all-done) | copy-start | bytes 1622020
  69.5 34.0 %all-to-all-start.1 = ((bf16[8,16,4224]{2,1,0:T(8,128)(2,1)}), bf16[8,16,4224]{2,1,0:T(8,128)(2,1)S(1)}, u32[]{:S(2)}, u32[]{:S(2)}) async-start(bf16[8,16,4224]{2,1,0:T(8,128)(2,1)} %bitcast.28), calls=%async_computation.1 | async-start | bytes 2162688 | tf_op jit(solution)/shard_map/all_to_all | solution.py:416
  76.5 37.4 %collective-permute-start.6 = (bf16[288,2048]{1,0:T(8,128)(2,1)}, bf16[288,2048]{1,0:T(8,128)(2,1)}, u32[]{:S(2)}, u32[]{:S(2)}) collective-permute-start(bf16[288,2048]{1,0:T(8,128)(2,1)} %get-tuple-element.49), channel_id=1, source_target_pairs={{0,3},{1,0},{2,1},{3,2},{4,7},{5,4},{6,5},{7,6},{8,11},{9,8},{10,9... | collective-permute-start | bytes 3538952 | tf_op jit(solution)/shard_map/ppermute | solution.py:28
  79.2 34.7 %collective-permute-start.7 = (bf16[288,2048]{1,0:T(8,128)(2,1)}, bf16[288,2048]{1,0:T(8,128)(2,1)}, u32[]{:S(2)}, u32[]{:S(2)}) collective-permute-start(bf16[288,2048]{1,0:T(8,128)(2,1)} %get-tuple-element.50), channel_id=1, source_target_pairs={{0,1},{1,2},{2,3},{3,0},{4,5},{5,6},{6,7},{7,4},{8,9},{9,10},{10,1... | collective-permute-start | bytes 3538952 | tf_op jit(solution)/shard_map/ppermute | solution.py:28
  83.5 11.5 %collective-permute-start.4 = (bf16[32,4224]{1,0:T(8,128)(2,1)}, bf16[32,4224]{1,0:T(8,128)(2,1)S(1)}, u32[]{:S(2)}, u32[]{:S(2)}) collective-permute-start(bf16[32,4224]{1,0:T(8,128)(2,1)} %get-tuple-element.42), channel_id=1, source_target_pairs={{0,284},{4,0},{8,4},{12,8},{16,12},{20,16},{24,20},{28,24},{256,28... | collective-permute-start | bytes 811016 | tf_op jit(solution)/shard_map/ppermute | solution.py:28
  88.9 11.4 %collective-permute-start.5 = (bf16[32,4224]{1,0:T(8,128)(2,1)}, bf16[32,4224]{1,0:T(8,128)(2,1)S(1)}, u32[]{:S(2)}, u32[]{:S(2)}) collective-permute-start(bf16[32,4224]{1,0:T(8,128)(2,1)} %get-tuple-element.43), channel_id=1, source_target_pairs={{0,4},{4,8},{8,12},{12,16},{16,20},{20,24},{24,28},{28,256},{256,2... | collective-permute-start | bytes 811016 | tf_op jit(solution)/shard_map/ppermute | solution.py:28
  103.4 15.0 %all-to-all-start.2 = ((bf16[8,8,4224]{2,1,0:T(8,128)(2,1)}), bf16[8,8,4224]{2,1,0:T(8,128)(2,1)S(1)}, u32[]{:S(2)}, u32[]{:S(2)}) async-start(bf16[8,8,4224]{2,1,0:T(8,128)(2,1)} %bitcast.29), calls=%async_computation.2 | async-start | bytes 1081344 | tf_op jit(solution)/shard_map/all_to_all | solution.py:416
  108.0 25.0 %collective-permute-start.8 = (bf16[192,2048]{1,0:T(8,128)(2,1)S(1)}, bf16[192,2048]{1,0:T(8,128)(2,1)S(1)}, u32[]{:S(2)}, u32[]{:S(2)}) collective-permute-start(bf16[192,2048]{1,0:T(8,128)(2,1)S(1)} %pad_maximum_fusion.3.refs_9_), channel_id=1, source_target_pairs={{0,1},{1,2},{2,3},{3,0},{4,5},{5,6},{6,7},{7,4},{8,9},{9,10},{10,1... | collective-permute-start | bytes 2359304 | tf_op jit(solution)/shard_map/ppermute | solution.py:28
  110.2 22.9 %collective-permute-start.9 = (bf16[192,2048]{1,0:T(8,128)(2,1)S(1)}, bf16[192,2048]{1,0:T(8,128)(2,1)}, u32[]{:S(2)}, u32[]{:S(2)}) collective-permute-start(bf16[192,2048]{1,0:T(8,128)(2,1)S(1)} %pad_maximum_fusion.3.refs_9_), channel_id=1, source_target_pairs={{0,3},{1,0},{2,1},{3,2},{4,7},{5,4},{6,5},{7,6},{8,11},{9,8},{10,9... | collective-permute-start | bytes 2359304 | tf_op jit(solution)/shard_map/ppermute | solution.py:28
  133.1 33.7 %collective-permute-start.11 = (bf16[320,2048]{1,0:T(8,128)(2,1)}, bf16[320,2048]{1,0:T(8,128)(2,1)}, u32[]{:S(2)}, u32[]{:S(2)}) collective-permute-start(bf16[320,2048]{1,0:T(8,128)(2,1)} %get-tuple-element.59), channel_id=1, source_target_pairs={{0,3},{1,0},{2,1},{3,2},{4,7},{5,4},{6,5},{7,6},{8,11},{9,8},{10,9... | collective-permute-start | bytes 3932168 | tf_op jit(solution)/shard_map/ppermute | solution.py:28
  135.7 33.9 %collective-permute-start.10 = (bf16[336,2048]{1,0:T(8,128)(2,1)}, bf16[336,2048]{1,0:T(8,128)(2,1)S(1)}, u32[]{:S(2)}, u32[]{:S(2)}) collective-permute-start(bf16[336,2048]{1,0:T(8,128)(2,1)} %get-tuple-element.58), channel_id=1, source_target_pairs={{0,1},{1,2},{2,3},{3,0},{4,5},{5,6},{6,7},{7,4},{8,9},{9,10},{10,1... | collective-permute-start | bytes 4128776 | tf_op jit(solution)/shard_map/ppermute | solution.py:28
  142.6 70.0 %all-to-all-start.3 = ((bf16[128,2,2176]{2,1,0:T(2,128)(2,1)}), bf16[128,2,2176]{2,1,0:T(2,128)(2,1)}, u32[]{:S(2)}, u32[]{:S(2)}) async-start(bf16[128,2,2176]{2,1,0:T(2,128)(2,1)} %reshape.40), calls=%async_computation.3 | async-start | bytes 2228224 | tf_op jit(solution)/shard_map/all_to_all | solution.py:440
  169.8 30.9 %copy-start.1 = (bf16[8,16,4224]{2,1,0:T(8,128)(2,1)S(1)}, bf16[8,16,4224]{2,1,0:T(8,128)(2,1)}, u32[]{:S(2)}) copy-start(bf16[8,16,4224]{2,1,0:T(8,128)(2,1)} %copy-done) | copy-start | bytes 3244036
  169.8 30.9 %copy-start.3 = (bf16[8,8,4224]{2,1,0:T(8,128)(2,1)S(1)}, bf16[8,8,4224]{2,1,0:T(8,128)(2,1)}, u32[]{:S(2)}) copy-start(bf16[8,8,4224]{2,1,0:T(8,128)(2,1)} %copy-done.2) | copy-start | bytes 1622020
  169.8 30.9 %copy-start.7 = (bf16[192,2048]{1,0:T(8,128)(2,1)S(1)}, bf16[192,2048]{1,0:T(8,128)(2,1)}, u32[]{:S(2)}) copy-start(bf16[192,2048]{1,0:T(8,128)(2,1)} %copy-done.6) | copy-start | bytes 2359300
  169.9 30.9 %copy-start.8 = (bf16[384,256]{1,0:T(8,128)(2,1)S(1)}, bf16[384,256]{1,0:T(8,128)(2,1)}, u32[]{:S(2)}) copy-start(bf16[384,256]{1,0:T(8,128)(2,1)} %get-tuple-element.55.refs_1_) | copy-start | bytes 589828
  169.9 30.9 %copy-start.9 = (bf16[192,256]{1,0:T(8,128)(2,1)S(1)}, bf16[192,256]{1,0:T(8,128)(2,1)}, u32[]{:S(2)}) copy-start(bf16[192,256]{1,0:T(8,128)(2,1)} %get-tuple-element.54.refs_0_) | copy-start | bytes 294916
  169.9 30.7 %collective-permute-start.12 = (bf16[256,2048]{1,0:T(8,128)(2,1)S(1)}, bf16[256,2048]{1,0:T(8,128)(2,1)S(1)}, u32[]{:S(2)}, u32[]{:S(2)}) collective-permute-start(bf16[256,2048]{1,0:T(8,128)(2,1)S(1)} %pad_maximum_fusion.1), channel_id=1, source_target_pairs={{0,1},{1,2},{2,3},{3,0},{4,5},{5,6},{6,7},{7,4},{8,9},{9,10},{10,1... | collective-permute-start | bytes 3145736 | tf_op jit(solution)/shard_map/ppermute | solution.py:28
  175.7 25.0 %collective-permute-start.13 = (bf16[240,2048]{1,0:T(8,128)(2,1)S(1)}, bf16[240,2048]{1,0:T(8,128)(2,1)S(1)}, u32[]{:S(2)}, u32[]{:S(2)}) collective-permute-start(bf16[240,2048]{1,0:T(8,128)(2,1)S(1)} %pad_maximum_fusion.2), channel_id=1, source_target_pairs={{0,3},{1,0},{2,1},{3,2},{4,7},{5,4},{6,5},{7,6},{8,11},{9,8},{10,9... | collective-permute-start | bytes 2949128 | tf_op jit(solution)/shard_map/ppermute | solution.py:28
  (12 other events, 106.9 us)
